TPU v7x, 32 devices: a whole 2x2x4 slice. The times are simulated.
32 devices in a mesh: rows: 16 (over z, y, core), cols: 2 (over x).
Axes of the slice: x: 2, y: 2, z: 4, core: 2. Of those that a mesh axis runs over, the one named last changes fastest.
Arguments:
- features: bfloat16 [16, 256, 256], P('rows', 'cols'), may hold values from -48 to 48
- projection: bfloat16 [256, 512], replicated, may hold values from -1 to 1
- first_kernel: bfloat16 [3, 3, 256, 128], replicated, may hold values from -0.125 to 0.125
- second_kernel: bfloat16 [3, 3, 128, 128], replicated, may hold values from -0.1875 to 0.1875
- cotangent: bfloat16 [16, 256, 128], P('rows', 'cols'), may hold values from -6 to 6
Outputs:
- output_map: bfloat16 [16, 256, 128], P('rows', 'cols')
- input_grad: bfloat16 [16, 256, 256], P('rows', 'cols')
- projection_grad: float32 [256, 512], replicated
- first_grad: float32 [3, 3, 256, 128], replicated
- second_grad: float32 [3, 3, 128, 128], replicated
All inputs are finite; a program needn't handle non-finite values.
Results may differ from a plain program's by a relative error of at most 0.033.
Values may be sent and summed in bfloat16 or wider, within the bound.
No kernel may reach another device: no remote copies, remote signals or barrier semaphores. Data moves between devices by JAX's collectives and lax.ppermute only.
A program may use at most 64 MiB of HBM per device.

v0:
```python
import math

import jax
import jax.numpy as jnp
from jax import lax
from jax.sharding import PartitionSpec as P

QK = 128
VAL = 256
HEADS = 8


def with_halo(shard, sides, width):
    for axis, dim in sides:
        peers, length = (lax.axis_size(axis), shard.shape[dim])
        up = [(i, (i + 1) % peers) for i in range(peers - 1)]
        down = [(j, i) for i, j in up]
        last = lax.slice_in_dim(shard, length - width, length, axis=dim)
        first = lax.slice_in_dim(shard, 0, width, axis=dim)
        before = lax.ppermute(last, axis, up)
        after = lax.ppermute(first, axis, down)
        shard = jnp.concatenate([before, shard, after], axis=dim)
    return shard


def conv_apply(padded, kernel):
    rows_out = padded.shape[0] - 2
    cols_out = padded.shape[1] - 2
    result = jnp.zeros((rows_out, cols_out, kernel.shape[3]), jnp.float32)
    for tap_row in range(3):
        for tap_col in range(3):
            window = padded[tap_row : tap_row + rows_out, tap_col : tap_col + cols_out]
            result = result + jnp.einsum(
                "rwc,cd->rwd", window, kernel[tap_row, tap_col], preferred_element_type=jnp.float32
            )
    return result


def conv_transpose(padded, kernel):
    rows_out = padded.shape[0] - 2
    cols_out = padded.shape[1] - 2
    result = jnp.zeros((rows_out, cols_out, kernel.shape[2]), jnp.float32)
    for tap_row in range(3):
        for tap_col in range(3):
            window = padded[
                2 - tap_row : 2 - tap_row + rows_out, 2 - tap_col : 2 - tap_col + cols_out
            ]
            result = result + jnp.einsum(
                "rwd,cd->rwc", window, kernel[tap_row, tap_col], preferred_element_type=jnp.float32
            )
    return result


def kernel_grad(padded, upstream):
    rows_out = upstream.shape[0]
    cols_out = upstream.shape[1]
    taps = []
    for tap_row in range(3):
        for tap_col in range(3):
            window = padded[tap_row : tap_row + rows_out, tap_col : tap_col + cols_out]
            taps.append(
                jnp.einsum("rwc,rwd->cd", window, upstream, preferred_element_type=jnp.float32)
            )
    return jnp.stack(taps).reshape(3, 3, padded.shape[2], upstream.shape[2])


def silu_slope(pre_act):
    sigma = jax.nn.sigmoid(pre_act)
    return sigma * (1.0 + pre_act * (1.0 - sigma))


def body(features, projection, first_kernel, second_kernel, cotangent):
    height, across, channels = features.shape
    head_qk = QK // HEADS
    head_val = VAL // HEADS
    scaling = head_qk ** (-0.5)
    flattened = features.reshape(height * across, channels)
    packed = jnp.dot(flattened, projection, preferred_element_type=jnp.float32).astype(jnp.bfloat16)
    query_all = packed[:, :QK].reshape(height, across, HEADS, head_qk)
    key_all = packed[:, QK : 2 * QK].reshape(height, across, HEADS, head_qk)
    value_all = packed[:, 2 * QK :].reshape(height, across, HEADS, head_val)
    key_flat = packed[:, QK : 2 * QK].reshape(height, across, QK)
    value_flat = packed[:, 2 * QK :].reshape(height, across, VAL)
    initial = (
        jnp.full((height, HEADS, across), -1e30, jnp.float32),
        jnp.zeros((height, HEADS, across), jnp.float32),
        jnp.zeros((height, across, HEADS, head_val), jnp.float32),
    )
    pieces = (
        lax.all_gather(key_flat, "cols", axis=1, tiled=True),
        lax.all_gather(value_flat, "cols", axis=1, tiled=True),
    )
    piece_width = pieces[0].shape[1]
    key_rows = pieces[0].reshape(height, piece_width, HEADS, head_qk)
    value_rows = pieces[1].reshape(height, piece_width, HEADS, head_val)

    def one_row(row_items):
        maxima, totals, accumulated, query_row, key_row, value_row = row_items
        scores = scaling * jnp.einsum(
            "qhd,khd->hqk", query_row, key_row, preferred_element_type=jnp.float32
        )
        new_max = jnp.maximum(maxima, jnp.max(scores, axis=-1))
        exponent = jnp.exp(scores - new_max[:, :, None])
        rescale = jnp.exp(maxima - new_max)
        new_total = totals * rescale + jnp.sum(exponent, axis=-1)
        weighted = jnp.einsum(
            "hqk,khd->qhd",
            exponent.astype(jnp.bfloat16),
            value_row,
            preferred_element_type=jnp.float32,
        )
        return (new_max, new_total, accumulated * jnp.transpose(rescale)[:, :, None] + weighted)

    maxima, totals, accumulated = lax.map(
        one_row, (initial[0], initial[1], initial[2], query_all, key_rows, value_rows)
    )
    attended4 = (accumulated / jnp.transpose(totals, (0, 2, 1))[:, :, :, None]).astype(jnp.bfloat16)
    log_total = maxima + jnp.log(totals)
    attended = attended4.reshape(height, across, VAL)
    attended_pad = with_halo(attended, (("rows", 0), ("cols", 1)), 1)
    pre_act = conv_apply(attended_pad, first_kernel)
    hidden = jax.nn.silu(pre_act).astype(jnp.bfloat16)
    hidden_pad = with_halo(hidden, (("rows", 0), ("cols", 1)), 1)
    output_map = conv_apply(hidden_pad, second_kernel).astype(jnp.bfloat16)
    cotangent_pad = with_halo(cotangent, (("rows", 0), ("cols", 1)), 1)
    second_sum = kernel_grad(hidden_pad, cotangent)
    slope_pre = (conv_transpose(cotangent_pad, second_kernel) * silu_slope(pre_act)).astype(
        jnp.bfloat16
    )
    slope_pad = with_halo(slope_pre, (("rows", 0), ("cols", 1)), 1)
    first_sum = kernel_grad(attended_pad, slope_pre)
    upstream = conv_transpose(slope_pad, first_kernel).astype(jnp.bfloat16)
    upstream4 = upstream.reshape(height, across, HEADS, head_val)
    inner = jnp.transpose(
        jnp.sum(upstream4.astype(jnp.float32) * attended4.astype(jnp.float32), axis=-1), (0, 2, 1)
    )
    all_lse, all_inner = (
        lax.all_gather(log_total, "cols", axis=2, tiled=True),
        lax.all_gather(inner, "cols", axis=2, tiled=True),
    )
    pieces = (
        lax.all_gather(key_flat, "cols", axis=1, tiled=True),
        lax.all_gather(value_flat, "cols", axis=1, tiled=True),
    )
    piece_width = pieces[0].shape[1]
    key_rows = pieces[0].reshape(height, piece_width, HEADS, head_qk)
    value_rows = pieces[1].reshape(height, piece_width, HEADS, head_val)

    def one_row(row_items):
        accumulated, query_row, up_row, lse_row, inner_row, key_row, value_row = row_items
        scores = scaling * jnp.einsum(
            "qhd,khd->hqk", query_row, key_row, preferred_element_type=jnp.float32
        )
        soft = jnp.exp(scores - lse_row[:, :, None])
        slopes = jnp.einsum("qhd,khd->hqk", up_row, value_row, preferred_element_type=jnp.float32)
        dscore = (soft * (slopes - inner_row[:, :, None])).astype(jnp.bfloat16)
        return accumulated + scaling * jnp.einsum(
            "hqk,khd->qhd", dscore, key_row, preferred_element_type=jnp.float32
        )

    grad_query = lax.map(
        one_row,
        (
            jnp.zeros((height, across, HEADS, head_qk), jnp.float32),
            query_all,
            upstream4,
            log_total,
            inner,
            key_rows,
            value_rows,
        ),
    )
    pieces = (
        lax.all_gather(packed[:, :QK].reshape(height, across, QK), "cols", axis=1, tiled=True),
        lax.all_gather(upstream, "cols", axis=1, tiled=True),
    )
    piece_width = pieces[0].shape[1]
    query_rows = pieces[0].reshape(height, piece_width, HEADS, head_qk)
    up_rows = pieces[1].reshape(height, piece_width, HEADS, head_val)

    def one_row(row_items):
        key_sum, value_sum, query_row, up_row, lse_row, inner_row, key_row, value_row = row_items
        scores = scaling * jnp.einsum(
            "qhd,khd->hqk", query_row, key_row, preferred_element_type=jnp.float32
        )
        soft = jnp.exp(scores - lse_row[:, :, None])
        slopes = jnp.einsum("qhd,khd->hqk", up_row, value_row, preferred_element_type=jnp.float32)
        dscore = (soft * (slopes - inner_row[:, :, None])).astype(jnp.bfloat16)
        new_key = key_sum + scaling * jnp.einsum(
            "hqk,qhd->khd", dscore, query_row, preferred_element_type=jnp.float32
        )
        new_value = value_sum + jnp.einsum(
            "hqk,qhd->khd", soft.astype(jnp.bfloat16), up_row, preferred_element_type=jnp.float32
        )
        return (new_key, new_value)

    grad_key, grad_value = lax.map(
        one_row,
        (
            jnp.zeros((height, across, HEADS, head_qk), jnp.float32),
            jnp.zeros((height, across, HEADS, head_val), jnp.float32),
            query_rows,
            up_rows,
            all_lse,
            all_inner,
            key_all,
            value_all,
        ),
    )
    grad_packed = jnp.concatenate(
        [
            grad_query.reshape(height * across, QK),
            grad_key.reshape(height * across, QK),
            grad_value.reshape(height * across, VAL),
        ],
        axis=-1,
    ).astype(jnp.bfloat16)
    input_grad = jnp.dot(grad_packed, projection.T, preferred_element_type=jnp.float32).astype(
        jnp.bfloat16
    )
    projection_sum = jnp.einsum(
        "pc,pd->cd", flattened, grad_packed, preferred_element_type=jnp.float32
    )
    totals_all = lax.psum((projection_sum, first_sum, second_sum), ("rows", "cols"))
    pixel_count = height * across * lax.axis_size("rows") * lax.axis_size("cols")
    factor = 1.0 / math.sqrt(pixel_count)
    return (
        output_map,
        input_grad.reshape(height, across, channels),
        totals_all[0] * factor,
        totals_all[1] * factor,
        totals_all[2] * factor,
    )


def solution(mesh):
    placed = (P("rows", "cols", None), P(), P(), P(), P("rows", "cols", None))
    return jax.shard_map(
        body,
        mesh=mesh,
        in_specs=placed,
        out_specs=(P("rows", "cols", None), P("rows", "cols", None), P(), P(), P()),
        check_vma=False,
    )
```

profile of v0, /device:TPU:0, one launch (start us, length us, event | category | flops | bytes accessed | tf_op | source)
XLA Modules:
  0.0 262.9 jit_solution(10055088899137831039)
XLA Ops:
  7.2 1.4 collective-permute-start.9
  8.7 3.7 %collective-permute-start.8 = (bf16[1,128,128]{2,1,0:T(8,128)(2,1)}, bf16[1,128,128]{2,1,0:T(8,128)(2,1)}, u32[]{:S(2)}, u32[]{:S(2)}) collective-permute-start(bf16[1,128,128]{2,1,0:T(8,128)(2,1)} %param.9), channel_id=1, source_target_pairs={{0,2},{2,4},{4,6},{6,8},{8,10},{10,12},{12,14},{14,16},{16,18},{18... | collective-permute-start | bytes 98312 | tf_op jit(solution)/shard_map/ppermute | solution.py:20
  13.4 5.7 %all-gather = bf16[256,128]{1,0:T(8,128)(2,1)S(1)} all-gather(bf16[128,128]{1,0:T(8,128)(2,1)S(1)} %get-tuple-element.98), channel_id=2, replica_groups=mesh['rows'=16,'cols'=2] {'cols'}, dimensions={0}, use_global_device_ids=true | all-gather | bytes 98304 | tf_op jit(solution)/shard_map/all_gather | solution.py:90
  20.2 5.1 %all-gather.1 = bf16[256,256]{1,0:T(8,128)(2,1)S(1)} all-gather(bf16[128,256]{1,0:T(8,128)(2,1)S(1)} %slice.271), channel_id=3, replica_groups=mesh['rows'=16,'cols'=2] {'cols'}, dimensions={0}, use_global_device_ids=true | all-gather | bytes 196608 | tf_op jit(solution)/shard_map/all_gather | solution.py:91
  25.7 1.3 collective-permute-start.1
  27.0 3.0 %collective-permute-start = (bf16[1,128,256]{1,2,0:T(8,128)(2,1)S(1)}, bf16[1,128,256]{1,2,0:T(8,128)(2,1)S(1)}, u32[]{:S(2)}, u32[]{:S(2)}) collective-permute-start(bf16[1,128,256]{1,2,0:T(8,128)(2,1)S(1)} %bitcast.414), channel_id=1, source_target_pairs={{0,2},{2,4},{4,6},{6,8},{8,10},{10,12},{12,14},{14,16},{16,18},{18... | collective-permute-start | bytes 196616 | tf_op jit(solution)/shard_map/ppermute | solution.py:20
  30.2 4.6 %all-gather.2 = bf16[256,128]{1,0:T(8,128)(2,1)S(1)} all-gather(bf16[128,128]{1,0:T(8,128)(2,1)S(1)} %get-tuple-element.99), channel_id=4, replica_groups=mesh['rows'=16,'cols'=2] {'cols'}, dimensions={0}, use_global_device_ids=true | all-gather | bytes 98304 | tf_op jit(solution)/shard_map/all_gather | solution.py:174
  34.9 4.3 %all_gather.23 = f32[1,8,256]{2,1,0:T(8,128)S(1)} all-gather(f32[1,8,128]{2,1,0:T(8,128)S(1)} %get-tuple-element.112), channel_id=1, replica_groups=mesh['rows'=16,'cols'=2] {'cols'}, dimensions={2}, use_global_device_ids=true | all-gather | bytes 12288 | tf_op jit(solution)/shard_map/all_gather | solution.py:138
  40.6 1.5 fusion.194
  44.5 1.3 collective-permute-start.10
  45.8 4.5 %collective-permute-start.11 = (bf16[3,1,128]{2,1,0:T(2,128)(2,1)S(1)}, bf16[3,1,128]{2,1,0:T(2,128)(2,1)S(1)}, u32[]{:S(2)}, u32[]{:S(2)}) collective-permute-start(bf16[3,1,128]{2,1,0:T(2,128)(2,1)S(1)} %get-tuple-element.109), channel_id=1, source_target_pairs={{0,1},{2,3},{4,5},{6,7},{8,9},{10,11},{12,13},{14,15},{16,17},{18,... | collective-permute-start | bytes 2312 | tf_op jit(solution)/shard_map/ppermute | solution.py:20
  56.3 3.6 %collective-permute-start.2 = (bf16[3,1,256]{1,2,0:T(8,128)(2,1)S(1)}, bf16[3,1,256]{1,2,0:T(8,128)(2,1)S(1)}, u32[]{:S(2)}, u32[]{:S(2)}) collective-permute-start(bf16[3,1,256]{1,2,0:T(8,128)(2,1)S(1)} %get-tuple-element.96), channel_id=1, source_target_pairs={{0,1},{2,3},{4,5},{6,7},{8,9},{10,11},{12,13},{14,15},{16,17},{18,... | collective-permute-start | bytes 4616 | tf_op jit(solution)/shard_map/ppermute | solution.py:20
  59.9 1.4 collective-permute-start.3
  61.8 1.3 collective-permute-done.2
  63.6 4.0 %collective-permute-done.3 = bf16[3,1,256]{1,2,0:T(8,128)(2,1)S(1)} collective-permute-done((bf16[3,1,256]{1,2,0:T(8,128)(2,1)S(1)}, bf16[3,1,256]{1,2,0:T(8,128)(2,1)S(1)}, u32[]{:S(2)}, u32[]{:S(2)}) %collective-permute-start.3) | collective-permute-done | bytes 1568 | tf_op jit(solution)/shard_map/ppermute | solution.py:21
  70.0 3.0 %collective-permute-start.4 = (bf16[1,128,128]{2,1,0:T(8,128)(2,1)S(1)}, bf16[1,128,128]{2,1,0:T(8,128)(2,1)S(1)}, u32[]{:S(2)}, u32[]{:S(2)}) collective-permute-start(bf16[1,128,128]{2,1,0:T(8,128)(2,1)S(1)} %bitcast.426), channel_id=1, source_target_pairs={{0,2},{2,4},{4,6},{6,8},{8,10},{10,12},{12,14},{14,16},{16,18},{18... | collective-permute-start | bytes 98312 | tf_op jit(solution)/shard_map/ppermute | solution.py:20
  74.5 4.0 %collective-permute-start.12 = (bf16[1,128,128]{2,1,0:T(8,128)(2,1)S(1)}, bf16[1,128,128]{2,1,0:T(8,128)(2,1)S(1)}, u32[]{:S(2)}, u32[]{:S(2)}) collective-permute-start(bf16[1,128,128]{2,1,0:T(8,128)(2,1)S(1)} %bitcast.405), channel_id=1, source_target_pairs={{0,2},{2,4},{4,6},{6,8},{8,10},{10,12},{12,14},{14,16},{16,18},{18... | collective-permute-start | bytes 98312 | tf_op jit(solution)/shard_map/ppermute | solution.py:20
  81.5 2.0 collective-permute-start.6
  86.1 4.5 %collective-permute-start.15 = (bf16[3,1,128]{2,1,0:T(2,128)(2,1)S(1)}, bf16[3,1,128]{2,1,0:T(2,128)(2,1)S(1)}, u32[]{:S(2)}, u32[]{:S(2)}) collective-permute-start(bf16[3,1,128]{2,1,0:T(2,128)(2,1)S(1)} %get-tuple-element.107), channel_id=1, source_target_pairs={{0,1},{2,3},{4,5},{6,7},{8,9},{10,11},{12,13},{14,15},{16,17},{18,... | collective-permute-start | bytes 2312 | tf_op jit(solution)/shard_map/ppermute | solution.py:20
  93.6 5.6 %all-gather.3 = bf16[256,256]{1,0:T(8,128)(2,1)S(1)} all-gather(bf16[128,256]{1,0:T(8,128)(2,1)S(1)} %fusion.25), channel_id=5, replica_groups=mesh['rows'=16,'cols'=2] {'cols'}, dimensions={0}, use_global_device_ids=true | all-gather | bytes 196608 | tf_op jit(solution)/shard_map/all_gather | solution.py:175
  100.0 1.5 fusion.218
  101.6 4.3 %all_gather.25 = f32[1,8,256]{2,1,0:T(8,128)S(1)} all-gather(f32[1,8,128]{2,1,0:T(8,128)S(1)} %bitcast.445), channel_id=1, replica_groups=mesh['rows'=16,'cols'=2] {'cols'}, dimensions={2}, use_global_device_ids=true | all-gather | bytes 12288 | tf_op jit(solution)/shard_map/all_gather | solution.py:139
  110.9 1.5 fusion.60
  117.4 134.5 %all-reduce.3.cloned.1.call-done = (f32[256,512]{0,1:T(8,128)}, f32[3,3,256,128]{3,2,1,0:T(8,128)}, f32[3,3,128,128]{3,2,1,0:T(8,128)}) async-done(((f32[256,512]{0,1:T(8,128)}, f32[3,3,256,128]{3,2,1,0:T(8,128)}, f32[3,3,128,128]{3,2,1,0:T(8,128)}), (f32[256,512]{0,1:T(8,128)}, f32[3,3,256,128]{3,2,1,0:T(8,128)}, f32[3,3,128,128]{3,2,1,0:T(8,128)})) %all-reduce.3.cloned.1.call-update) | async-done | bytes 2293776 | tf_op jit(solution)/shard_map/psum | solution.py:224
  (167 shorter events, 40.1 us)
Async XLA Ops:
  7.2 5.1 %copy-start = (bf16[256,512]{1,0:T(8,128)(2,1)S(1)}, bf16[256,512]{1,0:T(8,128)(2,1)}, u32[]{:S(2)}) copy-start(bf16[256,512]{1,0:T(8,128)(2,1)} %param.6) | copy-start | bytes 786436
  7.2 244.7 %all-reduce.3.cloned.1.call-start = ((), (), s32[]{:S(2)}) async-start(), calls=%async_computation | async-start | bytes 4587520 | tf_op jit(solution)/shard_map/psum | solution.py:224
  7.2 36.5 %collective-permute-start.9 = (bf16[1,128,128]{2,1,0:T(8,128)(2,1)}, bf16[1,128,128]{2,1,0:T(8,128)(2,1)}, u32[]{:S(2)}, u32[]{:S(2)}) collective-permute-start(bf16[1,128,128]{2,1,0:T(8,128)(2,1)} %param.9), channel_id=1, source_target_pairs={{2,0},{4,2},{6,4},{8,6},{10,8},{12,10},{14,12},{16,14},{18,16},{20... | collective-permute-start | bytes 98312 | tf_op jit(solution)/shard_map/ppermute | solution.py:21
  8.7 34.2 %collective-permute-start.8 = (bf16[1,128,128]{2,1,0:T(8,128)(2,1)}, bf16[1,128,128]{2,1,0:T(8,128)(2,1)}, u32[]{:S(2)}, u32[]{:S(2)}) collective-permute-start(bf16[1,128,128]{2,1,0:T(8,128)(2,1)} %param.9), channel_id=1, source_target_pairs={{0,2},{2,4},{4,6},{6,8},{8,10},{10,12},{12,14},{14,16},{16,18},{18... | collective-permute-start | bytes 98312 | tf_op jit(solution)/shard_map/ppermute | solution.py:20
  20.1 19.1 %copy-start.2 = (bf16[3,3,256,128]{3,2,1,0:T(8,128)(2,1)S(1)}, bf16[3,3,256,128]{3,2,1,0:T(8,128)(2,1)}, u32[]{:S(2)}) copy-start(bf16[3,3,256,128]{3,2,1,0:T(8,128)(2,1)} %param.7) | copy-start | bytes 1769476
  25.4 15.2 %copy-start.1 = (bf16[1,128,128]{2,1,0:T(8,128)(2,1)S(1)}, bf16[1,128,128]{2,1,0:T(8,128)(2,1)}, u32[]{:S(2)}) copy-start(bf16[1,128,128]{2,1,0:T(8,128)(2,1)} %param.9) | copy-start | bytes 98308
  25.7 30.4 %collective-permute-start.1 = (bf16[1,128,256]{1,2,0:T(8,128)(2,1)S(1)}, bf16[1,128,256]{1,2,0:T(8,128)(2,1)S(1)}, u32[]{:S(2)}, u32[]{:S(2)}) collective-permute-start(bf16[1,128,256]{1,2,0:T(8,128)(2,1)S(1)} %bitcast.413), channel_id=1, source_target_pairs={{2,0},{4,2},{6,4},{8,6},{10,8},{12,10},{14,12},{16,14},{18,16},{20... | collective-permute-start | bytes 196616 | tf_op jit(solution)/shard_map/ppermute | solution.py:21
  27.0 29.1 %collective-permute-start = (bf16[1,128,256]{1,2,0:T(8,128)(2,1)S(1)}, bf16[1,128,256]{1,2,0:T(8,128)(2,1)S(1)}, u32[]{:S(2)}, u32[]{:S(2)}) collective-permute-start(bf16[1,128,256]{1,2,0:T(8,128)(2,1)S(1)} %bitcast.414), channel_id=1, source_target_pairs={{0,2},{2,4},{4,6},{6,8},{8,10},{10,12},{12,14},{14,16},{16,18},{18... | collective-permute-start | bytes 196616 | tf_op jit(solution)/shard_map/ppermute | solution.py:20
  42.9 13.1 %copy-start.5 = (bf16[3,3,128,128]{3,2,1,0:T(8,128)(2,1)S(1)}, bf16[3,3,128,128]{3,2,1,0:T(8,128)(2,1)}, u32[]{:S(2)}) copy-start(bf16[3,3,128,128]{3,2,1,0:T(8,128)(2,1)} %param.8) | copy-start | bytes 884740
  44.5 9.5 %collective-permute-start.10 = (bf16[3,1,128]{2,1,0:T(2,128)(2,1)S(1)}, bf16[3,1,128]{2,1,0:T(2,128)(2,1)S(1)}, u32[]{:S(2)}, u32[]{:S(2)}) collective-permute-start(bf16[3,1,128]{2,1,0:T(2,128)(2,1)S(1)} %get-tuple-element.108), channel_id=1, source_target_pairs={{1,0},{3,2},{5,4},{7,6},{9,8},{11,10},{13,12},{15,14},{17,16},{19,... | collective-permute-start | bytes 2312 | tf_op jit(solution)/shard_map/ppermute | solution.py:21
  45.8 6.4 %collective-permute-start.11 = (bf16[3,1,128]{2,1,0:T(2,128)(2,1)S(1)}, bf16[3,1,128]{2,1,0:T(2,128)(2,1)S(1)}, u32[]{:S(2)}, u32[]{:S(2)}) collective-permute-start(bf16[3,1,128]{2,1,0:T(2,128)(2,1)S(1)} %get-tuple-element.109), channel_id=1, source_target_pairs={{0,1},{2,3},{4,5},{6,7},{8,9},{10,11},{12,13},{14,15},{16,17},{18,... | collective-permute-start | bytes 2312 | tf_op jit(solution)/shard_map/ppermute | solution.py:20
  56.3 6.8 %collective-permute-start.2 = (bf16[3,1,256]{1,2,0:T(8,128)(2,1)S(1)}, bf16[3,1,256]{1,2,0:T(8,128)(2,1)S(1)}, u32[]{:S(2)}, u32[]{:S(2)}) collective-permute-start(bf16[3,1,256]{1,2,0:T(8,128)(2,1)S(1)} %get-tuple-element.96), channel_id=1, source_target_pairs={{0,1},{2,3},{4,5},{6,7},{8,9},{10,11},{12,13},{14,15},{16,17},{18,... | collective-permute-start | bytes 4616 | tf_op jit(solution)/shard_map/ppermute | solution.py:20
  59.9 8.3 %copy-start.21 = (f32[128,128]{1,0:T(8,128)S(1)}, f32[128,128]{1,0:T(8,128)}, u32[]{:S(2)}) copy-start(f32[128,128]{1,0:T(8,128)} %fusion.93) | copy-start | bytes 196612
  59.9 7.7 %collective-permute-start.3 = (bf16[3,1,256]{1,2,0:T(8,128)(2,1)S(1)}, bf16[3,1,256]{1,2,0:T(8,128)(2,1)S(1)}, u32[]{:S(2)}, u32[]{:S(2)}) collective-permute-start(bf16[3,1,256]{1,2,0:T(8,128)(2,1)S(1)} %get-tuple-element.97), channel_id=1, source_target_pairs={{1,0},{3,2},{5,4},{7,6},{9,8},{11,10},{13,12},{15,14},{17,16},{19,... | collective-permute-start | bytes 4616 | tf_op jit(solution)/shard_map/ppermute | solution.py:21
  68.7 12.3 %collective-permute-start.5 = (bf16[1,128,128]{2,1,0:T(8,128)(2,1)S(1)}, bf16[1,128,128]{2,1,0:T(8,128)(2,1)S(1)}, u32[]{:S(2)}, u32[]{:S(2)}) collective-permute-start(bf16[1,128,128]{2,1,0:T(8,128)(2,1)S(1)} %bitcast.425), channel_id=1, source_target_pairs={{2,0},{4,2},{6,4},{8,6},{10,8},{12,10},{14,12},{16,14},{18,16},{20... | collective-permute-start | bytes 98312 | tf_op jit(solution)/shard_map/ppermute | solution.py:21
  70.0 11.0 %collective-permute-start.4 = (bf16[1,128,128]{2,1,0:T(8,128)(2,1)S(1)}, bf16[1,128,128]{2,1,0:T(8,128)(2,1)S(1)}, u32[]{:S(2)}, u32[]{:S(2)}) collective-permute-start(bf16[1,128,128]{2,1,0:T(8,128)(2,1)S(1)} %bitcast.426), channel_id=1, source_target_pairs={{0,2},{2,4},{4,6},{6,8},{8,10},{10,12},{12,14},{14,16},{16,18},{18... | collective-permute-start | bytes 98312 | tf_op jit(solution)/shard_map/ppermute | solution.py:20
  73.2 11.6 %collective-permute-start.13 = (bf16[1,128,128]{2,1,0:T(8,128)(2,1)S(1)}, bf16[1,128,128]{2,1,0:T(8,128)(2,1)S(1)}, u32[]{:S(2)}, u32[]{:S(2)}) collective-permute-start(bf16[1,128,128]{2,1,0:T(8,128)(2,1)S(1)} %bitcast.404), channel_id=1, source_target_pairs={{2,0},{4,2},{6,4},{8,6},{10,8},{12,10},{14,12},{16,14},{18,16},{20... | collective-permute-start | bytes 98312 | tf_op jit(solution)/shard_map/ppermute | solution.py:21
  74.5 10.3 %collective-permute-start.12 = (bf16[1,128,128]{2,1,0:T(8,128)(2,1)S(1)}, bf16[1,128,128]{2,1,0:T(8,128)(2,1)S(1)}, u32[]{:S(2)}, u32[]{:S(2)}) collective-permute-start(bf16[1,128,128]{2,1,0:T(8,128)(2,1)S(1)} %bitcast.405), channel_id=1, source_target_pairs={{0,2},{2,4},{4,6},{6,8},{8,10},{10,12},{12,14},{14,16},{16,18},{18... | collective-permute-start | bytes 98312 | tf_op jit(solution)/shard_map/ppermute | solution.py:20
  80.0 13.4 %copy-start.3 = (f32[9,256,128]{2,1,0:T(8,128)}, f32[9,256,128]{2,1,0:T(8,128)S(1)}, u32[]{:S(2)}) copy-start(f32[9,256,128]{2,1,0:T(8,128)S(1)} %fusion.10) | copy-start | bytes 3538948
  81.5 24.5 %collective-permute-start.6 = (bf16[3,1,128]{2,1,0:T(2,128)(2,1)}, bf16[3,1,128]{2,1,0:T(2,128)(2,1)}, u32[]{:S(2)}, u32[]{:S(2)}) collective-permute-start(bf16[3,1,128]{2,1,0:T(2,128)(2,1)} %get-tuple-element.110), channel_id=1, source_target_pairs={{0,1},{2,3},{4,5},{6,7},{8,9},{10,11},{12,13},{14,15},{16,17},{18,... | collective-permute-start | bytes 2312 | tf_op jit(solution)/shard_map/ppermute | solution.py:20
  83.5 15.8 %collective-permute-start.7 = (bf16[3,1,128]{2,1,0:T(2,128)(2,1)}, bf16[3,1,128]{2,1,0:T(2,128)(2,1)S(1)}, u32[]{:S(2)}, u32[]{:S(2)}) collective-permute-start(bf16[3,1,128]{2,1,0:T(2,128)(2,1)} %get-tuple-element.111), channel_id=1, source_target_pairs={{1,0},{3,2},{5,4},{7,6},{9,8},{11,10},{13,12},{15,14},{17,16},{19,... | collective-permute-start | bytes 2312 | tf_op jit(solution)/shard_map/ppermute | solution.py:21
  84.8 8.1 %collective-permute-start.14 = (bf16[3,1,128]{2,1,0:T(2,128)(2,1)S(1)}, bf16[3,1,128]{2,1,0:T(2,128)(2,1)S(1)}, u32[]{:S(2)}, u32[]{:S(2)}) collective-permute-start(bf16[3,1,128]{2,1,0:T(2,128)(2,1)S(1)} %get-tuple-element.106), channel_id=1, source_target_pairs={{1,0},{3,2},{5,4},{7,6},{9,8},{11,10},{13,12},{15,14},{17,16},{19,... | collective-permute-start | bytes 2312 | tf_op jit(solution)/shard_map/ppermute | solution.py:21
  86.1 6.4 %collective-permute-start.15 = (bf16[3,1,128]{2,1,0:T(2,128)(2,1)S(1)}, bf16[3,1,128]{2,1,0:T(2,128)(2,1)S(1)}, u32[]{:S(2)}, u32[]{:S(2)}) collective-permute-start(bf16[3,1,128]{2,1,0:T(2,128)(2,1)S(1)} %get-tuple-element.107), channel_id=1, source_target_pairs={{0,1},{2,3},{4,5},{6,7},{8,9},{10,11},{12,13},{14,15},{16,17},{18,... | collective-permute-start | bytes 2312 | tf_op jit(solution)/shard_map/ppermute | solution.py:20
  101.6 8.2 %copy-start.13 = (bf16[128,128]{1,0:T(8,128)(2,1)S(1)}, bf16[128,128]{1,0:T(8,128)(2,1)}, u32[]{:S(2)}) copy-start(bf16[128,128]{1,0:T(8,128)(2,1)} %get-tuple-element.102) | copy-start | bytes 98308
  (21 other events, 38.0 us)
Sparse Core Ops, SparseCore 0:
  114.5 137.4 all-reduce.2
where the time goes:
time: 264 us; the launch traced here: 263 us
  waiting for transfers between devices  140 us (53%)
  starting transfers between devices  39 us (15%)
  blocking collectives  29.6 us (11%)
  matrix products  28.2 us (11%)
  between operations  14.9 us (6%)
  other arithmetic  5.82 us (2%)
  local copies, waits for them, and re-layouts  5.43 us (2%)
    psum x1, waiting for transfers between devices, body(): lax.psum((projection_sum, first_sum, second_sum), ('rows', 'cols'))  134 us
    ppermute x8, starting transfers between devices, with_halo(): before = lax.ppermute(last, axis, up)  28.4 us
    ppermute x8, starting transfers between devices, with_halo(): after = lax.ppermute(first, axis, down)  10.6 us
    dot_general x18, matrix products, conv_transpose(): jnp.einsum('rwd,cd->rwc', window, kernel[tap_row, tap_col], preferred_ele...  8.89 us
    dot_general x18, matrix products, conv_apply(): jnp.einsum('rwc,cd->rwd', window, kernel[tap_row, tap_col], preferred_ele...  7.7 us
    all_gather x1, blocking collectives, body(): lax.all_gather(key_flat, 'cols', axis=1, tiled=True)  5.7 us
    all_gather x1, blocking collectives, body(): lax.all_gather(upstream, 'cols', axis=1, tiled=True)  5.59 us
  transfers between devices with their start and end apart: 17, of which 3 were waited for; matrix products, arithmetic and copies ran while one was open for 10% of the time, Pallas kernels for 0%

commit v1 on v0

v1 whole, which is shorter than its diff:
```python
import functools
import math

import jax
import jax.numpy as jnp
from jax import lax
from jax.experimental import pallas as pl
from jax.experimental.pallas import tpu as pltpu
from jax.sharding import PartitionSpec as P

QK = 128
VAL = 256
HEADS = 8
CONV = 128
HEAD_QK = QK // HEADS
HEAD_VAL = VAL // HEADS
PACKED = 2 * QK + VAL
BLOCK = 256
BF = jnp.bfloat16
F32 = jnp.float32
SCALING = HEAD_QK ** (-0.5)

PARTS = 8
FIRST_ROWS = 9 * VAL // PARTS
SECOND_ROWS = 9 * CONV // PARTS


def mm(a, b):
    return lax.dot_general(a, b, (((1,), (0,)), ((), ())), preferred_element_type=F32)


def mm_t(a, b):
    return lax.dot_general(a, b, (((1,), (1,)), ((), ())), preferred_element_type=F32)


def one_hot(shape, wanted):
    rows = lax.broadcasted_iota(jnp.int32, shape, 0)
    columns = lax.broadcasted_iota(jnp.int32, shape, 1)
    return jnp.where(columns == wanted(rows), 1.0, 0.0).astype(BF)


def identity(size):
    return one_hot((size, size), lambda rows: rows)


def head_of(values, head, width):
    lanes = lax.broadcasted_iota(jnp.int32, values.shape, 1)
    return jnp.where(lanes // width == head, values, jnp.zeros_like(values))


def moved(values, step):
    count = values.shape[0]
    turned = pltpu.roll(values, (-step) % count, 0)
    at = lax.broadcasted_iota(jnp.int32, values.shape, 0)
    return jnp.where(at == (count - 1 if step > 0 else 0), 0.0, turned)


def for_blocks(count, run):
    if count == 1:
        run(0)
    else:
        lax.fori_loop(0, count, lambda i, carry: (run(i), carry)[1], 0)


def block_at(index):
    return pl.ds(index if isinstance(index, int) else pl.multiple_of(index * BLOCK, BLOCK), BLOCK)


def forward_kernel(whole, *refs):
    pieces = refs[: 1 if whole else 2]
    projection, comb, local, lse, values_t = refs[len(pieces) :]
    across = comb.shape[0]
    for which, piece in enumerate(pieces):
        width = piece.shape[0]
        if whole:
            at = pl.ds(0, width)
        else:
            place = lax.rem(lax.axis_index("cols") + which, 2)
            at = pl.ds(pl.multiple_of(place * width, width), width)
        local[at, PACKED:] = piece[:, :VAL]
        comb[at, VAL:] = piece[:, VAL:]
    packed = mm(local[:, PACKED:], projection[...]).astype(BF)
    local[:, :PACKED] = packed
    keys = packed[:, QK : 2 * QK]
    values_t[...] = mm_t(identity(VAL), packed[:, 2 * QK :]).astype(BF)

    def block(index):
        at = block_at(index)
        queries = local[at, :QK]
        rows = []
        for head in range(HEADS):
            scores = SCALING * mm_t(head_of(keys, head, HEAD_QK), queries)
            maxima = jnp.max(scores, axis=0, keepdims=True)
            exponent = jnp.exp(scores - maxima)
            totals = jnp.sum(exponent, axis=0, keepdims=True)
            weighted = mm(values_t[head * HEAD_VAL : (head + 1) * HEAD_VAL, :], exponent.astype(BF))
            rows.append((weighted / totals).astype(BF))
            lse[head : head + 1, at] = maxima + jnp.log(totals)
        comb[at, :VAL] = mm_t(identity(BLOCK), jnp.concatenate(rows, axis=0)).astype(BF)

    for_blocks(across // BLOCK, block)


def backward_kernel(
    near2,
    near1,
    own,
    mate,
    mate1,
    local,
    lse,
    projection,
    first_kernel,
    second_kernel,
    output_map,
    input_grad,
    keep,
    send,
    proj_own,
    proj_mate,
    wide,
    upstream_ref,
    grad_t,
):
    across = own.shape[0]
    part_width = output_map.shape[0]
    row = lax.axis_index("rows")
    col = lax.axis_index("cols")
    core = lax.rem(row, 2)
    chip_bit = lax.rem(row // 2, 2)
    col_bit = lax.rem(col, 2)
    quarter = 2 * core + col_bit
    other_quarter = 2 * (1 - core) + col_bit
    inside = jnp.where(core == 0, row > 0, row < lax.axis_size("rows") - 1)
    slots = (near2, near1, own, mate, mate1)
    taps = [tap + core * (2 - 2 * tap) for tap in range(3)]

    def attended(slot):
        return slots[slot][:, :VAL]

    def cotangent(slot):
        return slots[slot][:, VAL:]

    def side(total, width, sign):
        left = moved(total[:, :width], -sign)
        right = moved(total[:, 2 * width :], sign)
        return left + total[:, width : 2 * width] + right

    def spread(values):
        return jnp.concatenate(
            [moved(values, 1).astype(BF), values.astype(BF), moved(values, -1).astype(BF)], axis=1
        )

    def beside(weights, tap):
        return jnp.concatenate([weights[taps[tap], b] for b in range(3)], axis=1)

    def stacked(weights, tap):
        return jnp.concatenate([weights[taps[tap], b] for b in range(3)], axis=0)

    hidden = {}
    slope = {}
    for slot in (1, 2, 3):
        pre = side(sum(mm(attended(slot + a - 1), beside(first_kernel, a)) for a in range(3)), CONV, 1)
        back = side(sum(mm_t(cotangent(slot + 1 - a), stacked(second_kernel, a)) for a in range(3)), CONV, -1)
        sigma = 1.0 / (1.0 + jnp.exp(-pre))
        hidden_wide = pre * sigma
        slope_wide = back * (sigma * (1.0 + pre * (1.0 - sigma)))
        if slot == 1:
            hidden_wide = jnp.where(inside, hidden_wide, 0.0)
            slope_wide = jnp.where(inside, slope_wide, 0.0)
        hidden[slot] = hidden_wide.astype(BF)
        slope[slot] = slope_wide

    wide[...] = side(sum(mm(hidden[1 + a], beside(second_kernel, a)) for a in range(3)), CONV, 1)
    mine = pl.ds(pl.multiple_of(col * part_width, part_width), part_width)
    output_map[...] = wide[mine, :].astype(BF)

    upstream_ref[...] = side(
        sum(mm_t(slope[3 - a].astype(BF), stacked(first_kernel, a)) for a in range(3)), VAL, -1
    ).astype(BF)

    def chosen(total, which):
        size = total // 4
        half = size // 2

        def wanted(rows):
            swapped = jnp.where(rows < half, rows + half, rows - half)
            return which * size + jnp.where(chip_bit == 0, rows, swapped)

        return one_hot((size, total), wanted)

    pick = chosen(VAL, quarter)
    attended_t = {slot: mm_t(pick, attended(slot)).astype(BF) for slot in (1, 2, 3, 4)}
    spread_slope = {slot: spread(slope[slot]) for slot in (2, 3)}
    step = VAL // PARTS
    for a in range(3):
        total = sum(mm(attended_t[slot + a - 1], spread_slope[slot]) for slot in (2, 3)).astype(BF)
        for b in range(3):
            at = pl.ds(pl.multiple_of((taps[a] * 3 + b) * step, step), step)
            keep[at, :] = total[:step, b * CONV : (b + 1) * CONV]
            send[at, :] = total[step:, b * CONV : (b + 1) * CONV]
    pick = chosen(CONV, quarter)
    hidden_t = {slot: mm_t(pick, hidden[slot]).astype(BF) for slot in (2, 3)}
    spread_cot = {slot: spread(cotangent(slot).astype(F32)) for slot in (1, 2, 3, 4)}
    step = CONV // PARTS
    for a in range(3):
        total = sum(mm(hidden_t[slot], spread_cot[slot + 1 - a]) for slot in (2, 3)).astype(BF)
        for b in range(3):
            at = pl.ds(pl.multiple_of(FIRST_ROWS + (taps[a] * 3 + b) * step, step), step)
            keep[at, :] = total[:step, b * CONV : (b + 1) * CONV]
            send[at, :] = total[step:, b * CONV : (b + 1) * CONV]

    keys = local[:, QK : 2 * QK]
    values = local[:, 2 * QK : PACKED]
    keys_t = mm_t(identity(QK), keys).astype(BF)
    blocks = across // BLOCK
    if blocks > 1:
        grad_t[...] = jnp.zeros_like(grad_t)

    def add_rows(start, count, terms):
        if blocks > 1:
            grad_t[start : start + count, :] += terms
        else:
            grad_t[start : start + count, :] = terms

    def block(index):
        at = block_at(index)
        queries = local[at, :QK]
        upstream = upstream_ref[at, :]
        queries_t = mm_t(identity(QK), queries).astype(BF)
        upstream_t = mm_t(identity(VAL), upstream)
        products = upstream_t * mm_t(identity(VAL), own[at, :VAL])
        upstream_t = upstream_t.astype(BF)
        for head in range(HEADS):
            qk_rows = slice(head * HEAD_QK, (head + 1) * HEAD_QK)
            val_rows = slice(head * HEAD_VAL, (head + 1) * HEAD_VAL)
            scores = SCALING * mm_t(head_of(keys, head, HEAD_QK), queries)
            soft = jnp.exp(scores - lse[head : head + 1, at])
            inner = jnp.sum(products[val_rows, :], axis=0, keepdims=True)
            slopes = mm_t(head_of(values, head, HEAD_VAL), upstream)
            dscore = (soft * (slopes - inner)).astype(BF)
            grad_t[qk_rows, at] = SCALING * mm(keys_t[qk_rows, :], dscore)
            add_rows(QK + head * HEAD_QK, HEAD_QK, SCALING * mm_t(queries_t[qk_rows, :], dscore))
            add_rows(2 * QK + head * HEAD_VAL, HEAD_VAL, mm_t(upstream_t[val_rows, :], soft.astype(BF)))

    for_blocks(blocks, block)

    grad = grad_t[...].astype(BF)
    own_pixels = one_hot((part_width, across), lambda rows: rows + col * part_width)
    grad_own = mm_t(own_pixels, grad).astype(BF)
    input_grad[...] = mm_t(grad_own, projection[...]).astype(BF)
    features = local[:, PACKED:]
    step = VAL // PARTS
    for target, which in ((proj_own, quarter), (proj_mate, other_quarter)):
        features_t = mm_t(chosen(VAL, which), features).astype(BF)
        total = mm_t(features_t, grad).astype(BF)
        for j in range(PACKED // CONV):
            target[0, j * step : (j + 1) * step, :] = total[:step, j * CONV : (j + 1) * CONV]
            target[1, j * step : (j + 1) * step, :] = total[step:, j * CONV : (j + 1) * CONV]


def unpack_kernel(factor, *refs):
    pieces = refs[:8]
    projection_grad, first_grad, second_grad = refs[8:]
    row = lax.axis_index("rows")
    core = lax.rem(row, 2)
    chip_bit = lax.rem(row // 2, 2)
    col_bit = lax.rem(lax.axis_index("cols"), 2)
    for which, piece in enumerate(pieces):
        core_flip, col_flip, chip_flip = which // 4, which // 2 % 2, which % 2
        part = (
            4 * lax.rem(core + core_flip, 2) + 2 * lax.rem(col_bit + col_flip, 2) + lax.rem(chip_bit + chip_flip, 2)
        )
        step = VAL // PARTS
        at = pl.ds(pl.multiple_of(part * step, step), step)
        for tap in range(9):
            first_grad[tap // 3, tap % 3, at, :] = piece[tap * step : (tap + 1) * step, :].astype(F32) * factor
        start = FIRST_ROWS + SECOND_ROWS
        for j in range(PACKED // CONV):
            projection_grad[at, j * CONV : (j + 1) * CONV] = (
                piece[start + j * step : start + (j + 1) * step, :].astype(F32) * factor
            )
        step = CONV // PARTS
        at = pl.ds(pl.multiple_of(part * step, step), step)
        for tap in range(9):
            begin = FIRST_ROWS + tap * step
            second_grad[tap // 3, tap % 3, at, :] = piece[begin : begin + step, :].astype(F32) * factor


def shape(*dims, dtype=BF):
    return jax.ShapeDtypeStruct(dims, dtype)


PARAMS = dict(compiler_params=pltpu.CompilerParams(vmem_limit_bytes=52 * 1024 * 1024))
VMEM = pl.BlockSpec(memory_space=pltpu.VMEM)


def body(features, projection, first_kernel, second_kernel, cotangent):
    height, part_width, channels = features.shape
    rows_size = lax.axis_size("rows")
    cols_size = lax.axis_size("cols")
    across = part_width * cols_size
    flat = PACKED // CONV * (VAL // PARTS)

    def rows_flip(values, bit):
        return lax.ppermute(values, "rows", [(i, i ^ bit) for i in range(rows_size)])

    def cols_flip(values):
        return lax.ppermute(values, "cols", [(i, i ^ 1) for i in range(cols_size)])

    both = jnp.concatenate([features[0], cotangent[0]], axis=-1)
    if cols_size == 2:
        pieces = (both, cols_flip(both))
    else:
        pieces = (lax.all_gather(both, "cols", axis=0, tiled=True),)
    own, local, lse = pl.pallas_call(
        functools.partial(forward_kernel, cols_size != 2),
        out_shape=(
            shape(across, VAL + CONV),
            shape(across, PACKED + channels),
            shape(HEADS, across, dtype=F32),
        ),
        in_specs=[VMEM] * (len(pieces) + 1),
        out_specs=[VMEM] * 3,
        scratch_shapes=[pltpu.VMEM((VAL, across), BF)],
        name="attention_forward",
        **PARAMS,
    )(*pieces, projection)

    far = [(i, i + 2) for i in range(0, rows_size - 2, 2)] + [(i, i - 2) for i in range(3, rows_size, 2)]
    near = [(i, i + 1) for i in range(1, rows_size - 1, 2)] + [(i + 1, i) for i in range(1, rows_size - 1, 2)]
    near1 = lax.ppermute(own, "rows", near)
    near2 = lax.ppermute(own, "rows", far)
    mate = rows_flip(own, 1)
    mate1 = rows_flip(near1, 1)

    output_map, input_grad, keep, send, proj_own, proj_mate = pl.pallas_call(
        backward_kernel,
        out_shape=(
            shape(part_width, CONV),
            shape(part_width, channels),
            shape(FIRST_ROWS + SECOND_ROWS, CONV),
            shape(FIRST_ROWS + SECOND_ROWS, CONV),
            shape(2, flat, CONV),
            shape(2, flat, CONV),
        ),
        in_specs=[VMEM] * 10,
        out_specs=[VMEM] * 6,
        scratch_shapes=[
            pltpu.VMEM((across, CONV), F32),
            pltpu.VMEM((across, VAL), BF),
            pltpu.VMEM((PACKED, across), F32),
        ],
        name="block_backward",
        **PARAMS,
    )(near2, near1, own, mate, mate1, local, lse, projection, first_kernel, second_kernel)

    proj_sum = (proj_own.astype(F32) + rows_flip(proj_mate, 1).astype(F32)).astype(BF)
    arrived = rows_flip(jnp.concatenate([send, proj_sum[1]], axis=0), 2)
    total = jnp.concatenate([keep, proj_sum[0]], axis=0)
    total = (total.astype(F32) + arrived.astype(F32)).astype(BF)
    bit = 4
    while bit < rows_size:
        total = (total.astype(F32) + rows_flip(total, bit).astype(F32)).astype(BF)
        bit *= 2
    chip = rows_flip(total, 2)
    side = cols_flip(total)
    corner = lax.ppermute(
        total,
        ("rows", "cols"),
        [(i * cols_size + j, (i ^ 2) * cols_size + (j ^ 1)) for i in range(rows_size) for j in range(cols_size)],
    )
    four = (total, chip, side, corner)
    eight = four + tuple(rows_flip(piece, 1) for piece in four)
    factor = 1.0 / math.sqrt(height * across * rows_size)
    projection_grad, first_grad, second_grad = pl.pallas_call(
        functools.partial(unpack_kernel, factor),
        out_shape=(
            shape(channels, PACKED, dtype=F32),
            shape(3, 3, VAL, CONV, dtype=F32),
            shape(3, 3, CONV, CONV, dtype=F32),
        ),
        in_specs=[VMEM] * 8,
        out_specs=[VMEM] * 3,
        name="unpack_sums",
        **PARAMS,
    )(*eight)
    return (output_map[None], input_grad[None], projection_grad, first_grad, second_grad)


def solution(mesh):
    placed = (P("rows", "cols", None), P(), P(), P(), P("rows", "cols", None))
    return jax.shard_map(
        body,
        mesh=mesh,
        in_specs=placed,
        out_specs=(P("rows", "cols", None), P("rows", "cols", None), P(), P(), P()),
        check_vma=False,
    )
```

time: 264 us -> 67.6 us (0.26)
  waiting for transfers between devices: 140 us -> 27.9 us
  blocking collectives: 29.6 us -> 0 us
  matrix products: 28.2 us -> 0 us
  starting transfers between devices: 39 us -> 22.7 us
  between operations: 14.9 us -> 0.73 us
  Pallas kernels: 0 us -> 11.4 us
  other arithmetic: 5.82 us -> 1.03 us
    psum x1 -> x0, waiting for transfers between devices: 134 us -> none  [body(): lax.psum((projection_sum, first_sum, second_sum), ('rows', 'cols'))]
    all_gather x6 -> x0, blocking collectives: 29.6 us -> none  [the longest x1 5.7 us: body(): lax.all_gather(key_flat, 'cols', axis=1, tiled=True)]
    dot_general x63 -> x0, matrix products: 28.2 us -> none  [the longest x18 8.89 us: conv_transpose(): jnp.einsum('rwd,cd->rwc', window, kernel[tap_row, tap_col], preferred_ele...]
    ppermute x16, waiting for transfers between devices: 5.39 us -> 27.9 us  [the longest x11 17 us: rows_flip(): lax.ppermute(values, 'rows', [(i, i ^ bit) for i in range(rows_size)])]
    ppermute x16, starting transfers between devices: 39 us -> 22.7 us  [the longest x11 13.5 us: rows_flip(): lax.ppermute(values, 'rows', [(i, i ^ bit) for i in range(rows_size)])]
    pallas_call x0 -> x3, Pallas kernels: none -> 11.4 us  [the longest x1 7.13 us: body(): pl.pallas_call(backward_kernel, out_shape=(shape(part_width, CONV), shape...]
    mul x3 -> x0, other arithmetic: 3.11 us -> none  [the longest x1 1.14 us: body(): totals_all[0] * factor]
  transfers between devices with their start and end apart: 17 -> 16, of which waited for: 3 -> 11; matrix products, arithmetic and copies ran while one was open for 10% -> 0% of each run, Pallas kernels for 0% -> 0%
where the time goes in v1:
time: 67.6 us; the launch traced here: 67.3 us
  waiting for transfers between devices  27.9 us (41%)
  starting transfers between devices  22.7 us (34%)
  Pallas kernels  11.4 us (17%)
  local copies, waits for them, and re-layouts  3.61 us (5%)
  other arithmetic  1.03 us (2%)
  between operations  0.73 us (1%)
    ppermute x11, waiting for transfers between devices, rows_flip(): lax.ppermute(values, 'rows', [(i, i ^ bit) for i in range(rows_size)])  17 us
    ppermute x11, starting transfers between devices, rows_flip(): lax.ppermute(values, 'rows', [(i, i ^ bit) for i in range(rows_size)])  13.5 us
    pallas_call x1, Pallas kernels, body(): pl.pallas_call(backward_kernel, out_shape=(shape(part_width, CONV), shape...  7.13 us
    ppermute x1, waiting for transfers between devices, body(): near2 = lax.ppermute(own, 'rows', far)  4.09 us
    ppermute x1, waiting for transfers between devices, body(): lax.ppermute(total, ('rows', 'cols'), [(i * cols_size + j, (i ^ 2) * cols...  3.71 us
    unnamed x8, local copies, waits for them, and re-layouts  3.6 us
    ppermute x2, starting transfers between devices, cols_flip(): return lax.ppermute(values, 'cols', [(i, i ^ 1) for i in range(cols_size)])  3.53 us
    ppermute x1, starting transfers between devices, body(): near2 = lax.ppermute(own, 'rows', far)  3.43 us
  transfers between devices with their start and end apart: 16, of which 11 were waited for; matrix products, arithmetic and copies ran while one was open for 0% of the time, Pallas kernels for 0%

profile of v1, /device:TPU:0, one launch (start us, length us, event | category | flops | bytes accessed | tf_op | source)
XLA Modules:
  0.0 67.3 jit_solution(13195161262418696205)
XLA Ops:
  1.5 3.0 %collective-permute-start = (bf16[128,384]{1,0:T(8,128)(2,1)S(1)}, bf16[128,384]{1,0:T(8,128)(2,1)S(1)}, u32[]{:S(2)}, u32[]{:S(2)}) collective-permute-start(bf16[128,384]{1,0:T(8,128)(2,1)S(1)} %pad_maximum_fusion.1.refs_0_), channel_id=1, source_target_pairs={{0,1},{1,0},{2,3},{3,2},{4,5},{5,4},{6,7},{7,6},{8,9},{9,8},{10,11... | collective-permute-start | bytes 294920 | tf_op jit(solution)/shard_map/ppermute | solution.py:309
  4.5 2.8 %collective-permute-done.refs_1_ = bf16[128,384]{1,0:T(8,128)(2,1)S(1)} collective-permute-done((bf16[128,384]{1,0:T(8,128)(2,1)S(1)}, bf16[128,384]{1,0:T(8,128)(2,1)S(1)}, u32[]{:S(2)}, u32[]{:S(2)}) %collective-permute-start) | collective-permute-done | bytes 98336 | tf_op jit(solution)/shard_map/ppermute | solution.py:309
  7.3 0.9 %copy-done = bf16[256,512]{1,0:T(8,128)(2,1)S(1)} copy-done((bf16[256,512]{1,0:T(8,128)(2,1)S(1)}, bf16[256,512]{1,0:T(8,128)(2,1)}, u32[]{:S(2)}) %copy-start) | copy-done | bytes 262168
  8.3 2.7 %attention_forward.1 = (bf16[256,384]{1,0:T(8,128)(2,1)S(1)}, bf16[256,768]{1,0:T(8,128)(2,1)S(1)}, f32[8,256]{1,0:T(8,128)S(1)}) custom-call(bf16[128,384]{1,0:T(8,128)(2,1)S(1)} %pad_maximum_fusion.1.refs_0_, bf16[128,384]{1,0:T(8,128)(2,1)S(1)} %collective-permute-done.refs_1_, bf16[256,512]{1,0:T(8,128)(2,1)S(1)} %copy-done), custom_call_target="tpu_custom_call" | custom-call | tf_op jit(solution)/shard_map/attention_forward/pallas_call | solution.py:316
  12.4 3.3 %collective-permute-start.3 = (bf16[256,384]{1,0:T(8,128)(2,1)S(1)}, bf16[256,384]{1,0:T(8,128)(2,1)S(1)}, u32[]{:S(2)}, u32[]{:S(2)}) collective-permute-start(bf16[256,384]{1,0:T(8,128)(2,1)S(1)} %get-tuple-element.17.own), channel_id=1, source_target_pairs={{0,2},{2,0},{4,6},{6,4},{8,10},{10,8},{12,14},{14,12},{16,18},{18,... | collective-permute-start | bytes 589832 | tf_op jit(solution)/shard_map/ppermute | solution.py:306
  15.6 3.4 %collective-permute-start.1 = (bf16[256,384]{1,0:T(8,128)(2,1)S(1)}, bf16[256,384]{1,0:T(8,128)(2,1)S(1)}, u32[]{:S(2)}, u32[]{:S(2)}) collective-permute-start(bf16[256,384]{1,0:T(8,128)(2,1)S(1)} %get-tuple-element.17.own), channel_id=1, source_target_pairs={{0,4},{4,8},{8,12},{12,16},{16,20},{20,24},{24,28},{6,2},{10,6},{1... | collective-permute-start | bytes 589832 | tf_op jit(solution)/shard_map/ppermute | solution.py:333
  19.1 1.2 %collective-permute-start.4 = (bf16[256,384]{1,0:T(8,128)(2,1)S(1)}, bf16[256,384]{1,0:T(8,128)(2,1)S(1)}, u32[]{:S(2)}, u32[]{:S(2)}) collective-permute-start(bf16[256,384]{1,0:T(8,128)(2,1)S(1)} %collective-permute-done.2.near1), channel_id=1, source_target_pairs={{0,2},{2,0},{4,6},{6,4},{8,10},{10,8},{12,14},{14,12},{16,18},{18,... | collective-permute-start | bytes 589832 | tf_op jit(solution)/shard_map/ppermute | solution.py:306
  20.3 4.1 %collective-permute-done.1.near2 = bf16[256,384]{1,0:T(8,128)(2,1)S(1)} collective-permute-done((bf16[256,384]{1,0:T(8,128)(2,1)S(1)}, bf16[256,384]{1,0:T(8,128)(2,1)S(1)}, u32[]{:S(2)}, u32[]{:S(2)}) %collective-permute-start.1) | collective-permute-done | bytes 196640 | tf_op jit(solution)/shard_map/ppermute | solution.py:333
  24.4 0.9 %copy-done.1 = bf16[256,512]{1,0:T(8,128)(2,1)S(1)} copy-done((bf16[256,512]{1,0:T(8,128)(2,1)S(1)}, bf16[256,512]{1,0:T(8,128)(2,1)}, u32[]{:S(2)}) %copy-start.1) | copy-done | bytes 262168
  25.3 1.0 %copy-done.3 = bf16[3,3,128,128]{3,2,1,0:T(8,128)(2,1)S(1)} copy-done((bf16[3,3,128,128]{3,2,1,0:T(8,128)(2,1)S(1)}, bf16[3,3,128,128]{3,2,1,0:T(8,128)(2,1)}, u32[]{:S(2)}) %copy-start.3) | copy-done | bytes 294936
  26.3 7.1 %block_backward.1 = (bf16[128,128]{1,0:T(8,128)(2,1)}, bf16[128,256]{1,0:T(8,128)(2,1)}, bf16[432,128]{1,0:T(8,128)(2,1)S(1)}, bf16[432,128]{1,0:T(8,128)(2,1)S(...) custom-call(bf16[256,384]{1,0:T(8,128)(2,1)S(1)} %collective-permute-done.1.near2, ...), custom_call_target="tpu_custom_call" | custom-call | tf_op jit(solution)/shard_map/block_backward/pallas_call | solution.py:337
  33.4 1.3 %collective-permute-done.5 = bf16[2,128,128]{2,1,0:T(8,128)(2,1)S(1)} collective-permute-done((bf16[2,128,128]{2,1,0:T(8,128)(2,1)S(1)}, bf16[2,128,128]{2,1,0:T(8,128)(2,1)S(1)}, u32[]{:S(2)}, u32[]{:S(2)}) %collective-permute-start.5) | collective-permute-done | bytes 65568 | tf_op jit(solution)/shard_map/ppermute | solution.py:306
  34.7 2.5 %collective-permute-start.6 = (bf16[560,128]{1,0:T(8,128)(2,1)S(1)}, bf16[560,128]{1,0:T(8,128)(2,1)S(1)}, u32[]{:S(2)}, u32[]{:S(2)}) collective-permute-start(bf16[560,128]{1,0:T(8,128)(2,1)S(1)} %pad_maximum_fusion), channel_id=1, source_target_pairs={{0,4},{2,6},{4,0},{6,2},{8,12},{10,14},{12,8},{14,10},{16,20},{18,... | collective-permute-start | bytes 430088 | tf_op jit(solution)/shard_map/ppermute | solution.py:306
  37.3 4.1 %collective-permute-done.6 = bf16[560,128]{1,0:T(8,128)(2,1)S(1)} collective-permute-done((bf16[560,128]{1,0:T(8,128)(2,1)S(1)}, bf16[560,128]{1,0:T(8,128)(2,1)S(1)}, u32[]{:S(2)}, u32[]{:S(2)}) %collective-permute-start.6) | collective-permute-done | bytes 143392 | tf_op jit(solution)/shard_map/ppermute | solution.py:306
  41.4 2.1 %collective-permute-start.7 = (bf16[560,128]{1,0:T(8,128)(2,1)S(1)}, bf16[560,128]{1,0:T(8,128)(2,1)S(1)}, u32[]{:S(2)}, u32[]{:S(2)}) collective-permute-start(bf16[560,128]{1,0:T(8,128)(2,1)S(1)} %add_convert_fusion.2), channel_id=1, source_target_pairs={{0,8},{2,10},{4,12},{6,14},{8,0},{10,2},{12,4},{14,6},{16,24},{18,... | collective-permute-start | bytes 430088 | tf_op jit(solution)/shard_map/ppermute | solution.py:306
  43.5 3.5 %collective-permute-done.7 = bf16[560,128]{1,0:T(8,128)(2,1)S(1)} collective-permute-done((bf16[560,128]{1,0:T(8,128)(2,1)S(1)}, bf16[560,128]{1,0:T(8,128)(2,1)S(1)}, u32[]{:S(2)}, u32[]{:S(2)}) %collective-permute-start.7) | collective-permute-done | bytes 143392 | tf_op jit(solution)/shard_map/ppermute | solution.py:306
  47.0 2.8 %collective-permute-start.8 = (bf16[560,128]{1,0:T(8,128)(2,1)S(1)}, bf16[560,128]{1,0:T(8,128)(2,1)S(1)}, u32[]{:S(2)}, u32[]{:S(2)}) collective-permute-start(bf16[560,128]{1,0:T(8,128)(2,1)S(1)} %add_convert_fusion.1), channel_id=1, source_target_pairs={{0,16},{2,18},{4,20},{6,22},{8,24},{10,26},{12,28},{14,30},{16,0},... | collective-permute-start | bytes 430088 | tf_op jit(solution)/shard_map/ppermute | solution.py:306
  49.8 5.8 %collective-permute-done.8 = bf16[560,128]{1,0:T(8,128)(2,1)S(1)} collective-permute-done((bf16[560,128]{1,0:T(8,128)(2,1)S(1)}, bf16[560,128]{1,0:T(8,128)(2,1)S(1)}, u32[]{:S(2)}, u32[]{:S(2)}) %collective-permute-start.8) | collective-permute-done | bytes 143392 | tf_op jit(solution)/shard_map/ppermute | solution.py:306
  55.7 1.6 %collective-permute-start.11 = (bf16[560,128]{1,0:T(8,128)(2,1)S(1)}, bf16[560,128]{1,0:T(8,128)(2,1)S(1)}, u32[]{:S(2)}, u32[]{:S(2)}) collective-permute-start(bf16[560,128]{1,0:T(8,128)(2,1)S(1)} %add_convert_fusion.refs_0_), channel_id=1, source_target_pairs={{0,5},{1,4},{2,7},{3,6},{4,1},{5,0},{6,3},{7,2},{8,13},{9,12},{10,... | collective-permute-start | bytes 430088 | tf_op jit(solution)/shard_map/ppermute | solution.py:368
  57.8 1.4 %collective-permute-start.9 = (bf16[560,128]{1,0:T(8,128)(2,1)S(1)}, bf16[560,128]{1,0:T(8,128)(2,1)S(1)}, u32[]{:S(2)}, u32[]{:S(2)}) collective-permute-start(bf16[560,128]{1,0:T(8,128)(2,1)S(1)} %add_convert_fusion.refs_0_), channel_id=1, source_target_pairs={{0,4},{2,6},{4,0},{6,2},{8,12},{10,14},{12,8},{14,10},{16,20},{18,... | collective-permute-start | bytes 430088 | tf_op jit(solution)/shard_map/ppermute | solution.py:306
  59.2 3.7 %collective-permute-done.11.refs_3_ = bf16[560,128]{1,0:T(8,128)(2,1)S(1)} collective-permute-done((bf16[560,128]{1,0:T(8,128)(2,1)S(1)}, bf16[560,128]{1,0:T(8,128)(2,1)S(1)}, u32[]{:S(2)}, u32[]{:S(2)}) %collective-permute-start.11) | collective-permute-done | bytes 143392 | tf_op jit(solution)/shard_map/ppermute | solution.py:368
  63.4 1.0 %collective-permute-done.9.refs_1_ = bf16[560,128]{1,0:T(8,128)(2,1)S(1)} collective-permute-done((bf16[560,128]{1,0:T(8,128)(2,1)S(1)}, bf16[560,128]{1,0:T(8,128)(2,1)S(1)}, u32[]{:S(2)}, u32[]{:S(2)}) %collective-permute-start.9) | collective-permute-done | bytes 143392 | tf_op jit(solution)/shard_map/ppermute | solution.py:306
  64.6 1.1 %collective-permute-done.13.refs_5_ = bf16[560,128]{1,0:T(8,128)(2,1)S(1)} collective-permute-done((bf16[560,128]{1,0:T(8,128)(2,1)S(1)}, bf16[560,128]{1,0:T(8,128)(2,1)S(1)}, u32[]{:S(2)}, u32[]{:S(2)}) %collective-permute-start.13) | collective-permute-done | bytes 143392 | tf_op jit(solution)/shard_map/ppermute | solution.py:306
  65.8 1.5 %unpack_sums.1 = (f32[256,512]{1,0:T(8,128)}, f32[3,3,256,128]{3,2,1,0:T(8,128)}, f32[3,3,128,128]{3,2,1,0:T(8,128)}) custom-call(bf16[560,128]{1,0:T(8,128)(2,1)S(1)} %add_convert_fusion.refs_0_, bf16[560,128]{1,0:T(8,128)(2,1)S(1)} %collective-permute-done.9.refs_1_, bf16[560,128]{1,0:T(8,128)(2,1)S(1)} %collective-permute-done.10.refs_2_, ...), custom_call_target="tpu_custom_call" | custom-call | tf_op jit(solution)/shard_map/unpack_sums/pallas_call | solution.py:376
  (26 shorter events, 3.7 us)
Async XLA Ops:
  1.5 5.8 %collective-permute-start = (bf16[128,384]{1,0:T(8,128)(2,1)S(1)}, bf16[128,384]{1,0:T(8,128)(2,1)S(1)}, u32[]{:S(2)}, u32[]{:S(2)}) collective-permute-start(bf16[128,384]{1,0:T(8,128)(2,1)S(1)} %pad_maximum_fusion.1.refs_0_), channel_id=1, source_target_pairs={{0,1},{1,0},{2,3},{3,2},{4,5},{5,4},{6,7},{7,6},{8,9},{9,8},{10,11... | collective-permute-start | bytes 294920 | tf_op jit(solution)/shard_map/ppermute | solution.py:309
  7.3 1.0 %copy-start = (bf16[256,512]{1,0:T(8,128)(2,1)S(1)}, bf16[256,512]{1,0:T(8,128)(2,1)}, u32[]{:S(2)}) copy-start(bf16[256,512]{1,0:T(8,128)(2,1)} %projection.1) | copy-start | bytes 786436
  10.9 0.7 %copy-start.2 = (bf16[256,768]{1,0:T(8,128)(2,1)}, bf16[256,768]{1,0:T(8,128)(2,1)S(1)}, u32[]{:S(2)}) copy-start(bf16[256,768]{1,0:T(8,128)(2,1)S(1)} %get-tuple-element.18.local) | copy-start | bytes 1179652
  11.7 7.4 %collective-permute-start.2 = (bf16[256,384]{1,0:T(8,128)(2,1)S(1)}, bf16[256,384]{1,0:T(8,128)(2,1)S(1)}, u32[]{:S(2)}, u32[]{:S(2)}) collective-permute-start(bf16[256,384]{1,0:T(8,128)(2,1)S(1)} %get-tuple-element.17.own), channel_id=1, source_target_pairs={{2,4},{6,8},{10,12},{14,16},{18,20},{22,24},{26,28},{4,2},{8,6},{1... | collective-permute-start | bytes 589832 | tf_op jit(solution)/shard_map/ppermute | solution.py:332
  12.4 7.9 %collective-permute-start.3 = (bf16[256,384]{1,0:T(8,128)(2,1)S(1)}, bf16[256,384]{1,0:T(8,128)(2,1)S(1)}, u32[]{:S(2)}, u32[]{:S(2)}) collective-permute-start(bf16[256,384]{1,0:T(8,128)(2,1)S(1)} %get-tuple-element.17.own), channel_id=1, source_target_pairs={{0,2},{2,0},{4,6},{6,4},{8,10},{10,8},{12,14},{14,12},{16,18},{18,... | collective-permute-start | bytes 589832 | tf_op jit(solution)/shard_map/ppermute | solution.py:306
  15.6 8.7 %collective-permute-start.1 = (bf16[256,384]{1,0:T(8,128)(2,1)S(1)}, bf16[256,384]{1,0:T(8,128)(2,1)S(1)}, u32[]{:S(2)}, u32[]{:S(2)}) collective-permute-start(bf16[256,384]{1,0:T(8,128)(2,1)S(1)} %get-tuple-element.17.own), channel_id=1, source_target_pairs={{0,4},{4,8},{8,12},{12,16},{16,20},{20,24},{24,28},{6,2},{10,6},{1... | collective-permute-start | bytes 589832 | tf_op jit(solution)/shard_map/ppermute | solution.py:333
  19.1 5.3 %collective-permute-start.4 = (bf16[256,384]{1,0:T(8,128)(2,1)S(1)}, bf16[256,384]{1,0:T(8,128)(2,1)S(1)}, u32[]{:S(2)}, u32[]{:S(2)}) collective-permute-start(bf16[256,384]{1,0:T(8,128)(2,1)S(1)} %collective-permute-done.2.near1), channel_id=1, source_target_pairs={{0,2},{2,0},{4,6},{6,4},{8,10},{10,8},{12,14},{14,12},{16,18},{18,... | collective-permute-start | bytes 589832 | tf_op jit(solution)/shard_map/ppermute | solution.py:306
  24.4 1.0 %copy-start.1 = (bf16[256,512]{1,0:T(8,128)(2,1)S(1)}, bf16[256,512]{1,0:T(8,128)(2,1)}, u32[]{:S(2)}) copy-start(bf16[256,512]{1,0:T(8,128)(2,1)} %projection.1) | copy-start | bytes 786436
  25.3 1.0 %copy-start.3 = (bf16[3,3,128,128]{3,2,1,0:T(8,128)(2,1)S(1)}, bf16[3,3,128,128]{3,2,1,0:T(8,128)(2,1)}, u32[]{:S(2)}) copy-start(bf16[3,3,128,128]{3,2,1,0:T(8,128)(2,1)} %second_kernel.1) | copy-start | bytes 884740
  33.4 1.3 %collective-permute-start.5 = (bf16[2,128,128]{2,1,0:T(8,128)(2,1)S(1)}, bf16[2,128,128]{2,1,0:T(8,128)(2,1)S(1)}, u32[]{:S(2)}, u32[]{:S(2)}) collective-permute-start(bf16[2,128,128]{2,1,0:T(8,128)(2,1)S(1)} %get-tuple-element.24), channel_id=1, source_target_pairs={{0,2},{2,0},{4,6},{6,4},{8,10},{10,8},{12,14},{14,12},{16,18},{18,... | collective-permute-start | bytes 196616 | tf_op jit(solution)/shard_map/ppermute | solution.py:306
  34.7 6.6 %collective-permute-start.6 = (bf16[560,128]{1,0:T(8,128)(2,1)S(1)}, bf16[560,128]{1,0:T(8,128)(2,1)S(1)}, u32[]{:S(2)}, u32[]{:S(2)}) collective-permute-start(bf16[560,128]{1,0:T(8,128)(2,1)S(1)} %pad_maximum_fusion), channel_id=1, source_target_pairs={{0,4},{2,6},{4,0},{6,2},{8,12},{10,14},{12,8},{14,10},{16,20},{18,... | collective-permute-start | bytes 430088 | tf_op jit(solution)/shard_map/ppermute | solution.py:306
  41.4 5.5 %collective-permute-start.7 = (bf16[560,128]{1,0:T(8,128)(2,1)S(1)}, bf16[560,128]{1,0:T(8,128)(2,1)S(1)}, u32[]{:S(2)}, u32[]{:S(2)}) collective-permute-start(bf16[560,128]{1,0:T(8,128)(2,1)S(1)} %add_convert_fusion.2), channel_id=1, source_target_pairs={{0,8},{2,10},{4,12},{6,14},{8,0},{10,2},{12,4},{14,6},{16,24},{18,... | collective-permute-start | bytes 430088 | tf_op jit(solution)/shard_map/ppermute | solution.py:306
  47.0 8.6 %collective-permute-start.8 = (bf16[560,128]{1,0:T(8,128)(2,1)S(1)}, bf16[560,128]{1,0:T(8,128)(2,1)S(1)}, u32[]{:S(2)}, u32[]{:S(2)}) collective-permute-start(bf16[560,128]{1,0:T(8,128)(2,1)S(1)} %add_convert_fusion.1), channel_id=1, source_target_pairs={{0,16},{2,18},{4,20},{6,22},{8,24},{10,26},{12,28},{14,30},{16,0},... | collective-permute-start | bytes 430088 | tf_op jit(solution)/shard_map/ppermute | solution.py:306
  55.7 7.3 %collective-permute-start.11 = (bf16[560,128]{1,0:T(8,128)(2,1)S(1)}, bf16[560,128]{1,0:T(8,128)(2,1)S(1)}, u32[]{:S(2)}, u32[]{:S(2)}) collective-permute-start(bf16[560,128]{1,0:T(8,128)(2,1)S(1)} %add_convert_fusion.refs_0_), channel_id=1, source_target_pairs={{0,5},{1,4},{2,7},{3,6},{4,1},{5,0},{6,3},{7,2},{8,13},{9,12},{10,... | collective-permute-start | bytes 430088 | tf_op jit(solution)/shard_map/ppermute | solution.py:368
  57.3 6.0 %collective-permute-start.10 = (bf16[560,128]{1,0:T(8,128)(2,1)S(1)}, bf16[560,128]{1,0:T(8,128)(2,1)S(1)}, u32[]{:S(2)}, u32[]{:S(2)}) collective-permute-start(bf16[560,128]{1,0:T(8,128)(2,1)S(1)} %add_convert_fusion.refs_0_), channel_id=1, source_target_pairs={{0,1},{1,0},{2,3},{3,2},{4,5},{5,4},{6,7},{7,6},{8,9},{9,8},{10,11... | collective-permute-start | bytes 430088 | tf_op jit(solution)/shard_map/ppermute | solution.py:309
  57.8 6.6 %collective-permute-start.9 = (bf16[560,128]{1,0:T(8,128)(2,1)S(1)}, bf16[560,128]{1,0:T(8,128)(2,1)S(1)}, u32[]{:S(2)}, u32[]{:S(2)}) collective-permute-start(bf16[560,128]{1,0:T(8,128)(2,1)S(1)} %add_convert_fusion.refs_0_), channel_id=1, source_target_pairs={{0,4},{2,6},{4,0},{6,2},{8,12},{10,14},{12,8},{14,10},{16,20},{18,... | collective-permute-start | bytes 430088 | tf_op jit(solution)/shard_map/ppermute | solution.py:306
  59.2 5.2 %collective-permute-start.12 = (bf16[560,128]{1,0:T(8,128)(2,1)S(1)}, bf16[560,128]{1,0:T(8,128)(2,1)S(1)}, u32[]{:S(2)}, u32[]{:S(2)}) collective-permute-start(bf16[560,128]{1,0:T(8,128)(2,1)S(1)} %add_convert_fusion.refs_0_), channel_id=1, source_target_pairs={{0,2},{2,0},{4,6},{6,4},{8,10},{10,8},{12,14},{14,12},{16,18},{18,... | collective-permute-start | bytes 430088 | tf_op jit(solution)/shard_map/ppermute | solution.py:306
  62.9 1.5 %collective-permute-start.15 = (bf16[560,128]{1,0:T(8,128)(2,1)S(1)}, bf16[560,128]{1,0:T(8,128)(2,1)S(1)}, u32[]{:S(2)}, u32[]{:S(2)}) collective-permute-start(bf16[560,128]{1,0:T(8,128)(2,1)S(1)} %collective-permute-done.11.refs_3_), channel_id=1, source_target_pairs={{0,2},{2,0},{4,6},{6,4},{8,10},{10,8},{12,14},{14,12},{16,18},{18,... | collective-permute-start | bytes 430088 | tf_op jit(solution)/shard_map/ppermute | solution.py:306
  63.3 1.4 %collective-permute-start.14 = (bf16[560,128]{1,0:T(8,128)(2,1)S(1)}, bf16[560,128]{1,0:T(8,128)(2,1)S(1)}, u32[]{:S(2)}, u32[]{:S(2)}) collective-permute-start(bf16[560,128]{1,0:T(8,128)(2,1)S(1)} %collective-permute-done.10.refs_2_), channel_id=1, source_target_pairs={{0,2},{2,0},{4,6},{6,4},{8,10},{10,8},{12,14},{14,12},{16,18},{18,... | collective-permute-start | bytes 430088 | tf_op jit(solution)/shard_map/ppermute | solution.py:306
  64.4 1.4 %collective-permute-start.13 = (bf16[560,128]{1,0:T(8,128)(2,1)S(1)}, bf16[560,128]{1,0:T(8,128)(2,1)S(1)}, u32[]{:S(2)}, u32[]{:S(2)}) collective-permute-start(bf16[560,128]{1,0:T(8,128)(2,1)S(1)} %collective-permute-done.9.refs_1_), channel_id=1, source_target_pairs={{0,2},{2,0},{4,6},{6,4},{8,10},{10,8},{12,14},{14,12},{16,18},{18,... | collective-permute-start | bytes 430088 | tf_op jit(solution)/shard_map/ppermute | solution.py:306

commit v2 on v1

--- a/solution.py
+++ b/solution.py
@@ -66,19 +66,30 @@
     return pl.ds(index if isinstance(index, int) else pl.multiple_of(index * BLOCK, BLOCK), BLOCK)
 
 
+def fetch_kernel(*refs):
+    count = (len(refs) - 1) // 2
+    copies = [pltpu.make_async_copy(refs[i], refs[count + i], refs[-1].at[i]) for i in range(count)]
+    for copy in copies:
+        copy.start()
+    for copy in copies:
+        copy.wait()
+
+
 def forward_kernel(whole, *refs):
-    pieces = refs[: 1 if whole else 2]
-    projection, comb, local, lse, values_t = refs[len(pieces) :]
+    count = 1 if whole else 2
+    features = refs[:count]
+    cotangent = refs[count : 2 * count]
+    projection, comb, local, lse, values_t = refs[2 * count :]
     across = comb.shape[0]
-    for which, piece in enumerate(pieces):
-        width = piece.shape[0]
+    for which in range(count):
+        width = features[which].shape[0]
         if whole:
             at = pl.ds(0, width)
         else:
             place = lax.rem(lax.axis_index("cols") + which, 2)
             at = pl.ds(pl.multiple_of(place * width, width), width)
-        local[at, PACKED:] = piece[:, :VAL]
-        comb[at, VAL:] = piece[:, VAL:]
+        local[at, PACKED:] = features[which][...]
+        comb[at, VAL:] = cotangent[which][...]
     packed = mm(local[:, PACKED:], projection[...]).astype(BF)
     local[:, :PACKED] = packed
     keys = packed[:, QK : 2 * QK]
@@ -291,8 +302,12 @@
     return jax.ShapeDtypeStruct(dims, dtype)
 
 
-PARAMS = dict(compiler_params=pltpu.CompilerParams(vmem_limit_bytes=52 * 1024 * 1024))
+def granted(across):
+    return dict(compiler_params=pltpu.CompilerParams(vmem_limit_bytes=across * 64 * 1024))
+
+
 VMEM = pl.BlockSpec(memory_space=pltpu.VMEM)
+HBM = pl.BlockSpec(memory_space=pltpu.HBM)
 
 
 def body(features, projection, first_kernel, second_kernel, cotangent):
@@ -308,11 +323,22 @@
     def cols_flip(values):
         return lax.ppermute(values, "cols", [(i, i ^ 1) for i in range(cols_size)])
 
-    both = jnp.concatenate([features[0], cotangent[0]], axis=-1)
+    params = granted(across)
+    weights = (projection, first_kernel, second_kernel)
+    projection, first_kernel, second_kernel = pl.pallas_call(
+        fetch_kernel,
+        out_shape=tuple(shape(*array.shape) for array in weights),
+        in_specs=[HBM] * 3,
+        out_specs=[VMEM] * 3,
+        scratch_shapes=[pltpu.SemaphoreType.DMA((3,))],
+        cost_estimate=pl.CostEstimate(flops=0, bytes_accessed=4 * 1024 * 1024, transcendentals=0),
+        name="fetch_weights",
+        **granted(32),
+    )(*weights)
     if cols_size == 2:
-        pieces = (both, cols_flip(both))
+        pieces = (features[0], cols_flip(features[0]), cotangent[0], cols_flip(cotangent[0]))
     else:
-        pieces = (lax.all_gather(both, "cols", axis=0, tiled=True),)
+        pieces = tuple(lax.all_gather(array[0], "cols", axis=0, tiled=True) for array in (features, cotangent))
     own, local, lse = pl.pallas_call(
         functools.partial(forward_kernel, cols_size != 2),
         out_shape=(
@@ -324,7 +350,7 @@
         out_specs=[VMEM] * 3,
         scratch_shapes=[pltpu.VMEM((VAL, across), BF)],
         name="attention_forward",
-        **PARAMS,
+        **params,
     )(*pieces, projection)
 
     far = [(i, i + 2) for i in range(0, rows_size - 2, 2)] + [(i, i - 2) for i in range(3, rows_size, 2)]
@@ -352,7 +378,7 @@
             pltpu.VMEM((PACKED, across), F32),
         ],
         name="block_backward",
-        **PARAMS,
+        **params,
     )(near2, near1, own, mate, mate1, local, lse, projection, first_kernel, second_kernel)
 
     proj_sum = (proj_own.astype(F32) + rows_flip(proj_mate, 1).astype(F32)).astype(BF)
@@ -383,7 +409,7 @@
         in_specs=[VMEM] * 8,
         out_specs=[VMEM] * 3,
         name="unpack_sums",
-        **PARAMS,
+        **params,
     )(*eight)
     return (output_map[None], input_grad[None], projection_grad, first_grad, second_grad)
 

time: 67.6 us -> 64 us (0.947)
  waiting for transfers between devices: 27.9 us -> 26 us
  Pallas kernels: 11.4 us -> 10.4 us
  other arithmetic: 1.03 us -> 0.16 us
    ppermute x2 -> x3, waiting for transfers between devices: 3.14 us -> 1.18 us  [cols_flip(): return lax.ppermute(values, 'cols', [(i, i ^ 1) for i in range(cols_size)])]
    pallas_call x1, Pallas kernels: 7.13 us -> 5.94 us  [body(): pl.pallas_call(backward_kernel, out_shape=(shape(part_width, CONV), shape...]
    concatenate x1 -> x0, other arithmetic: 0.87 us -> none  [body(): both = jnp.concatenate([features[0], cotangent[0]], axis=-1)]
    unnamed x8 -> x10, local copies, waits for them, and re-layouts: 3.6 us -> 3.73 us
    ppermute x2 -> x3, starting transfers between devices: 3.53 us -> 3.61 us  [cols_flip(): return lax.ppermute(values, 'cols', [(i, i ^ 1) for i in range(cols_size)])]
  transfers between devices with their start and end apart: 16 -> 17, of which waited for: 11 -> 11; matrix products, arithmetic and copies ran while one was open for 0% -> 0% of each run, Pallas kernels for 0% -> 0%
where the time goes in v2:
time: 64 us; the launch traced here: 63.6 us
  waiting for transfers between devices  26 us (41%)
  starting transfers between devices  22.7 us (35%)
  Pallas kernels  10.4 us (16%)
  local copies, waits for them, and re-layouts  3.74 us (6%)
  between operations  0.73 us (1%)
    ppermute x11, waiting for transfers between devices, rows_flip(): lax.ppermute(values, 'rows', [(i, i ^ bit) for i in range(rows_size)])  17 us
    ppermute x11, starting transfers between devices, rows_flip(): lax.ppermute(values, 'rows', [(i, i ^ bit) for i in range(rows_size)])  13.4 us
    pallas_call x1, Pallas kernels, body(): pl.pallas_call(backward_kernel, out_shape=(shape(part_width, CONV), shape...  5.94 us
    ppermute x1, waiting for transfers between devices, body(): near2 = lax.ppermute(own, 'rows', far)  4.09 us
    unnamed x10, local copies, waits for them, and re-layouts  3.73 us
    ppermute x1, waiting for transfers between devices, body(): lax.ppermute(total, ('rows', 'cols'), [(i * cols_size + j, (i ^ 2) * cols...  3.71 us
    ppermute x3, starting transfers between devices, cols_flip(): return lax.ppermute(values, 'cols', [(i, i ^ 1) for i in range(cols_size)])  3.61 us
    ppermute x1, starting transfers between devices, body(): near2 = lax.ppermute(own, 'rows', far)  3.42 us
  transfers between devices with their start and end apart: 17, of which 11 were waited for; matrix products, arithmetic and copies ran while one was open for 0% of the time, Pallas kernels for 0%

profile of v2, /device:TPU:0, one launch (start us, length us, event | category | flops | bytes accessed | tf_op | source)
XLA Modules:
  0.0 63.6 jit_solution(9096478556151791434)
XLA Ops:
  0.6 3.0 %collective-permute-start = (bf16[128,256]{1,0:T(8,128)(2,1)}, bf16[128,256]{1,0:T(8,128)(2,1)S(1)}, u32[]{:S(2)}, u32[]{:S(2)}) collective-permute-start(bf16[128,256]{1,0:T(8,128)(2,1)} %bitcast.8), channel_id=1, source_target_pairs={{0,1},{1,0},{2,3},{3,2},{4,5},{5,4},{6,7},{7,6},{8,9},{9,8},{10,11... | collective-permute-start | bytes 196616 | tf_op jit(solution)/shard_map/ppermute | solution.py:324
  3.7 1.1 %copy-done = bf16[3,3,256,128]{3,2,1,0:T(8,128)(2,1)S(1)} copy-done((bf16[3,3,256,128]{3,2,1,0:T(8,128)(2,1)S(1)}, bf16[3,3,256,128]{3,2,1,0:T(8,128)(2,1)}, u32[]{:S(2)}) %copy-start) | copy-done | bytes 589848
  4.8 1.0 %copy-done.1 = bf16[3,3,128,128]{3,2,1,0:T(8,128)(2,1)S(1)} copy-done((bf16[3,3,128,128]{3,2,1,0:T(8,128)(2,1)S(1)}, bf16[3,3,128,128]{3,2,1,0:T(8,128)(2,1)}, u32[]{:S(2)}) %copy-start.1) | copy-done | bytes 294936
  5.7 0.9 %copy-done.2 = bf16[256,512]{1,0:T(8,128)(2,1)S(1)} copy-done((bf16[256,512]{1,0:T(8,128)(2,1)S(1)}, bf16[256,512]{1,0:T(8,128)(2,1)}, u32[]{:S(2)}) %copy-start.2) | copy-done | bytes 262168
  6.9 0.8 %collective-permute-done.1.refs_3_ = bf16[128,128]{1,0:T(8,128)(2,1)S(1)} collective-permute-done((bf16[128,128]{1,0:T(8,128)(2,1)}, bf16[128,128]{1,0:T(8,128)(2,1)S(1)}, u32[]{:S(2)}, u32[]{:S(2)}) %collective-permute-start.1) | collective-permute-done | bytes 32800 | tf_op jit(solution)/shard_map/ppermute | solution.py:324
  8.5 2.7 %attention_forward.1 = (bf16[256,384]{1,0:T(8,128)(2,1)S(1)}, bf16[256,768]{1,0:T(8,128)(2,1)S(1)}, f32[8,256]{1,0:T(8,128)S(1)}) custom-call(bf16[128,256]{1,0:T(8,128)(2,1)S(1)} %bitcast.9, bf16[128,256]{1,0:T(8,128)(2,1)S(1)} %collective-permute-done.refs_1_, bf16[128,128]{1,0:T(8,128)(2,1)S(1)} %bitcast.11, ...), custom_call_target="tpu_custom_call" | custom-call | tf_op jit(solution)/shard_map/attention_forward/pallas_call | solution.py:342
  11.9 3.2 %collective-permute-start.4 = (bf16[256,384]{1,0:T(8,128)(2,1)S(1)}, bf16[256,384]{1,0:T(8,128)(2,1)S(1)}, u32[]{:S(2)}, u32[]{:S(2)}) collective-permute-start(bf16[256,384]{1,0:T(8,128)(2,1)S(1)} %get-tuple-element.21.own), channel_id=1, source_target_pairs={{0,2},{2,0},{4,6},{6,4},{8,10},{10,8},{12,14},{14,12},{16,18},{18,... | collective-permute-start | bytes 589832 | tf_op jit(solution)/shard_map/ppermute | solution.py:321
  15.0 3.4 %collective-permute-start.2 = (bf16[256,384]{1,0:T(8,128)(2,1)S(1)}, bf16[256,384]{1,0:T(8,128)(2,1)S(1)}, u32[]{:S(2)}, u32[]{:S(2)}) collective-permute-start(bf16[256,384]{1,0:T(8,128)(2,1)S(1)} %get-tuple-element.21.own), channel_id=1, source_target_pairs={{0,4},{4,8},{8,12},{12,16},{16,20},{20,24},{24,28},{6,2},{10,6},{1... | collective-permute-start | bytes 589832 | tf_op jit(solution)/shard_map/ppermute | solution.py:359
  18.5 1.2 %collective-permute-start.5 = (bf16[256,384]{1,0:T(8,128)(2,1)S(1)}, bf16[256,384]{1,0:T(8,128)(2,1)S(1)}, u32[]{:S(2)}, u32[]{:S(2)}) collective-permute-start(bf16[256,384]{1,0:T(8,128)(2,1)S(1)} %collective-permute-done.3.near1), channel_id=1, source_target_pairs={{0,2},{2,0},{4,6},{6,4},{8,10},{10,8},{12,14},{14,12},{16,18},{18,... | collective-permute-start | bytes 589832 | tf_op jit(solution)/shard_map/ppermute | solution.py:321
  19.7 4.1 %collective-permute-done.2.near2 = bf16[256,384]{1,0:T(8,128)(2,1)S(1)} collective-permute-done((bf16[256,384]{1,0:T(8,128)(2,1)S(1)}, bf16[256,384]{1,0:T(8,128)(2,1)S(1)}, u32[]{:S(2)}, u32[]{:S(2)}) %collective-permute-start.2) | collective-permute-done | bytes 196640 | tf_op jit(solution)/shard_map/ppermute | solution.py:359
  23.8 5.9 %block_backward.1 = (bf16[128,128]{1,0:T(8,128)(2,1)}, bf16[128,256]{1,0:T(8,128)(2,1)}, bf16[432,128]{1,0:T(8,128)(2,1)S(1)}, bf16[432,128]{1,0:T(8,128)(2,1)S(...) custom-call(bf16[256,384]{1,0:T(8,128)(2,1)S(1)} %collective-permute-done.2.near2, ...), custom_call_target="tpu_custom_call" | custom-call | tf_op jit(solution)/shard_map/block_backward/pallas_call | solution.py:363
  29.7 1.3 %collective-permute-done.6 = bf16[2,128,128]{2,1,0:T(8,128)(2,1)S(1)} collective-permute-done((bf16[2,128,128]{2,1,0:T(8,128)(2,1)S(1)}, bf16[2,128,128]{2,1,0:T(8,128)(2,1)S(1)}, u32[]{:S(2)}, u32[]{:S(2)}) %collective-permute-start.6) | collective-permute-done | bytes 65568 | tf_op jit(solution)/shard_map/ppermute | solution.py:321
  31.0 2.5 %collective-permute-start.7 = (bf16[560,128]{1,0:T(8,128)(2,1)S(1)}, bf16[560,128]{1,0:T(8,128)(2,1)S(1)}, u32[]{:S(2)}, u32[]{:S(2)}) collective-permute-start(bf16[560,128]{1,0:T(8,128)(2,1)S(1)} %pad_maximum_fusion), channel_id=1, source_target_pairs={{0,4},{2,6},{4,0},{6,2},{8,12},{10,14},{12,8},{14,10},{16,20},{18,... | collective-permute-start | bytes 430088 | tf_op jit(solution)/shard_map/ppermute | solution.py:321
  33.6 4.1 %collective-permute-done.7 = bf16[560,128]{1,0:T(8,128)(2,1)S(1)} collective-permute-done((bf16[560,128]{1,0:T(8,128)(2,1)S(1)}, bf16[560,128]{1,0:T(8,128)(2,1)S(1)}, u32[]{:S(2)}, u32[]{:S(2)}) %collective-permute-start.7) | collective-permute-done | bytes 143392 | tf_op jit(solution)/shard_map/ppermute | solution.py:321
  37.7 2.1 %collective-permute-start.8 = (bf16[560,128]{1,0:T(8,128)(2,1)S(1)}, bf16[560,128]{1,0:T(8,128)(2,1)S(1)}, u32[]{:S(2)}, u32[]{:S(2)}) collective-permute-start(bf16[560,128]{1,0:T(8,128)(2,1)S(1)} %add_convert_fusion.2), channel_id=1, source_target_pairs={{0,8},{2,10},{4,12},{6,14},{8,0},{10,2},{12,4},{14,6},{16,24},{18,... | collective-permute-start | bytes 430088 | tf_op jit(solution)/shard_map/ppermute | solution.py:321
  39.8 3.5 %collective-permute-done.8 = bf16[560,128]{1,0:T(8,128)(2,1)S(1)} collective-permute-done((bf16[560,128]{1,0:T(8,128)(2,1)S(1)}, bf16[560,128]{1,0:T(8,128)(2,1)S(1)}, u32[]{:S(2)}, u32[]{:S(2)}) %collective-permute-start.8) | collective-permute-done | bytes 143392 | tf_op jit(solution)/shard_map/ppermute | solution.py:321
  43.3 2.8 %collective-permute-start.9 = (bf16[560,128]{1,0:T(8,128)(2,1)S(1)}, bf16[560,128]{1,0:T(8,128)(2,1)S(1)}, u32[]{:S(2)}, u32[]{:S(2)}) collective-permute-start(bf16[560,128]{1,0:T(8,128)(2,1)S(1)} %add_convert_fusion.1), channel_id=1, source_target_pairs={{0,16},{2,18},{4,20},{6,22},{8,24},{10,26},{12,28},{14,30},{16,0},... | collective-permute-start | bytes 430088 | tf_op jit(solution)/shard_map/ppermute | solution.py:321
  46.1 5.8 %collective-permute-done.9 = bf16[560,128]{1,0:T(8,128)(2,1)S(1)} collective-permute-done((bf16[560,128]{1,0:T(8,128)(2,1)S(1)}, bf16[560,128]{1,0:T(8,128)(2,1)S(1)}, u32[]{:S(2)}, u32[]{:S(2)}) %collective-permute-start.9) | collective-permute-done | bytes 143392 | tf_op jit(solution)/shard_map/ppermute | solution.py:321
  52.0 1.6 %collective-permute-start.12 = (bf16[560,128]{1,0:T(8,128)(2,1)S(1)}, bf16[560,128]{1,0:T(8,128)(2,1)S(1)}, u32[]{:S(2)}, u32[]{:S(2)}) collective-permute-start(bf16[560,128]{1,0:T(8,128)(2,1)S(1)} %add_convert_fusion.refs_0_), channel_id=1, source_target_pairs={{0,5},{1,4},{2,7},{3,6},{4,1},{5,0},{6,3},{7,2},{8,13},{9,12},{10,... | collective-permute-start | bytes 430088 | tf_op jit(solution)/shard_map/ppermute | solution.py:394
  54.1 1.4 %collective-permute-start.10 = (bf16[560,128]{1,0:T(8,128)(2,1)S(1)}, bf16[560,128]{1,0:T(8,128)(2,1)S(1)}, u32[]{:S(2)}, u32[]{:S(2)}) collective-permute-start(bf16[560,128]{1,0:T(8,128)(2,1)S(1)} %add_convert_fusion.refs_0_), channel_id=1, source_target_pairs={{0,4},{2,6},{4,0},{6,2},{8,12},{10,14},{12,8},{14,10},{16,20},{18,... | collective-permute-start | bytes 430088 | tf_op jit(solution)/shard_map/ppermute | solution.py:321
  55.5 3.7 %collective-permute-done.12.refs_3_ = bf16[560,128]{1,0:T(8,128)(2,1)S(1)} collective-permute-done((bf16[560,128]{1,0:T(8,128)(2,1)S(1)}, bf16[560,128]{1,0:T(8,128)(2,1)S(1)}, u32[]{:S(2)}, u32[]{:S(2)}) %collective-permute-start.12) | collective-permute-done | bytes 143392 | tf_op jit(solution)/shard_map/ppermute | solution.py:394
  59.8 1.0 %collective-permute-done.10.refs_1_ = bf16[560,128]{1,0:T(8,128)(2,1)S(1)} collective-permute-done((bf16[560,128]{1,0:T(8,128)(2,1)S(1)}, bf16[560,128]{1,0:T(8,128)(2,1)S(1)}, u32[]{:S(2)}, u32[]{:S(2)}) %collective-permute-start.10) | collective-permute-done | bytes 143392 | tf_op jit(solution)/shard_map/ppermute | solution.py:321
  61.0 1.1 %collective-permute-done.14.refs_5_ = bf16[560,128]{1,0:T(8,128)(2,1)S(1)} collective-permute-done((bf16[560,128]{1,0:T(8,128)(2,1)S(1)}, bf16[560,128]{1,0:T(8,128)(2,1)S(1)}, u32[]{:S(2)}, u32[]{:S(2)}) %collective-permute-start.14) | collective-permute-done | bytes 143392 | tf_op jit(solution)/shard_map/ppermute | solution.py:321
  62.1 1.5 %unpack_sums.1 = (f32[256,512]{1,0:T(8,128)}, f32[3,3,256,128]{3,2,1,0:T(8,128)}, f32[3,3,128,128]{3,2,1,0:T(8,128)}) custom-call(bf16[560,128]{1,0:T(8,128)(2,1)S(1)} %add_convert_fusion.refs_0_, bf16[560,128]{1,0:T(8,128)(2,1)S(1)} %collective-permute-done.10.refs_1_, bf16[560,128]{1,0:T(8,128)(2,1)S(1)} %collective-permute-done.11.refs_2_, ...), custom_call_target="tpu_custom_call" | custom-call | tf_op jit(solution)/shard_map/unpack_sums/pallas_call | solution.py:402
  (30 shorter events, 3.2 us)
Async XLA Ops:
  0.6 7.1 %collective-permute-start = (bf16[128,256]{1,0:T(8,128)(2,1)}, bf16[128,256]{1,0:T(8,128)(2,1)S(1)}, u32[]{:S(2)}, u32[]{:S(2)}) collective-permute-start(bf16[128,256]{1,0:T(8,128)(2,1)} %bitcast.8), channel_id=1, source_target_pairs={{0,1},{1,0},{2,3},{3,2},{4,5},{5,4},{6,7},{7,6},{8,9},{9,8},{10,11... | collective-permute-start | bytes 196616 | tf_op jit(solution)/shard_map/ppermute | solution.py:324
  3.6 4.1 %collective-permute-start.1 = (bf16[128,128]{1,0:T(8,128)(2,1)}, bf16[128,128]{1,0:T(8,128)(2,1)S(1)}, u32[]{:S(2)}, u32[]{:S(2)}) collective-permute-start(bf16[128,128]{1,0:T(8,128)(2,1)} %bitcast.10), channel_id=1, source_target_pairs={{0,1},{1,0},{2,3},{3,2},{4,5},{5,4},{6,7},{7,6},{8,9},{9,8},{10,11... | collective-permute-start | bytes 98312 | tf_op jit(solution)/shard_map/ppermute | solution.py:324
  3.7 1.1 %copy-start = (bf16[3,3,256,128]{3,2,1,0:T(8,128)(2,1)S(1)}, bf16[3,3,256,128]{3,2,1,0:T(8,128)(2,1)}, u32[]{:S(2)}) copy-start(bf16[3,3,256,128]{3,2,1,0:T(8,128)(2,1)} %refs_1_.1) | copy-start | bytes 1769476
  4.8 1.0 %copy-start.1 = (bf16[3,3,128,128]{3,2,1,0:T(8,128)(2,1)S(1)}, bf16[3,3,128,128]{3,2,1,0:T(8,128)(2,1)}, u32[]{:S(2)}) copy-start(bf16[3,3,128,128]{3,2,1,0:T(8,128)(2,1)} %refs_2_.1) | copy-start | bytes 884740
  5.7 0.9 %copy-start.2 = (bf16[256,512]{1,0:T(8,128)(2,1)S(1)}, bf16[256,512]{1,0:T(8,128)(2,1)}, u32[]{:S(2)}) copy-start(bf16[256,512]{1,0:T(8,128)(2,1)} %refs_0_.1) | copy-start | bytes 786436
  6.7 1.1 %copy-start.3 = (bf16[1,128,256]{2,1,0:T(8,128)(2,1)S(1)}, bf16[1,128,256]{2,1,0:T(8,128)(2,1)}, u32[]{:S(2)}) copy-start(bf16[1,128,256]{2,1,0:T(8,128)(2,1)} %param.5) | copy-start | bytes 196612
  7.8 0.8 %copy-start.4 = (bf16[1,128,128]{2,1,0:T(8,128)(2,1)S(1)}, bf16[1,128,128]{2,1,0:T(8,128)(2,1)}, u32[]{:S(2)}) copy-start(bf16[1,128,128]{2,1,0:T(8,128)(2,1)} %param.9) | copy-start | bytes 98308
  11.2 7.3 %collective-permute-start.3 = (bf16[256,384]{1,0:T(8,128)(2,1)S(1)}, bf16[256,384]{1,0:T(8,128)(2,1)S(1)}, u32[]{:S(2)}, u32[]{:S(2)}) collective-permute-start(bf16[256,384]{1,0:T(8,128)(2,1)S(1)} %get-tuple-element.21.own), channel_id=1, source_target_pairs={{2,4},{6,8},{10,12},{14,16},{18,20},{22,24},{26,28},{4,2},{8,6},{1... | collective-permute-start | bytes 589832 | tf_op jit(solution)/shard_map/ppermute | solution.py:358
  11.9 7.8 %collective-permute-start.4 = (bf16[256,384]{1,0:T(8,128)(2,1)S(1)}, bf16[256,384]{1,0:T(8,128)(2,1)S(1)}, u32[]{:S(2)}, u32[]{:S(2)}) collective-permute-start(bf16[256,384]{1,0:T(8,128)(2,1)S(1)} %get-tuple-element.21.own), channel_id=1, source_target_pairs={{0,2},{2,0},{4,6},{6,4},{8,10},{10,8},{12,14},{14,12},{16,18},{18,... | collective-permute-start | bytes 589832 | tf_op jit(solution)/shard_map/ppermute | solution.py:321
  15.0 8.7 %collective-permute-start.2 = (bf16[256,384]{1,0:T(8,128)(2,1)S(1)}, bf16[256,384]{1,0:T(8,128)(2,1)S(1)}, u32[]{:S(2)}, u32[]{:S(2)}) collective-permute-start(bf16[256,384]{1,0:T(8,128)(2,1)S(1)} %get-tuple-element.21.own), channel_id=1, source_target_pairs={{0,4},{4,8},{8,12},{12,16},{16,20},{20,24},{24,28},{6,2},{10,6},{1... | collective-permute-start | bytes 589832 | tf_op jit(solution)/shard_map/ppermute | solution.py:359
  18.5 5.3 %collective-permute-start.5 = (bf16[256,384]{1,0:T(8,128)(2,1)S(1)}, bf16[256,384]{1,0:T(8,128)(2,1)S(1)}, u32[]{:S(2)}, u32[]{:S(2)}) collective-permute-start(bf16[256,384]{1,0:T(8,128)(2,1)S(1)} %collective-permute-done.3.near1), channel_id=1, source_target_pairs={{0,2},{2,0},{4,6},{6,4},{8,10},{10,8},{12,14},{14,12},{16,18},{18,... | collective-permute-start | bytes 589832 | tf_op jit(solution)/shard_map/ppermute | solution.py:321
  29.7 1.3 %collective-permute-start.6 = (bf16[2,128,128]{2,1,0:T(8,128)(2,1)S(1)}, bf16[2,128,128]{2,1,0:T(8,128)(2,1)S(1)}, u32[]{:S(2)}, u32[]{:S(2)}) collective-permute-start(bf16[2,128,128]{2,1,0:T(8,128)(2,1)S(1)} %get-tuple-element.30), channel_id=1, source_target_pairs={{0,2},{2,0},{4,6},{6,4},{8,10},{10,8},{12,14},{14,12},{16,18},{18,... | collective-permute-start | bytes 196616 | tf_op jit(solution)/shard_map/ppermute | solution.py:321
  31.0 6.6 %collective-permute-start.7 = (bf16[560,128]{1,0:T(8,128)(2,1)S(1)}, bf16[560,128]{1,0:T(8,128)(2,1)S(1)}, u32[]{:S(2)}, u32[]{:S(2)}) collective-permute-start(bf16[560,128]{1,0:T(8,128)(2,1)S(1)} %pad_maximum_fusion), channel_id=1, source_target_pairs={{0,4},{2,6},{4,0},{6,2},{8,12},{10,14},{12,8},{14,10},{16,20},{18,... | collective-permute-start | bytes 430088 | tf_op jit(solution)/shard_map/ppermute | solution.py:321
  37.7 5.5 %collective-permute-start.8 = (bf16[560,128]{1,0:T(8,128)(2,1)S(1)}, bf16[560,128]{1,0:T(8,128)(2,1)S(1)}, u32[]{:S(2)}, u32[]{:S(2)}) collective-permute-start(bf16[560,128]{1,0:T(8,128)(2,1)S(1)} %add_convert_fusion.2), channel_id=1, source_target_pairs={{0,8},{2,10},{4,12},{6,14},{8,0},{10,2},{12,4},{14,6},{16,24},{18,... | collective-permute-start | bytes 430088 | tf_op jit(solution)/shard_map/ppermute | solution.py:321
  43.3 8.6 %collective-permute-start.9 = (bf16[560,128]{1,0:T(8,128)(2,1)S(1)}, bf16[560,128]{1,0:T(8,128)(2,1)S(1)}, u32[]{:S(2)}, u32[]{:S(2)}) collective-permute-start(bf16[560,128]{1,0:T(8,128)(2,1)S(1)} %add_convert_fusion.1), channel_id=1, source_target_pairs={{0,16},{2,18},{4,20},{6,22},{8,24},{10,26},{12,28},{14,30},{16,0},... | collective-permute-start | bytes 430088 | tf_op jit(solution)/shard_map/ppermute | solution.py:321
  52.0 7.3 %collective-permute-start.12 = (bf16[560,128]{1,0:T(8,128)(2,1)S(1)}, bf16[560,128]{1,0:T(8,128)(2,1)S(1)}, u32[]{:S(2)}, u32[]{:S(2)}) collective-permute-start(bf16[560,128]{1,0:T(8,128)(2,1)S(1)} %add_convert_fusion.refs_0_), channel_id=1, source_target_pairs={{0,5},{1,4},{2,7},{3,6},{4,1},{5,0},{6,3},{7,2},{8,13},{9,12},{10,... | collective-permute-start | bytes 430088 | tf_op jit(solution)/shard_map/ppermute | solution.py:394
  53.6 6.0 %collective-permute-start.11 = (bf16[560,128]{1,0:T(8,128)(2,1)S(1)}, bf16[560,128]{1,0:T(8,128)(2,1)S(1)}, u32[]{:S(2)}, u32[]{:S(2)}) collective-permute-start(bf16[560,128]{1,0:T(8,128)(2,1)S(1)} %add_convert_fusion.refs_0_), channel_id=1, source_target_pairs={{0,1},{1,0},{2,3},{3,2},{4,5},{5,4},{6,7},{7,6},{8,9},{9,8},{10,11... | collective-permute-start | bytes 430088 | tf_op jit(solution)/shard_map/ppermute | solution.py:324
  54.1 6.6 %collective-permute-start.10 = (bf16[560,128]{1,0:T(8,128)(2,1)S(1)}, bf16[560,128]{1,0:T(8,128)(2,1)S(1)}, u32[]{:S(2)}, u32[]{:S(2)}) collective-permute-start(bf16[560,128]{1,0:T(8,128)(2,1)S(1)} %add_convert_fusion.refs_0_), channel_id=1, source_target_pairs={{0,4},{2,6},{4,0},{6,2},{8,12},{10,14},{12,8},{14,10},{16,20},{18,... | collective-permute-start | bytes 430088 | tf_op jit(solution)/shard_map/ppermute | solution.py:321
  55.5 5.2 %collective-permute-start.13 = (bf16[560,128]{1,0:T(8,128)(2,1)S(1)}, bf16[560,128]{1,0:T(8,128)(2,1)S(1)}, u32[]{:S(2)}, u32[]{:S(2)}) collective-permute-start(bf16[560,128]{1,0:T(8,128)(2,1)S(1)} %add_convert_fusion.refs_0_), channel_id=1, source_target_pairs={{0,2},{2,0},{4,6},{6,4},{8,10},{10,8},{12,14},{14,12},{16,18},{18,... | collective-permute-start | bytes 430088 | tf_op jit(solution)/shard_map/ppermute | solution.py:321
  59.2 1.5 %collective-permute-start.16 = (bf16[560,128]{1,0:T(8,128)(2,1)S(1)}, bf16[560,128]{1,0:T(8,128)(2,1)S(1)}, u32[]{:S(2)}, u32[]{:S(2)}) collective-permute-start(bf16[560,128]{1,0:T(8,128)(2,1)S(1)} %collective-permute-done.12.refs_3_), channel_id=1, source_target_pairs={{0,2},{2,0},{4,6},{6,4},{8,10},{10,8},{12,14},{14,12},{16,18},{18,... | collective-permute-start | bytes 430088 | tf_op jit(solution)/shard_map/ppermute | solution.py:321
  59.6 1.4 %collective-permute-start.15 = (bf16[560,128]{1,0:T(8,128)(2,1)S(1)}, bf16[560,128]{1,0:T(8,128)(2,1)S(1)}, u32[]{:S(2)}, u32[]{:S(2)}) collective-permute-start(bf16[560,128]{1,0:T(8,128)(2,1)S(1)} %collective-permute-done.11.refs_2_), channel_id=1, source_target_pairs={{0,2},{2,0},{4,6},{6,4},{8,10},{10,8},{12,14},{14,12},{16,18},{18,... | collective-permute-start | bytes 430088 | tf_op jit(solution)/shard_map/ppermute | solution.py:321
  60.7 1.4 %collective-permute-start.14 = (bf16[560,128]{1,0:T(8,128)(2,1)S(1)}, bf16[560,128]{1,0:T(8,128)(2,1)S(1)}, u32[]{:S(2)}, u32[]{:S(2)}) collective-permute-start(bf16[560,128]{1,0:T(8,128)(2,1)S(1)} %collective-permute-done.10.refs_1_), channel_id=1, source_target_pairs={{0,2},{2,0},{4,6},{6,4},{8,10},{10,8},{12,14},{14,12},{16,18},{18,... | collective-permute-start | bytes 430088 | tf_op jit(solution)/shard_map/ppermute | solution.py:321

commit v3 on v2

v3 whole, which is shorter than its diff:
```python
import functools
import math

import jax
import jax.numpy as jnp
from jax import lax
from jax.experimental import pallas as pl
from jax.experimental.pallas import tpu as pltpu
from jax.sharding import PartitionSpec as P

QK = 128
VAL = 256
HEADS = 8
CONV = 128
HEAD_QK = QK // HEADS
HEAD_VAL = VAL // HEADS
PACKED = 2 * QK + VAL
BLOCK = 256
BF = jnp.bfloat16
F32 = jnp.float32
SCALING = HEAD_QK ** (-0.5)
EXP2_SCALING = SCALING * math.log2(math.e)

PARTS = 8
FIRST_ROWS = 9 * VAL // PARTS
SECOND_ROWS = 9 * CONV // PARTS
CONV_ROWS = FIRST_ROWS + SECOND_ROWS
PROJ_ROWS = PACKED // CONV * (VAL // PARTS)


def mm(a, b):
    return lax.dot_general(a, b, (((1,), (0,)), ((), ())), preferred_element_type=F32)


def mm_t(a, b):
    return lax.dot_general(a, b, (((1,), (1,)), ((), ())), preferred_element_type=F32)


def one_hot(shape, wanted):
    rows = lax.broadcasted_iota(jnp.int32, shape, 0)
    columns = lax.broadcasted_iota(jnp.int32, shape, 1)
    return jnp.where(columns == wanted(rows), 1.0, 0.0).astype(BF)


def identity(size):
    return one_hot((size, size), lambda rows: rows)


def head_of(values, head, width):
    lanes = lax.broadcasted_iota(jnp.int32, values.shape, 1)
    return jnp.where(lanes // width == head, values, jnp.zeros_like(values))


def moved(values, step):
    count = values.shape[0]
    turned = pltpu.roll(values, (-step) % count, 0)
    at = lax.broadcasted_iota(jnp.int32, values.shape, 0)
    return jnp.where(at == (count - 1 if step > 0 else 0), 0.0, turned)


def for_blocks(count, run):
    if count == 1:
        run(0)
    else:
        lax.fori_loop(0, count, lambda i, carry: (run(i), carry)[1], 0)


def block_at(index):
    return pl.ds(index if isinstance(index, int) else pl.multiple_of(index * BLOCK, BLOCK), BLOCK)


def fetch_kernel(count, *refs):
    targets = refs[-1 - count : -1]
    copies = [pltpu.make_async_copy(refs[i], targets[i], refs[-1].at[i]) for i in range(count)]
    for copy in copies:
        copy.start()
    for copy in copies:
        copy.wait()


def fetch(arrays, after=()):
    return pl.pallas_call(
        functools.partial(fetch_kernel, len(arrays)),
        out_shape=tuple(shape(*array.shape) for array in arrays),
        in_specs=[HBM] * (len(arrays) + len(after)),
        out_specs=[VMEM] * len(arrays),
        scratch_shapes=[pltpu.SemaphoreType.DMA((len(arrays),))],
        cost_estimate=pl.CostEstimate(flops=0, bytes_accessed=4 * 1024 * 1024, transcendentals=0),
        name="fetch",
        **granted(32),
    )(*arrays, *after)


def forward_kernel(whole, *refs):
    count = 1 if whole else 2
    features = refs[:count]
    cotangent = refs[count : 2 * count]
    projection, comb, local, lse, values_t = refs[2 * count :]
    across = comb.shape[0]
    for which in range(count):
        width = features[which].shape[0]
        if whole:
            at = pl.ds(0, width)
        else:
            place = lax.rem(lax.axis_index("cols") + which, 2)
            at = pl.ds(pl.multiple_of(place * width, width), width)
        local[at, PACKED:] = features[which][...]
        comb[at, VAL:] = cotangent[which][...]
    packed = mm(local[:, PACKED:], projection[...]).astype(BF)
    local[:, :PACKED] = packed
    keys = packed[:, QK : 2 * QK]
    values_t[...] = mm_t(identity(VAL), packed[:, 2 * QK :]).astype(BF)

    def block(index):
        at = block_at(index)
        queries = local[at, :QK]
        rows = []
        all_scores = mm_t(jnp.concatenate([head_of(keys, h, HEAD_QK) for h in range(HEADS)], axis=0), queries)
        for head in range(HEADS):
            scores = all_scores[head * across : (head + 1) * across, :]
            maxima = jnp.max(scores, axis=0, keepdims=True)
            exponent = jnp.exp2((scores - maxima) * EXP2_SCALING)
            totals = jnp.sum(exponent, axis=0, keepdims=True)
            weighted = mm(values_t[head * HEAD_VAL : (head + 1) * HEAD_VAL, :], exponent.astype(BF))
            rows.append((weighted * (1.0 / totals)).astype(BF))
            lse[head : head + 1, at] = maxima * EXP2_SCALING + jnp.log2(totals)
        comb[at, :VAL] = mm_t(identity(BLOCK), jnp.concatenate(rows, axis=0)).astype(BF)

    for_blocks(across // BLOCK, block)


class Place:
    def __init__(self):
        row = lax.axis_index("rows")
        self.col = lax.axis_index("cols")
        self.core = lax.rem(row, 2)
        self.chip_bit = lax.rem(row // 2, 2)
        self.col_bit = lax.rem(self.col, 2)
        self.near_inside = jnp.where(self.core == 0, row > 0, row < lax.axis_size("rows") - 1)
        self.taps = [tap + self.core * (2 - 2 * tap) for tap in range(3)]

    def chosen(self, total, half):
        size = total // 4
        middle = size // 2

        def wanted(rows):
            swapped = jnp.where(rows < middle, rows + middle, rows - middle)
            return (2 * half + self.col_bit) * size + jnp.where(self.chip_bit == 0, rows, swapped)

        return one_hot((size, total), wanted)

    def beside(self, weights, tap):
        return jnp.concatenate([weights[self.taps[tap], b] for b in range(3)], axis=1)

    def stacked(self, weights, tap):
        return jnp.concatenate([weights[self.taps[tap], b] for b in range(3)], axis=0)


def side(total, width, sign):
    left = moved(total[:, :width], -sign)
    right = moved(total[:, 2 * width :], sign)
    return left + total[:, width : 2 * width] + right


def spread(values):
    return jnp.concatenate(
        [moved(values, 1).astype(BF), values.astype(BF), moved(values, -1).astype(BF)], axis=1
    )


def middle_kernel(far, near, own, mate, mate1, first_kernel, second_kernel, near_out, own_out, mate_out):
    place = Place()
    slots = (far, near, own, mate, mate1)
    first = [place.beside(first_kernel, a) for a in range(3)]
    second = [place.stacked(second_kernel, a) for a in range(3)]
    for slot, out in ((1, near_out), (2, own_out), (3, mate_out)):
        pre = side(sum(mm(slots[slot + a - 1][:, :VAL], first[a]) for a in range(3)), CONV, 1)
        back = side(sum(mm_t(slots[slot + 1 - a][:, VAL:], second[a]) for a in range(3)), CONV, -1)
        sigma = 1.0 / (1.0 + jnp.exp(-pre))
        hidden = pre * sigma
        slope = back * (sigma * (1.0 + pre * (1.0 - sigma)))
        if slot == 1:
            hidden = jnp.where(place.near_inside, hidden, 0.0)
            slope = jnp.where(place.near_inside, slope, 0.0)
        out[:, :CONV] = hidden.astype(BF)
        out[:, CONV:] = slope.astype(BF)


def conv_grads_kernel(near, own, mate, mate1, own_mid, mate_mid, keep, send):
    place = Place()
    slots = (near, own, mate, mate1)
    mids = {1: own_mid, 2: mate_mid}

    def store(total, start, step, a):
        for b in range(3):
            at = pl.ds(pl.multiple_of(start + (place.taps[a] * 3 + b) * step, step), step)
            keep[at, :] = total[:step, b * CONV : (b + 1) * CONV]
            send[at, :] = total[step:, b * CONV : (b + 1) * CONV]

    pick = place.chosen(VAL, place.core)
    attended_t = [mm_t(pick, slot[:, :VAL]).astype(BF) for slot in slots]
    slope = {slot: spread(mid[:, CONV:].astype(F32)) for slot, mid in mids.items()}
    for a in range(3):
        total = sum(mm(attended_t[slot + a - 1], slope[slot]) for slot in mids).astype(BF)
        store(total, 0, VAL // PARTS, a)
    pick = place.chosen(CONV, place.core)
    hidden_t = {slot: mm_t(pick, mid[:, :CONV]).astype(BF) for slot, mid in mids.items()}
    cotangent = [spread(slot[:, VAL:].astype(F32)) for slot in slots]
    for a in range(3):
        total = sum(mm(hidden_t[slot], cotangent[slot + 1 - a]) for slot in mids).astype(BF)
        store(total, FIRST_ROWS, CONV // PARTS, a)


def attention_backward_kernel(
    near_mid, own_mid, mate_mid, own, local, lse, first_kernel, grad_own, proj_own, proj_mate, upstream_ref, grad_t
):
    place = Place()
    across = own.shape[0]
    part_width = grad_own.shape[0]
    mids = (near_mid, own_mid, mate_mid)
    upstream_ref[...] = side(
        sum(mm_t(mids[2 - a][:, CONV:], place.stacked(first_kernel, a)) for a in range(3)), VAL, -1
    ).astype(BF)
    keys = local[:, QK : 2 * QK]
    values = local[:, 2 * QK : PACKED]
    keys_t = mm_t(identity(QK), keys).astype(BF)
    blocks = across // BLOCK
    if blocks > 1:
        grad_t[...] = jnp.zeros_like(grad_t)

    def add_rows(start, count, terms):
        if blocks > 1:
            grad_t[start : start + count, :] += terms
        else:
            grad_t[start : start + count, :] = terms

    def block(index):
        at = block_at(index)
        queries = local[at, :QK]
        upstream = upstream_ref[at, :]
        queries_t = mm_t(identity(QK), queries).astype(BF)
        upstream_t = mm_t(identity(VAL), upstream)
        products = upstream_t * mm_t(identity(VAL), own[at, :VAL])
        upstream_t = upstream_t.astype(BF)
        all_scores = mm_t(jnp.concatenate([head_of(keys, h, HEAD_QK) for h in range(HEADS)], axis=0), queries)
        all_slopes = mm_t(jnp.concatenate([head_of(values, h, HEAD_VAL) for h in range(HEADS)], axis=0), upstream)
        for head in range(HEADS):
            qk_rows = slice(head * HEAD_QK, (head + 1) * HEAD_QK)
            val_rows = slice(head * HEAD_VAL, (head + 1) * HEAD_VAL)
            scores = all_scores[head * across : (head + 1) * across, :]
            soft = jnp.exp2(scores * EXP2_SCALING - lse[head : head + 1, at])
            inner = jnp.sum(products[val_rows, :], axis=0, keepdims=True)
            slopes = all_slopes[head * across : (head + 1) * across, :]
            dscore = (soft * (slopes - inner)).astype(BF)
            grad_t[qk_rows, at] = SCALING * mm(keys_t[qk_rows, :], dscore)
            add_rows(QK + head * HEAD_QK, HEAD_QK, SCALING * mm_t(queries_t[qk_rows, :], dscore))
            add_rows(2 * QK + head * HEAD_VAL, HEAD_VAL, mm_t(upstream_t[val_rows, :], soft.astype(BF)))

    for_blocks(blocks, block)

    grad = grad_t[...].astype(BF)
    features = local[:, PACKED:]
    step = VAL // PARTS
    for target, half in ((proj_own, place.core), (proj_mate, 1 - place.core)):
        total = mm_t(mm_t(place.chosen(VAL, half), features).astype(BF), grad).astype(BF)
        for j in range(PACKED // CONV):
            target[0, j * step : (j + 1) * step, :] = total[:step, j * CONV : (j + 1) * CONV]
            target[1, j * step : (j + 1) * step, :] = total[step:, j * CONV : (j + 1) * CONV]
    own_pixels = one_hot((part_width, across), lambda rows: rows + place.col * part_width)
    grad_own[...] = mm_t(own_pixels, grad).astype(BF)


def backward_kernel(
    far,
    near,
    own,
    mate,
    mate1,
    local,
    lse,
    first_kernel,
    second_kernel,
    near_mid,
    own_mid,
    mate_mid,
    grad_own,
    keep,
    send,
    proj_own,
    proj_mate,
    upstream,
    grad_t,
):
    middle_kernel(far, near, own, mate, mate1, first_kernel, second_kernel, near_mid, own_mid, mate_mid)
    conv_grads_kernel(near, own, mate, mate1, own_mid, mate_mid, keep, send)
    attention_backward_kernel(
        near_mid, own_mid, mate_mid, own, local, lse, first_kernel, grad_own, proj_own, proj_mate, upstream, grad_t
    )


def outputs_kernel(near_mid, own_mid, mate_mid, grad_own, projection, second_kernel, output_map, input_grad, rows):
    place = Place()
    part_width = output_map.shape[0]
    mids = (near_mid, own_mid, mate_mid)
    rows[...] = side(sum(mm(mids[a][:, :CONV], place.beside(second_kernel, a)) for a in range(3)), CONV, 1)
    output_map[...] = rows[pl.ds(pl.multiple_of(place.col * part_width, part_width), part_width), :].astype(BF)
    input_grad[...] = mm_t(grad_own[...], projection[...]).astype(BF)


def unpack_kernel(factor, *refs):
    pieces = refs[:8]
    projection_grad, first_grad, second_grad = refs[8:]
    row = lax.axis_index("rows")
    core = lax.rem(row, 2)
    chip_bit = lax.rem(row // 2, 2)
    col_bit = lax.rem(lax.axis_index("cols"), 2)
    for which, piece in enumerate(pieces):
        core_flip, col_flip, chip_flip = which // 4, which // 2 % 2, which % 2
        part = (
            4 * lax.rem(core + core_flip, 2) + 2 * lax.rem(col_bit + col_flip, 2) + lax.rem(chip_bit + chip_flip, 2)
        )
        step = VAL // PARTS
        at = pl.ds(pl.multiple_of(part * step, step), step)
        for tap in range(9):
            first_grad[tap // 3, tap % 3, at, :] = piece[tap * step : (tap + 1) * step, :].astype(F32) * factor
        start = FIRST_ROWS + SECOND_ROWS
        for j in range(PACKED // CONV):
            projection_grad[at, j * CONV : (j + 1) * CONV] = (
                piece[start + j * step : start + (j + 1) * step, :].astype(F32) * factor
            )
        step = CONV // PARTS
        at = pl.ds(pl.multiple_of(part * step, step), step)
        for tap in range(9):
            begin = FIRST_ROWS + tap * step
            second_grad[tap // 3, tap % 3, at, :] = piece[begin : begin + step, :].astype(F32) * factor


def shape(*dims, dtype=BF):
    return jax.ShapeDtypeStruct(dims, dtype)


def granted(across):
    return dict(compiler_params=pltpu.CompilerParams(vmem_limit_bytes=across * 64 * 1024))


VMEM = pl.BlockSpec(memory_space=pltpu.VMEM)
HBM = pl.BlockSpec(memory_space=pltpu.HBM)


def body(features, projection, first_kernel, second_kernel, cotangent):
    height, part_width, channels = features.shape
    rows_size = lax.axis_size("rows")
    cols_size = lax.axis_size("cols")
    across = part_width * cols_size

    def rows_flip(values, bit):
        return lax.ppermute(values, "rows", [(i, i ^ bit) for i in range(rows_size)])

    def cols_flip(values):
        return lax.ppermute(values, "cols", [(i, i ^ 1) for i in range(cols_size)])

    def wide(values):
        return values.astype(F32)

    def added(one, two):
        return (one + two).astype(BF)

    def call(kernel, out_shape, operands, scratch=(), name=None):
        return pl.pallas_call(
            kernel,
            out_shape=out_shape,
            in_specs=[VMEM] * len(operands),
            out_specs=[VMEM] * len(out_shape),
            scratch_shapes=scratch,
            cost_estimate=pl.CostEstimate(flops=10**9, bytes_accessed=4 * 1024 * 1024, transcendentals=0),
            name=name,
            **granted(across),
        )(*operands)

    given = (features, cotangent)
    projection, features, cotangent = fetch((projection, features[0], cotangent[0]))
    if cols_size == 2:
        pieces = (features, cols_flip(given[0][0]), cotangent, cols_flip(given[1][0]))
    else:
        pieces = tuple(lax.all_gather(array[0], "cols", axis=0, tiled=True) for array in given)
    own, local, lse = call(
        functools.partial(forward_kernel, cols_size != 2),
        (
            shape(across, VAL + CONV),
            shape(across, PACKED + channels),
            shape(HEADS, across, dtype=F32),
        ),
        (*pieces, projection),
        (pltpu.VMEM((VAL, across), BF),),
        name="attention_forward",
    )

    first_kernel, second_kernel = fetch((first_kernel, second_kernel), (lse,))
    near = [(i, i + 1) for i in range(1, rows_size - 1, 2)] + [(i + 1, i) for i in range(1, rows_size - 1, 2)]
    far = [(i, i + 2) for i in range(0, rows_size - 2, 2)] + [(i, i - 2) for i in range(3, rows_size, 2)]
    near1 = lax.ppermute(own, "rows", near)
    near2 = lax.ppermute(own, "rows", far)
    mate = rows_flip(own, 1)
    mate1 = rows_flip(near1, 1)
    near_mid, own_mid, mate_mid, grad_own, keep, send, proj_own, proj_mate = call(
        backward_kernel,
        (
            shape(across, 2 * CONV),
            shape(across, 2 * CONV),
            shape(across, 2 * CONV),
            shape(part_width, PACKED),
            shape(FIRST_ROWS + SECOND_ROWS, CONV),
            shape(FIRST_ROWS + SECOND_ROWS, CONV),
            shape(2, PROJ_ROWS, CONV),
            shape(2, PROJ_ROWS, CONV),
        ),
        (near2, near1, own, mate, mate1, local, lse, first_kernel, second_kernel),
        (pltpu.VMEM((across, VAL), BF), pltpu.VMEM((PACKED, across), F32)),
        name="block_backward",
    )
    output_map, input_grad = call(
        outputs_kernel,
        (shape(part_width, CONV), shape(part_width, channels)),
        (near_mid, own_mid, mate_mid, grad_own, projection, second_kernel),
        (pltpu.VMEM((across, CONV), F32),),
        name="outputs",
    )
    proj_sum = added(wide(proj_own), wide(rows_flip(proj_mate, 1)))
    sent = jnp.concatenate([send, proj_sum[1]], axis=0)
    kept = jnp.concatenate([keep, proj_sum[0]], axis=0)
    if rows_size > 4:
        total = added(wide(kept) + wide(rows_flip(kept, 4)), wide(rows_flip(sent, 2)) + wide(rows_flip(sent, 6)))
    else:
        total = added(wide(kept), wide(rows_flip(sent, 2)))
    bit = 8
    while bit < rows_size:
        total = added(wide(total), wide(rows_flip(total, bit)))
        bit *= 2
    chip = rows_flip(total, 2)
    side = cols_flip(total)
    corner = lax.ppermute(
        total,
        ("rows", "cols"),
        [(i * cols_size + j, (i ^ 2) * cols_size + (j ^ 1)) for i in range(rows_size) for j in range(cols_size)],
    )
    four = (total, chip, side, corner)
    eight = four + tuple(rows_flip(piece, 1) for piece in four)
    factor = 1.0 / math.sqrt(height * across * rows_size)
    projection_grad, first_grad, second_grad = call(
        functools.partial(unpack_kernel, factor),
        (
            shape(channels, PACKED, dtype=F32),
            shape(3, 3, VAL, CONV, dtype=F32),
            shape(3, 3, CONV, CONV, dtype=F32),
        ),
        eight,
        name="unpack_sums",
    )
    return (output_map[None], input_grad[None], projection_grad, first_grad, second_grad)


def solution(mesh):
    placed = (P("rows", "cols", None), P(), P(), P(), P("rows", "cols", None))
    return jax.shard_map(
        body,
        mesh=mesh,
        in_specs=placed,
        out_specs=(P("rows", "cols", None), P("rows", "cols", None), P(), P(), P()),
        check_vma=False,
    )
```

time: 64 us -> 60.2 us (0.941)
  Pallas kernels: 10.4 us -> 8.56 us
  local copies, waits for them, and re-layouts: 3.74 us -> 2.56 us
  starting transfers between devices: 22.7 us -> 21.9 us
    pallas_call x4 -> x6, Pallas kernels: 10.4 us -> 8.56 us  [the longest x4 8.19 us: call(): pl.pallas_call(kernel, out_shape=out_shape, in_specs=[VMEM] * len(operand...]
    unnamed x10, local copies, waits for them, and re-layouts: 3.73 us -> 2.55 us
    ppermute x11 -> x12, starting transfers between devices: 13.4 us -> 12.5 us  [rows_flip(): lax.ppermute(values, 'rows', [(i, i ^ bit) for i in range(rows_size)])]
    ppermute x3, starting transfers between devices: 3.61 us -> 4.4 us  [cols_flip(): return lax.ppermute(values, 'cols', [(i, i ^ 1) for i in range(cols_size)])]
    ppermute x1, starting transfers between devices: 1.61 us -> 0.87 us  [body(): lax.ppermute(total, ('rows', 'cols'), [(i * cols_size + j, (i ^ 2) * cols...]
    ppermute x3, waiting for transfers between devices: 1.18 us -> 1.9 us  [cols_flip(): return lax.ppermute(values, 'cols', [(i, i ^ 1) for i in range(cols_size)])]
    ppermute x11 -> x12, waiting for transfers between devices: 17 us -> 16.6 us  [rows_flip(): lax.ppermute(values, 'rows', [(i, i ^ bit) for i in range(rows_size)])]
  transfers between devices with their start and end apart: 17 -> 18, of which waited for: 11 -> 11; matrix products, arithmetic and copies ran while one was open for 0% -> 0% of each run, Pallas kernels for 0% -> 2%
where the time goes in v3:
time: 60.2 us; the launch traced here: 60 us
  waiting for transfers between devices  26.1 us (43%)
  starting transfers between devices  21.9 us (36%)
  Pallas kernels  8.56 us (14%)
  local copies, waits for them, and re-layouts  2.56 us (4%)
  between operations  0.76 us (1%)
    ppermute x12, waiting for transfers between devices, rows_flip(): lax.ppermute(values, 'rows', [(i, i ^ bit) for i in range(rows_size)])  16.6 us
    ppermute x12, starting transfers between devices, rows_flip(): lax.ppermute(values, 'rows', [(i, i ^ bit) for i in range(rows_size)])  12.5 us
    pallas_call x4, Pallas kernels, call(): pl.pallas_call(kernel, out_shape=out_shape, in_specs=[VMEM] * len(operand...  8.19 us
    ppermute x3, starting transfers between devices, cols_flip(): return lax.ppermute(values, 'cols', [(i, i ^ 1) for i in range(cols_size)])  4.4 us
    ppermute x1, waiting for transfers between devices, body(): near2 = lax.ppermute(own, 'rows', far)  3.88 us
    ppermute x1, waiting for transfers between devices, body(): lax.ppermute(total, ('rows', 'cols'), [(i * cols_size + j, (i ^ 2) * cols...  3.65 us
    ppermute x1, starting transfers between devices, body(): near2 = lax.ppermute(own, 'rows', far)  3.42 us
    unnamed x10, local copies, waits for them, and re-layouts  2.55 us
  transfers between devices with their start and end apart: 18, of which 11 were waited for; matrix products, arithmetic and copies ran while one was open for 0% of the time, Pallas kernels for 2%

profile of v3, /device:TPU:0, one launch (start us, length us, event | category | flops | bytes accessed | tf_op | source)
XLA Modules:
  0.0 60.0 jit_solution(526190664673624041)
XLA Ops:
  0.6 3.0 %collective-permute-start = (bf16[128,256]{1,0:T(8,128)(2,1)}, bf16[128,256]{1,0:T(8,128)(2,1)S(1)}, u32[]{:S(2)}, u32[]{:S(2)}) collective-permute-start(bf16[128,256]{1,0:T(8,128)(2,1)} %bitcast.8), channel_id=1, source_target_pairs={{0,1},{1,0},{2,3},{3,2},{4,5},{5,4},{6,7},{7,6},{8,9},{9,8},{10,11... | collective-permute-start | bytes 196616 | tf_op jit(solution)/shard_map/ppermute | solution.py:360
  3.7 0.9 %copy-done.2 = bf16[256,512]{1,0:T(8,128)(2,1)S(1)} copy-done((bf16[256,512]{1,0:T(8,128)(2,1)S(1)}, bf16[256,512]{1,0:T(8,128)(2,1)}, u32[]{:S(2)}) %copy-start.2) | copy-done | bytes 262168
  6.4 1.3 %collective-permute-done.1.refs_3_ = bf16[128,128]{1,0:T(8,128)(2,1)S(1)} collective-permute-done((bf16[128,128]{1,0:T(8,128)(2,1)}, bf16[128,128]{1,0:T(8,128)(2,1)S(1)}, u32[]{:S(2)}, u32[]{:S(2)}) %collective-permute-start.1) | collective-permute-done | bytes 32800 | tf_op jit(solution)/shard_map/ppermute | solution.py:360
  7.8 1.3 %attention_forward.1 = (bf16[256,384]{1,0:T(8,128)(2,1)S(1)}, bf16[256,768]{1,0:T(8,128)(2,1)S(1)}, f32[8,256]{1,0:T(8,128)S(1)}) custom-call(bf16[128,256]{1,0:T(8,128)(2,1)S(1)} %get-tuple-element.26.refs_0_, bf16[128,256]{1,0:T(8,128)(2,1)S(1)} %collective-permute-done.refs_1_, bf16[128,128]{1,0:T(8,128)(2,1)S(1)} %get-tuple-element.27.refs_2_, ...), custom_call_target="tpu_custom_call" | custom-call | flops 1000000000 | bytes 4194304 | tf_op jit(solution)/shard_map/attention_forward/pallas_call | solution.py:369
  9.8 2.9 %collective-permute-start.4 = (bf16[256,384]{1,0:T(8,128)(2,1)S(1)}, bf16[256,384]{1,0:T(8,128)(2,1)S(1)}, u32[]{:S(2)}, u32[]{:S(2)}) collective-permute-start(bf16[256,384]{1,0:T(8,128)(2,1)S(1)} %get-tuple-element.29.own), channel_id=1, source_target_pairs={{0,2},{2,0},{4,6},{6,4},{8,10},{10,8},{12,14},{14,12},{16,18},{18,... | collective-permute-start | bytes 589832 | tf_op jit(solution)/shard_map/ppermute | solution.py:357
  12.7 3.4 %collective-permute-start.2 = (bf16[256,384]{1,0:T(8,128)(2,1)S(1)}, bf16[256,384]{1,0:T(8,128)(2,1)S(1)}, u32[]{:S(2)}, u32[]{:S(2)}) collective-permute-start(bf16[256,384]{1,0:T(8,128)(2,1)S(1)} %get-tuple-element.29.own), channel_id=1, source_target_pairs={{0,4},{4,8},{8,12},{12,16},{16,20},{20,24},{24,28},{6,2},{10,6},{1... | collective-permute-start | bytes 589832 | tf_op jit(solution)/shard_map/ppermute | solution.py:402
  16.2 1.2 %collective-permute-start.5 = (bf16[256,384]{1,0:T(8,128)(2,1)S(1)}, bf16[256,384]{1,0:T(8,128)(2,1)S(1)}, u32[]{:S(2)}, u32[]{:S(2)}) collective-permute-start(bf16[256,384]{1,0:T(8,128)(2,1)S(1)} %collective-permute-done.3.near), channel_id=1, source_target_pairs={{0,2},{2,0},{4,6},{6,4},{8,10},{10,8},{12,14},{14,12},{16,18},{18,... | collective-permute-start | bytes 589832 | tf_op jit(solution)/shard_map/ppermute | solution.py:357
  17.6 3.9 %collective-permute-done.2.far = bf16[256,384]{1,0:T(8,128)(2,1)S(1)} collective-permute-done((bf16[256,384]{1,0:T(8,128)(2,1)S(1)}, bf16[256,384]{1,0:T(8,128)(2,1)S(1)}, u32[]{:S(2)}, u32[]{:S(2)}) %collective-permute-start.2) | collective-permute-done | bytes 196640 | tf_op jit(solution)/shard_map/ppermute | solution.py:402
  21.5 4.3 %block_backward.1 = (bf16[256,256]{1,0:T(8,128)(2,1)S(1)}, bf16[256,256]{1,0:T(8,128)(2,1)S(1)}, bf16[256,256]{1,0:T(8,128)(2,1)S(1)}, bf16[128,512]{1,0:T(8,128...) custom-call(bf16[256,384]{1,0:T(8,128)(2,1)S(1)} %collective-permute, ...), custom_call_target="tpu_custom_call" | custom-call | flops 1000000000 | bytes 4194304 | tf_op jit(solution)/shard_map/block_backward/pallas_call | solution.py:369
  25.8 1.2 %collective-permute-done.6 = bf16[2,128,128]{2,1,0:T(8,128)(2,1)S(1)} collective-permute-done((bf16[2,128,128]{2,1,0:T(8,128)(2,1)S(1)}, bf16[2,128,128]{2,1,0:T(8,128)(2,1)S(1)}, u32[]{:S(2)}, u32[]{:S(2)}) %collective-permute-start.6) | collective-permute-done | bytes 65568 | tf_op jit(solution)/shard_map/ppermute | solution.py:357
  27.1 2.6 %collective-permute-start.7 = (bf16[560,128]{1,0:T(8,128)(2,1)S(1)}, bf16[560,128]{1,0:T(8,128)(2,1)S(1)}, u32[]{:S(2)}, u32[]{:S(2)}) collective-permute-start(bf16[560,128]{1,0:T(8,128)(2,1)S(1)} %pad_maximum_fusion), channel_id=1, source_target_pairs={{0,8},{2,10},{4,12},{6,14},{8,0},{10,2},{12,4},{14,6},{16,24},{18,... | collective-permute-start | bytes 430088 | tf_op jit(solution)/shard_map/ppermute | solution.py:357
  29.8 1.5 %collective-permute-start.9 = (bf16[560,128]{1,0:T(8,128)(2,1)S(1)}, bf16[560,128]{1,0:T(8,128)(2,1)S(1)}, u32[]{:S(2)}, u32[]{:S(2)}) collective-permute-start(bf16[560,128]{1,0:T(8,128)(2,1)S(1)} %pad_maximum_fusion.1), channel_id=1, source_target_pairs={{0,12},{2,14},{4,8},{6,10},{8,4},{10,6},{12,0},{14,2},{16,28},{18,... | collective-permute-start | bytes 430088 | tf_op jit(solution)/shard_map/ppermute | solution.py:357
  31.4 2.9 %collective-permute-done.7 = bf16[560,128]{1,0:T(8,128)(2,1)S(1)} collective-permute-done((bf16[560,128]{1,0:T(8,128)(2,1)S(1)}, bf16[560,128]{1,0:T(8,128)(2,1)S(1)}, u32[]{:S(2)}, u32[]{:S(2)}) %collective-permute-start.7) | collective-permute-done | bytes 143392 | tf_op jit(solution)/shard_map/ppermute | solution.py:357
  34.4 3.8 %collective-permute-done.9 = bf16[560,128]{1,0:T(8,128)(2,1)S(1)} collective-permute-done((bf16[560,128]{1,0:T(8,128)(2,1)S(1)}, bf16[560,128]{1,0:T(8,128)(2,1)S(1)}, u32[]{:S(2)}, u32[]{:S(2)}) %collective-permute-start.9) | collective-permute-done | bytes 143392 | tf_op jit(solution)/shard_map/ppermute | solution.py:357
  38.1 1.4 %collective-permute-done.8 = bf16[560,128]{1,0:T(8,128)(2,1)S(1)} collective-permute-done((bf16[560,128]{1,0:T(8,128)(2,1)S(1)}, bf16[560,128]{1,0:T(8,128)(2,1)S(1)}, u32[]{:S(2)}, u32[]{:S(2)}) %collective-permute-start.8) | collective-permute-done | bytes 143392 | tf_op jit(solution)/shard_map/ppermute | solution.py:357
  39.6 2.6 %collective-permute-start.10 = (bf16[560,128]{1,0:T(8,128)(2,1)S(1)}, bf16[560,128]{1,0:T(8,128)(2,1)S(1)}, u32[]{:S(2)}, u32[]{:S(2)}) collective-permute-start(bf16[560,128]{1,0:T(8,128)(2,1)S(1)} %add_convert_fusion.1), channel_id=1, source_target_pairs={{0,16},{2,18},{4,20},{6,22},{8,24},{10,26},{12,28},{14,30},{16,0},... | collective-permute-start | bytes 430088 | tf_op jit(solution)/shard_map/ppermute | solution.py:357
  42.3 6.1 %collective-permute-done.10 = bf16[560,128]{1,0:T(8,128)(2,1)S(1)} collective-permute-done((bf16[560,128]{1,0:T(8,128)(2,1)S(1)}, bf16[560,128]{1,0:T(8,128)(2,1)S(1)}, u32[]{:S(2)}, u32[]{:S(2)}) %collective-permute-start.10) | collective-permute-done | bytes 143392 | tf_op jit(solution)/shard_map/ppermute | solution.py:357
  48.4 0.9 %collective-permute-start.13 = (bf16[560,128]{1,0:T(8,128)(2,1)S(1)}, bf16[560,128]{1,0:T(8,128)(2,1)S(1)}, u32[]{:S(2)}, u32[]{:S(2)}) collective-permute-start(bf16[560,128]{1,0:T(8,128)(2,1)S(1)} %add_convert_fusion.refs_0_), channel_id=1, source_target_pairs={{0,5},{1,4},{2,7},{3,6},{4,1},{5,0},{6,3},{7,2},{8,13},{9,12},{10,... | collective-permute-start | bytes 430088 | tf_op jit(solution)/shard_map/ppermute | solution.py:441
  49.3 1.3 %collective-permute-start.12 = (bf16[560,128]{1,0:T(8,128)(2,1)S(1)}, bf16[560,128]{1,0:T(8,128)(2,1)S(1)}, u32[]{:S(2)}, u32[]{:S(2)}) collective-permute-start(bf16[560,128]{1,0:T(8,128)(2,1)S(1)} %add_convert_fusion.refs_0_), channel_id=1, source_target_pairs={{0,1},{1,0},{2,3},{3,2},{4,5},{5,4},{6,7},{7,6},{8,9},{9,8},{10,11... | collective-permute-start | bytes 430088 | tf_op jit(solution)/shard_map/ppermute | solution.py:360
  50.6 1.4 %collective-permute-start.11 = (bf16[560,128]{1,0:T(8,128)(2,1)S(1)}, bf16[560,128]{1,0:T(8,128)(2,1)S(1)}, u32[]{:S(2)}, u32[]{:S(2)}) collective-permute-start(bf16[560,128]{1,0:T(8,128)(2,1)S(1)} %add_convert_fusion.refs_0_), channel_id=1, source_target_pairs={{0,4},{2,6},{4,0},{6,2},{8,12},{10,14},{12,8},{14,10},{16,20},{18,... | collective-permute-start | bytes 430088 | tf_op jit(solution)/shard_map/ppermute | solution.py:357
  52.0 3.7 %collective-permute-done.13.refs_3_ = bf16[560,128]{1,0:T(8,128)(2,1)S(1)} collective-permute-done((bf16[560,128]{1,0:T(8,128)(2,1)S(1)}, bf16[560,128]{1,0:T(8,128)(2,1)S(1)}, u32[]{:S(2)}, u32[]{:S(2)}) %collective-permute-start.13) | collective-permute-done | bytes 143392 | tf_op jit(solution)/shard_map/ppermute | solution.py:441
  56.2 0.8 %collective-permute-done.11.refs_1_ = bf16[560,128]{1,0:T(8,128)(2,1)S(1)} collective-permute-done((bf16[560,128]{1,0:T(8,128)(2,1)S(1)}, bf16[560,128]{1,0:T(8,128)(2,1)S(1)}, u32[]{:S(2)}, u32[]{:S(2)}) %collective-permute-start.11) | collective-permute-done | bytes 143392 | tf_op jit(solution)/shard_map/ppermute | solution.py:357
  57.0 1.0 %outputs.1 = (bf16[128,128]{1,0:T(8,128)(2,1)}, bf16[128,256]{1,0:T(8,128)(2,1)}) custom-call(bf16[256,256]{1,0:T(8,128)(2,1)S(1)} %get-tuple-element.34.near_mid, bf16[256,256]{1,0:T(8,128)(2,1)S(1)} %get-tuple-element.35.own_mid, bf16[256,256]{1,0:T(8,128)(2,1)S(1)} %get-tuple-element.36.mate_mid, bf16[128,512]{1,0:T(8,128)(2,1)S(1)} %get-tuple-element.37.grad_own, ...), custom_call_target="tpu_custom_call" | custom-call | flops 1000000000 | bytes 4194304 | tf_op jit(solution)/shard_map/outputs/pallas_call | solution.py:369
  58.4 1.5 %unpack_sums.1 = (f32[256,512]{1,0:T(8,128)}, f32[3,3,256,128]{3,2,1,0:T(8,128)}, f32[3,3,128,128]{3,2,1,0:T(8,128)}) custom-call(bf16[560,128]{1,0:T(8,128)(2,1)S(1)} %add_convert_fusion.refs_0_, bf16[560,128]{1,0:T(8,128)(2,1)S(1)} %collective-permute-done.11.refs_1_, bf16[560,128]{1,0:T(8,128)(2,1)S(1)} %collective-permute-done.12.refs_2_, ...), custom_call_target="tpu_custom_call" | custom-call | flops 1000000000 | bytes 4194304 | tf_op jit(solution)/shard_map/unpack_sums/pallas_call | solution.py:369
  (34 shorter events, 4.1 us)
Async XLA Ops:
  0.6 7.1 %collective-permute-start = (bf16[128,256]{1,0:T(8,128)(2,1)}, bf16[128,256]{1,0:T(8,128)(2,1)S(1)}, u32[]{:S(2)}, u32[]{:S(2)}) collective-permute-start(bf16[128,256]{1,0:T(8,128)(2,1)} %bitcast.8), channel_id=1, source_target_pairs={{0,1},{1,0},{2,3},{3,2},{4,5},{5,4},{6,7},{7,6},{8,9},{9,8},{10,11... | collective-permute-start | bytes 196616 | tf_op jit(solution)/shard_map/ppermute | solution.py:360
  3.6 4.1 %collective-permute-start.1 = (bf16[128,128]{1,0:T(8,128)(2,1)}, bf16[128,128]{1,0:T(8,128)(2,1)S(1)}, u32[]{:S(2)}, u32[]{:S(2)}) collective-permute-start(bf16[128,128]{1,0:T(8,128)(2,1)} %bitcast.10), channel_id=1, source_target_pairs={{0,1},{1,0},{2,3},{3,2},{4,5},{5,4},{6,7},{7,6},{8,9},{9,8},{10,11... | collective-permute-start | bytes 98312 | tf_op jit(solution)/shard_map/ppermute | solution.py:360
  3.7 0.9 %copy-start.2 = (bf16[256,512]{1,0:T(8,128)(2,1)S(1)}, bf16[256,512]{1,0:T(8,128)(2,1)}, u32[]{:S(2)}) copy-start(bf16[256,512]{1,0:T(8,128)(2,1)} %refs_0_.2) | copy-start | bytes 786436
  4.7 0.8 %copy-start.3 = (bf16[1,128,256]{2,1,0:T(8,128)(2,1)S(1)}, bf16[1,128,256]{2,1,0:T(8,128)(2,1)}, u32[]{:S(2)}) copy-start(bf16[1,128,256]{2,1,0:T(8,128)(2,1)} %param.5) | copy-start | bytes 196612
  5.5 0.8 %copy-start.4 = (bf16[1,128,128]{2,1,0:T(8,128)(2,1)S(1)}, bf16[1,128,128]{2,1,0:T(8,128)(2,1)}, u32[]{:S(2)}) copy-start(bf16[1,128,128]{2,1,0:T(8,128)(2,1)} %param.9) | copy-start | bytes 98308
  7.8 9.6 %copy-start = (bf16[3,3,256,128]{3,2,1,0:T(8,128)(2,1)S(1)}, bf16[3,3,256,128]{3,2,1,0:T(8,128)(2,1)}, u32[]{:S(2)}) copy-start(bf16[3,3,256,128]{3,2,1,0:T(8,128)(2,1)} %refs_0_.3) | copy-start | bytes 1769476
  7.8 9.6 %copy-start.1 = (bf16[3,3,128,128]{3,2,1,0:T(8,128)(2,1)S(1)}, bf16[3,3,128,128]{3,2,1,0:T(8,128)(2,1)}, u32[]{:S(2)}) copy-start(bf16[3,3,128,128]{3,2,1,0:T(8,128)(2,1)} %refs_1_.1) | copy-start | bytes 884740
  9.1 7.0 %collective-permute-start.3 = (bf16[256,384]{1,0:T(8,128)(2,1)S(1)}, bf16[256,384]{1,0:T(8,128)(2,1)S(1)}, u32[]{:S(2)}, u32[]{:S(2)}) collective-permute-start(bf16[256,384]{1,0:T(8,128)(2,1)S(1)} %get-tuple-element.29.own), channel_id=1, source_target_pairs={{2,4},{6,8},{10,12},{14,16},{18,20},{22,24},{26,28},{4,2},{8,6},{1... | collective-permute-start | bytes 589832 | tf_op jit(solution)/shard_map/ppermute | solution.py:401
  9.8 7.8 %collective-permute-start.4 = (bf16[256,384]{1,0:T(8,128)(2,1)S(1)}, bf16[256,384]{1,0:T(8,128)(2,1)S(1)}, u32[]{:S(2)}, u32[]{:S(2)}) collective-permute-start(bf16[256,384]{1,0:T(8,128)(2,1)S(1)} %get-tuple-element.29.own), channel_id=1, source_target_pairs={{0,2},{2,0},{4,6},{6,4},{8,10},{10,8},{12,14},{14,12},{16,18},{18,... | collective-permute-start | bytes 589832 | tf_op jit(solution)/shard_map/ppermute | solution.py:357
  12.7 8.7 %collective-permute-start.2 = (bf16[256,384]{1,0:T(8,128)(2,1)S(1)}, bf16[256,384]{1,0:T(8,128)(2,1)S(1)}, u32[]{:S(2)}, u32[]{:S(2)}) collective-permute-start(bf16[256,384]{1,0:T(8,128)(2,1)S(1)} %get-tuple-element.29.own), channel_id=1, source_target_pairs={{0,4},{4,8},{8,12},{12,16},{16,20},{20,24},{24,28},{6,2},{10,6},{1... | collective-permute-start | bytes 589832 | tf_op jit(solution)/shard_map/ppermute | solution.py:402
  16.2 5.3 %collective-permute-start.5 = (bf16[256,384]{1,0:T(8,128)(2,1)S(1)}, bf16[256,384]{1,0:T(8,128)(2,1)S(1)}, u32[]{:S(2)}, u32[]{:S(2)}) collective-permute-start(bf16[256,384]{1,0:T(8,128)(2,1)S(1)} %collective-permute-done.3.near), channel_id=1, source_target_pairs={{0,2},{2,0},{4,6},{6,4},{8,10},{10,8},{12,14},{14,12},{16,18},{18,... | collective-permute-start | bytes 589832 | tf_op jit(solution)/shard_map/ppermute | solution.py:357
  25.8 1.3 %collective-permute-start.6 = (bf16[2,128,128]{2,1,0:T(8,128)(2,1)S(1)}, bf16[2,128,128]{2,1,0:T(8,128)(2,1)S(1)}, u32[]{:S(2)}, u32[]{:S(2)}) collective-permute-start(bf16[2,128,128]{2,1,0:T(8,128)(2,1)S(1)} %get-tuple-element.42), channel_id=1, source_target_pairs={{0,2},{2,0},{4,6},{6,4},{8,10},{10,8},{12,14},{14,12},{16,18},{18,... | collective-permute-start | bytes 196616 | tf_op jit(solution)/shard_map/ppermute | solution.py:357
  27.1 7.2 %collective-permute-start.7 = (bf16[560,128]{1,0:T(8,128)(2,1)S(1)}, bf16[560,128]{1,0:T(8,128)(2,1)S(1)}, u32[]{:S(2)}, u32[]{:S(2)}) collective-permute-start(bf16[560,128]{1,0:T(8,128)(2,1)S(1)} %pad_maximum_fusion), channel_id=1, source_target_pairs={{0,8},{2,10},{4,12},{6,14},{8,0},{10,2},{12,4},{14,6},{16,24},{18,... | collective-permute-start | bytes 430088 | tf_op jit(solution)/shard_map/ppermute | solution.py:357
  29.8 8.4 %collective-permute-start.9 = (bf16[560,128]{1,0:T(8,128)(2,1)S(1)}, bf16[560,128]{1,0:T(8,128)(2,1)S(1)}, u32[]{:S(2)}, u32[]{:S(2)}) collective-permute-start(bf16[560,128]{1,0:T(8,128)(2,1)S(1)} %pad_maximum_fusion.1), channel_id=1, source_target_pairs={{0,12},{2,14},{4,8},{6,10},{8,4},{10,6},{12,0},{14,2},{16,28},{18,... | collective-permute-start | bytes 430088 | tf_op jit(solution)/shard_map/ppermute | solution.py:357
  31.2 8.3 %collective-permute-start.8 = (bf16[560,128]{1,0:T(8,128)(2,1)S(1)}, bf16[560,128]{1,0:T(8,128)(2,1)S(1)}, u32[]{:S(2)}, u32[]{:S(2)}) collective-permute-start(bf16[560,128]{1,0:T(8,128)(2,1)S(1)} %pad_maximum_fusion.1), channel_id=1, source_target_pairs={{0,4},{2,6},{4,0},{6,2},{8,12},{10,14},{12,8},{14,10},{16,20},{18,... | collective-permute-start | bytes 430088 | tf_op jit(solution)/shard_map/ppermute | solution.py:357
  39.6 8.7 %collective-permute-start.10 = (bf16[560,128]{1,0:T(8,128)(2,1)S(1)}, bf16[560,128]{1,0:T(8,128)(2,1)S(1)}, u32[]{:S(2)}, u32[]{:S(2)}) collective-permute-start(bf16[560,128]{1,0:T(8,128)(2,1)S(1)} %add_convert_fusion.1), channel_id=1, source_target_pairs={{0,16},{2,18},{4,20},{6,22},{8,24},{10,26},{12,28},{14,30},{16,0},... | collective-permute-start | bytes 430088 | tf_op jit(solution)/shard_map/ppermute | solution.py:357
  48.4 7.2 %collective-permute-start.13 = (bf16[560,128]{1,0:T(8,128)(2,1)S(1)}, bf16[560,128]{1,0:T(8,128)(2,1)S(1)}, u32[]{:S(2)}, u32[]{:S(2)}) collective-permute-start(bf16[560,128]{1,0:T(8,128)(2,1)S(1)} %add_convert_fusion.refs_0_), channel_id=1, source_target_pairs={{0,5},{1,4},{2,7},{3,6},{4,1},{5,0},{6,3},{7,2},{8,13},{9,12},{10,... | collective-permute-start | bytes 430088 | tf_op jit(solution)/shard_map/ppermute | solution.py:441
  49.3 6.9 %collective-permute-start.12 = (bf16[560,128]{1,0:T(8,128)(2,1)S(1)}, bf16[560,128]{1,0:T(8,128)(2,1)S(1)}, u32[]{:S(2)}, u32[]{:S(2)}) collective-permute-start(bf16[560,128]{1,0:T(8,128)(2,1)S(1)} %add_convert_fusion.refs_0_), channel_id=1, source_target_pairs={{0,1},{1,0},{2,3},{3,2},{4,5},{5,4},{6,7},{7,6},{8,9},{9,8},{10,11... | collective-permute-start | bytes 430088 | tf_op jit(solution)/shard_map/ppermute | solution.py:360
  50.6 6.5 %collective-permute-start.11 = (bf16[560,128]{1,0:T(8,128)(2,1)S(1)}, bf16[560,128]{1,0:T(8,128)(2,1)S(1)}, u32[]{:S(2)}, u32[]{:S(2)}) collective-permute-start(bf16[560,128]{1,0:T(8,128)(2,1)S(1)} %add_convert_fusion.refs_0_), channel_id=1, source_target_pairs={{0,4},{2,6},{4,0},{6,2},{8,12},{10,14},{12,8},{14,10},{16,20},{18,... | collective-permute-start | bytes 430088 | tf_op jit(solution)/shard_map/ppermute | solution.py:357
  52.0 6.1 %collective-permute-start.14 = (bf16[560,128]{1,0:T(8,128)(2,1)S(1)}, bf16[560,128]{1,0:T(8,128)(2,1)S(1)}, u32[]{:S(2)}, u32[]{:S(2)}) collective-permute-start(bf16[560,128]{1,0:T(8,128)(2,1)S(1)} %add_convert_fusion.refs_0_), channel_id=1, source_target_pairs={{0,2},{2,0},{4,6},{6,4},{8,10},{10,8},{12,14},{14,12},{16,18},{18,... | collective-permute-start | bytes 430088 | tf_op jit(solution)/shard_map/ppermute | solution.py:357
  55.6 2.5 %collective-permute-start.17 = (bf16[560,128]{1,0:T(8,128)(2,1)S(1)}, bf16[560,128]{1,0:T(8,128)(2,1)S(1)}, u32[]{:S(2)}, u32[]{:S(2)}) collective-permute-start(bf16[560,128]{1,0:T(8,128)(2,1)S(1)} %collective-permute-done.13.refs_3_), channel_id=1, source_target_pairs={{0,2},{2,0},{4,6},{6,4},{8,10},{10,8},{12,14},{14,12},{16,18},{18,... | collective-permute-start | bytes 430088 | tf_op jit(solution)/shard_map/ppermute | solution.py:357
  56.2 1.9 %collective-permute-start.16 = (bf16[560,128]{1,0:T(8,128)(2,1)S(1)}, bf16[560,128]{1,0:T(8,128)(2,1)S(1)}, u32[]{:S(2)}, u32[]{:S(2)}) collective-permute-start(bf16[560,128]{1,0:T(8,128)(2,1)S(1)} %collective-permute-done.12.refs_2_), channel_id=1, source_target_pairs={{0,2},{2,0},{4,6},{6,4},{8,10},{10,8},{12,14},{14,12},{16,18},{18,... | collective-permute-start | bytes 430088 | tf_op jit(solution)/shard_map/ppermute | solution.py:357
  57.0 1.4 %collective-permute-start.15 = (bf16[560,128]{1,0:T(8,128)(2,1)S(1)}, bf16[560,128]{1,0:T(8,128)(2,1)S(1)}, u32[]{:S(2)}, u32[]{:S(2)}) collective-permute-start(bf16[560,128]{1,0:T(8,128)(2,1)S(1)} %collective-permute-done.11.refs_1_), channel_id=1, source_target_pairs={{0,2},{2,0},{4,6},{6,4},{8,10},{10,8},{12,14},{14,12},{16,18},{18,... | collective-permute-start | bytes 430088 | tf_op jit(solution)/shard_map/ppermute | solution.py:357

commit v4 on v3

--- a/solution.py
+++ b/solution.py
@@ -137,6 +137,7 @@
         self.chip_bit = lax.rem(row // 2, 2)
         self.col_bit = lax.rem(self.col, 2)
         self.near_inside = jnp.where(self.core == 0, row > 0, row < lax.axis_size("rows") - 1)
+        self.mate_inside = jnp.where(self.core == 0, row < lax.axis_size("rows") - 2, row > 1)
         self.taps = [tap + self.core * (2 - 2 * tap) for tap in range(3)]
 
     def chosen(self, total, half):
@@ -168,27 +169,50 @@
     )
 
 
-def middle_kernel(far, near, own, mate, mate1, first_kernel, second_kernel, near_out, own_out, mate_out):
+def prepare_kernel(own, local, lse, soft, keys_t, queries_t, attended_t, features_t):
     place = Place()
-    slots = (far, near, own, mate, mate1)
+    across = own.shape[0]
+    keys = local[:, QK : 2 * QK]
+    keys_t[...] = mm_t(identity(QK), keys).astype(BF)
+    pick = jnp.concatenate([place.chosen(VAL, place.core), place.chosen(VAL, 1 - place.core)], axis=0)
+    features_t[...] = mm_t(pick, local[:, PACKED:]).astype(BF)
+
+    def block(index):
+        at = block_at(index)
+        queries = local[at, :QK]
+        queries_t[:, at] = mm_t(identity(QK), queries).astype(BF)
+        attended_t[:, at] = mm_t(identity(VAL), own[at, :VAL]).astype(BF)
+        scores = mm_t(jnp.concatenate([head_of(keys, h, HEAD_QK) for h in range(HEADS)], axis=0), queries)
+        for head in range(HEADS):
+            rows = slice(head * across, (head + 1) * across)
+            soft[rows, at] = jnp.exp2(scores[rows, :] * EXP2_SCALING - lse[head : head + 1, at]).astype(BF)
+
+    for_blocks(across // BLOCK, block)
+
+
+def masked(inside, row):
+    return jnp.where(inside, row, jnp.zeros_like(row))
+
+
+def middle(place, slots, first_kernel, second_kernel, outs):
     first = [place.beside(first_kernel, a) for a in range(3)]
     second = [place.stacked(second_kernel, a) for a in range(3)]
-    for slot, out in ((1, near_out), (2, own_out), (3, mate_out)):
+    for slot, out in enumerate(outs, 1):
         pre = side(sum(mm(slots[slot + a - 1][:, :VAL], first[a]) for a in range(3)), CONV, 1)
         back = side(sum(mm_t(slots[slot + 1 - a][:, VAL:], second[a]) for a in range(3)), CONV, -1)
         sigma = 1.0 / (1.0 + jnp.exp(-pre))
         hidden = pre * sigma
         slope = back * (sigma * (1.0 + pre * (1.0 - sigma)))
         if slot == 1:
-            hidden = jnp.where(place.near_inside, hidden, 0.0)
-            slope = jnp.where(place.near_inside, slope, 0.0)
+            hidden = masked(place.near_inside, hidden)
+            slope = masked(place.near_inside, slope)
         out[:, :CONV] = hidden.astype(BF)
         out[:, CONV:] = slope.astype(BF)
 
 
 def conv_grads_kernel(near, own, mate, mate1, own_mid, mate_mid, keep, send):
     place = Place()
-    slots = (near, own, mate, mate1)
+    slots = (masked(place.near_inside, near[...]), own[...], mate[...], masked(place.mate_inside, mate1[...]))
     mids = {1: own_mid, 2: mate_mid}
 
     def store(total, start, step, a):
@@ -211,65 +235,6 @@
         store(total, FIRST_ROWS, CONV // PARTS, a)
 
 
-def attention_backward_kernel(
-    near_mid, own_mid, mate_mid, own, local, lse, first_kernel, grad_own, proj_own, proj_mate, upstream_ref, grad_t
-):
-    place = Place()
-    across = own.shape[0]
-    part_width = grad_own.shape[0]
-    mids = (near_mid, own_mid, mate_mid)
-    upstream_ref[...] = side(
-        sum(mm_t(mids[2 - a][:, CONV:], place.stacked(first_kernel, a)) for a in range(3)), VAL, -1
-    ).astype(BF)
-    keys = local[:, QK : 2 * QK]
-    values = local[:, 2 * QK : PACKED]
-    keys_t = mm_t(identity(QK), keys).astype(BF)
-    blocks = across // BLOCK
-    if blocks > 1:
-        grad_t[...] = jnp.zeros_like(grad_t)
-
-    def add_rows(start, count, terms):
-        if blocks > 1:
-            grad_t[start : start + count, :] += terms
-        else:
-            grad_t[start : start + count, :] = terms
-
-    def block(index):
-        at = block_at(index)
-        queries = local[at, :QK]
-        upstream = upstream_ref[at, :]
-        queries_t = mm_t(identity(QK), queries).astype(BF)
-        upstream_t = mm_t(identity(VAL), upstream)
-        products = upstream_t * mm_t(identity(VAL), own[at, :VAL])
-        upstream_t = upstream_t.astype(BF)
-        all_scores = mm_t(jnp.concatenate([head_of(keys, h, HEAD_QK) for h in range(HEADS)], axis=0), queries)
-        all_slopes = mm_t(jnp.concatenate([head_of(values, h, HEAD_VAL) for h in range(HEADS)], axis=0), upstream)
-        for head in range(HEADS):
-            qk_rows = slice(head * HEAD_QK, (head + 1) * HEAD_QK)
-            val_rows = slice(head * HEAD_VAL, (head + 1) * HEAD_VAL)
-            scores = all_scores[head * across : (head + 1) * across, :]
-            soft = jnp.exp2(scores * EXP2_SCALING - lse[head : head + 1, at])
-            inner = jnp.sum(products[val_rows, :], axis=0, keepdims=True)
-            slopes = all_slopes[head * across : (head + 1) * across, :]
-            dscore = (soft * (slopes - inner)).astype(BF)
-            grad_t[qk_rows, at] = SCALING * mm(keys_t[qk_rows, :], dscore)
-            add_rows(QK + head * HEAD_QK, HEAD_QK, SCALING * mm_t(queries_t[qk_rows, :], dscore))
-            add_rows(2 * QK + head * HEAD_VAL, HEAD_VAL, mm_t(upstream_t[val_rows, :], soft.astype(BF)))
-
-    for_blocks(blocks, block)
-
-    grad = grad_t[...].astype(BF)
-    features = local[:, PACKED:]
-    step = VAL // PARTS
-    for target, half in ((proj_own, place.core), (proj_mate, 1 - place.core)):
-        total = mm_t(mm_t(place.chosen(VAL, half), features).astype(BF), grad).astype(BF)
-        for j in range(PACKED // CONV):
-            target[0, j * step : (j + 1) * step, :] = total[:step, j * CONV : (j + 1) * CONV]
-            target[1, j * step : (j + 1) * step, :] = total[step:, j * CONV : (j + 1) * CONV]
-    own_pixels = one_hot((part_width, across), lambda rows: rows + place.col * part_width)
-    grad_own[...] = mm_t(own_pixels, grad).astype(BF)
-
-
 def backward_kernel(
     far,
     near,
@@ -277,25 +242,72 @@
     mate,
     mate1,
     local,
-    lse,
+    soft,
+    keys_t,
+    queries_t,
+    attended_t,
+    features_t,
     first_kernel,
     second_kernel,
     near_mid,
     own_mid,
     mate_mid,
     grad_own,
-    keep,
-    send,
     proj_own,
     proj_mate,
-    upstream,
+    upstream_ref,
     grad_t,
 ):
-    middle_kernel(far, near, own, mate, mate1, first_kernel, second_kernel, near_mid, own_mid, mate_mid)
-    conv_grads_kernel(near, own, mate, mate1, own_mid, mate_mid, keep, send)
-    attention_backward_kernel(
-        near_mid, own_mid, mate_mid, own, local, lse, first_kernel, grad_own, proj_own, proj_mate, upstream, grad_t
-    )
+    place = Place()
+    across = own.shape[0]
+    part_width = grad_own.shape[0]
+    slots = (far[...], masked(place.near_inside, near[...]), own[...], mate[...], masked(place.mate_inside, mate1[...]))
+    mids = (near_mid, own_mid, mate_mid)
+    middle(place, slots, first_kernel, second_kernel, mids)
+    upstream_ref[...] = side(
+        sum(mm_t(mids[2 - a][:, CONV:], place.stacked(first_kernel, a)) for a in range(3)), VAL, -1
+    ).astype(BF)
+    values = local[:, 2 * QK : PACKED]
+    blocks = across // BLOCK
+    if blocks > 1:
+        grad_t[...] = jnp.zeros_like(grad_t)
+
+    def add_rows(start, count, terms):
+        if blocks > 1:
+            grad_t[start : start + count, :] += terms
+        else:
+            grad_t[start : start + count, :] = terms
+
+    def block(index):
+        at = block_at(index)
+        upstream = upstream_ref[at, :]
+        upstream_t = mm_t(identity(VAL), upstream)
+        products = upstream_t * attended_t[:, at].astype(F32)
+        upstream_t = upstream_t.astype(BF)
+        slopes = mm_t(jnp.concatenate([head_of(values, h, HEAD_VAL) for h in range(HEADS)], axis=0), upstream)
+        for head in range(HEADS):
+            rows = slice(head * across, (head + 1) * across)
+            qk_rows = slice(head * HEAD_QK, (head + 1) * HEAD_QK)
+            val_rows = slice(head * HEAD_VAL, (head + 1) * HEAD_VAL)
+            weights = soft[rows, at]
+            inner = jnp.sum(products[val_rows, :], axis=0, keepdims=True)
+            dscore = (weights.astype(F32) * (slopes[rows, :] - inner)).astype(BF)
+            grad_t[qk_rows, at] = SCALING * mm(keys_t[qk_rows, :], dscore)
+            add_rows(QK + head * HEAD_QK, HEAD_QK, SCALING * mm_t(queries_t[qk_rows, at], dscore))
+            add_rows(2 * QK + head * HEAD_VAL, HEAD_VAL, mm_t(upstream_t[val_rows, :], weights))
+
+    for_blocks(blocks, block)
+
+    grad = grad_t[...].astype(BF)
+    step = VAL // PARTS
+    total = mm_t(features_t[...], grad).astype(BF)
+    for which, target in enumerate((proj_own, proj_mate)):
+        for j in range(PACKED // CONV):
+            for part in range(2):
+                begin = (2 * which + part) * step
+                target[part, j * step : (j + 1) * step, :] = total[begin : begin + step, j * CONV : (j + 1) * CONV]
+    own_pixels = one_hot((part_width, across), lambda rows: rows + place.col * part_width)
+    grad_own[...] = mm_t(own_pixels, grad).astype(BF)
 
 
 def outputs_kernel(near_mid, own_mid, mate_mid, grad_own, projection, second_kernel, output_map, input_grad, rows):
@@ -307,32 +319,69 @@
     input_grad[...] = mm_t(grad_own[...], projection[...]).astype(BF)
 
 
-def unpack_kernel(factor, *refs):
-    pieces = refs[:8]
-    projection_grad, first_grad, second_grad = refs[8:]
+def unpack_kernel(factor, core_flip, *refs):
+    pieces = refs[:4]
+    outs = refs[-7:-4]
+    blocks = refs[-4:-1]
+    sem = refs[-1]
+    projection_block, first_block, second_block = blocks
     row = lax.axis_index("rows")
-    core = lax.rem(row, 2)
+    half = lax.rem(row + core_flip, 2)
     chip_bit = lax.rem(row // 2, 2)
     col_bit = lax.rem(lax.axis_index("cols"), 2)
+    parts = [2 * lax.rem(col_bit + which // 2, 2) + lax.rem(chip_bit + which % 2, 2) for which in range(4)]
+    copies = []
+
+    def send(index, block, out):
+        copies.append(pltpu.make_async_copy(block, out, sem.at[index]))
+        copies[-1].start()
+
+    def rows_of(which, step):
+        return pl.ds(pl.multiple_of(parts[which] * step, step), step)
+
+    def half_of(rows):
+        return pl.ds(pl.multiple_of(half * rows, rows), rows)
+
+    step = VAL // PARTS
+    for a in range(3):
+        for which, piece in enumerate(pieces):
+            for b in range(3):
+                begin = (3 * a + b) * step
+                first_block[a, b, rows_of(which, step), :] = piece[begin : begin + step, :].astype(F32) * factor
+        send(a, first_block.at[a], outs[1].at[a, :, half_of(VAL // 2), :])
     for which, piece in enumerate(pieces):
-        core_flip, col_flip, chip_flip = which // 4, which // 2 % 2, which % 2
-        part = (
-            4 * lax.rem(core + core_flip, 2) + 2 * lax.rem(col_bit + col_flip, 2) + lax.rem(chip_bit + chip_flip, 2)
-        )
-        step = VAL // PARTS
-        at = pl.ds(pl.multiple_of(part * step, step), step)
-        for tap in range(9):
-            first_grad[tap // 3, tap % 3, at, :] = piece[tap * step : (tap + 1) * step, :].astype(F32) * factor
-        start = FIRST_ROWS + SECOND_ROWS
         for j in range(PACKED // CONV):
-            projection_grad[at, j * CONV : (j + 1) * CONV] = (
-                piece[start + j * step : start + (j + 1) * step, :].astype(F32) * factor
+            begin = FIRST_ROWS + SECOND_ROWS + j * step
+            projection_block[rows_of(which, step), j * CONV : (j + 1) * CONV] = (
+                piece[begin : begin + step, :].astype(F32) * factor
             )
-        step = CONV // PARTS
-        at = pl.ds(pl.multiple_of(part * step, step), step)
+    send(3, projection_block, outs[0].at[half_of(VAL // 2), :])
+    step = CONV // PARTS
+    for which, piece in enumerate(pieces):
         for tap in range(9):
             begin = FIRST_ROWS + tap * step
-            second_grad[tap // 3, tap % 3, at, :] = piece[begin : begin + step, :].astype(F32) * factor
+            second_block[tap // 3, tap % 3, rows_of(which, step), :] = (
+                piece[begin : begin + step, :].astype(F32) * factor
+            )
+    send(4, second_block, outs[2].at[:, :, half_of(CONV // 2), :])
+    for copy in copies:
+        copy.wait()
+
+
+def unpack(factor, core_flip, pieces, into, **params):
+    dims = ((2 * QK, PACKED), (3, 3, VAL, CONV), (3, 3, CONV, CONV))
+    return pl.pallas_call(
+        functools.partial(unpack_kernel, factor, core_flip),
+        out_shape=tuple(shape(*size, dtype=F32) for size in dims),
+        in_specs=[VMEM] * 4 + [HBM] * len(into),
+        out_specs=[HBM] * 3,
+        scratch_shapes=[pltpu.VMEM(size[:-2] + (size[-2] // 2, size[-1]), F32) for size in dims]
+        + [pltpu.SemaphoreType.DMA((5,))],
+        input_output_aliases={4 + i: i for i in range(len(into))},
+        cost_estimate=pl.CostEstimate(flops=10**9, bytes_accessed=4 * 1024 * 1024, transcendentals=0),
+        name="unpack_sums",
+        **params,
+    )(*pieces, *into)
 
 
 def shape(*dims, dtype=BF):
@@ -396,27 +445,59 @@
     )
 
     first_kernel, second_kernel = fetch((first_kernel, second_kernel), (lse,))
-    near = [(i, i + 1) for i in range(1, rows_size - 1, 2)] + [(i + 1, i) for i in range(1, rows_size - 1, 2)]
-    far = [(i, i + 2) for i in range(0, rows_size - 2, 2)] + [(i, i - 2) for i in range(3, rows_size, 2)]
-    near1 = lax.ppermute(own, "rows", near)
-    near2 = lax.ppermute(own, "rows", far)
+    last = rows_size - 1
+    out = [(i, i + 2) for i in range(0, last - 1, 2)] + [(i, i - 2) for i in range(3, rows_size, 2)]
+    out += [(last - 1, last), (1, 0)]
+    back = [(j, i) for i, j in out]
+    mate1 = lax.ppermute(own, "rows", back)
+    far = lax.ppermute(own, "rows", out)
     mate = rows_flip(own, 1)
-    mate1 = rows_flip(near1, 1)
-    near_mid, own_mid, mate_mid, grad_own, keep, send, proj_own, proj_mate = call(
+    near = rows_flip(mate1, 1)
+    soft, keys_t, queries_t, attended_t, features_t = call(
+        prepare_kernel,
+        (
+            shape(HEADS * across, across),
+            shape(QK, across),
+            shape(QK, across),
+            shape(VAL, across),
+            shape(VAL // 2, across),
+        ),
+        (own, local, lse),
+        name="prepare",
+    )
+    near_mid, own_mid, mate_mid, grad_own, proj_own, proj_mate = call(
         backward_kernel,
         (
             shape(across, 2 * CONV),
             shape(across, 2 * CONV),
             shape(across, 2 * CONV),
             shape(part_width, PACKED),
-            shape(FIRST_ROWS + SECOND_ROWS, CONV),
-            shape(FIRST_ROWS + SECOND_ROWS, CONV),
             shape(2, PROJ_ROWS, CONV),
             shape(2, PROJ_ROWS, CONV),
         ),
-        (near2, near1, own, mate, mate1, local, lse, first_kernel, second_kernel),
+        (
+            far,
+            near,
+            own,
+            mate,
+            mate1,
+            local,
+            soft,
+            keys_t,
+            queries_t,
+            attended_t,
+            features_t,
+            first_kernel,
+            second_kernel,
+        ),
         (pltpu.VMEM((across, VAL), BF), pltpu.VMEM((PACKED, across), F32)),
         name="block_backward",
+    )
+    keep, send = call(
+        conv_grads_kernel,
+        (shape(FIRST_ROWS + SECOND_ROWS, CONV),) * 2,
+        (near, own, mate, mate1, own_mid, mate_mid),
+        name="conv_grads",
     )
     output_map, input_grad = call(
         outputs_kernel,
@@ -436,6 +517,7 @@
     while bit < rows_size:
         total = added(wide(total), wide(rows_flip(total, bit)))
         bit *= 2
+    total, output_map, input_grad = lax.optimization_barrier((total, output_map, input_grad))
     chip = rows_flip(total, 2)
     side = cols_flip(total)
     corner = lax.ppermute(
@@ -444,17 +526,10 @@
         [(i * cols_size + j, (i ^ 2) * cols_size + (j ^ 1)) for i in range(rows_size) for j in range(cols_size)],
     )
     four = (total, chip, side, corner)
-    eight = four + tuple(rows_flip(piece, 1) for piece in four)
     factor = 1.0 / math.sqrt(height * across * rows_size)
-    projection_grad, first_grad, second_grad = call(
-        functools.partial(unpack_kernel, factor),
-        (
-            shape(channels, PACKED, dtype=F32),
-            shape(3, 3, VAL, CONV, dtype=F32),
-            shape(3, 3, CONV, CONV, dtype=F32),
-        ),
-        eight,
-        name="unpack_sums",
+    halves = unpack(factor, 0, four, (), **granted(across))
+    projection_grad, first_grad, second_grad = unpack(
+        factor, 1, [rows_flip(piece, 1) for piece in four], halves, **granted(across)
     )
     return (output_map[None], input_grad[None], projection_grad, first_grad, second_grad)
 

time: 60.2 us -> 57 us (0.947)
  starting transfers between devices: 21.9 us -> 18.4 us
  Pallas kernels: 8.56 us -> 9.41 us
  waiting for transfers between devices: 26.1 us -> 25.4 us
    ppermute x12, waiting for transfers between devices: 16.6 us -> 12.9 us  [rows_flip(): lax.ppermute(values, 'rows', [(i, i ^ bit) for i in range(rows_size)])]
    ppermute x2, waiting for transfers between devices: 3.88 us -> 6.32 us  [the longest x1 5.07 us: body(): mate1 = lax.ppermute(own, 'rows', back)]
    pallas_call x0 -> x2, Pallas kernels: none -> 2.16 us  [unpack(): pl.pallas_call(functools.partial(unpack_kernel, factor, core_flip), out_s...]
    ppermute x12, starting transfers between devices: 12.5 us -> 10.4 us  [rows_flip(): lax.ppermute(values, 'rows', [(i, i ^ bit) for i in range(rows_size)])]
    ppermute x2, starting transfers between devices: 4.09 us -> 2.07 us  [the longest x1 2.01 us: body(): far = lax.ppermute(own, 'rows', out)]
    pallas_call x4 -> x5, Pallas kernels: 8.19 us -> 6.87 us  [call(): pl.pallas_call(kernel, out_shape=out_shape, in_specs=[VMEM] * len(operand...]
    ppermute x3, waiting for transfers between devices: 1.9 us -> 2.8 us  [cols_flip(): return lax.ppermute(values, 'cols', [(i, i ^ 1) for i in range(cols_size)])]
    ppermute x1, starting transfers between devices: 0.87 us -> 1.73 us  [body(): lax.ppermute(total, ('rows', 'cols'), [(i * cols_size + j, (i ^ 2) * cols...]
  transfers between devices with their start and end apart: 18 -> 18, of which waited for: 11 -> 10; matrix products, arithmetic and copies ran while one was open for 0% -> 0% of each run, Pallas kernels for 2% -> 7%
where the time goes in v4:
time: 57 us; the launch traced here: 56.7 us
  waiting for transfers between devices  25.4 us (45%)
  starting transfers between devices  18.4 us (32%)
  Pallas kernels  9.41 us (17%)
  local copies, waits for them, and re-layouts  2.56 us (4%)
  between operations  0.79 us (1%)
    ppermute x12, waiting for transfers between devices, rows_flip(): lax.ppermute(values, 'rows', [(i, i ^ bit) for i in range(rows_size)])  12.9 us
    ppermute x12, starting transfers between devices, rows_flip(): lax.ppermute(values, 'rows', [(i, i ^ bit) for i in range(rows_size)])  10.4 us
    pallas_call x5, Pallas kernels, call(): pl.pallas_call(kernel, out_shape=out_shape, in_specs=[VMEM] * len(operand...  6.87 us
    ppermute x1, waiting for transfers between devices, body(): mate1 = lax.ppermute(own, 'rows', back)  5.07 us
    ppermute x3, starting transfers between devices, cols_flip(): return lax.ppermute(values, 'cols', [(i, i ^ 1) for i in range(cols_size)])  4.21 us
    ppermute x1, waiting for transfers between devices, body(): lax.ppermute(total, ('rows', 'cols'), [(i * cols_size + j, (i ^ 2) * cols...  3.41 us
    ppermute x3, waiting for transfers between devices, cols_flip(): return lax.ppermute(values, 'cols', [(i, i ^ 1) for i in range(cols_size)])  2.8 us
    unnamed x10, local copies, waits for them, and re-layouts  2.55 us
  transfers between devices with their start and end apart: 18, of which 10 were waited for; matrix products, arithmetic and copies ran while one was open for 0% of the time, Pallas kernels for 7%

profile of v4, /device:TPU:0, one launch (start us, length us, event | category | flops | bytes accessed | tf_op | source)
XLA Modules:
  0.0 56.7 jit_solution(18400697895116447784)
XLA Ops:
  0.6 3.0 %collective-permute-start = (bf16[128,256]{1,0:T(8,128)(2,1)}, bf16[128,256]{1,0:T(8,128)(2,1)S(1)}, u32[]{:S(2)}, u32[]{:S(2)}) collective-permute-start(bf16[128,256]{1,0:T(8,128)(2,1)} %bitcast.8), channel_id=1, source_target_pairs={{0,1},{1,0},{2,3},{3,2},{4,5},{5,4},{6,7},{7,6},{8,9},{9,8},{10,11... | collective-permute-start | bytes 196616 | tf_op jit(solution)/shard_map/ppermute | solution.py:409
  3.7 0.9 %copy-done.2 = bf16[256,512]{1,0:T(8,128)(2,1)S(1)} copy-done((bf16[256,512]{1,0:T(8,128)(2,1)S(1)}, bf16[256,512]{1,0:T(8,128)(2,1)}, u32[]{:S(2)}) %copy-start.2) | copy-done | bytes 262168
  4.7 0.8 %copy-done.3 = bf16[1,128,256]{2,1,0:T(8,128)(2,1)S(1)} copy-done((bf16[1,128,256]{2,1,0:T(8,128)(2,1)S(1)}, bf16[1,128,256]{2,1,0:T(8,128)(2,1)}, u32[]{:S(2)}) %copy-start.3) | copy-done | bytes 65560
  6.4 1.3 %collective-permute-done.1.refs_3_ = bf16[128,128]{1,0:T(8,128)(2,1)S(1)} collective-permute-done((bf16[128,128]{1,0:T(8,128)(2,1)}, bf16[128,128]{1,0:T(8,128)(2,1)S(1)}, u32[]{:S(2)}, u32[]{:S(2)}) %collective-permute-start.1) | collective-permute-done | bytes 32800 | tf_op jit(solution)/shard_map/ppermute | solution.py:409
  7.8 1.3 %attention_forward.1 = (bf16[256,384]{1,0:T(8,128)(2,1)S(1)}, bf16[256,768]{1,0:T(8,128)(2,1)S(1)}, f32[8,256]{1,0:T(8,128)S(1)}) custom-call(bf16[128,256]{1,0:T(8,128)(2,1)S(1)} %get-tuple-element.37.refs_0_, bf16[128,256]{1,0:T(8,128)(2,1)S(1)} %collective-permute-done.refs_1_, bf16[128,128]{1,0:T(8,128)(2,1)S(1)} %get-tuple-element.38.refs_2_, ...), custom_call_target="tpu_custom_call" | custom-call | flops 1000000000 | bytes 4194304 | tf_op jit(solution)/shard_map/attention_forward/pallas_call | solution.py:418
  9.2 2.0 %collective-permute-start.5 = (bf16[256,384]{1,0:T(8,128)(2,1)S(1)}, bf16[256,384]{1,0:T(8,128)(2,1)S(1)}, u32[]{:S(2)}, u32[]{:S(2)}) collective-permute-start(bf16[256,384]{1,0:T(8,128)(2,1)S(1)} %get-tuple-element.40.own), channel_id=1, source_target_pairs={{0,4},{4,8},{8,12},{12,16},{16,20},{20,24},{24,28},{6,2},{10,6},{1... | collective-permute-start | bytes 589832 | tf_op jit(solution)/shard_map/ppermute | solution.py:453
  11.2 5.1 %collective-permute-done.2.mate1 = bf16[256,384]{1,0:T(8,128)(2,1)S(1)} collective-permute-done((bf16[256,384]{1,0:T(8,128)(2,1)S(1)}, bf16[256,384]{1,0:T(8,128)(2,1)S(1)}, u32[]{:S(2)}, u32[]{:S(2)}) %collective-permute-start.2) | collective-permute-done | bytes 196640 | tf_op jit(solution)/shard_map/ppermute | solution.py:452
  17.1 1.2 %collective-permute-done.5.far = bf16[256,384]{1,0:T(8,128)(2,1)S(1)} collective-permute-done((bf16[256,384]{1,0:T(8,128)(2,1)S(1)}, bf16[256,384]{1,0:T(8,128)(2,1)S(1)}, u32[]{:S(2)}, u32[]{:S(2)}) %collective-permute-start.5) | collective-permute-done | bytes 196640 | tf_op jit(solution)/shard_map/ppermute | solution.py:453
  18.3 3.2 %block_backward.1 = (bf16[256,256]{1,0:T(8,128)(2,1)S(1)}, bf16[256,256]{1,0:T(8,128)(2,1)S(1)}, bf16[256,256]{1,0:T(8,128)(2,1)S(1)}, bf16[128,512]{1,0:T(8,128...) custom-call(bf16[256,384]{1,0:T(8,128)(2,1)S(1)} %collective-permute-done.5.far, ...), custom_call_target="tpu_custom_call" | custom-call | flops 1000000000 | bytes 4194304 | tf_op jit(solution)/shard_map/block_backward/pallas_call | solution.py:418
  21.5 0.8 %conv_grads.1 = (bf16[432,128]{1,0:T(8,128)(2,1)S(1)}, bf16[432,128]{1,0:T(8,128)(2,1)S(1)}) custom-call(bf16[256,384]{1,0:T(8,128)(2,1)S(1)} %collective-permute-done.3.near, bf16[256,384]{1,0:T(8,128)(2,1)S(1)} %get-tuple-element.40.own, bf16[256,384]{1,0:T(8,128)(2,1)S(1)} %collective-permute-done.4.mate, ...), custom_call_target="tpu_custom_call" | custom-call | flops 1000000000 | bytes 4194304 | tf_op jit(solution)/shard_map/conv_grads/pallas_call | solution.py:418
  22.8 4.9 %collective-permute-start.7 = (bf16[560,128]{1,0:T(8,128)(2,1)S(1)}, bf16[560,128]{1,0:T(8,128)(2,1)S(1)}, u32[]{:S(2)}, u32[]{:S(2)}) collective-permute-start(bf16[560,128]{1,0:T(8,128)(2,1)S(1)} %pad_maximum_fusion), channel_id=1, source_target_pairs={{0,8},{2,10},{4,12},{6,14},{8,0},{10,2},{12,4},{14,6},{16,24},{18,... | collective-permute-start | bytes 430088 | tf_op jit(solution)/shard_map/ppermute | solution.py:406
  27.8 1.5 %collective-permute-start.8 = (bf16[560,128]{1,0:T(8,128)(2,1)S(1)}, bf16[560,128]{1,0:T(8,128)(2,1)S(1)}, u32[]{:S(2)}, u32[]{:S(2)}) collective-permute-start(bf16[560,128]{1,0:T(8,128)(2,1)S(1)} %pad_maximum_fusion.1), channel_id=1, source_target_pairs={{0,4},{2,6},{4,0},{6,2},{8,12},{10,14},{12,8},{14,10},{16,20},{18,... | collective-permute-start | bytes 430088 | tf_op jit(solution)/shard_map/ppermute | solution.py:406
  29.3 3.0 %collective-permute-done.7 = bf16[560,128]{1,0:T(8,128)(2,1)S(1)} collective-permute-done((bf16[560,128]{1,0:T(8,128)(2,1)S(1)}, bf16[560,128]{1,0:T(8,128)(2,1)S(1)}, u32[]{:S(2)}, u32[]{:S(2)}) %collective-permute-start.7) | collective-permute-done | bytes 143392 | tf_op jit(solution)/shard_map/ppermute | solution.py:406
  32.3 2.1 %collective-permute-done.9 = bf16[560,128]{1,0:T(8,128)(2,1)S(1)} collective-permute-done((bf16[560,128]{1,0:T(8,128)(2,1)S(1)}, bf16[560,128]{1,0:T(8,128)(2,1)S(1)}, u32[]{:S(2)}, u32[]{:S(2)}) %collective-permute-start.9) | collective-permute-done | bytes 143392 | tf_op jit(solution)/shard_map/ppermute | solution.py:406
  34.4 2.1 %collective-permute-done.8 = bf16[560,128]{1,0:T(8,128)(2,1)S(1)} collective-permute-done((bf16[560,128]{1,0:T(8,128)(2,1)S(1)}, bf16[560,128]{1,0:T(8,128)(2,1)S(1)}, u32[]{:S(2)}, u32[]{:S(2)}) %collective-permute-start.8) | collective-permute-done | bytes 143392 | tf_op jit(solution)/shard_map/ppermute | solution.py:406
  36.6 2.7 %collective-permute-start.10 = (bf16[560,128]{1,0:T(8,128)(2,1)S(1)}, bf16[560,128]{1,0:T(8,128)(2,1)S(1)}, u32[]{:S(2)}, u32[]{:S(2)}) collective-permute-start(bf16[560,128]{1,0:T(8,128)(2,1)S(1)} %add_convert_fusion.1), channel_id=1, source_target_pairs={{0,16},{2,18},{4,20},{6,22},{8,24},{10,26},{12,28},{14,30},{16,0},... | collective-permute-start | bytes 430088 | tf_op jit(solution)/shard_map/ppermute | solution.py:406
  39.3 1.0 %outputs.1 = (bf16[128,128]{1,0:T(8,128)(2,1)}, bf16[128,256]{1,0:T(8,128)(2,1)}) custom-call(bf16[256,256]{1,0:T(8,128)(2,1)S(1)} %get-tuple-element.56.near_mid, bf16[256,256]{1,0:T(8,128)(2,1)S(1)} %get-tuple-element.50.own_mid, bf16[256,256]{1,0:T(8,128)(2,1)S(1)} %get-tuple-element.51.mate_mid, bf16[128,512]{1,0:T(8,128)(2,1)S(1)} %get-tuple-element.57.grad_own, ...), custom_call_target="tpu_custom_call" | custom-call | flops 1000000000 | bytes 4194304 | tf_op jit(solution)/shard_map/outputs/pallas_call | solution.py:418
  40.3 5.2 %collective-permute-done.10 = bf16[560,128]{1,0:T(8,128)(2,1)S(1)} collective-permute-done((bf16[560,128]{1,0:T(8,128)(2,1)S(1)}, bf16[560,128]{1,0:T(8,128)(2,1)S(1)}, u32[]{:S(2)}, u32[]{:S(2)}) %collective-permute-start.10) | collective-permute-done | bytes 143392 | tf_op jit(solution)/shard_map/ppermute | solution.py:406
  45.5 1.7 %collective-permute-start.16 = (bf16[560,128]{1,0:T(8,128)(2,1)S(1)}, bf16[560,128]{1,0:T(8,128)(2,1)S(1)}, u32[]{:S(2)}, u32[]{:S(2)}) collective-permute-start(bf16[560,128]{1,0:T(8,128)(2,1)S(1)} %add_convert_fusion.refs_0_), channel_id=1, source_target_pairs={{0,5},{1,4},{2,7},{3,6},{4,1},{5,0},{6,3},{7,2},{8,13},{9,12},{10,... | collective-permute-start | bytes 430088 | tf_op jit(solution)/shard_map/ppermute | solution.py:523
  47.3 1.1 %collective-permute-start.14 = (bf16[560,128]{1,0:T(8,128)(2,1)S(1)}, bf16[560,128]{1,0:T(8,128)(2,1)S(1)}, u32[]{:S(2)}, u32[]{:S(2)}) collective-permute-start(bf16[560,128]{1,0:T(8,128)(2,1)S(1)} %add_convert_fusion.refs_0_), channel_id=1, source_target_pairs={{0,1},{1,0},{2,3},{3,2},{4,5},{5,4},{6,7},{7,6},{8,9},{9,8},{10,11... | collective-permute-start | bytes 430088 | tf_op jit(solution)/shard_map/ppermute | solution.py:409
  49.1 3.4 %collective-permute-done.16.refs_3_ = bf16[560,128]{1,0:T(8,128)(2,1)S(1)} collective-permute-done((bf16[560,128]{1,0:T(8,128)(2,1)S(1)}, bf16[560,128]{1,0:T(8,128)(2,1)S(1)}, u32[]{:S(2)}, u32[]{:S(2)}) %collective-permute-start.16) | collective-permute-done | bytes 143392 | tf_op jit(solution)/shard_map/ppermute | solution.py:523
  52.5 1.5 %collective-permute-done.14.refs_2_ = bf16[560,128]{1,0:T(8,128)(2,1)S(1)} collective-permute-done((bf16[560,128]{1,0:T(8,128)(2,1)S(1)}, bf16[560,128]{1,0:T(8,128)(2,1)S(1)}, u32[]{:S(2)}, u32[]{:S(2)}) %collective-permute-start.14) | collective-permute-done | bytes 143392 | tf_op jit(solution)/shard_map/ppermute | solution.py:409
  54.5 1.1 %unpack_sums.2 = (f32[256,512]{1,0:T(8,128)}, f32[3,3,256,128]{3,2,1,0:T(8,128)}, f32[3,3,128,128]{3,2,1,0:T(8,128)}) custom-call(bf16[560,128]{1,0:T(8,128)(2,1)S(1)} %add_convert_fusion.refs_0_, bf16[560,128]{1,0:T(8,128)(2,1)S(1)} %collective-permute-done.12.refs_1_, bf16[560,128]{1,0:T(8,128)(2,1)S(1)} %collective-permute-done.14.refs_2_, ...), custom_call_target="tpu_custom_call" | custom-call | flops 1000000000 | bytes 4194304 | tf_op jit(solution)/shard_map/unpack_sums/pallas_call | solution.py:373
  55.6 1.1 %unpack_sums.3 = (f32[256,512]{1,0:T(8,128)}, f32[3,3,256,128]{3,2,1,0:T(8,128)}, f32[3,3,128,128]{3,2,1,0:T(8,128)}) custom-call(bf16[560,128]{1,0:T(8,128)(2,1)S(1)} %collective-permute-done.11.refs_0_, bf16[560,128]{1,0:T(8,128)(2,1)S(1)} %collective-permute-done.13.refs_1_, ...), custom_call_target="tpu_custom_call", output_to_operand_aliasing={{0}: (4, {}), {1}: (5, {}), {2}: (6, {})} | custom-call | flops 1000000000 | bytes 4194304 | tf_op jit(solution)/shard_map/unpack_sums/pallas_call | solution.py:373
  (37 shorter events, 3.8 us)
Async XLA Ops:
  0.6 7.1 %collective-permute-start = (bf16[128,256]{1,0:T(8,128)(2,1)}, bf16[128,256]{1,0:T(8,128)(2,1)S(1)}, u32[]{:S(2)}, u32[]{:S(2)}) collective-permute-start(bf16[128,256]{1,0:T(8,128)(2,1)} %bitcast.8), channel_id=1, source_target_pairs={{0,1},{1,0},{2,3},{3,2},{4,5},{5,4},{6,7},{7,6},{8,9},{9,8},{10,11... | collective-permute-start | bytes 196616 | tf_op jit(solution)/shard_map/ppermute | solution.py:409
  3.6 4.1 %collective-permute-start.1 = (bf16[128,128]{1,0:T(8,128)(2,1)}, bf16[128,128]{1,0:T(8,128)(2,1)S(1)}, u32[]{:S(2)}, u32[]{:S(2)}) collective-permute-start(bf16[128,128]{1,0:T(8,128)(2,1)} %bitcast.10), channel_id=1, source_target_pairs={{0,1},{1,0},{2,3},{3,2},{4,5},{5,4},{6,7},{7,6},{8,9},{9,8},{10,11... | collective-permute-start | bytes 98312 | tf_op jit(solution)/shard_map/ppermute | solution.py:409
  3.7 0.9 %copy-start.2 = (bf16[256,512]{1,0:T(8,128)(2,1)S(1)}, bf16[256,512]{1,0:T(8,128)(2,1)}, u32[]{:S(2)}) copy-start(bf16[256,512]{1,0:T(8,128)(2,1)} %refs_0_.2) | copy-start | bytes 786436
  4.7 0.8 %copy-start.3 = (bf16[1,128,256]{2,1,0:T(8,128)(2,1)S(1)}, bf16[1,128,256]{2,1,0:T(8,128)(2,1)}, u32[]{:S(2)}) copy-start(bf16[1,128,256]{2,1,0:T(8,128)(2,1)} %param.5) | copy-start | bytes 196612
  5.5 0.8 %copy-start.4 = (bf16[1,128,128]{2,1,0:T(8,128)(2,1)S(1)}, bf16[1,128,128]{2,1,0:T(8,128)(2,1)}, u32[]{:S(2)}) copy-start(bf16[1,128,128]{2,1,0:T(8,128)(2,1)} %param.9) | copy-start | bytes 98308
  7.8 8.5 %copy-start = (bf16[3,3,256,128]{3,2,1,0:T(8,128)(2,1)S(1)}, bf16[3,3,256,128]{3,2,1,0:T(8,128)(2,1)}, u32[]{:S(2)}) copy-start(bf16[3,3,256,128]{3,2,1,0:T(8,128)(2,1)} %refs_0_.3) | copy-start | bytes 1769476
  7.8 8.5 %copy-start.1 = (bf16[3,3,128,128]{3,2,1,0:T(8,128)(2,1)S(1)}, bf16[3,3,128,128]{3,2,1,0:T(8,128)(2,1)}, u32[]{:S(2)}) copy-start(bf16[3,3,128,128]{3,2,1,0:T(8,128)(2,1)} %refs_1_.1) | copy-start | bytes 884740
  9.1 7.2 %collective-permute-start.2 = (bf16[256,384]{1,0:T(8,128)(2,1)S(1)}, bf16[256,384]{1,0:T(8,128)(2,1)S(1)}, u32[]{:S(2)}, u32[]{:S(2)}) collective-permute-start(bf16[256,384]{1,0:T(8,128)(2,1)S(1)} %get-tuple-element.40.own), channel_id=1, source_target_pairs={{4,0},{8,4},{12,8},{16,12},{20,16},{24,20},{28,24},{2,6},{6,10},{1... | collective-permute-start | bytes 589832 | tf_op jit(solution)/shard_map/ppermute | solution.py:452
  9.2 9.1 %collective-permute-start.5 = (bf16[256,384]{1,0:T(8,128)(2,1)S(1)}, bf16[256,384]{1,0:T(8,128)(2,1)S(1)}, u32[]{:S(2)}, u32[]{:S(2)}) collective-permute-start(bf16[256,384]{1,0:T(8,128)(2,1)S(1)} %get-tuple-element.40.own), channel_id=1, source_target_pairs={{0,4},{4,8},{8,12},{12,16},{16,20},{20,24},{24,28},{6,2},{10,6},{1... | collective-permute-start | bytes 589832 | tf_op jit(solution)/shard_map/ppermute | solution.py:453
  11.2 7.1 %collective-permute-start.4 = (bf16[256,384]{1,0:T(8,128)(2,1)S(1)}, bf16[256,384]{1,0:T(8,128)(2,1)S(1)}, u32[]{:S(2)}, u32[]{:S(2)}) collective-permute-start(bf16[256,384]{1,0:T(8,128)(2,1)S(1)} %get-tuple-element.40.own), channel_id=1, source_target_pairs={{0,2},{2,0},{4,6},{6,4},{8,10},{10,8},{12,14},{14,12},{16,18},{18,... | collective-permute-start | bytes 589832 | tf_op jit(solution)/shard_map/ppermute | solution.py:406
  16.3 2.0 %collective-permute-start.3 = (bf16[256,384]{1,0:T(8,128)(2,1)S(1)}, bf16[256,384]{1,0:T(8,128)(2,1)S(1)}, u32[]{:S(2)}, u32[]{:S(2)}) collective-permute-start(bf16[256,384]{1,0:T(8,128)(2,1)S(1)} %collective-permute-done.2.mate1), channel_id=1, source_target_pairs={{0,2},{2,0},{4,6},{6,4},{8,10},{10,8},{12,14},{14,12},{16,18},{18,... | collective-permute-start | bytes 589832 | tf_op jit(solution)/shard_map/ppermute | solution.py:406
  21.5 1.3 %collective-permute-start.6 = (bf16[2,128,128]{2,1,0:T(8,128)(2,1)S(1)}, bf16[2,128,128]{2,1,0:T(8,128)(2,1)S(1)}, u32[]{:S(2)}, u32[]{:S(2)}) collective-permute-start(bf16[2,128,128]{2,1,0:T(8,128)(2,1)S(1)} %get-tuple-element.54), channel_id=1, source_target_pairs={{0,2},{2,0},{4,6},{6,4},{8,10},{10,8},{12,14},{14,12},{16,18},{18,... | collective-permute-start | bytes 196616 | tf_op jit(solution)/shard_map/ppermute | solution.py:406
  22.8 9.5 %collective-permute-start.7 = (bf16[560,128]{1,0:T(8,128)(2,1)S(1)}, bf16[560,128]{1,0:T(8,128)(2,1)S(1)}, u32[]{:S(2)}, u32[]{:S(2)}) collective-permute-start(bf16[560,128]{1,0:T(8,128)(2,1)S(1)} %pad_maximum_fusion), channel_id=1, source_target_pairs={{0,8},{2,10},{4,12},{6,14},{8,0},{10,2},{12,4},{14,6},{16,24},{18,... | collective-permute-start | bytes 430088 | tf_op jit(solution)/shard_map/ppermute | solution.py:406
  27.8 6.6 %collective-permute-start.9 = (bf16[560,128]{1,0:T(8,128)(2,1)S(1)}, bf16[560,128]{1,0:T(8,128)(2,1)S(1)}, u32[]{:S(2)}, u32[]{:S(2)}) collective-permute-start(bf16[560,128]{1,0:T(8,128)(2,1)S(1)} %pad_maximum_fusion.1), channel_id=1, source_target_pairs={{0,12},{2,14},{4,8},{6,10},{8,4},{10,6},{12,0},{14,2},{16,28},{18,... | collective-permute-start | bytes 430088 | tf_op jit(solution)/shard_map/ppermute | solution.py:406
  27.8 8.7 %collective-permute-start.8 = (bf16[560,128]{1,0:T(8,128)(2,1)S(1)}, bf16[560,128]{1,0:T(8,128)(2,1)S(1)}, u32[]{:S(2)}, u32[]{:S(2)}) collective-permute-start(bf16[560,128]{1,0:T(8,128)(2,1)S(1)} %pad_maximum_fusion.1), channel_id=1, source_target_pairs={{0,4},{2,6},{4,0},{6,2},{8,12},{10,14},{12,8},{14,10},{16,20},{18,... | collective-permute-start | bytes 430088 | tf_op jit(solution)/shard_map/ppermute | solution.py:406
  36.6 8.9 %collective-permute-start.10 = (bf16[560,128]{1,0:T(8,128)(2,1)S(1)}, bf16[560,128]{1,0:T(8,128)(2,1)S(1)}, u32[]{:S(2)}, u32[]{:S(2)}) collective-permute-start(bf16[560,128]{1,0:T(8,128)(2,1)S(1)} %add_convert_fusion.1), channel_id=1, source_target_pairs={{0,16},{2,18},{4,20},{6,22},{8,24},{10,26},{12,28},{14,30},{16,0},... | collective-permute-start | bytes 430088 | tf_op jit(solution)/shard_map/ppermute | solution.py:406
  45.5 7.0 %collective-permute-start.16 = (bf16[560,128]{1,0:T(8,128)(2,1)S(1)}, bf16[560,128]{1,0:T(8,128)(2,1)S(1)}, u32[]{:S(2)}, u32[]{:S(2)}) collective-permute-start(bf16[560,128]{1,0:T(8,128)(2,1)S(1)} %add_convert_fusion.refs_0_), channel_id=1, source_target_pairs={{0,5},{1,4},{2,7},{3,6},{4,1},{5,0},{6,3},{7,2},{8,13},{9,12},{10,... | collective-permute-start | bytes 430088 | tf_op jit(solution)/shard_map/ppermute | solution.py:523
  47.3 6.7 %collective-permute-start.14 = (bf16[560,128]{1,0:T(8,128)(2,1)S(1)}, bf16[560,128]{1,0:T(8,128)(2,1)S(1)}, u32[]{:S(2)}, u32[]{:S(2)}) collective-permute-start(bf16[560,128]{1,0:T(8,128)(2,1)S(1)} %add_convert_fusion.refs_0_), channel_id=1, source_target_pairs={{0,1},{1,0},{2,3},{3,2},{4,5},{5,4},{6,7},{7,6},{8,9},{9,8},{10,11... | collective-permute-start | bytes 430088 | tf_op jit(solution)/shard_map/ppermute | solution.py:409
  48.4 5.6 %collective-permute-start.12 = (bf16[560,128]{1,0:T(8,128)(2,1)S(1)}, bf16[560,128]{1,0:T(8,128)(2,1)S(1)}, u32[]{:S(2)}, u32[]{:S(2)}) collective-permute-start(bf16[560,128]{1,0:T(8,128)(2,1)S(1)} %add_convert_fusion.refs_0_), channel_id=1, source_target_pairs={{0,4},{2,6},{4,0},{6,2},{8,12},{10,14},{12,8},{14,10},{16,20},{18,... | collective-permute-start | bytes 430088 | tf_op jit(solution)/shard_map/ppermute | solution.py:406
  49.1 6.5 %collective-permute-start.11 = (bf16[560,128]{1,0:T(8,128)(2,1)S(1)}, bf16[560,128]{1,0:T(8,128)(2,1)S(1)}, u32[]{:S(2)}, u32[]{:S(2)}) collective-permute-start(bf16[560,128]{1,0:T(8,128)(2,1)S(1)} %add_convert_fusion.refs_0_), channel_id=1, source_target_pairs={{0,2},{2,0},{4,6},{6,4},{8,10},{10,8},{12,14},{14,12},{16,18},{18,... | collective-permute-start | bytes 430088 | tf_op jit(solution)/shard_map/ppermute | solution.py:406
  52.5 3.1 %collective-permute-start.17 = (bf16[560,128]{1,0:T(8,128)(2,1)S(1)}, bf16[560,128]{1,0:T(8,128)(2,1)S(1)}, u32[]{:S(2)}, u32[]{:S(2)}) collective-permute-start(bf16[560,128]{1,0:T(8,128)(2,1)S(1)} %collective-permute-done.16.refs_3_), channel_id=1, source_target_pairs={{0,2},{2,0},{4,6},{6,4},{8,10},{10,8},{12,14},{14,12},{16,18},{18,... | collective-permute-start | bytes 430088 | tf_op jit(solution)/shard_map/ppermute | solution.py:406
  54.0 1.6 %collective-permute-start.15 = (bf16[560,128]{1,0:T(8,128)(2,1)S(1)}, bf16[560,128]{1,0:T(8,128)(2,1)S(1)}, u32[]{:S(2)}, u32[]{:S(2)}) collective-permute-start(bf16[560,128]{1,0:T(8,128)(2,1)S(1)} %collective-permute-done.14.refs_2_), channel_id=1, source_target_pairs={{0,2},{2,0},{4,6},{6,4},{8,10},{10,8},{12,14},{14,12},{16,18},{18,... | collective-permute-start | bytes 430088 | tf_op jit(solution)/shard_map/ppermute | solution.py:406
  54.0 1.6 %collective-permute-start.13 = (bf16[560,128]{1,0:T(8,128)(2,1)S(1)}, bf16[560,128]{1,0:T(8,128)(2,1)S(1)}, u32[]{:S(2)}, u32[]{:S(2)}) collective-permute-start(bf16[560,128]{1,0:T(8,128)(2,1)S(1)} %collective-permute-done.12.refs_1_), channel_id=1, source_target_pairs={{0,2},{2,0},{4,6},{6,4},{8,10},{10,8},{12,14},{14,12},{16,18},{18,... | collective-permute-start | bytes 430088 | tf_op jit(solution)/shard_map/ppermute | solution.py:406

commit v5 on v4

--- a/solution.py
+++ b/solution.py
@@ -78,14 +78,14 @@
         copy.wait()
 
 
-def fetch(arrays, after=()):
+def fetch(arrays, after=(), nbytes=4 * 1024 * 1024):
     return pl.pallas_call(
         functools.partial(fetch_kernel, len(arrays)),
         out_shape=tuple(shape(*array.shape) for array in arrays),
         in_specs=[HBM] * (len(arrays) + len(after)),
         out_specs=[VMEM] * len(arrays),
         scratch_shapes=[pltpu.SemaphoreType.DMA((len(arrays),))],
-        cost_estimate=pl.CostEstimate(flops=0, bytes_accessed=4 * 1024 * 1024, transcendentals=0),
+        cost_estimate=pl.CostEstimate(flops=0, bytes_accessed=nbytes, transcendentals=0),
         name="fetch",
         **granted(32),
     )(*arrays, *after)
@@ -169,6 +169,17 @@
     )
 
 
+def far_term_kernel(own, first_kernel, term):
+    term[:, :CONV] = side(mm(own[:, :VAL], Place().beside(first_kernel, 0)), CONV, 1).astype(BF)
+    term[:, CONV:] = own[:, VAL:]
+
+
+def far_back_kernel(far, second_kernel, out):
+    back = side(mm_t(far[:, CONV:], Place().stacked(second_kernel, 2)), CONV, -1)
+    out[:, :CONV] = far[:, :CONV].astype(F32)
+    out[:, CONV:] = back
+
+
 def prepare_kernel(own, local, lse, soft, keys_t, queries_t, attended_t, features_t):
     place = Place()
     across = own.shape[0]
@@ -198,8 +209,14 @@
     first = [place.beside(first_kernel, a) for a in range(3)]
     second = [place.stacked(second_kernel, a) for a in range(3)]
     for slot, out in enumerate(outs, 1):
-        pre = side(sum(mm(slots[slot + a - 1][:, :VAL], first[a]) for a in range(3)), CONV, 1)
-        back = side(sum(mm_t(slots[slot + 1 - a][:, VAL:], second[a]) for a in range(3)), CONV, -1)
+        pre = side(sum(mm(slots[slot + a - 1][:, :VAL], first[a]) for a in range(3) if slot + a > 1), CONV, 1)
+        if slot == 1:
+            pre = pre + slots[0][:, :CONV]
+        back = side(
+            sum(mm_t(slots[slot + 1 - a][:, -CONV:], second[a]) for a in range(3) if slot + 1 - a > 0), CONV, -1
+        )
+        if slot == 1:
+            back = back + slots[0][:, CONV:]
         sigma = 1.0 / (1.0 + jnp.exp(-pre))
         hidden = pre * sigma
         slope = back * (sigma * (1.0 + pre * (1.0 - sigma)))
@@ -414,14 +431,14 @@
     def added(one, two):
         return (one + two).astype(BF)
 
-    def call(kernel, out_shape, operands, scratch=(), name=None):
+    def call(kernel, out_shape, operands, scratch=(), name=None, flops=10**9):
         return pl.pallas_call(
             kernel,
             out_shape=out_shape,
             in_specs=[VMEM] * len(operands),
             out_specs=[VMEM] * len(out_shape),
             scratch_shapes=scratch,
-            cost_estimate=pl.CostEstimate(flops=10**9, bytes_accessed=4 * 1024 * 1024, transcendentals=0),
+            cost_estimate=pl.CostEstimate(flops=flops, bytes_accessed=flops // 250, transcendentals=0),
             name=name,
             **granted(across),
         )(*operands)
@@ -444,13 +461,19 @@
         name="attention_forward",
     )
 
-    first_kernel, second_kernel = fetch((first_kernel, second_kernel), (lse,))
+    given_first = first_kernel
+    first_kernel, second_kernel = fetch((first_kernel, second_kernel), (lse,), 10**5)
     last = rows_size - 1
     out = [(i, i + 2) for i in range(0, last - 1, 2)] + [(i, i - 2) for i in range(3, rows_size, 2)]
     out += [(last - 1, last), (1, 0)]
     back = [(j, i) for i, j in out]
+    (term,) = call(far_term_kernel, (shape(across, 2 * CONV),), (own, given_first), name="far_term")
+    own, term = lax.optimization_barrier((own, term))
     mate1 = lax.ppermute(own, "rows", back)
-    far = lax.ppermute(own, "rows", out)
+    far = lax.ppermute(term, "rows", out)
+    (far,) = call(
+        far_back_kernel, (shape(across, 2 * CONV, dtype=F32),), (far, second_kernel), name="far_back", flops=4 * 10**9
+    )
     mate = rows_flip(own, 1)
     near = rows_flip(mate1, 1)
     soft, keys_t, queries_t, attended_t, features_t = call(
@@ -464,6 +487,7 @@
         ),
         (own, local, lse),
         name="prepare",
+        flops=10**7,
     )
     near_mid, own_mid, mate_mid, grad_own, proj_own, proj_mate = call(
         backward_kernel,

time: 57 us -> 55.7 us (0.977)
  waiting for transfers between devices: 25.4 us -> 24 us
    ppermute x1, waiting for transfers between devices: 5.07 us -> 3.58 us  [body(): mate1 = lax.ppermute(own, 'rows', back)]
    pallas_call x5 -> x7, Pallas kernels: 6.87 us -> 7.26 us  [call(): pl.pallas_call(kernel, out_shape=out_shape, in_specs=[VMEM] * len(operand...]
where the time goes in v5:
time: 55.7 us; the launch traced here: 55.5 us
  waiting for transfers between devices  24 us (43%)
  starting transfers between devices  18.1 us (32%)
  Pallas kernels  9.79 us (18%)
  local copies, waits for them, and re-layouts  2.56 us (5%)
  between operations  0.83 us (1%)
    ppermute x12, waiting for transfers between devices, rows_flip(): lax.ppermute(values, 'rows', [(i, i ^ bit) for i in range(rows_size)])  12.9 us
    ppermute x12, starting transfers between devices, rows_flip(): lax.ppermute(values, 'rows', [(i, i ^ bit) for i in range(rows_size)])  10.1 us
    pallas_call x7, Pallas kernels, call(): pl.pallas_call(kernel, out_shape=out_shape, in_specs=[VMEM] * len(operand...  7.26 us
    ppermute x3, starting transfers between devices, cols_flip(): return lax.ppermute(values, 'cols', [(i, i ^ 1) for i in range(cols_size)])  4.22 us
    ppermute x1, waiting for transfers between devices, body(): mate1 = lax.ppermute(own, 'rows', back)  3.58 us
    ppermute x1, waiting for transfers between devices, body(): lax.ppermute(total, ('rows', 'cols'), [(i * cols_size + j, (i ^ 2) * cols...  3.41 us
    ppermute x3, waiting for transfers between devices, cols_flip(): return lax.ppermute(values, 'cols', [(i, i ^ 1) for i in range(cols_size)])  2.8 us
    unnamed x10, local copies, waits for them, and re-layouts  2.56 us
  transfers between devices with their start and end apart: 18, of which 10 were waited for; matrix products, arithmetic and copies ran while one was open for 0% of the time, Pallas kernels for 7%

profile of v5, /device:TPU:0, one launch (start us, length us, event | category | flops | bytes accessed | tf_op | source)
XLA Modules:
  0.0 55.5 jit_solution(5764931002870130967)
XLA Ops:
  0.6 3.0 %collective-permute-start = (bf16[128,256]{1,0:T(8,128)(2,1)}, bf16[128,256]{1,0:T(8,128)(2,1)S(1)}, u32[]{:S(2)}, u32[]{:S(2)}) collective-permute-start(bf16[128,256]{1,0:T(8,128)(2,1)} %bitcast.8), channel_id=1, source_target_pairs={{0,1},{1,0},{2,3},{3,2},{4,5},{5,4},{6,7},{7,6},{8,9},{9,8},{10,11... | collective-permute-start | bytes 196616 | tf_op jit(solution)/shard_map/ppermute | solution.py:426
  3.7 0.9 %copy-done.2 = bf16[256,512]{1,0:T(8,128)(2,1)S(1)} copy-done((bf16[256,512]{1,0:T(8,128)(2,1)S(1)}, bf16[256,512]{1,0:T(8,128)(2,1)}, u32[]{:S(2)}) %copy-start.2) | copy-done | bytes 262168
  4.7 0.8 %copy-done.3 = bf16[1,128,256]{2,1,0:T(8,128)(2,1)S(1)} copy-done((bf16[1,128,256]{2,1,0:T(8,128)(2,1)S(1)}, bf16[1,128,256]{2,1,0:T(8,128)(2,1)}, u32[]{:S(2)}) %copy-start.3) | copy-done | bytes 65560
  6.4 1.3 %collective-permute-done.1.refs_3_ = bf16[128,128]{1,0:T(8,128)(2,1)S(1)} collective-permute-done((bf16[128,128]{1,0:T(8,128)(2,1)}, bf16[128,128]{1,0:T(8,128)(2,1)S(1)}, u32[]{:S(2)}, u32[]{:S(2)}) %collective-permute-start.1) | collective-permute-done | bytes 32800 | tf_op jit(solution)/shard_map/ppermute | solution.py:426
  7.8 1.3 %attention_forward.1 = (bf16[256,384]{1,0:T(8,128)(2,1)S(1)}, bf16[256,768]{1,0:T(8,128)(2,1)S(1)}, f32[8,256]{1,0:T(8,128)S(1)}) custom-call(bf16[128,256]{1,0:T(8,128)(2,1)S(1)} %get-tuple-element.39.refs_0_, bf16[128,256]{1,0:T(8,128)(2,1)S(1)} %collective-permute-done.refs_1_, bf16[128,128]{1,0:T(8,128)(2,1)S(1)} %get-tuple-element.40.refs_2_, ...), custom_call_target="tpu_custom_call" | custom-call | flops 1000000000 | bytes 4000000 | tf_op jit(solution)/shard_map/attention_forward/pallas_call | solution.py:435
  9.4 2.0 %collective-permute-start.5 = (bf16[256,256]{1,0:T(8,128)(2,1)S(1)}, bf16[256,256]{1,0:T(8,128)(2,1)S(1)}, u32[]{:S(2)}, u32[]{:S(2)}) collective-permute-start(bf16[256,256]{1,0:T(8,128)(2,1)S(1)} %far_term.1), channel_id=1, source_target_pairs={{0,4},{4,8},{8,12},{12,16},{16,20},{20,24},{24,28},{6,2},{10,6},{1... | collective-permute-start | bytes 393224 | tf_op jit(solution)/shard_map/ppermute | solution.py:473
  12.2 3.6 %collective-permute-done.2.mate1 = bf16[256,384]{1,0:T(8,128)(2,1)S(1)} collective-permute-done((bf16[256,384]{1,0:T(8,128)(2,1)S(1)}, bf16[256,384]{1,0:T(8,128)(2,1)S(1)}, u32[]{:S(2)}, u32[]{:S(2)}) %collective-permute-start.2) | collective-permute-done | bytes 196640 | tf_op jit(solution)/shard_map/ppermute | solution.py:472
  15.8 1.3 %collective-permute-done.5.far = bf16[256,256]{1,0:T(8,128)(2,1)S(1)} collective-permute-done((bf16[256,256]{1,0:T(8,128)(2,1)S(1)}, bf16[256,256]{1,0:T(8,128)(2,1)S(1)}, u32[]{:S(2)}, u32[]{:S(2)}) %collective-permute-start.5) | collective-permute-done | bytes 131104 | tf_op jit(solution)/shard_map/ppermute | solution.py:473
  17.4 3.1 %block_backward.1 = (bf16[256,256]{1,0:T(8,128)(2,1)S(1)}, bf16[256,256]{1,0:T(8,128)(2,1)S(1)}, bf16[256,256]{1,0:T(8,128)(2,1)S(1)}, bf16[128,512]{1,0:T(8,128...) custom-call(f32[256,256]{1,0:T(8,128)S(1)} %far_back.1.far, ...), custom_call_target="tpu_custom_call" | custom-call | flops 1000000000 | bytes 4000000 | tf_op jit(solution)/shard_map/block_backward/pallas_call | solution.py:435
  20.6 0.8 %conv_grads.1 = (bf16[432,128]{1,0:T(8,128)(2,1)S(1)}, bf16[432,128]{1,0:T(8,128)(2,1)S(1)}) custom-call(bf16[256,384]{1,0:T(8,128)(2,1)S(1)} %collective-permute-done.3.near, bf16[256,384]{1,0:T(8,128)(2,1)S(1)} %get-tuple-element.43.own, bf16[256,384]{1,0:T(8,128)(2,1)S(1)} %collective-permute-done.4.mate, ...), custom_call_target="tpu_custom_call" | custom-call | flops 1000000000 | bytes 4000000 | tf_op jit(solution)/shard_map/conv_grads/pallas_call | solution.py:435
  21.9 4.6 %collective-permute-start.7 = (bf16[560,128]{1,0:T(8,128)(2,1)S(1)}, bf16[560,128]{1,0:T(8,128)(2,1)S(1)}, u32[]{:S(2)}, u32[]{:S(2)}) collective-permute-start(bf16[560,128]{1,0:T(8,128)(2,1)S(1)} %pad_maximum_fusion), channel_id=1, source_target_pairs={{0,8},{2,10},{4,12},{6,14},{8,0},{10,2},{12,4},{14,6},{16,24},{18,... | collective-permute-start | bytes 430088 | tf_op jit(solution)/shard_map/ppermute | solution.py:423
  26.6 1.5 %collective-permute-start.8 = (bf16[560,128]{1,0:T(8,128)(2,1)S(1)}, bf16[560,128]{1,0:T(8,128)(2,1)S(1)}, u32[]{:S(2)}, u32[]{:S(2)}) collective-permute-start(bf16[560,128]{1,0:T(8,128)(2,1)S(1)} %pad_maximum_fusion.1), channel_id=1, source_target_pairs={{0,4},{2,6},{4,0},{6,2},{8,12},{10,14},{12,8},{14,10},{16,20},{18,... | collective-permute-start | bytes 430088 | tf_op jit(solution)/shard_map/ppermute | solution.py:423
  28.1 3.0 %collective-permute-done.7 = bf16[560,128]{1,0:T(8,128)(2,1)S(1)} collective-permute-done((bf16[560,128]{1,0:T(8,128)(2,1)S(1)}, bf16[560,128]{1,0:T(8,128)(2,1)S(1)}, u32[]{:S(2)}, u32[]{:S(2)}) %collective-permute-start.7) | collective-permute-done | bytes 143392 | tf_op jit(solution)/shard_map/ppermute | solution.py:423
  31.1 2.1 %collective-permute-done.9 = bf16[560,128]{1,0:T(8,128)(2,1)S(1)} collective-permute-done((bf16[560,128]{1,0:T(8,128)(2,1)S(1)}, bf16[560,128]{1,0:T(8,128)(2,1)S(1)}, u32[]{:S(2)}, u32[]{:S(2)}) %collective-permute-start.9) | collective-permute-done | bytes 143392 | tf_op jit(solution)/shard_map/ppermute | solution.py:423
  33.2 2.1 %collective-permute-done.8 = bf16[560,128]{1,0:T(8,128)(2,1)S(1)} collective-permute-done((bf16[560,128]{1,0:T(8,128)(2,1)S(1)}, bf16[560,128]{1,0:T(8,128)(2,1)S(1)}, u32[]{:S(2)}, u32[]{:S(2)}) %collective-permute-start.8) | collective-permute-done | bytes 143392 | tf_op jit(solution)/shard_map/ppermute | solution.py:423
  35.4 2.7 %collective-permute-start.10 = (bf16[560,128]{1,0:T(8,128)(2,1)S(1)}, bf16[560,128]{1,0:T(8,128)(2,1)S(1)}, u32[]{:S(2)}, u32[]{:S(2)}) collective-permute-start(bf16[560,128]{1,0:T(8,128)(2,1)S(1)} %add_convert_fusion.1), channel_id=1, source_target_pairs={{0,16},{2,18},{4,20},{6,22},{8,24},{10,26},{12,28},{14,30},{16,0},... | collective-permute-start | bytes 430088 | tf_op jit(solution)/shard_map/ppermute | solution.py:423
  38.0 1.0 %outputs.1 = (bf16[128,128]{1,0:T(8,128)(2,1)}, bf16[128,256]{1,0:T(8,128)(2,1)}) custom-call(bf16[256,256]{1,0:T(8,128)(2,1)S(1)} %get-tuple-element.60.near_mid, bf16[256,256]{1,0:T(8,128)(2,1)S(1)} %get-tuple-element.54.own_mid, bf16[256,256]{1,0:T(8,128)(2,1)S(1)} %get-tuple-element.55.mate_mid, bf16[128,512]{1,0:T(8,128)(2,1)S(1)} %get-tuple-element.61.grad_own, ...), custom_call_target="tpu_custom_call" | custom-call | flops 1000000000 | bytes 4000000 | tf_op jit(solution)/shard_map/outputs/pallas_call | solution.py:435
  39.1 5.2 %collective-permute-done.10 = bf16[560,128]{1,0:T(8,128)(2,1)S(1)} collective-permute-done((bf16[560,128]{1,0:T(8,128)(2,1)S(1)}, bf16[560,128]{1,0:T(8,128)(2,1)S(1)}, u32[]{:S(2)}, u32[]{:S(2)}) %collective-permute-start.10) | collective-permute-done | bytes 143392 | tf_op jit(solution)/shard_map/ppermute | solution.py:423
  44.3 1.7 %collective-permute-start.16 = (bf16[560,128]{1,0:T(8,128)(2,1)S(1)}, bf16[560,128]{1,0:T(8,128)(2,1)S(1)}, u32[]{:S(2)}, u32[]{:S(2)}) collective-permute-start(bf16[560,128]{1,0:T(8,128)(2,1)S(1)} %add_convert_fusion.refs_0_), channel_id=1, source_target_pairs={{0,5},{1,4},{2,7},{3,6},{4,1},{5,0},{6,3},{7,2},{8,13},{9,12},{10,... | collective-permute-start | bytes 430088 | tf_op jit(solution)/shard_map/ppermute | solution.py:547
  46.0 1.1 %collective-permute-start.14 = (bf16[560,128]{1,0:T(8,128)(2,1)S(1)}, bf16[560,128]{1,0:T(8,128)(2,1)S(1)}, u32[]{:S(2)}, u32[]{:S(2)}) collective-permute-start(bf16[560,128]{1,0:T(8,128)(2,1)S(1)} %add_convert_fusion.refs_0_), channel_id=1, source_target_pairs={{0,1},{1,0},{2,3},{3,2},{4,5},{5,4},{6,7},{7,6},{8,9},{9,8},{10,11... | collective-permute-start | bytes 430088 | tf_op jit(solution)/shard_map/ppermute | solution.py:426
  47.9 3.4 %collective-permute-done.16.refs_3_ = bf16[560,128]{1,0:T(8,128)(2,1)S(1)} collective-permute-done((bf16[560,128]{1,0:T(8,128)(2,1)S(1)}, bf16[560,128]{1,0:T(8,128)(2,1)S(1)}, u32[]{:S(2)}, u32[]{:S(2)}) %collective-permute-start.16) | collective-permute-done | bytes 143392 | tf_op jit(solution)/shard_map/ppermute | solution.py:547
  51.3 1.5 %collective-permute-done.14.refs_2_ = bf16[560,128]{1,0:T(8,128)(2,1)S(1)} collective-permute-done((bf16[560,128]{1,0:T(8,128)(2,1)S(1)}, bf16[560,128]{1,0:T(8,128)(2,1)S(1)}, u32[]{:S(2)}, u32[]{:S(2)}) %collective-permute-start.14) | collective-permute-done | bytes 143392 | tf_op jit(solution)/shard_map/ppermute | solution.py:426
  53.3 1.1 %unpack_sums.2 = (f32[256,512]{1,0:T(8,128)}, f32[3,3,256,128]{3,2,1,0:T(8,128)}, f32[3,3,128,128]{3,2,1,0:T(8,128)}) custom-call(bf16[560,128]{1,0:T(8,128)(2,1)S(1)} %add_convert_fusion.refs_0_, bf16[560,128]{1,0:T(8,128)(2,1)S(1)} %collective-permute-done.12.refs_1_, bf16[560,128]{1,0:T(8,128)(2,1)S(1)} %collective-permute-done.14.refs_2_, ...), custom_call_target="tpu_custom_call" | custom-call | flops 1000000000 | bytes 4194304 | tf_op jit(solution)/shard_map/unpack_sums/pallas_call | solution.py:390
  54.4 1.1 %unpack_sums.3 = (f32[256,512]{1,0:T(8,128)}, f32[3,3,256,128]{3,2,1,0:T(8,128)}, f32[3,3,128,128]{3,2,1,0:T(8,128)}) custom-call(bf16[560,128]{1,0:T(8,128)(2,1)S(1)} %collective-permute-done.11.refs_0_, bf16[560,128]{1,0:T(8,128)(2,1)S(1)} %collective-permute-done.13.refs_1_, ...), custom_call_target="tpu_custom_call", output_to_operand_aliasing={{0}: (4, {}), {1}: (5, {}), {2}: (6, {})} | custom-call | flops 1000000000 | bytes 4194304 | tf_op jit(solution)/shard_map/unpack_sums/pallas_call | solution.py:390
  (39 shorter events, 4.3 us)
Async XLA Ops:
  0.6 7.1 %collective-permute-start = (bf16[128,256]{1,0:T(8,128)(2,1)}, bf16[128,256]{1,0:T(8,128)(2,1)S(1)}, u32[]{:S(2)}, u32[]{:S(2)}) collective-permute-start(bf16[128,256]{1,0:T(8,128)(2,1)} %bitcast.8), channel_id=1, source_target_pairs={{0,1},{1,0},{2,3},{3,2},{4,5},{5,4},{6,7},{7,6},{8,9},{9,8},{10,11... | collective-permute-start | bytes 196616 | tf_op jit(solution)/shard_map/ppermute | solution.py:426
  3.6 4.1 %collective-permute-start.1 = (bf16[128,128]{1,0:T(8,128)(2,1)}, bf16[128,128]{1,0:T(8,128)(2,1)S(1)}, u32[]{:S(2)}, u32[]{:S(2)}) collective-permute-start(bf16[128,128]{1,0:T(8,128)(2,1)} %bitcast.10), channel_id=1, source_target_pairs={{0,1},{1,0},{2,3},{3,2},{4,5},{5,4},{6,7},{7,6},{8,9},{9,8},{10,11... | collective-permute-start | bytes 98312 | tf_op jit(solution)/shard_map/ppermute | solution.py:426
  3.7 0.9 %copy-start.2 = (bf16[256,512]{1,0:T(8,128)(2,1)S(1)}, bf16[256,512]{1,0:T(8,128)(2,1)}, u32[]{:S(2)}) copy-start(bf16[256,512]{1,0:T(8,128)(2,1)} %refs_0_.2) | copy-start | bytes 786436
  4.7 0.8 %copy-start.3 = (bf16[1,128,256]{2,1,0:T(8,128)(2,1)S(1)}, bf16[1,128,256]{2,1,0:T(8,128)(2,1)}, u32[]{:S(2)}) copy-start(bf16[1,128,256]{2,1,0:T(8,128)(2,1)} %param.5) | copy-start | bytes 196612
  5.5 0.8 %copy-start.4 = (bf16[1,128,128]{2,1,0:T(8,128)(2,1)S(1)}, bf16[1,128,128]{2,1,0:T(8,128)(2,1)}, u32[]{:S(2)}) copy-start(bf16[1,128,128]{2,1,0:T(8,128)(2,1)} %param.9) | copy-start | bytes 98308
  7.8 1.3 %copy-start = (bf16[3,3,256,128]{3,2,1,0:T(8,128)(2,1)S(1)}, bf16[3,3,256,128]{3,2,1,0:T(8,128)(2,1)}, u32[]{:S(2)}) copy-start(bf16[3,3,256,128]{3,2,1,0:T(8,128)(2,1)} %refs_0_.3) | copy-start | bytes 1769476
  9.1 2.3 %copy-start.1 = (bf16[3,3,128,128]{3,2,1,0:T(8,128)(2,1)S(1)}, bf16[3,3,128,128]{3,2,1,0:T(8,128)(2,1)}, u32[]{:S(2)}) copy-start(bf16[3,3,128,128]{3,2,1,0:T(8,128)(2,1)} %refs_1_.1) | copy-start | bytes 884740
  9.4 6.4 %collective-permute-start.2 = (bf16[256,384]{1,0:T(8,128)(2,1)S(1)}, bf16[256,384]{1,0:T(8,128)(2,1)S(1)}, u32[]{:S(2)}, u32[]{:S(2)}) collective-permute-start(bf16[256,384]{1,0:T(8,128)(2,1)S(1)} %get-tuple-element.43.own), channel_id=1, source_target_pairs={{4,0},{8,4},{12,8},{16,12},{20,16},{24,20},{28,24},{2,6},{6,10},{1... | collective-permute-start | bytes 589832 | tf_op jit(solution)/shard_map/ppermute | solution.py:472
  9.4 7.7 %collective-permute-start.5 = (bf16[256,256]{1,0:T(8,128)(2,1)S(1)}, bf16[256,256]{1,0:T(8,128)(2,1)S(1)}, u32[]{:S(2)}, u32[]{:S(2)}) collective-permute-start(bf16[256,256]{1,0:T(8,128)(2,1)S(1)} %far_term.1), channel_id=1, source_target_pairs={{0,4},{4,8},{8,12},{12,16},{16,20},{20,24},{24,28},{6,2},{10,6},{1... | collective-permute-start | bytes 393224 | tf_op jit(solution)/shard_map/ppermute | solution.py:473
  11.5 5.9 %collective-permute-start.4 = (bf16[256,384]{1,0:T(8,128)(2,1)S(1)}, bf16[256,384]{1,0:T(8,128)(2,1)S(1)}, u32[]{:S(2)}, u32[]{:S(2)}) collective-permute-start(bf16[256,384]{1,0:T(8,128)(2,1)S(1)} %get-tuple-element.43.own), channel_id=1, source_target_pairs={{0,2},{2,0},{4,6},{6,4},{8,10},{10,8},{12,14},{14,12},{16,18},{18,... | collective-permute-start | bytes 589832 | tf_op jit(solution)/shard_map/ppermute | solution.py:423
  15.8 1.6 %collective-permute-start.3 = (bf16[256,384]{1,0:T(8,128)(2,1)S(1)}, bf16[256,384]{1,0:T(8,128)(2,1)S(1)}, u32[]{:S(2)}, u32[]{:S(2)}) collective-permute-start(bf16[256,384]{1,0:T(8,128)(2,1)S(1)} %collective-permute-done.2.mate1), channel_id=1, source_target_pairs={{0,2},{2,0},{4,6},{6,4},{8,10},{10,8},{12,14},{14,12},{16,18},{18,... | collective-permute-start | bytes 589832 | tf_op jit(solution)/shard_map/ppermute | solution.py:423
  20.5 1.3 %collective-permute-start.6 = (bf16[2,128,128]{2,1,0:T(8,128)(2,1)S(1)}, bf16[2,128,128]{2,1,0:T(8,128)(2,1)S(1)}, u32[]{:S(2)}, u32[]{:S(2)}) collective-permute-start(bf16[2,128,128]{2,1,0:T(8,128)(2,1)S(1)} %get-tuple-element.58), channel_id=1, source_target_pairs={{0,2},{2,0},{4,6},{6,4},{8,10},{10,8},{12,14},{14,12},{16,18},{18,... | collective-permute-start | bytes 196616 | tf_op jit(solution)/shard_map/ppermute | solution.py:423
  21.9 9.2 %collective-permute-start.7 = (bf16[560,128]{1,0:T(8,128)(2,1)S(1)}, bf16[560,128]{1,0:T(8,128)(2,1)S(1)}, u32[]{:S(2)}, u32[]{:S(2)}) collective-permute-start(bf16[560,128]{1,0:T(8,128)(2,1)S(1)} %pad_maximum_fusion), channel_id=1, source_target_pairs={{0,8},{2,10},{4,12},{6,14},{8,0},{10,2},{12,4},{14,6},{16,24},{18,... | collective-permute-start | bytes 430088 | tf_op jit(solution)/shard_map/ppermute | solution.py:423
  26.5 6.6 %collective-permute-start.9 = (bf16[560,128]{1,0:T(8,128)(2,1)S(1)}, bf16[560,128]{1,0:T(8,128)(2,1)S(1)}, u32[]{:S(2)}, u32[]{:S(2)}) collective-permute-start(bf16[560,128]{1,0:T(8,128)(2,1)S(1)} %pad_maximum_fusion.1), channel_id=1, source_target_pairs={{0,12},{2,14},{4,8},{6,10},{8,4},{10,6},{12,0},{14,2},{16,28},{18,... | collective-permute-start | bytes 430088 | tf_op jit(solution)/shard_map/ppermute | solution.py:423
  26.6 8.7 %collective-permute-start.8 = (bf16[560,128]{1,0:T(8,128)(2,1)S(1)}, bf16[560,128]{1,0:T(8,128)(2,1)S(1)}, u32[]{:S(2)}, u32[]{:S(2)}) collective-permute-start(bf16[560,128]{1,0:T(8,128)(2,1)S(1)} %pad_maximum_fusion.1), channel_id=1, source_target_pairs={{0,4},{2,6},{4,0},{6,2},{8,12},{10,14},{12,8},{14,10},{16,20},{18,... | collective-permute-start | bytes 430088 | tf_op jit(solution)/shard_map/ppermute | solution.py:423
  35.4 8.9 %collective-permute-start.10 = (bf16[560,128]{1,0:T(8,128)(2,1)S(1)}, bf16[560,128]{1,0:T(8,128)(2,1)S(1)}, u32[]{:S(2)}, u32[]{:S(2)}) collective-permute-start(bf16[560,128]{1,0:T(8,128)(2,1)S(1)} %add_convert_fusion.1), channel_id=1, source_target_pairs={{0,16},{2,18},{4,20},{6,22},{8,24},{10,26},{12,28},{14,30},{16,0},... | collective-permute-start | bytes 430088 | tf_op jit(solution)/shard_map/ppermute | solution.py:423
  44.3 7.0 %collective-permute-start.16 = (bf16[560,128]{1,0:T(8,128)(2,1)S(1)}, bf16[560,128]{1,0:T(8,128)(2,1)S(1)}, u32[]{:S(2)}, u32[]{:S(2)}) collective-permute-start(bf16[560,128]{1,0:T(8,128)(2,1)S(1)} %add_convert_fusion.refs_0_), channel_id=1, source_target_pairs={{0,5},{1,4},{2,7},{3,6},{4,1},{5,0},{6,3},{7,2},{8,13},{9,12},{10,... | collective-permute-start | bytes 430088 | tf_op jit(solution)/shard_map/ppermute | solution.py:547
  46.0 6.7 %collective-permute-start.14 = (bf16[560,128]{1,0:T(8,128)(2,1)S(1)}, bf16[560,128]{1,0:T(8,128)(2,1)S(1)}, u32[]{:S(2)}, u32[]{:S(2)}) collective-permute-start(bf16[560,128]{1,0:T(8,128)(2,1)S(1)} %add_convert_fusion.refs_0_), channel_id=1, source_target_pairs={{0,1},{1,0},{2,3},{3,2},{4,5},{5,4},{6,7},{7,6},{8,9},{9,8},{10,11... | collective-permute-start | bytes 430088 | tf_op jit(solution)/shard_map/ppermute | solution.py:426
  47.2 5.6 %collective-permute-start.12 = (bf16[560,128]{1,0:T(8,128)(2,1)S(1)}, bf16[560,128]{1,0:T(8,128)(2,1)S(1)}, u32[]{:S(2)}, u32[]{:S(2)}) collective-permute-start(bf16[560,128]{1,0:T(8,128)(2,1)S(1)} %add_convert_fusion.refs_0_), channel_id=1, source_target_pairs={{0,4},{2,6},{4,0},{6,2},{8,12},{10,14},{12,8},{14,10},{16,20},{18,... | collective-permute-start | bytes 430088 | tf_op jit(solution)/shard_map/ppermute | solution.py:423
  47.9 6.5 %collective-permute-start.11 = (bf16[560,128]{1,0:T(8,128)(2,1)S(1)}, bf16[560,128]{1,0:T(8,128)(2,1)S(1)}, u32[]{:S(2)}, u32[]{:S(2)}) collective-permute-start(bf16[560,128]{1,0:T(8,128)(2,1)S(1)} %add_convert_fusion.refs_0_), channel_id=1, source_target_pairs={{0,2},{2,0},{4,6},{6,4},{8,10},{10,8},{12,14},{14,12},{16,18},{18,... | collective-permute-start | bytes 430088 | tf_op jit(solution)/shard_map/ppermute | solution.py:423
  51.3 3.1 %collective-permute-start.17 = (bf16[560,128]{1,0:T(8,128)(2,1)S(1)}, bf16[560,128]{1,0:T(8,128)(2,1)S(1)}, u32[]{:S(2)}, u32[]{:S(2)}) collective-permute-start(bf16[560,128]{1,0:T(8,128)(2,1)S(1)} %collective-permute-done.16.refs_3_), channel_id=1, source_target_pairs={{0,2},{2,0},{4,6},{6,4},{8,10},{10,8},{12,14},{14,12},{16,18},{18,... | collective-permute-start | bytes 430088 | tf_op jit(solution)/shard_map/ppermute | solution.py:423
  52.8 1.6 %collective-permute-start.15 = (bf16[560,128]{1,0:T(8,128)(2,1)S(1)}, bf16[560,128]{1,0:T(8,128)(2,1)S(1)}, u32[]{:S(2)}, u32[]{:S(2)}) collective-permute-start(bf16[560,128]{1,0:T(8,128)(2,1)S(1)} %collective-permute-done.14.refs_2_), channel_id=1, source_target_pairs={{0,2},{2,0},{4,6},{6,4},{8,10},{10,8},{12,14},{14,12},{16,18},{18,... | collective-permute-start | bytes 430088 | tf_op jit(solution)/shard_map/ppermute | solution.py:423
  52.8 1.6 %collective-permute-start.13 = (bf16[560,128]{1,0:T(8,128)(2,1)S(1)}, bf16[560,128]{1,0:T(8,128)(2,1)S(1)}, u32[]{:S(2)}, u32[]{:S(2)}) collective-permute-start(bf16[560,128]{1,0:T(8,128)(2,1)S(1)} %collective-permute-done.12.refs_1_), channel_id=1, source_target_pairs={{0,2},{2,0},{4,6},{6,4},{8,10},{10,8},{12,14},{14,12},{16,18},{18,... | collective-permute-start | bytes 430088 | tf_op jit(solution)/shard_map/ppermute | solution.py:423

commit v6 on v5

--- a/solution.py
+++ b/solution.py
@@ -205,26 +205,40 @@
     return jnp.where(inside, row, jnp.zeros_like(row))
 
 
-def middle(place, slots, first_kernel, second_kernel, outs):
-    first = [place.beside(first_kernel, a) for a in range(3)]
-    second = [place.stacked(second_kernel, a) for a in range(3)]
-    for slot, out in enumerate(outs, 1):
-        pre = side(sum(mm(slots[slot + a - 1][:, :VAL], first[a]) for a in range(3) if slot + a > 1), CONV, 1)
-        if slot == 1:
-            pre = pre + slots[0][:, :CONV]
-        back = side(
-            sum(mm_t(slots[slot + 1 - a][:, -CONV:], second[a]) for a in range(3) if slot + 1 - a > 0), CONV, -1
-        )
-        if slot == 1:
-            back = back + slots[0][:, CONV:]
-        sigma = 1.0 / (1.0 + jnp.exp(-pre))
-        hidden = pre * sigma
-        slope = back * (sigma * (1.0 + pre * (1.0 - sigma)))
-        if slot == 1:
-            hidden = masked(place.near_inside, hidden)
-            slope = masked(place.near_inside, slope)
-        out[:, :CONV] = hidden.astype(BF)
-        out[:, CONV:] = slope.astype(BF)
+def conv_term(place, row, kernel, tap):
+    return side(mm(row[:, :VAL], place.beside(kernel, tap)), CONV, 1)
+
+
+def back_term(place, row, kernel, tap):
+    return side(mm_t(row[:, VAL:], place.stacked(kernel, tap)), CONV, -1)
+
+
+def store_middle(pre, back, out):
+    sigma = 1.0 / (1.0 + jnp.exp(-pre))
+    out[:, :CONV] = (pre * sigma).astype(BF)
+    out[:, CONV:] = (back * (sigma * (1.0 + pre * (1.0 - sigma)))).astype(BF)
+
+
+def inner_kernel(own, mate, mate1, first_kernel, second_kernel, mate_mid, near_part, own_part):
+    place = Place()
+    mate1 = masked(place.mate_inside, mate1[...])
+    near_part[:, :CONV] = conv_term(place, own, first_kernel, 2)
+    near_part[:, CONV:] = back_term(place, own, second_kernel, 0)
+    own_part[:, :CONV] = conv_term(place, own, first_kernel, 1) + conv_term(place, mate, first_kernel, 2)
+    own_part[:, CONV:] = back_term(place, own, second_kernel, 1) + back_term(place, mate, second_kernel, 0)
+    rows = (own, mate, mate1)
+    pre = sum(conv_term(place, row, first_kernel, a) for a, row in enumerate(rows))
+    back = sum(back_term(place, row, second_kernel, 2 - a) for a, row in enumerate(rows))
+    store_middle(pre, back, mate_mid)
+
+
+def middle(place, far, near, near_part, own_part, first_kernel, second_kernel, near_mid, own_mid):
+    pre = near_part[:, :CONV] + far[:, :CONV] + conv_term(place, near, first_kernel, 1)
+    back = near_part[:, CONV:] + far[:, CONV:] + back_term(place, near, second_kernel, 1)
+    store_middle(masked(place.near_inside, pre), masked(place.near_inside, back), near_mid)
+    pre = own_part[:, :CONV] + conv_term(place, near, first_kernel, 0)
+    back = own_part[:, CONV:] + back_term(place, near, second_kernel, 2)
+    store_middle(pre, back, own_mid)
 
 
 def conv_grads_kernel(near, own, mate, mate1, own_mid, mate_mid, keep, send):
@@ -255,9 +269,9 @@
 def backward_kernel(
     far,
     near,
-    own,
-    mate,
-    mate1,
+    mate_mid,
+    near_part,
+    own_part,
     local,
     soft,
     keys_t,
@@ -268,7 +282,6 @@
     second_kernel,
     near_mid,
     own_mid,
-    mate_mid,
     grad_own,
     proj_own,
     proj_mate,
@@ -276,11 +289,11 @@
     grad_t,
 ):
     place = Place()
-    across = own.shape[0]
+    across = near.shape[0]
     part_width = grad_own.shape[0]
-    slots = (far[...], masked(place.near_inside, near[...]), own[...], mate[...], masked(place.mate_inside, mate1[...]))
+    near = masked(place.near_inside, near[...])
     mids = (near_mid, own_mid, mate_mid)
-    middle(place, slots, first_kernel, second_kernel, mids)
+    middle(place, far, near, near_part, own_part, first_kernel, second_kernel, near_mid, own_mid)
     upstream_ref[...] = side(
         sum(mm_t(mids[2 - a][:, CONV:], place.stacked(first_kernel, a)) for a in range(3)), VAL, -1
     ).astype(BF)
@@ -489,10 +502,15 @@
         name="prepare",
         flops=10**7,
     )
-    near_mid, own_mid, mate_mid, grad_own, proj_own, proj_mate = call(
+    mate_mid, near_part, own_part = call(
+        inner_kernel,
+        (shape(across, 2 * CONV), shape(across, 2 * CONV, dtype=F32), shape(across, 2 * CONV, dtype=F32)),
+        (own, mate, mate1, first_kernel, second_kernel),
+        name="inner",
+    )
+    near_mid, own_mid, grad_own, proj_own, proj_mate = call(
         backward_kernel,
         (
-            shape(across, 2 * CONV),
             shape(across, 2 * CONV),
             shape(across, 2 * CONV),
             shape(part_width, PACKED),
@@ -502,9 +520,9 @@
         (
             far,
             near,
-            own,
-            mate,
-            mate1,
+            mate_mid,
+            near_part,
+            own_part,
             local,
             soft,
             keys_t,

time: 55.7 us -> 55.3 us (level)
  starting transfers between devices: 18.1 us -> 17.2 us
    ppermute x12, starting transfers between devices: 10.1 us -> 9.1 us  [rows_flip(): lax.ppermute(values, 'rows', [(i, i ^ bit) for i in range(rows_size)])]
    pallas_call x7 -> x8, Pallas kernels: 7.26 us -> 7.6 us  [call(): pl.pallas_call(kernel, out_shape=out_shape, in_specs=[VMEM] * len(operand...]
  transfers between devices with their start and end apart: 18 -> 18, of which waited for: 10 -> 10; matrix products, arithmetic and copies ran while one was open for 0% -> 0% of each run, Pallas kernels for 7% -> 9%
where the time goes in v6:
time: 55.3 us; the launch traced here: 55 us
  waiting for transfers between devices  24.1 us (44%)
  starting transfers between devices  17.2 us (31%)
  Pallas kernels  10.1 us (18%)
  local copies, waits for them, and re-layouts  2.56 us (5%)
  between operations  0.84 us (2%)
    ppermute x12, waiting for transfers between devices, rows_flip(): lax.ppermute(values, 'rows', [(i, i ^ bit) for i in range(rows_size)])  12.8 us
    ppermute x12, starting transfers between devices, rows_flip(): lax.ppermute(values, 'rows', [(i, i ^ bit) for i in range(rows_size)])  9.1 us
    pallas_call x8, Pallas kernels, call(): pl.pallas_call(kernel, out_shape=out_shape, in_specs=[VMEM] * len(operand...  7.6 us
    ppermute x3, starting transfers between devices, cols_flip(): return lax.ppermute(values, 'cols', [(i, i ^ 1) for i in range(cols_size)])  4.22 us
    ppermute x1, waiting for transfers between devices, body(): mate1 = lax.ppermute(own, 'rows', back)  3.58 us
    ppermute x1, waiting for transfers between devices, body(): lax.ppermute(total, ('rows', 'cols'), [(i * cols_size + j, (i ^ 2) * cols...  3.38 us
    ppermute x3, waiting for transfers between devices, cols_flip(): return lax.ppermute(values, 'cols', [(i, i ^ 1) for i in range(cols_size)])  2.97 us
    unnamed x10, local copies, waits for them, and re-layouts  2.56 us
  transfers between devices with their start and end apart: 18, of which 10 were waited for; matrix products, arithmetic and copies ran while one was open for 0% of the time, Pallas kernels for 9%

profile of v6, /device:TPU:0, one launch (start us, length us, event | category | flops | bytes accessed | tf_op | source)
XLA Modules:
  0.0 55.0 jit_solution(14737172167741239010)
XLA Ops:
  0.6 3.0 %collective-permute-start = (bf16[128,256]{1,0:T(8,128)(2,1)}, bf16[128,256]{1,0:T(8,128)(2,1)S(1)}, u32[]{:S(2)}, u32[]{:S(2)}) collective-permute-start(bf16[128,256]{1,0:T(8,128)(2,1)} %bitcast.8), channel_id=1, source_target_pairs={{0,1},{1,0},{2,3},{3,2},{4,5},{5,4},{6,7},{7,6},{8,9},{9,8},{10,11... | collective-permute-start | bytes 196616 | tf_op jit(solution)/shard_map/ppermute | solution.py:439
  3.7 0.9 %copy-done.2 = bf16[256,512]{1,0:T(8,128)(2,1)S(1)} copy-done((bf16[256,512]{1,0:T(8,128)(2,1)S(1)}, bf16[256,512]{1,0:T(8,128)(2,1)}, u32[]{:S(2)}) %copy-start.2) | copy-done | bytes 262168
  4.7 0.8 %copy-done.3 = bf16[1,128,256]{2,1,0:T(8,128)(2,1)S(1)} copy-done((bf16[1,128,256]{2,1,0:T(8,128)(2,1)S(1)}, bf16[1,128,256]{2,1,0:T(8,128)(2,1)}, u32[]{:S(2)}) %copy-start.3) | copy-done | bytes 65560
  6.4 1.3 %collective-permute-done.1.refs_3_ = bf16[128,128]{1,0:T(8,128)(2,1)S(1)} collective-permute-done((bf16[128,128]{1,0:T(8,128)(2,1)}, bf16[128,128]{1,0:T(8,128)(2,1)S(1)}, u32[]{:S(2)}, u32[]{:S(2)}) %collective-permute-start.1) | collective-permute-done | bytes 32800 | tf_op jit(solution)/shard_map/ppermute | solution.py:439
  7.8 1.3 %attention_forward.1 = (bf16[256,384]{1,0:T(8,128)(2,1)S(1)}, bf16[256,768]{1,0:T(8,128)(2,1)S(1)}, f32[8,256]{1,0:T(8,128)S(1)}) custom-call(bf16[128,256]{1,0:T(8,128)(2,1)S(1)} %get-tuple-element.41.refs_0_, bf16[128,256]{1,0:T(8,128)(2,1)S(1)} %collective-permute-done.refs_1_, bf16[128,128]{1,0:T(8,128)(2,1)S(1)} %get-tuple-element.42.refs_2_, ...), custom_call_target="tpu_custom_call" | custom-call | flops 1000000000 | bytes 4000000 | tf_op jit(solution)/shard_map/attention_forward/pallas_call | solution.py:448
  9.4 2.0 %collective-permute-start.5 = (bf16[256,256]{1,0:T(8,128)(2,1)S(1)}, bf16[256,256]{1,0:T(8,128)(2,1)S(1)}, u32[]{:S(2)}, u32[]{:S(2)}) collective-permute-start(bf16[256,256]{1,0:T(8,128)(2,1)S(1)} %far_term.1), channel_id=1, source_target_pairs={{0,4},{4,8},{8,12},{12,16},{16,20},{20,24},{24,28},{6,2},{10,6},{1... | collective-permute-start | bytes 393224 | tf_op jit(solution)/shard_map/ppermute | solution.py:486
  12.2 3.6 %collective-permute-done.2.mate1 = bf16[256,384]{1,0:T(8,128)(2,1)S(1)} collective-permute-done((bf16[256,384]{1,0:T(8,128)(2,1)S(1)}, bf16[256,384]{1,0:T(8,128)(2,1)S(1)}, u32[]{:S(2)}, u32[]{:S(2)}) %collective-permute-start.2) | collective-permute-done | bytes 196640 | tf_op jit(solution)/shard_map/ppermute | solution.py:485
  15.8 1.3 %collective-permute-done.5.far = bf16[256,256]{1,0:T(8,128)(2,1)S(1)} collective-permute-done((bf16[256,256]{1,0:T(8,128)(2,1)S(1)}, bf16[256,256]{1,0:T(8,128)(2,1)S(1)}, u32[]{:S(2)}, u32[]{:S(2)}) %collective-permute-start.5) | collective-permute-done | bytes 131104 | tf_op jit(solution)/shard_map/ppermute | solution.py:486
  17.4 0.9 %inner.1 = (bf16[256,256]{1,0:T(8,128)(2,1)S(1)}, f32[256,256]{1,0:T(8,128)S(1)}, f32[256,256]{1,0:T(8,128)S(1)}) custom-call(bf16[256,384]{1,0:T(8,128)(2,1)S(1)} %get-tuple-element.45.own, bf16[256,384]{1,0:T(8,128)(2,1)S(1)} %collective-permute-done.4.mate, bf16[256,384]{1,0:T(8,128)(2,1)S(1)} %collective-permute-done.2.mate1, ...), custom_call_target="tpu_custom_call" | custom-call | flops 1000000000 | bytes 4000000 | tf_op jit(solution)/shard_map/inner/pallas_call | solution.py:448
  18.3 2.5 %block_backward.1 = (bf16[256,256]{1,0:T(8,128)(2,1)S(1)}, bf16[256,256]{1,0:T(8,128)(2,1)S(1)}, bf16[128,512]{1,0:T(8,128)(2,1)S(1)}, bf16[2,128,128]{2,1,0:T(8,128)(2,1)S(1)}, bf16[2,128,128]{2,1,0:T(8,128)(2,1)S(1)}) custom-call(f32[256,256]{1,0:T(8,128)S(1)} %far_back.1.far, bf16[256,384]{1,0:T(8,128)(2,1)S(1)} %collective-permute-done.3.near, ...), custom_call_target="tpu_custom_call" | custom-call | flops 1000000000 | bytes 4000000 | tf_op jit(solution)/shard_map/block_backward/pallas_call | solution.py:448
  22.2 3.7 %collective-permute-start.7 = (bf16[560,128]{1,0:T(8,128)(2,1)S(1)}, bf16[560,128]{1,0:T(8,128)(2,1)S(1)}, u32[]{:S(2)}, u32[]{:S(2)}) collective-permute-start(bf16[560,128]{1,0:T(8,128)(2,1)S(1)} %pad_maximum_fusion), channel_id=1, source_target_pairs={{0,8},{2,10},{4,12},{6,14},{8,0},{10,2},{12,4},{14,6},{16,24},{18,... | collective-permute-start | bytes 430088 | tf_op jit(solution)/shard_map/ppermute | solution.py:436
  26.3 1.2 %collective-permute-start.8 = (bf16[560,128]{1,0:T(8,128)(2,1)S(1)}, bf16[560,128]{1,0:T(8,128)(2,1)S(1)}, u32[]{:S(2)}, u32[]{:S(2)}) collective-permute-start(bf16[560,128]{1,0:T(8,128)(2,1)S(1)} %pad_maximum_fusion.1), channel_id=1, source_target_pairs={{0,4},{2,6},{4,0},{6,2},{8,12},{10,14},{12,8},{14,10},{16,20},{18,... | collective-permute-start | bytes 430088 | tf_op jit(solution)/shard_map/ppermute | solution.py:436
  27.5 3.0 %collective-permute-done.7 = bf16[560,128]{1,0:T(8,128)(2,1)S(1)} collective-permute-done((bf16[560,128]{1,0:T(8,128)(2,1)S(1)}, bf16[560,128]{1,0:T(8,128)(2,1)S(1)}, u32[]{:S(2)}, u32[]{:S(2)}) %collective-permute-start.7) | collective-permute-done | bytes 143392 | tf_op jit(solution)/shard_map/ppermute | solution.py:436
  30.5 2.7 %collective-permute-done.9 = bf16[560,128]{1,0:T(8,128)(2,1)S(1)} collective-permute-done((bf16[560,128]{1,0:T(8,128)(2,1)S(1)}, bf16[560,128]{1,0:T(8,128)(2,1)S(1)}, u32[]{:S(2)}, u32[]{:S(2)}) %collective-permute-start.9) | collective-permute-done | bytes 143392 | tf_op jit(solution)/shard_map/ppermute | solution.py:436
  33.2 1.6 %collective-permute-done.8 = bf16[560,128]{1,0:T(8,128)(2,1)S(1)} collective-permute-done((bf16[560,128]{1,0:T(8,128)(2,1)S(1)}, bf16[560,128]{1,0:T(8,128)(2,1)S(1)}, u32[]{:S(2)}, u32[]{:S(2)}) %collective-permute-start.8) | collective-permute-done | bytes 143392 | tf_op jit(solution)/shard_map/ppermute | solution.py:436
  34.9 2.7 %collective-permute-start.10 = (bf16[560,128]{1,0:T(8,128)(2,1)S(1)}, bf16[560,128]{1,0:T(8,128)(2,1)S(1)}, u32[]{:S(2)}, u32[]{:S(2)}) collective-permute-start(bf16[560,128]{1,0:T(8,128)(2,1)S(1)} %add_convert_fusion.1), channel_id=1, source_target_pairs={{0,16},{2,18},{4,20},{6,22},{8,24},{10,26},{12,28},{14,30},{16,0},... | collective-permute-start | bytes 430088 | tf_op jit(solution)/shard_map/ppermute | solution.py:436
  37.6 1.0 %outputs.1 = (bf16[128,128]{1,0:T(8,128)(2,1)}, bf16[128,256]{1,0:T(8,128)(2,1)}) custom-call(bf16[256,256]{1,0:T(8,128)(2,1)S(1)} %get-tuple-element.64.near_mid, bf16[256,256]{1,0:T(8,128)(2,1)S(1)} %get-tuple-element.59.own_mid, bf16[256,256]{1,0:T(8,128)(2,1)S(1)} %get-tuple-element.50.mate_mid, bf16[128,512]{1,0:T(8,128)(2,1)S(1)} %get-tuple-element.65.grad_own, ...), custom_call_target="tpu_custom_call" | custom-call | flops 1000000000 | bytes 4000000 | tf_op jit(solution)/shard_map/outputs/pallas_call | solution.py:448
  38.6 5.1 %collective-permute-done.10 = bf16[560,128]{1,0:T(8,128)(2,1)S(1)} collective-permute-done((bf16[560,128]{1,0:T(8,128)(2,1)S(1)}, bf16[560,128]{1,0:T(8,128)(2,1)S(1)}, u32[]{:S(2)}, u32[]{:S(2)}) %collective-permute-start.10) | collective-permute-done | bytes 143392 | tf_op jit(solution)/shard_map/ppermute | solution.py:436
  43.7 1.9 %collective-permute-start.16 = (bf16[560,128]{1,0:T(8,128)(2,1)S(1)}, bf16[560,128]{1,0:T(8,128)(2,1)S(1)}, u32[]{:S(2)}, u32[]{:S(2)}) collective-permute-start(bf16[560,128]{1,0:T(8,128)(2,1)S(1)} %add_convert_fusion.refs_0_), channel_id=1, source_target_pairs={{0,5},{1,4},{2,7},{3,6},{4,1},{5,0},{6,3},{7,2},{8,13},{9,12},{10,... | collective-permute-start | bytes 430088 | tf_op jit(solution)/shard_map/ppermute | solution.py:565
  45.6 1.1 %collective-permute-start.14 = (bf16[560,128]{1,0:T(8,128)(2,1)S(1)}, bf16[560,128]{1,0:T(8,128)(2,1)S(1)}, u32[]{:S(2)}, u32[]{:S(2)}) collective-permute-start(bf16[560,128]{1,0:T(8,128)(2,1)S(1)} %add_convert_fusion.refs_0_), channel_id=1, source_target_pairs={{0,1},{1,0},{2,3},{3,2},{4,5},{5,4},{6,7},{7,6},{8,9},{9,8},{10,11... | collective-permute-start | bytes 430088 | tf_op jit(solution)/shard_map/ppermute | solution.py:439
  47.3 3.4 %collective-permute-done.16.refs_3_ = bf16[560,128]{1,0:T(8,128)(2,1)S(1)} collective-permute-done((bf16[560,128]{1,0:T(8,128)(2,1)S(1)}, bf16[560,128]{1,0:T(8,128)(2,1)S(1)}, u32[]{:S(2)}, u32[]{:S(2)}) %collective-permute-start.16) | collective-permute-done | bytes 143392 | tf_op jit(solution)/shard_map/ppermute | solution.py:565
  50.7 1.6 %collective-permute-done.14.refs_2_ = bf16[560,128]{1,0:T(8,128)(2,1)S(1)} collective-permute-done((bf16[560,128]{1,0:T(8,128)(2,1)S(1)}, bf16[560,128]{1,0:T(8,128)(2,1)S(1)}, u32[]{:S(2)}, u32[]{:S(2)}) %collective-permute-start.14) | collective-permute-done | bytes 143392 | tf_op jit(solution)/shard_map/ppermute | solution.py:439
  52.8 1.1 %unpack_sums.2 = (f32[256,512]{1,0:T(8,128)}, f32[3,3,256,128]{3,2,1,0:T(8,128)}, f32[3,3,128,128]{3,2,1,0:T(8,128)}) custom-call(bf16[560,128]{1,0:T(8,128)(2,1)S(1)} %add_convert_fusion.refs_0_, bf16[560,128]{1,0:T(8,128)(2,1)S(1)} %collective-permute-done.12.refs_1_, bf16[560,128]{1,0:T(8,128)(2,1)S(1)} %collective-permute-done.14.refs_2_, ...), custom_call_target="tpu_custom_call" | custom-call | flops 1000000000 | bytes 4194304 | tf_op jit(solution)/shard_map/unpack_sums/pallas_call | solution.py:403
  53.9 1.1 %unpack_sums.3 = (f32[256,512]{1,0:T(8,128)}, f32[3,3,256,128]{3,2,1,0:T(8,128)}, f32[3,3,128,128]{3,2,1,0:T(8,128)}) custom-call(bf16[560,128]{1,0:T(8,128)(2,1)S(1)} %collective-permute-done.11.refs_0_, bf16[560,128]{1,0:T(8,128)(2,1)S(1)} %collective-permute-done.13.refs_1_, ...), custom_call_target="tpu_custom_call", output_to_operand_aliasing={{0}: (4, {}), {1}: (5, {}), {2}: (6, {})} | custom-call | flops 1000000000 | bytes 4194304 | tf_op jit(solution)/shard_map/unpack_sums/pallas_call | solution.py:403
  (40 shorter events, 5.2 us)
Async XLA Ops:
  0.6 7.1 %collective-permute-start = (bf16[128,256]{1,0:T(8,128)(2,1)}, bf16[128,256]{1,0:T(8,128)(2,1)S(1)}, u32[]{:S(2)}, u32[]{:S(2)}) collective-permute-start(bf16[128,256]{1,0:T(8,128)(2,1)} %bitcast.8), channel_id=1, source_target_pairs={{0,1},{1,0},{2,3},{3,2},{4,5},{5,4},{6,7},{7,6},{8,9},{9,8},{10,11... | collective-permute-start | bytes 196616 | tf_op jit(solution)/shard_map/ppermute | solution.py:439
  3.6 4.1 %collective-permute-start.1 = (bf16[128,128]{1,0:T(8,128)(2,1)}, bf16[128,128]{1,0:T(8,128)(2,1)S(1)}, u32[]{:S(2)}, u32[]{:S(2)}) collective-permute-start(bf16[128,128]{1,0:T(8,128)(2,1)} %bitcast.10), channel_id=1, source_target_pairs={{0,1},{1,0},{2,3},{3,2},{4,5},{5,4},{6,7},{7,6},{8,9},{9,8},{10,11... | collective-permute-start | bytes 98312 | tf_op jit(solution)/shard_map/ppermute | solution.py:439
  3.7 0.9 %copy-start.2 = (bf16[256,512]{1,0:T(8,128)(2,1)S(1)}, bf16[256,512]{1,0:T(8,128)(2,1)}, u32[]{:S(2)}) copy-start(bf16[256,512]{1,0:T(8,128)(2,1)} %refs_0_.2) | copy-start | bytes 786436
  4.7 0.8 %copy-start.3 = (bf16[1,128,256]{2,1,0:T(8,128)(2,1)S(1)}, bf16[1,128,256]{2,1,0:T(8,128)(2,1)}, u32[]{:S(2)}) copy-start(bf16[1,128,256]{2,1,0:T(8,128)(2,1)} %param.5) | copy-start | bytes 196612
  5.5 0.8 %copy-start.4 = (bf16[1,128,128]{2,1,0:T(8,128)(2,1)S(1)}, bf16[1,128,128]{2,1,0:T(8,128)(2,1)}, u32[]{:S(2)}) copy-start(bf16[1,128,128]{2,1,0:T(8,128)(2,1)} %param.9) | copy-start | bytes 98308
  7.8 1.3 %copy-start = (bf16[3,3,256,128]{3,2,1,0:T(8,128)(2,1)S(1)}, bf16[3,3,256,128]{3,2,1,0:T(8,128)(2,1)}, u32[]{:S(2)}) copy-start(bf16[3,3,256,128]{3,2,1,0:T(8,128)(2,1)} %refs_0_.3) | copy-start | bytes 1769476
  9.1 2.3 %copy-start.1 = (bf16[3,3,128,128]{3,2,1,0:T(8,128)(2,1)S(1)}, bf16[3,3,128,128]{3,2,1,0:T(8,128)(2,1)}, u32[]{:S(2)}) copy-start(bf16[3,3,128,128]{3,2,1,0:T(8,128)(2,1)} %refs_1_.1) | copy-start | bytes 884740
  9.4 6.4 %collective-permute-start.2 = (bf16[256,384]{1,0:T(8,128)(2,1)S(1)}, bf16[256,384]{1,0:T(8,128)(2,1)S(1)}, u32[]{:S(2)}, u32[]{:S(2)}) collective-permute-start(bf16[256,384]{1,0:T(8,128)(2,1)S(1)} %get-tuple-element.45.own), channel_id=1, source_target_pairs={{4,0},{8,4},{12,8},{16,12},{20,16},{24,20},{28,24},{2,6},{6,10},{1... | collective-permute-start | bytes 589832 | tf_op jit(solution)/shard_map/ppermute | solution.py:485
  9.4 7.7 %collective-permute-start.5 = (bf16[256,256]{1,0:T(8,128)(2,1)S(1)}, bf16[256,256]{1,0:T(8,128)(2,1)S(1)}, u32[]{:S(2)}, u32[]{:S(2)}) collective-permute-start(bf16[256,256]{1,0:T(8,128)(2,1)S(1)} %far_term.1), channel_id=1, source_target_pairs={{0,4},{4,8},{8,12},{12,16},{16,20},{20,24},{24,28},{6,2},{10,6},{1... | collective-permute-start | bytes 393224 | tf_op jit(solution)/shard_map/ppermute | solution.py:486
  11.5 5.9 %collective-permute-start.4 = (bf16[256,384]{1,0:T(8,128)(2,1)S(1)}, bf16[256,384]{1,0:T(8,128)(2,1)S(1)}, u32[]{:S(2)}, u32[]{:S(2)}) collective-permute-start(bf16[256,384]{1,0:T(8,128)(2,1)S(1)} %get-tuple-element.45.own), channel_id=1, source_target_pairs={{0,2},{2,0},{4,6},{6,4},{8,10},{10,8},{12,14},{14,12},{16,18},{18,... | collective-permute-start | bytes 589832 | tf_op jit(solution)/shard_map/ppermute | solution.py:436
  15.8 2.5 %collective-permute-start.3 = (bf16[256,384]{1,0:T(8,128)(2,1)S(1)}, bf16[256,384]{1,0:T(8,128)(2,1)S(1)}, u32[]{:S(2)}, u32[]{:S(2)}) collective-permute-start(bf16[256,384]{1,0:T(8,128)(2,1)S(1)} %collective-permute-done.2.mate1), channel_id=1, source_target_pairs={{0,2},{2,0},{4,6},{6,4},{8,10},{10,8},{12,14},{14,12},{16,18},{18,... | collective-permute-start | bytes 589832 | tf_op jit(solution)/shard_map/ppermute | solution.py:436
  20.8 1.3 %collective-permute-start.6 = (bf16[2,128,128]{2,1,0:T(8,128)(2,1)S(1)}, bf16[2,128,128]{2,1,0:T(8,128)(2,1)S(1)}, u32[]{:S(2)}, u32[]{:S(2)}) collective-permute-start(bf16[2,128,128]{2,1,0:T(8,128)(2,1)S(1)} %get-tuple-element.62), channel_id=1, source_target_pairs={{0,2},{2,0},{4,6},{6,4},{8,10},{10,8},{12,14},{14,12},{16,18},{18,... | collective-permute-start | bytes 196616 | tf_op jit(solution)/shard_map/ppermute | solution.py:436
  22.2 8.3 %collective-permute-start.7 = (bf16[560,128]{1,0:T(8,128)(2,1)S(1)}, bf16[560,128]{1,0:T(8,128)(2,1)S(1)}, u32[]{:S(2)}, u32[]{:S(2)}) collective-permute-start(bf16[560,128]{1,0:T(8,128)(2,1)S(1)} %pad_maximum_fusion), channel_id=1, source_target_pairs={{0,8},{2,10},{4,12},{6,14},{8,0},{10,2},{12,4},{14,6},{16,24},{18,... | collective-permute-start | bytes 430088 | tf_op jit(solution)/shard_map/ppermute | solution.py:436
  26.0 7.2 %collective-permute-start.9 = (bf16[560,128]{1,0:T(8,128)(2,1)S(1)}, bf16[560,128]{1,0:T(8,128)(2,1)S(1)}, u32[]{:S(2)}, u32[]{:S(2)}) collective-permute-start(bf16[560,128]{1,0:T(8,128)(2,1)S(1)} %pad_maximum_fusion.1), channel_id=1, source_target_pairs={{0,12},{2,14},{4,8},{6,10},{8,4},{10,6},{12,0},{14,2},{16,28},{18,... | collective-permute-start | bytes 430088 | tf_op jit(solution)/shard_map/ppermute | solution.py:436
  26.3 8.5 %collective-permute-start.8 = (bf16[560,128]{1,0:T(8,128)(2,1)S(1)}, bf16[560,128]{1,0:T(8,128)(2,1)S(1)}, u32[]{:S(2)}, u32[]{:S(2)}) collective-permute-start(bf16[560,128]{1,0:T(8,128)(2,1)S(1)} %pad_maximum_fusion.1), channel_id=1, source_target_pairs={{0,4},{2,6},{4,0},{6,2},{8,12},{10,14},{12,8},{14,10},{16,20},{18,... | collective-permute-start | bytes 430088 | tf_op jit(solution)/shard_map/ppermute | solution.py:436
  34.9 8.8 %collective-permute-start.10 = (bf16[560,128]{1,0:T(8,128)(2,1)S(1)}, bf16[560,128]{1,0:T(8,128)(2,1)S(1)}, u32[]{:S(2)}, u32[]{:S(2)}) collective-permute-start(bf16[560,128]{1,0:T(8,128)(2,1)S(1)} %add_convert_fusion.1), channel_id=1, source_target_pairs={{0,16},{2,18},{4,20},{6,22},{8,24},{10,26},{12,28},{14,30},{16,0},... | collective-permute-start | bytes 430088 | tf_op jit(solution)/shard_map/ppermute | solution.py:436
  43.7 6.9 %collective-permute-start.16 = (bf16[560,128]{1,0:T(8,128)(2,1)S(1)}, bf16[560,128]{1,0:T(8,128)(2,1)S(1)}, u32[]{:S(2)}, u32[]{:S(2)}) collective-permute-start(bf16[560,128]{1,0:T(8,128)(2,1)S(1)} %add_convert_fusion.refs_0_), channel_id=1, source_target_pairs={{0,5},{1,4},{2,7},{3,6},{4,1},{5,0},{6,3},{7,2},{8,13},{9,12},{10,... | collective-permute-start | bytes 430088 | tf_op jit(solution)/shard_map/ppermute | solution.py:565
  45.6 6.7 %collective-permute-start.14 = (bf16[560,128]{1,0:T(8,128)(2,1)S(1)}, bf16[560,128]{1,0:T(8,128)(2,1)S(1)}, u32[]{:S(2)}, u32[]{:S(2)}) collective-permute-start(bf16[560,128]{1,0:T(8,128)(2,1)S(1)} %add_convert_fusion.refs_0_), channel_id=1, source_target_pairs={{0,1},{1,0},{2,3},{3,2},{4,5},{5,4},{6,7},{7,6},{8,9},{9,8},{10,11... | collective-permute-start | bytes 430088 | tf_op jit(solution)/shard_map/ppermute | solution.py:439
  46.7 5.6 %collective-permute-start.12 = (bf16[560,128]{1,0:T(8,128)(2,1)S(1)}, bf16[560,128]{1,0:T(8,128)(2,1)S(1)}, u32[]{:S(2)}, u32[]{:S(2)}) collective-permute-start(bf16[560,128]{1,0:T(8,128)(2,1)S(1)} %add_convert_fusion.refs_0_), channel_id=1, source_target_pairs={{0,4},{2,6},{4,0},{6,2},{8,12},{10,14},{12,8},{14,10},{16,20},{18,... | collective-permute-start | bytes 430088 | tf_op jit(solution)/shard_map/ppermute | solution.py:436
  47.3 6.6 %collective-permute-start.11 = (bf16[560,128]{1,0:T(8,128)(2,1)S(1)}, bf16[560,128]{1,0:T(8,128)(2,1)S(1)}, u32[]{:S(2)}, u32[]{:S(2)}) collective-permute-start(bf16[560,128]{1,0:T(8,128)(2,1)S(1)} %add_convert_fusion.refs_0_), channel_id=1, source_target_pairs={{0,2},{2,0},{4,6},{6,4},{8,10},{10,8},{12,14},{14,12},{16,18},{18,... | collective-permute-start | bytes 430088 | tf_op jit(solution)/shard_map/ppermute | solution.py:436
  50.7 3.3 %collective-permute-start.17 = (bf16[560,128]{1,0:T(8,128)(2,1)S(1)}, bf16[560,128]{1,0:T(8,128)(2,1)S(1)}, u32[]{:S(2)}, u32[]{:S(2)}) collective-permute-start(bf16[560,128]{1,0:T(8,128)(2,1)S(1)} %collective-permute-done.16.refs_3_), channel_id=1, source_target_pairs={{0,2},{2,0},{4,6},{6,4},{8,10},{10,8},{12,14},{14,12},{16,18},{18,... | collective-permute-start | bytes 430088 | tf_op jit(solution)/shard_map/ppermute | solution.py:436
  52.3 1.6 %collective-permute-start.15 = (bf16[560,128]{1,0:T(8,128)(2,1)S(1)}, bf16[560,128]{1,0:T(8,128)(2,1)S(1)}, u32[]{:S(2)}, u32[]{:S(2)}) collective-permute-start(bf16[560,128]{1,0:T(8,128)(2,1)S(1)} %collective-permute-done.14.refs_2_), channel_id=1, source_target_pairs={{0,2},{2,0},{4,6},{6,4},{8,10},{10,8},{12,14},{14,12},{16,18},{18,... | collective-permute-start | bytes 430088 | tf_op jit(solution)/shard_map/ppermute | solution.py:436
  52.3 1.6 %collective-permute-start.13 = (bf16[560,128]{1,0:T(8,128)(2,1)S(1)}, bf16[560,128]{1,0:T(8,128)(2,1)S(1)}, u32[]{:S(2)}, u32[]{:S(2)}) collective-permute-start(bf16[560,128]{1,0:T(8,128)(2,1)S(1)} %collective-permute-done.12.refs_1_), channel_id=1, source_target_pairs={{0,2},{2,0},{4,6},{6,4},{8,10},{10,8},{12,14},{14,12},{16,18},{18,... | collective-permute-start | bytes 430088 | tf_op jit(solution)/shard_map/ppermute | solution.py:436

commit v7 on v6

--- a/solution.py
+++ b/solution.py
@@ -91,21 +91,21 @@
     )(*arrays, *after)
 
 
-def forward_kernel(whole, *refs):
-    count = 1 if whole else 2
-    features = refs[:count]
-    cotangent = refs[count : 2 * count]
-    projection, comb, local, lse, values_t = refs[2 * count :]
-    across = comb.shape[0]
-    for which in range(count):
-        width = features[which].shape[0]
-        if whole:
-            at = pl.ds(0, width)
+def lay_out(pieces, target, lanes):
+    for which, piece in enumerate(pieces):
+        width = piece.shape[0]
+        if len(pieces) == 1:
+            at = slice(None)
         else:
             place = lax.rem(lax.axis_index("cols") + which, 2)
             at = pl.ds(pl.multiple_of(place * width, width), width)
-        local[at, PACKED:] = features[which][...]
-        comb[at, VAL:] = cotangent[which][...]
+        target[at, lanes] = piece[...]
+
+
+def forward_kernel(count, *refs):
+    projection, attended, local, lse, values_t = refs[count:]
+    across = attended.shape[0]
+    lay_out(refs[:count], local, slice(PACKED, None))
     packed = mm(local[:, PACKED:], projection[...]).astype(BF)
     local[:, :PACKED] = packed
     keys = packed[:, QK : 2 * QK]
@@ -124,7 +124,7 @@
             weighted = mm(values_t[head * HEAD_VAL : (head + 1) * HEAD_VAL, :], exponent.astype(BF))
             rows.append((weighted * (1.0 / totals)).astype(BF))
             lse[head : head + 1, at] = maxima * EXP2_SCALING + jnp.log2(totals)
-        comb[at, :VAL] = mm_t(identity(BLOCK), jnp.concatenate(rows, axis=0)).astype(BF)
+        attended[at, :] = mm_t(identity(BLOCK), jnp.concatenate(rows, axis=0)).astype(BF)
 
     for_blocks(across // BLOCK, block)
 
@@ -169,9 +169,12 @@
     )
 
 
-def far_term_kernel(own, first_kernel, term):
-    term[:, :CONV] = side(mm(own[:, :VAL], Place().beside(first_kernel, 0)), CONV, 1).astype(BF)
-    term[:, CONV:] = own[:, VAL:]
+def rows_kernel(count, *refs):
+    attended, first_kernel, row, term = refs[count:]
+    lay_out(refs[:count], row, slice(VAL, None))
+    lay_out(refs[:count], term, slice(CONV, None))
+    row[:, :VAL] = attended[...]
+    term[:, :CONV] = side(mm(attended[...], Place().beside(first_kernel, 0)), CONV, 1).astype(BF)
 
 
 def far_back_kernel(far, second_kernel, out):
@@ -180,13 +183,15 @@
     out[:, CONV:] = back
 
 
-def prepare_kernel(own, local, lse, soft, keys_t, queries_t, attended_t, features_t):
+def prepare_kernel(own, local, lse, soft, keys_t, queries_t, attended_t, features_t, values):
     place = Place()
     across = own.shape[0]
     keys = local[:, QK : 2 * QK]
     keys_t[...] = mm_t(identity(QK), keys).astype(BF)
     pick = jnp.concatenate([place.chosen(VAL, place.core), place.chosen(VAL, 1 - place.core)], axis=0)
     features_t[...] = mm_t(pick, local[:, PACKED:]).astype(BF)
+    for head in range(HEADS):
+        values[head * across : (head + 1) * across, :] = head_of(local[:, 2 * QK : PACKED], head, HEAD_VAL)
 
     def block(index):
         at = block_at(index)
@@ -272,7 +277,7 @@
     mate_mid,
     near_part,
     own_part,
-    local,
+    values,
     soft,
     keys_t,
     queries_t,
@@ -282,7 +287,7 @@
     second_kernel,
     near_mid,
     own_mid,
-    grad_own,
+    grad_out,
     proj_own,
     proj_mate,
     upstream_ref,
@@ -290,14 +295,12 @@
 ):
     place = Place()
     across = near.shape[0]
-    part_width = grad_own.shape[0]
     near = masked(place.near_inside, near[...])
     mids = (near_mid, own_mid, mate_mid)
     middle(place, far, near, near_part, own_part, first_kernel, second_kernel, near_mid, own_mid)
     upstream_ref[...] = side(
         sum(mm_t(mids[2 - a][:, CONV:], place.stacked(first_kernel, a)) for a in range(3)), VAL, -1
     ).astype(BF)
-    values = local[:, 2 * QK : PACKED]
     blocks = across // BLOCK
     if blocks > 1:
         grad_t[...] = jnp.zeros_like(grad_t)
@@ -314,7 +317,7 @@
         upstream_t = mm_t(identity(VAL), upstream)
         products = upstream_t * attended_t[:, at].astype(F32)
         upstream_t = upstream_t.astype(BF)
-        slopes = mm_t(jnp.concatenate([head_of(values, h, HEAD_VAL) for h in range(HEADS)], axis=0), upstream)
+        slopes = mm_t(values[...], upstream)
         for head in range(HEADS):
             rows = slice(head * across, (head + 1) * across)
             qk_rows = slice(head * HEAD_QK, (head + 1) * HEAD_QK)
@@ -329,6 +332,7 @@
     for_blocks(blocks, block)
 
     grad = grad_t[...].astype(BF)
+    grad_out[...] = grad
     step = VAL // PARTS
     total = mm_t(features_t[...], grad).astype(BF)
     for which, target in enumerate((proj_own, proj_mate)):
@@ -336,17 +340,16 @@
             for part in range(2):
                 begin = (2 * which + part) * step
                 target[part, j * step : (j + 1) * step, :] = total[begin : begin + step, j * CONV : (j + 1) * CONV]
-    own_pixels = one_hot((part_width, across), lambda rows: rows + place.col * part_width)
-    grad_own[...] = mm_t(own_pixels, grad).astype(BF)
-
-
-def outputs_kernel(near_mid, own_mid, mate_mid, grad_own, projection, second_kernel, output_map, input_grad, rows):
+
+
+def outputs_kernel(near_mid, own_mid, mate_mid, grad, projection, second_kernel, output_map, input_grad, rows):
     place = Place()
     part_width = output_map.shape[0]
     mids = (near_mid, own_mid, mate_mid)
     rows[...] = side(sum(mm(mids[a][:, :CONV], place.beside(second_kernel, a)) for a in range(3)), CONV, 1)
     output_map[...] = rows[pl.ds(pl.multiple_of(place.col * part_width, part_width), part_width), :].astype(BF)
-    input_grad[...] = mm_t(grad_own[...], projection[...]).astype(BF)
+    own_pixels = one_hot((part_width, rows.shape[0]), lambda pixels: pixels + place.col * part_width)
+    input_grad[...] = mm_t(mm_t(own_pixels, grad[...]).astype(BF), projection[...]).astype(BF)
 
 
 def unpack_kernel(factor, core_flip, *refs):
@@ -456,32 +459,34 @@
             **granted(across),
         )(*operands)
 
-    given = (features, cotangent)
-    projection, features, cotangent = fetch((projection, features[0], cotangent[0]))
+    features, cotangent = (features[0], cotangent[0])
     if cols_size == 2:
-        pieces = (features, cols_flip(given[0][0]), cotangent, cols_flip(given[1][0]))
+        swapped = cols_flip(features)
+        cotangent = (cotangent, cols_flip(cotangent))
+        projection, features = fetch((projection, features))
+        features = (features, swapped)
     else:
-        pieces = tuple(lax.all_gather(array[0], "cols", axis=0, tiled=True) for array in given)
-    own, local, lse = call(
-        functools.partial(forward_kernel, cols_size != 2),
-        (
-            shape(across, VAL + CONV),
-            shape(across, PACKED + channels),
-            shape(HEADS, across, dtype=F32),
-        ),
-        (*pieces, projection),
+        features, cotangent = (
+            (lax.all_gather(array, "cols", axis=0, tiled=True),) for array in (features, cotangent)
+        )
+    attended, local, lse = call(
+        functools.partial(forward_kernel, len(features)),
+        (shape(across, VAL), shape(across, PACKED + channels), shape(HEADS, across, dtype=F32)),
+        (*features, projection),
         (pltpu.VMEM((VAL, across), BF),),
         name="attention_forward",
     )
-
-    given_first = first_kernel
+    own, term = call(
+        functools.partial(rows_kernel, len(cotangent)),
+        (shape(across, VAL + CONV), shape(across, 2 * CONV)),
+        (*cotangent, attended, first_kernel),
+        name="rows",
+    )
     first_kernel, second_kernel = fetch((first_kernel, second_kernel), (lse,), 10**5)
     last = rows_size - 1
     out = [(i, i + 2) for i in range(0, last - 1, 2)] + [(i, i - 2) for i in range(3, rows_size, 2)]
     out += [(last - 1, last), (1, 0)]
     back = [(j, i) for i, j in out]
-    (term,) = call(far_term_kernel, (shape(across, 2 * CONV),), (own, given_first), name="far_term")
-    own, term = lax.optimization_barrier((own, term))
     mate1 = lax.ppermute(own, "rows", back)
     far = lax.ppermute(term, "rows", out)
     (far,) = call(
@@ -489,7 +494,7 @@
     )
     mate = rows_flip(own, 1)
     near = rows_flip(mate1, 1)
-    soft, keys_t, queries_t, attended_t, features_t = call(
+    soft, keys_t, queries_t, attended_t, features_t, values = call(
         prepare_kernel,
         (
             shape(HEADS * across, across),
@@ -497,6 +502,7 @@
             shape(QK, across),
             shape(VAL, across),
             shape(VAL // 2, across),
+            shape(HEADS * across, VAL),
         ),
         (own, local, lse),
         name="prepare",
@@ -508,12 +514,12 @@
         (own, mate, mate1, first_kernel, second_kernel),
         name="inner",
     )
-    near_mid, own_mid, grad_own, proj_own, proj_mate = call(
+    near_mid, own_mid, grad, proj_own, proj_mate = call(
         backward_kernel,
         (
             shape(across, 2 * CONV),
             shape(across, 2 * CONV),
-            shape(part_width, PACKED),
+            shape(PACKED, across),
             shape(2, PROJ_ROWS, CONV),
             shape(2, PROJ_ROWS, CONV),
         ),
@@ -523,7 +529,7 @@
             mate_mid,
             near_part,
             own_part,
-            local,
+            values,
             soft,
             keys_t,
             queries_t,
@@ -544,7 +550,7 @@
     output_map, input_grad = call(
         outputs_kernel,
         (shape(part_width, CONV), shape(part_width, channels)),
-        (near_mid, own_mid, mate_mid, grad_own, projection, second_kernel),
+        (near_mid, own_mid, mate_mid, grad, projection, second_kernel),
         (pltpu.VMEM((across, CONV), F32),),
         name="outputs",
     )

time: 55.3 us -> 53.8 us (0.973)
  waiting for transfers between devices: 24.1 us -> 23.3 us
  local copies, waits for them, and re-layouts: 2.56 us -> 1.81 us
    unnamed x10, local copies, waits for them, and re-layouts: 2.56 us -> 1.8 us
    ppermute x1, starting transfers between devices: 1.85 us -> 2.42 us  [body(): lax.ppermute(total, ('rows', 'cols'), [(i * cols_size + j, (i ^ 2) * cols...]
    ppermute x3, starting transfers between devices: 4.22 us -> 3.65 us  [cols_flip(): return lax.ppermute(values, 'cols', [(i, i ^ 1) for i in range(cols_size)])]
  transfers between devices with their start and end apart: 18 -> 18, of which waited for: 10 -> 11; matrix products, arithmetic and copies ran while one was open for 0% -> 0% of each run, Pallas kernels for 9% -> 12%
where the time goes in v7:
time: 53.8 us; the launch traced here: 53.6 us
  waiting for transfers between devices  23.3 us (43%)
  starting transfers between devices  17.4 us (32%)
  Pallas kernels  10.2 us (19%)
  local copies, waits for them, and re-layouts  1.81 us (3%)
  between operations  0.82 us (2%)
    ppermute x12, waiting for transfers between devices, rows_flip(): lax.ppermute(values, 'rows', [(i, i ^ bit) for i in range(rows_size)])  12.7 us
    ppermute x12, starting transfers between devices, rows_flip(): lax.ppermute(values, 'rows', [(i, i ^ bit) for i in range(rows_size)])  9.1 us
    pallas_call x8, Pallas kernels, call(): pl.pallas_call(kernel, out_shape=out_shape, in_specs=[VMEM] * len(operand...  7.7 us
    ppermute x3, starting transfers between devices, cols_flip(): return lax.ppermute(values, 'cols', [(i, i ^ 1) for i in range(cols_size)])  3.65 us
    ppermute x1, waiting for transfers between devices, body(): mate1 = lax.ppermute(own, 'rows', back)  3.41 us
    ppermute x1, waiting for transfers between devices, body(): lax.ppermute(total, ('rows', 'cols'), [(i * cols_size + j, (i ^ 2) * cols...  3.38 us
    ppermute x3, waiting for transfers between devices, cols_flip(): return lax.ppermute(values, 'cols', [(i, i ^ 1) for i in range(cols_size)])  2.44 us
    ppermute x1, starting transfers between devices, body(): lax.ppermute(total, ('rows', 'cols'), [(i * cols_size + j, (i ^ 2) * cols...  2.42 us
  transfers between devices with their start and end apart: 18, of which 11 were waited for; matrix products, arithmetic and copies ran while one was open for 0% of the time, Pallas kernels for 12%

profile of v7, /device:TPU:0, one launch (start us, length us, event | category | flops | bytes accessed | tf_op | source)
XLA Modules:
  0.0 53.6 jit_solution(11585499190624965231)
XLA Ops:
  0.6 3.0 %collective-permute-start.1 = (bf16[128,256]{1,0:T(8,128)(2,1)}, bf16[128,256]{1,0:T(8,128)(2,1)S(1)}, u32[]{:S(2)}, u32[]{:S(2)}) collective-permute-start(bf16[128,256]{1,0:T(8,128)(2,1)} %bitcast.8), channel_id=1, source_target_pairs={{0,1},{1,0},{2,3},{3,2},{4,5},{5,4},{6,7},{7,6},{8,9},{9,8},{10,11... | collective-permute-start | bytes 196616 | tf_op jit(solution)/shard_map/ppermute | solution.py:442
  3.7 0.9 %copy-done.2 = bf16[256,512]{1,0:T(8,128)(2,1)S(1)} copy-done((bf16[256,512]{1,0:T(8,128)(2,1)S(1)}, bf16[256,512]{1,0:T(8,128)(2,1)}, u32[]{:S(2)}) %copy-start.2) | copy-done | bytes 262168
  4.7 0.8 %copy-done.3 = bf16[1,128,256]{2,1,0:T(8,128)(2,1)S(1)} copy-done((bf16[1,128,256]{2,1,0:T(8,128)(2,1)S(1)}, bf16[1,128,256]{2,1,0:T(8,128)(2,1)}, u32[]{:S(2)}) %copy-start.3) | copy-done | bytes 65560
  5.6 0.6 %collective-permute-done.1.refs_1_ = bf16[128,256]{1,0:T(8,128)(2,1)S(1)} collective-permute-done((bf16[128,256]{1,0:T(8,128)(2,1)}, bf16[128,256]{1,0:T(8,128)(2,1)S(1)}, u32[]{:S(2)}, u32[]{:S(2)}) %collective-permute-start.1) | collective-permute-done | bytes 65568 | tf_op jit(solution)/shard_map/ppermute | solution.py:442
  6.2 1.3 %attention_forward.1 = (bf16[256,256]{1,0:T(8,128)(2,1)S(1)}, bf16[256,768]{1,0:T(8,128)(2,1)S(1)}, f32[8,256]{1,0:T(8,128)S(1)}) custom-call(bf16[128,256]{1,0:T(8,128)(2,1)S(1)} %get-tuple-element.41.refs_0_, bf16[128,256]{1,0:T(8,128)(2,1)S(1)} %collective-permute-done.1.refs_1_, bf16[256,512]{1,0:T(8,128)(2,1)S(1)} %get-tuple-element.42.refs_2_.projection), custom_call_target="tpu_custom_call" | custom-call | flops 1000000000 | bytes 4000000 | tf_op jit(solution)/shard_map/attention_forward/pallas_call | solution.py:451
  8.1 2.2 %collective-permute-start.5 = (bf16[256,256]{1,0:T(8,128)(2,1)S(1)}, bf16[256,256]{1,0:T(8,128)(2,1)S(1)}, u32[]{:S(2)}, u32[]{:S(2)}) collective-permute-start(bf16[256,256]{1,0:T(8,128)(2,1)S(1)} %get-tuple-element.45), channel_id=1, source_target_pairs={{0,4},{4,8},{8,12},{12,16},{16,20},{20,24},{24,28},{6,2},{10,6},{1... | collective-permute-start | bytes 393224 | tf_op jit(solution)/shard_map/ppermute | solution.py:491
  11.1 3.4 %collective-permute-done.2.mate1 = bf16[256,384]{1,0:T(8,128)(2,1)S(1)} collective-permute-done((bf16[256,384]{1,0:T(8,128)(2,1)S(1)}, bf16[256,384]{1,0:T(8,128)(2,1)S(1)}, u32[]{:S(2)}, u32[]{:S(2)}) %collective-permute-start.2) | collective-permute-done | bytes 196640 | tf_op jit(solution)/shard_map/ppermute | solution.py:490
  14.5 1.3 %collective-permute-done.5.far = bf16[256,256]{1,0:T(8,128)(2,1)S(1)} collective-permute-done((bf16[256,256]{1,0:T(8,128)(2,1)S(1)}, bf16[256,256]{1,0:T(8,128)(2,1)S(1)}, u32[]{:S(2)}, u32[]{:S(2)}) %collective-permute-start.5) | collective-permute-done | bytes 131104 | tf_op jit(solution)/shard_map/ppermute | solution.py:491
  16.1 0.9 %inner.1 = (bf16[256,256]{1,0:T(8,128)(2,1)S(1)}, f32[256,256]{1,0:T(8,128)S(1)}, f32[256,256]{1,0:T(8,128)S(1)}) custom-call(bf16[256,384]{1,0:T(8,128)(2,1)S(1)} %get-tuple-element.44.own, bf16[256,384]{1,0:T(8,128)(2,1)S(1)} %collective-permute-done.4.mate, bf16[256,384]{1,0:T(8,128)(2,1)S(1)} %collective-permute-done.2.mate1, ...), custom_call_target="tpu_custom_call" | custom-call | flops 1000000000 | bytes 4000000 | tf_op jit(solution)/shard_map/inner/pallas_call | solution.py:451
  17.0 2.4 %block_backward.1 = (bf16[256,256]{1,0:T(8,128)(2,1)S(1)}, bf16[256,256]{1,0:T(8,128)(2,1)S(1)}, bf16[512,256]{1,0:T(8,128)(2,1)S(1)}, bf16[2,128,128]{2,1,0:T(8,128)(2,1)S(1)}, bf16[2,128,128]{2,1,0:T(8,128)(2,1)S(1)}) custom-call(f32[256,256]{1,0:T(8,128)S(1)} %far_back.1.far, bf16[256,384]{1,0:T(8,128)(2,1)S(1)} %collective-permute-done.3.near, ...), custom_call_target="tpu_custom_call" | custom-call | flops 1000000000 | bytes 4000000 | tf_op jit(solution)/shard_map/block_backward/pallas_call | solution.py:451
  19.5 0.8 %conv_grads.1 = (bf16[432,128]{1,0:T(8,128)(2,1)S(1)}, bf16[432,128]{1,0:T(8,128)(2,1)S(1)}) custom-call(bf16[256,384]{1,0:T(8,128)(2,1)S(1)} %collective-permute-done.3.near, bf16[256,384]{1,0:T(8,128)(2,1)S(1)} %get-tuple-element.44.own, bf16[256,384]{1,0:T(8,128)(2,1)S(1)} %collective-permute-done.4.mate, ...), custom_call_target="tpu_custom_call" | custom-call | flops 1000000000 | bytes 4000000 | tf_op jit(solution)/shard_map/conv_grads/pallas_call | solution.py:451
  20.8 3.7 %collective-permute-start.7 = (bf16[560,128]{1,0:T(8,128)(2,1)S(1)}, bf16[560,128]{1,0:T(8,128)(2,1)S(1)}, u32[]{:S(2)}, u32[]{:S(2)}) collective-permute-start(bf16[560,128]{1,0:T(8,128)(2,1)S(1)} %pad_maximum_fusion), channel_id=1, source_target_pairs={{0,8},{2,10},{4,12},{6,14},{8,0},{10,2},{12,4},{14,6},{16,24},{18,... | collective-permute-start | bytes 430088 | tf_op jit(solution)/shard_map/ppermute | solution.py:439
  24.9 1.2 %collective-permute-start.8 = (bf16[560,128]{1,0:T(8,128)(2,1)S(1)}, bf16[560,128]{1,0:T(8,128)(2,1)S(1)}, u32[]{:S(2)}, u32[]{:S(2)}) collective-permute-start(bf16[560,128]{1,0:T(8,128)(2,1)S(1)} %pad_maximum_fusion.1), channel_id=1, source_target_pairs={{0,4},{2,6},{4,0},{6,2},{8,12},{10,14},{12,8},{14,10},{16,20},{18,... | collective-permute-start | bytes 430088 | tf_op jit(solution)/shard_map/ppermute | solution.py:439
  26.1 3.0 %collective-permute-done.7 = bf16[560,128]{1,0:T(8,128)(2,1)S(1)} collective-permute-done((bf16[560,128]{1,0:T(8,128)(2,1)S(1)}, bf16[560,128]{1,0:T(8,128)(2,1)S(1)}, u32[]{:S(2)}, u32[]{:S(2)}) %collective-permute-start.7) | collective-permute-done | bytes 143392 | tf_op jit(solution)/shard_map/ppermute | solution.py:439
  29.1 2.7 %collective-permute-done.9 = bf16[560,128]{1,0:T(8,128)(2,1)S(1)} collective-permute-done((bf16[560,128]{1,0:T(8,128)(2,1)S(1)}, bf16[560,128]{1,0:T(8,128)(2,1)S(1)}, u32[]{:S(2)}, u32[]{:S(2)}) %collective-permute-start.9) | collective-permute-done | bytes 143392 | tf_op jit(solution)/shard_map/ppermute | solution.py:439
  31.8 1.6 %collective-permute-done.8 = bf16[560,128]{1,0:T(8,128)(2,1)S(1)} collective-permute-done((bf16[560,128]{1,0:T(8,128)(2,1)S(1)}, bf16[560,128]{1,0:T(8,128)(2,1)S(1)}, u32[]{:S(2)}, u32[]{:S(2)}) %collective-permute-start.8) | collective-permute-done | bytes 143392 | tf_op jit(solution)/shard_map/ppermute | solution.py:439
  33.5 2.7 %collective-permute-start.10 = (bf16[560,128]{1,0:T(8,128)(2,1)S(1)}, bf16[560,128]{1,0:T(8,128)(2,1)S(1)}, u32[]{:S(2)}, u32[]{:S(2)}) collective-permute-start(bf16[560,128]{1,0:T(8,128)(2,1)S(1)} %add_convert_fusion.1), channel_id=1, source_target_pairs={{0,16},{2,18},{4,20},{6,22},{8,24},{10,26},{12,28},{14,30},{16,0},... | collective-permute-start | bytes 430088 | tf_op jit(solution)/shard_map/ppermute | solution.py:439
  36.2 1.2 %outputs.1 = (bf16[128,128]{1,0:T(8,128)(2,1)}, bf16[128,256]{1,0:T(8,128)(2,1)}) custom-call(bf16[256,256]{1,0:T(8,128)(2,1)S(1)} %get-tuple-element.64.near_mid, bf16[256,256]{1,0:T(8,128)(2,1)S(1)} %get-tuple-element.59.own_mid, bf16[256,256]{1,0:T(8,128)(2,1)S(1)} %get-tuple-element.49.mate_mid, bf16[512,256]{1,0:T(8,128)(2,1)S(1)} %get-tuple-element.65.grad, ...), custom_call_target="tpu_custom_call" | custom-call | flops 1000000000 | bytes 4000000 | tf_op jit(solution)/shard_map/outputs/pallas_call | solution.py:451
  37.3 4.9 %collective-permute-done.10 = bf16[560,128]{1,0:T(8,128)(2,1)S(1)} collective-permute-done((bf16[560,128]{1,0:T(8,128)(2,1)S(1)}, bf16[560,128]{1,0:T(8,128)(2,1)S(1)}, u32[]{:S(2)}, u32[]{:S(2)}) %collective-permute-start.10) | collective-permute-done | bytes 143392 | tf_op jit(solution)/shard_map/ppermute | solution.py:439
  42.3 2.4 %collective-permute-start.16 = (bf16[560,128]{1,0:T(8,128)(2,1)S(1)}, bf16[560,128]{1,0:T(8,128)(2,1)S(1)}, u32[]{:S(2)}, u32[]{:S(2)}) collective-permute-start(bf16[560,128]{1,0:T(8,128)(2,1)S(1)} %add_convert_fusion.refs_0_), channel_id=1, source_target_pairs={{0,5},{1,4},{2,7},{3,6},{4,1},{5,0},{6,3},{7,2},{8,13},{9,12},{10,... | collective-permute-start | bytes 430088 | tf_op jit(solution)/shard_map/ppermute | solution.py:571
  45.9 3.4 %collective-permute-done.16.refs_3_ = bf16[560,128]{1,0:T(8,128)(2,1)S(1)} collective-permute-done((bf16[560,128]{1,0:T(8,128)(2,1)S(1)}, bf16[560,128]{1,0:T(8,128)(2,1)S(1)}, u32[]{:S(2)}, u32[]{:S(2)}) %collective-permute-start.16) | collective-permute-done | bytes 143392 | tf_op jit(solution)/shard_map/ppermute | solution.py:571
  49.2 1.7 %collective-permute-done.14.refs_2_ = bf16[560,128]{1,0:T(8,128)(2,1)S(1)} collective-permute-done((bf16[560,128]{1,0:T(8,128)(2,1)S(1)}, bf16[560,128]{1,0:T(8,128)(2,1)S(1)}, u32[]{:S(2)}, u32[]{:S(2)}) %collective-permute-start.14) | collective-permute-done | bytes 143392 | tf_op jit(solution)/shard_map/ppermute | solution.py:442
  51.4 1.1 %unpack_sums.2 = (f32[256,512]{1,0:T(8,128)}, f32[3,3,256,128]{3,2,1,0:T(8,128)}, f32[3,3,128,128]{3,2,1,0:T(8,128)}) custom-call(bf16[560,128]{1,0:T(8,128)(2,1)S(1)} %add_convert_fusion.refs_0_, bf16[560,128]{1,0:T(8,128)(2,1)S(1)} %collective-permute-done.12.refs_1_, bf16[560,128]{1,0:T(8,128)(2,1)S(1)} %collective-permute-done.14.refs_2_, ...), custom_call_target="tpu_custom_call" | custom-call | flops 1000000000 | bytes 4194304 | tf_op jit(solution)/shard_map/unpack_sums/pallas_call | solution.py:406
  52.5 1.1 %unpack_sums.3 = (f32[256,512]{1,0:T(8,128)}, f32[3,3,256,128]{3,2,1,0:T(8,128)}, f32[3,3,128,128]{3,2,1,0:T(8,128)}) custom-call(bf16[560,128]{1,0:T(8,128)(2,1)S(1)} %collective-permute-done.11.refs_0_, bf16[560,128]{1,0:T(8,128)(2,1)S(1)} %collective-permute-done.13.refs_1_, ...), custom_call_target="tpu_custom_call", output_to_operand_aliasing={{0}: (4, {}), {1}: (5, {}), {2}: (6, {})} | custom-call | flops 1000000000 | bytes 4194304 | tf_op jit(solution)/shard_map/unpack_sums/pallas_call | solution.py:406
  (40 shorter events, 4.4 us)
Async XLA Ops:
  0.6 5.6 %collective-permute-start.1 = (bf16[128,256]{1,0:T(8,128)(2,1)}, bf16[128,256]{1,0:T(8,128)(2,1)S(1)}, u32[]{:S(2)}, u32[]{:S(2)}) collective-permute-start(bf16[128,256]{1,0:T(8,128)(2,1)} %bitcast.8), channel_id=1, source_target_pairs={{0,1},{1,0},{2,3},{3,2},{4,5},{5,4},{6,7},{7,6},{8,9},{9,8},{10,11... | collective-permute-start | bytes 196616 | tf_op jit(solution)/shard_map/ppermute | solution.py:442
  3.6 4.1 %collective-permute-start = (bf16[128,128]{1,0:T(8,128)(2,1)}, bf16[128,128]{1,0:T(8,128)(2,1)S(1)}, u32[]{:S(2)}, u32[]{:S(2)}) collective-permute-start(bf16[128,128]{1,0:T(8,128)(2,1)} %bitcast.10), channel_id=1, source_target_pairs={{0,1},{1,0},{2,3},{3,2},{4,5},{5,4},{6,7},{7,6},{8,9},{9,8},{10,11... | collective-permute-start | bytes 98312 | tf_op jit(solution)/shard_map/ppermute | solution.py:442
  3.7 0.9 %copy-start.2 = (bf16[256,512]{1,0:T(8,128)(2,1)S(1)}, bf16[256,512]{1,0:T(8,128)(2,1)}, u32[]{:S(2)}) copy-start(bf16[256,512]{1,0:T(8,128)(2,1)} %refs_0_.2) | copy-start | bytes 786436
  4.7 0.8 %copy-start.3 = (bf16[1,128,256]{2,1,0:T(8,128)(2,1)S(1)}, bf16[1,128,256]{2,1,0:T(8,128)(2,1)}, u32[]{:S(2)}) copy-start(bf16[1,128,256]{2,1,0:T(8,128)(2,1)} %param.5) | copy-start | bytes 196612
  6.2 1.5 %copy-start = (bf16[3,3,256,128]{3,2,1,0:T(8,128)(2,1)S(1)}, bf16[3,3,256,128]{3,2,1,0:T(8,128)(2,1)}, u32[]{:S(2)}) copy-start(bf16[3,3,256,128]{3,2,1,0:T(8,128)(2,1)} %refs_0_.3) | copy-start | bytes 1769476
  6.2 1.5 %copy-start.4 = (bf16[1,128,128]{2,1,0:T(8,128)(2,1)S(1)}, bf16[1,128,128]{2,1,0:T(8,128)(2,1)}, u32[]{:S(2)}) copy-start(bf16[1,128,128]{2,1,0:T(8,128)(2,1)} %param.9) | copy-start | bytes 98308
  7.8 2.5 %copy-start.1 = (bf16[3,3,128,128]{3,2,1,0:T(8,128)(2,1)S(1)}, bf16[3,3,128,128]{3,2,1,0:T(8,128)(2,1)}, u32[]{:S(2)}) copy-start(bf16[3,3,128,128]{3,2,1,0:T(8,128)(2,1)} %refs_1_.1) | copy-start | bytes 884740
  8.0 6.4 %collective-permute-start.2 = (bf16[256,384]{1,0:T(8,128)(2,1)S(1)}, bf16[256,384]{1,0:T(8,128)(2,1)S(1)}, u32[]{:S(2)}, u32[]{:S(2)}) collective-permute-start(bf16[256,384]{1,0:T(8,128)(2,1)S(1)} %get-tuple-element.44.own), channel_id=1, source_target_pairs={{4,0},{8,4},{12,8},{16,12},{20,16},{24,20},{28,24},{2,6},{6,10},{1... | collective-permute-start | bytes 589832 | tf_op jit(solution)/shard_map/ppermute | solution.py:490
  8.1 7.7 %collective-permute-start.5 = (bf16[256,256]{1,0:T(8,128)(2,1)S(1)}, bf16[256,256]{1,0:T(8,128)(2,1)S(1)}, u32[]{:S(2)}, u32[]{:S(2)}) collective-permute-start(bf16[256,256]{1,0:T(8,128)(2,1)S(1)} %get-tuple-element.45), channel_id=1, source_target_pairs={{0,4},{4,8},{8,12},{12,16},{16,20},{20,24},{24,28},{6,2},{10,6},{1... | collective-permute-start | bytes 393224 | tf_op jit(solution)/shard_map/ppermute | solution.py:491
  10.3 5.8 %collective-permute-start.4 = (bf16[256,384]{1,0:T(8,128)(2,1)S(1)}, bf16[256,384]{1,0:T(8,128)(2,1)S(1)}, u32[]{:S(2)}, u32[]{:S(2)}) collective-permute-start(bf16[256,384]{1,0:T(8,128)(2,1)S(1)} %get-tuple-element.44.own), channel_id=1, source_target_pairs={{0,2},{2,0},{4,6},{6,4},{8,10},{10,8},{12,14},{14,12},{16,18},{18,... | collective-permute-start | bytes 589832 | tf_op jit(solution)/shard_map/ppermute | solution.py:439
  14.5 2.5 %collective-permute-start.3 = (bf16[256,384]{1,0:T(8,128)(2,1)S(1)}, bf16[256,384]{1,0:T(8,128)(2,1)S(1)}, u32[]{:S(2)}, u32[]{:S(2)}) collective-permute-start(bf16[256,384]{1,0:T(8,128)(2,1)S(1)} %collective-permute-done.2.mate1), channel_id=1, source_target_pairs={{0,2},{2,0},{4,6},{6,4},{8,10},{10,8},{12,14},{14,12},{16,18},{18,... | collective-permute-start | bytes 589832 | tf_op jit(solution)/shard_map/ppermute | solution.py:439
  19.4 1.3 %collective-permute-start.6 = (bf16[2,128,128]{2,1,0:T(8,128)(2,1)S(1)}, bf16[2,128,128]{2,1,0:T(8,128)(2,1)S(1)}, u32[]{:S(2)}, u32[]{:S(2)}) collective-permute-start(bf16[2,128,128]{2,1,0:T(8,128)(2,1)S(1)} %get-tuple-element.62), channel_id=1, source_target_pairs={{0,2},{2,0},{4,6},{6,4},{8,10},{10,8},{12,14},{14,12},{16,18},{18,... | collective-permute-start | bytes 196616 | tf_op jit(solution)/shard_map/ppermute | solution.py:439
  20.8 8.3 %collective-permute-start.7 = (bf16[560,128]{1,0:T(8,128)(2,1)S(1)}, bf16[560,128]{1,0:T(8,128)(2,1)S(1)}, u32[]{:S(2)}, u32[]{:S(2)}) collective-permute-start(bf16[560,128]{1,0:T(8,128)(2,1)S(1)} %pad_maximum_fusion), channel_id=1, source_target_pairs={{0,8},{2,10},{4,12},{6,14},{8,0},{10,2},{12,4},{14,6},{16,24},{18,... | collective-permute-start | bytes 430088 | tf_op jit(solution)/shard_map/ppermute | solution.py:439
  24.6 7.2 %collective-permute-start.9 = (bf16[560,128]{1,0:T(8,128)(2,1)S(1)}, bf16[560,128]{1,0:T(8,128)(2,1)S(1)}, u32[]{:S(2)}, u32[]{:S(2)}) collective-permute-start(bf16[560,128]{1,0:T(8,128)(2,1)S(1)} %pad_maximum_fusion.1), channel_id=1, source_target_pairs={{0,12},{2,14},{4,8},{6,10},{8,4},{10,6},{12,0},{14,2},{16,28},{18,... | collective-permute-start | bytes 430088 | tf_op jit(solution)/shard_map/ppermute | solution.py:439
  24.9 8.5 %collective-permute-start.8 = (bf16[560,128]{1,0:T(8,128)(2,1)S(1)}, bf16[560,128]{1,0:T(8,128)(2,1)S(1)}, u32[]{:S(2)}, u32[]{:S(2)}) collective-permute-start(bf16[560,128]{1,0:T(8,128)(2,1)S(1)} %pad_maximum_fusion.1), channel_id=1, source_target_pairs={{0,4},{2,6},{4,0},{6,2},{8,12},{10,14},{12,8},{14,10},{16,20},{18,... | collective-permute-start | bytes 430088 | tf_op jit(solution)/shard_map/ppermute | solution.py:439
  33.5 8.8 %collective-permute-start.10 = (bf16[560,128]{1,0:T(8,128)(2,1)S(1)}, bf16[560,128]{1,0:T(8,128)(2,1)S(1)}, u32[]{:S(2)}, u32[]{:S(2)}) collective-permute-start(bf16[560,128]{1,0:T(8,128)(2,1)S(1)} %add_convert_fusion.1), channel_id=1, source_target_pairs={{0,16},{2,18},{4,20},{6,22},{8,24},{10,26},{12,28},{14,30},{16,0},... | collective-permute-start | bytes 430088 | tf_op jit(solution)/shard_map/ppermute | solution.py:439
  42.3 6.9 %collective-permute-start.16 = (bf16[560,128]{1,0:T(8,128)(2,1)S(1)}, bf16[560,128]{1,0:T(8,128)(2,1)S(1)}, u32[]{:S(2)}, u32[]{:S(2)}) collective-permute-start(bf16[560,128]{1,0:T(8,128)(2,1)S(1)} %add_convert_fusion.refs_0_), channel_id=1, source_target_pairs={{0,5},{1,4},{2,7},{3,6},{4,1},{5,0},{6,3},{7,2},{8,13},{9,12},{10,... | collective-permute-start | bytes 430088 | tf_op jit(solution)/shard_map/ppermute | solution.py:571
  44.7 6.2 %collective-permute-start.14 = (bf16[560,128]{1,0:T(8,128)(2,1)S(1)}, bf16[560,128]{1,0:T(8,128)(2,1)S(1)}, u32[]{:S(2)}, u32[]{:S(2)}) collective-permute-start(bf16[560,128]{1,0:T(8,128)(2,1)S(1)} %add_convert_fusion.refs_0_), channel_id=1, source_target_pairs={{0,1},{1,0},{2,3},{3,2},{4,5},{5,4},{6,7},{7,6},{8,9},{9,8},{10,11... | collective-permute-start | bytes 430088 | tf_op jit(solution)/shard_map/ppermute | solution.py:442
  45.3 5.6 %collective-permute-start.12 = (bf16[560,128]{1,0:T(8,128)(2,1)S(1)}, bf16[560,128]{1,0:T(8,128)(2,1)S(1)}, u32[]{:S(2)}, u32[]{:S(2)}) collective-permute-start(bf16[560,128]{1,0:T(8,128)(2,1)S(1)} %add_convert_fusion.refs_0_), channel_id=1, source_target_pairs={{0,4},{2,6},{4,0},{6,2},{8,12},{10,14},{12,8},{14,10},{16,20},{18,... | collective-permute-start | bytes 430088 | tf_op jit(solution)/shard_map/ppermute | solution.py:439
  45.9 6.6 %collective-permute-start.11 = (bf16[560,128]{1,0:T(8,128)(2,1)S(1)}, bf16[560,128]{1,0:T(8,128)(2,1)S(1)}, u32[]{:S(2)}, u32[]{:S(2)}) collective-permute-start(bf16[560,128]{1,0:T(8,128)(2,1)S(1)} %add_convert_fusion.refs_0_), channel_id=1, source_target_pairs={{0,2},{2,0},{4,6},{6,4},{8,10},{10,8},{12,14},{14,12},{16,18},{18,... | collective-permute-start | bytes 430088 | tf_op jit(solution)/shard_map/ppermute | solution.py:439
  49.2 3.3 %collective-permute-start.17 = (bf16[560,128]{1,0:T(8,128)(2,1)S(1)}, bf16[560,128]{1,0:T(8,128)(2,1)S(1)}, u32[]{:S(2)}, u32[]{:S(2)}) collective-permute-start(bf16[560,128]{1,0:T(8,128)(2,1)S(1)} %collective-permute-done.16.refs_3_), channel_id=1, source_target_pairs={{0,2},{2,0},{4,6},{6,4},{8,10},{10,8},{12,14},{14,12},{16,18},{18,... | collective-permute-start | bytes 430088 | tf_op jit(solution)/shard_map/ppermute | solution.py:439
  50.9 1.6 %collective-permute-start.15 = (bf16[560,128]{1,0:T(8,128)(2,1)S(1)}, bf16[560,128]{1,0:T(8,128)(2,1)S(1)}, u32[]{:S(2)}, u32[]{:S(2)}) collective-permute-start(bf16[560,128]{1,0:T(8,128)(2,1)S(1)} %collective-permute-done.14.refs_2_), channel_id=1, source_target_pairs={{0,2},{2,0},{4,6},{6,4},{8,10},{10,8},{12,14},{14,12},{16,18},{18,... | collective-permute-start | bytes 430088 | tf_op jit(solution)/shard_map/ppermute | solution.py:439
  50.9 1.6 %collective-permute-start.13 = (bf16[560,128]{1,0:T(8,128)(2,1)S(1)}, bf16[560,128]{1,0:T(8,128)(2,1)S(1)}, u32[]{:S(2)}, u32[]{:S(2)}) collective-permute-start(bf16[560,128]{1,0:T(8,128)(2,1)S(1)} %collective-permute-done.12.refs_1_), channel_id=1, source_target_pairs={{0,2},{2,0},{4,6},{6,4},{8,10},{10,8},{12,14},{14,12},{16,18},{18,... | collective-permute-start | bytes 430088 | tf_op jit(solution)/shard_map/ppermute | solution.py:439

commit v8 on v7

--- a/solution.py
+++ b/solution.py
@@ -177,10 +177,18 @@
     term[:, :CONV] = side(mm(attended[...], Place().beside(first_kernel, 0)), CONV, 1).astype(BF)
 
 
-def far_back_kernel(far, second_kernel, out):
-    back = side(mm_t(far[:, CONV:], Place().stacked(second_kernel, 2)), CONV, -1)
+def far_back_kernel(far, second_t, out):
+    back = side(mm(far[:, CONV:], second_t[2]), CONV, -1)
     out[:, :CONV] = far[:, :CONV].astype(F32)
     out[:, CONV:] = back
+
+
+def turn_kernel(first_kernel, second_kernel, first_t, second_t):
+    place = Place()
+    eye = identity(CONV)
+    for a in range(3):
+        first_t[a * CONV : (a + 1) * CONV, :] = mm_t(eye, place.stacked(first_kernel, a)).astype(BF)
+        second_t[a] = mm_t(eye, place.stacked(second_kernel, a)).astype(BF)
 
 
 def prepare_kernel(own, local, lse, soft, keys_t, queries_t, attended_t, features_t, values):
@@ -214,8 +222,8 @@
     return side(mm(row[:, :VAL], place.beside(kernel, tap)), CONV, 1)
 
 
-def back_term(place, row, kernel, tap):
-    return side(mm_t(row[:, VAL:], place.stacked(kernel, tap)), CONV, -1)
+def back_term(row, second_t, tap):
+    return side(mm(row[:, VAL:], second_t[tap]), CONV, -1)
 
 
 def store_middle(pre, back, out):
@@ -224,25 +232,25 @@
     out[:, CONV:] = (back * (sigma * (1.0 + pre * (1.0 - sigma)))).astype(BF)
 
 
-def inner_kernel(own, mate, mate1, first_kernel, second_kernel, mate_mid, near_part, own_part):
+def inner_kernel(own, mate, mate1, first_kernel, second_t, mate_mid, near_part, own_part):
     place = Place()
     mate1 = masked(place.mate_inside, mate1[...])
     near_part[:, :CONV] = conv_term(place, own, first_kernel, 2)
-    near_part[:, CONV:] = back_term(place, own, second_kernel, 0)
+    near_part[:, CONV:] = back_term(own, second_t, 0)
     own_part[:, :CONV] = conv_term(place, own, first_kernel, 1) + conv_term(place, mate, first_kernel, 2)
-    own_part[:, CONV:] = back_term(place, own, second_kernel, 1) + back_term(place, mate, second_kernel, 0)
+    own_part[:, CONV:] = back_term(own, second_t, 1) + back_term(mate, second_t, 0)
     rows = (own, mate, mate1)
     pre = sum(conv_term(place, row, first_kernel, a) for a, row in enumerate(rows))
-    back = sum(back_term(place, row, second_kernel, 2 - a) for a, row in enumerate(rows))
+    back = sum(back_term(row, second_t, 2 - a) for a, row in enumerate(rows))
     store_middle(pre, back, mate_mid)
 
 
-def middle(place, far, near, near_part, own_part, first_kernel, second_kernel, near_mid, own_mid):
+def middle(place, far, near, near_part, own_part, first_kernel, second_t, near_mid, own_mid):
     pre = near_part[:, :CONV] + far[:, :CONV] + conv_term(place, near, first_kernel, 1)
-    back = near_part[:, CONV:] + far[:, CONV:] + back_term(place, near, second_kernel, 1)
+    back = near_part[:, CONV:] + far[:, CONV:] + back_term(near, second_t, 1)
     store_middle(masked(place.near_inside, pre), masked(place.near_inside, back), near_mid)
     pre = own_part[:, :CONV] + conv_term(place, near, first_kernel, 0)
-    back = own_part[:, CONV:] + back_term(place, near, second_kernel, 2)
+    back = own_part[:, CONV:] + back_term(near, second_t, 2)
     store_middle(pre, back, own_mid)
 
 
@@ -284,7 +292,8 @@
     attended_t,
     features_t,
     first_kernel,
-    second_kernel,
+    first_t,
+    second_t,
     near_mid,
     own_mid,
     grad_out,
@@ -297,10 +306,9 @@
     across = near.shape[0]
     near = masked(place.near_inside, near[...])
     mids = (near_mid, own_mid, mate_mid)
-    middle(place, far, near, near_part, own_part, first_kernel, second_kernel, near_mid, own_mid)
-    upstream_ref[...] = side(
-        sum(mm_t(mids[2 - a][:, CONV:], place.stacked(first_kernel, a)) for a in range(3)), VAL, -1
-    ).astype(BF)
+    middle(place, far, near, near_part, own_part, first_kernel, second_t, near_mid, own_mid)
+    slopes_beside = jnp.concatenate([mids[2 - a][:, CONV:] for a in range(3)], axis=1)
+    upstream_ref[...] = side(mm(slopes_beside, first_t[...]), VAL, -1).astype(BF)
     blocks = across // BLOCK
     if blocks > 1:
         grad_t[...] = jnp.zeros_like(grad_t)
@@ -487,10 +495,17 @@
     out = [(i, i + 2) for i in range(0, last - 1, 2)] + [(i, i - 2) for i in range(3, rows_size, 2)]
     out += [(last - 1, last), (1, 0)]
     back = [(j, i) for i, j in out]
+    first_t, second_t = call(
+        turn_kernel,
+        (shape(3 * CONV, 3 * VAL), shape(3, CONV, 3 * CONV)),
+        (first_kernel, second_kernel),
+        name="turn",
+        flops=10**7,
+    )
     mate1 = lax.ppermute(own, "rows", back)
     far = lax.ppermute(term, "rows", out)
     (far,) = call(
-        far_back_kernel, (shape(across, 2 * CONV, dtype=F32),), (far, second_kernel), name="far_back", flops=4 * 10**9
+        far_back_kernel, (shape(across, 2 * CONV, dtype=F32),), (far, second_t), name="far_back", flops=4 * 10**9
     )
     mate = rows_flip(own, 1)
     near = rows_flip(mate1, 1)
@@ -511,7 +526,7 @@
     mate_mid, near_part, own_part = call(
         inner_kernel,
         (shape(across, 2 * CONV), shape(across, 2 * CONV, dtype=F32), shape(across, 2 * CONV, dtype=F32)),
-        (own, mate, mate1, first_kernel, second_kernel),
+        (own, mate, mate1, first_kernel, second_t),
         name="inner",
     )
     near_mid, own_mid, grad, proj_own, proj_mate = call(
@@ -536,7 +551,8 @@
             attended_t,
             features_t,
             first_kernel,
-            second_kernel,
+            first_t,
+            second_t,
         ),
         (pltpu.VMEM((across, VAL), BF), pltpu.VMEM((PACKED, across), F32)),
         name="block_backward",

time: 53.8 us -> 53.6 us (level)
    pallas_call x8 -> x9, Pallas kernels: 7.7 us -> 7.98 us  [call(): pl.pallas_call(kernel, out_shape=out_shape, in_specs=[VMEM] * len(operand...]
  transfers between devices with their start and end apart: 18 -> 18, of which waited for: 11 -> 11; matrix products, arithmetic and copies ran while one was open for 0% -> 0% of each run, Pallas kernels for 12% -> 13%
where the time goes in v8:
time: 53.6 us; the launch traced here: 53.5 us
  waiting for transfers between devices  22.8 us (43%)
  starting transfers between devices  17.4 us (32%)
  Pallas kernels  10.5 us (20%)
  local copies, waits for them, and re-layouts  1.81 us (3%)
  between operations  0.83 us (2%)
    ppermute x12, waiting for transfers between devices, rows_flip(): lax.ppermute(values, 'rows', [(i, i ^ bit) for i in range(rows_size)])  12.6 us
    ppermute x12, starting transfers between devices, rows_flip(): lax.ppermute(values, 'rows', [(i, i ^ bit) for i in range(rows_size)])  9.12 us
    pallas_call x9, Pallas kernels, call(): pl.pallas_call(kernel, out_shape=out_shape, in_specs=[VMEM] * len(operand...  7.98 us
    ppermute x3, starting transfers between devices, cols_flip(): return lax.ppermute(values, 'cols', [(i, i ^ 1) for i in range(cols_size)])  3.65 us
    ppermute x1, waiting for transfers between devices, body(): lax.ppermute(total, ('rows', 'cols'), [(i * cols_size + j, (i ^ 2) * cols...  3.38 us
    ppermute x1, waiting for transfers between devices, body(): mate1 = lax.ppermute(own, 'rows', back)  2.98 us
    ppermute x3, waiting for transfers between devices, cols_flip(): return lax.ppermute(values, 'cols', [(i, i ^ 1) for i in range(cols_size)])  2.44 us
    ppermute x1, starting transfers between devices, body(): lax.ppermute(total, ('rows', 'cols'), [(i * cols_size + j, (i ^ 2) * cols...  2.43 us
  transfers between devices with their start and end apart: 18, of which 11 were waited for; matrix products, arithmetic and copies ran while one was open for 0% of the time, Pallas kernels for 13%

profile of v8, /device:TPU:0, one launch (start us, length us, event | category | flops | bytes accessed | tf_op | source)
XLA Modules:
  0.0 53.5 jit_solution(1661723540350456553)
XLA Ops:
  0.6 3.0 %collective-permute-start.1 = (bf16[128,256]{1,0:T(8,128)(2,1)}, bf16[128,256]{1,0:T(8,128)(2,1)S(1)}, u32[]{:S(2)}, u32[]{:S(2)}) collective-permute-start(bf16[128,256]{1,0:T(8,128)(2,1)} %bitcast.8), channel_id=1, source_target_pairs={{0,1},{1,0},{2,3},{3,2},{4,5},{5,4},{6,7},{7,6},{8,9},{9,8},{10,11... | collective-permute-start | bytes 196616 | tf_op jit(solution)/shard_map/ppermute | solution.py:450
  3.7 0.9 %copy-done.2 = bf16[256,512]{1,0:T(8,128)(2,1)S(1)} copy-done((bf16[256,512]{1,0:T(8,128)(2,1)S(1)}, bf16[256,512]{1,0:T(8,128)(2,1)}, u32[]{:S(2)}) %copy-start.2) | copy-done | bytes 262168
  4.7 0.8 %copy-done.3 = bf16[1,128,256]{2,1,0:T(8,128)(2,1)S(1)} copy-done((bf16[1,128,256]{2,1,0:T(8,128)(2,1)S(1)}, bf16[1,128,256]{2,1,0:T(8,128)(2,1)}, u32[]{:S(2)}) %copy-start.3) | copy-done | bytes 65560
  5.6 0.6 %collective-permute-done.1.refs_1_ = bf16[128,256]{1,0:T(8,128)(2,1)S(1)} collective-permute-done((bf16[128,256]{1,0:T(8,128)(2,1)}, bf16[128,256]{1,0:T(8,128)(2,1)S(1)}, u32[]{:S(2)}, u32[]{:S(2)}) %collective-permute-start.1) | collective-permute-done | bytes 65568 | tf_op jit(solution)/shard_map/ppermute | solution.py:450
  6.2 1.3 %attention_forward.1 = (bf16[256,256]{1,0:T(8,128)(2,1)S(1)}, bf16[256,768]{1,0:T(8,128)(2,1)S(1)}, f32[8,256]{1,0:T(8,128)S(1)}) custom-call(bf16[128,256]{1,0:T(8,128)(2,1)S(1)} %get-tuple-element.43.refs_0_, bf16[128,256]{1,0:T(8,128)(2,1)S(1)} %collective-permute-done.1.refs_1_, bf16[256,512]{1,0:T(8,128)(2,1)S(1)} %get-tuple-element.44.refs_2_.projection), custom_call_target="tpu_custom_call" | custom-call | flops 1000000000 | bytes 4000000 | tf_op jit(solution)/shard_map/attention_forward/pallas_call | solution.py:459
  8.1 2.2 %collective-permute-start.5 = (bf16[256,256]{1,0:T(8,128)(2,1)S(1)}, bf16[256,256]{1,0:T(8,128)(2,1)S(1)}, u32[]{:S(2)}, u32[]{:S(2)}) collective-permute-start(bf16[256,256]{1,0:T(8,128)(2,1)S(1)} %get-tuple-element.47), channel_id=1, source_target_pairs={{0,4},{4,8},{8,12},{12,16},{16,20},{20,24},{24,28},{6,2},{10,6},{1... | collective-permute-start | bytes 393224 | tf_op jit(solution)/shard_map/ppermute | solution.py:506
  11.5 3.0 %collective-permute-done.2.mate1 = bf16[256,384]{1,0:T(8,128)(2,1)S(1)} collective-permute-done((bf16[256,384]{1,0:T(8,128)(2,1)S(1)}, bf16[256,384]{1,0:T(8,128)(2,1)S(1)}, u32[]{:S(2)}, u32[]{:S(2)}) %collective-permute-start.2) | collective-permute-done | bytes 196640 | tf_op jit(solution)/shard_map/ppermute | solution.py:505
  14.5 1.3 %collective-permute-done.5.far = bf16[256,256]{1,0:T(8,128)(2,1)S(1)} collective-permute-done((bf16[256,256]{1,0:T(8,128)(2,1)S(1)}, bf16[256,256]{1,0:T(8,128)(2,1)S(1)}, u32[]{:S(2)}, u32[]{:S(2)}) %collective-permute-start.5) | collective-permute-done | bytes 131104 | tf_op jit(solution)/shard_map/ppermute | solution.py:506
  16.0 0.9 %inner.1 = (bf16[256,256]{1,0:T(8,128)(2,1)S(1)}, f32[256,256]{1,0:T(8,128)S(1)}, f32[256,256]{1,0:T(8,128)S(1)}) custom-call(bf16[256,384]{1,0:T(8,128)(2,1)S(1)} %get-tuple-element.46.own, bf16[256,384]{1,0:T(8,128)(2,1)S(1)} %collective-permute-done.4.mate, bf16[256,384]{1,0:T(8,128)(2,1)S(1)} %collective-permute-done.2.mate1, ...), custom_call_target="tpu_custom_call" | custom-call | flops 1000000000 | bytes 4000000 | tf_op jit(solution)/shard_map/inner/pallas_call | solution.py:459
  16.9 2.3 %block_backward.1 = (bf16[256,256]{1,0:T(8,128)(2,1)S(1)}, bf16[256,256]{1,0:T(8,128)(2,1)S(1)}, bf16[512,256]{1,0:T(8,128)(2,1)S(1)}, bf16[2,128,128]{2,1,0:T(8,128)(2,1)S(1)}, bf16[2,128,128]{2,1,0:T(8,128)(2,1)S(1)}) custom-call(f32[256,256]{1,0:T(8,128)S(1)} %far_back.1.far, bf16[256,384]{1,0:T(8,128)(2,1)S(1)} %collective-permute-done.3.near, ...), custom_call_target="tpu_custom_call" | custom-call | flops 1000000000 | bytes 4000000 | tf_op jit(solution)/shard_map/block_backward/pallas_call | solution.py:459
  19.4 0.8 %conv_grads.1 = (bf16[432,128]{1,0:T(8,128)(2,1)S(1)}, bf16[432,128]{1,0:T(8,128)(2,1)S(1)}) custom-call(bf16[256,384]{1,0:T(8,128)(2,1)S(1)} %collective-permute-done.3.near, bf16[256,384]{1,0:T(8,128)(2,1)S(1)} %get-tuple-element.46.own, bf16[256,384]{1,0:T(8,128)(2,1)S(1)} %collective-permute-done.4.mate, ...), custom_call_target="tpu_custom_call" | custom-call | flops 1000000000 | bytes 4000000 | tf_op jit(solution)/shard_map/conv_grads/pallas_call | solution.py:459
  20.7 3.8 %collective-permute-start.7 = (bf16[560,128]{1,0:T(8,128)(2,1)S(1)}, bf16[560,128]{1,0:T(8,128)(2,1)S(1)}, u32[]{:S(2)}, u32[]{:S(2)}) collective-permute-start(bf16[560,128]{1,0:T(8,128)(2,1)S(1)} %pad_maximum_fusion), channel_id=1, source_target_pairs={{0,8},{2,10},{4,12},{6,14},{8,0},{10,2},{12,4},{14,6},{16,24},{18,... | collective-permute-start | bytes 430088 | tf_op jit(solution)/shard_map/ppermute | solution.py:447
  24.7 1.2 %collective-permute-start.8 = (bf16[560,128]{1,0:T(8,128)(2,1)S(1)}, bf16[560,128]{1,0:T(8,128)(2,1)S(1)}, u32[]{:S(2)}, u32[]{:S(2)}) collective-permute-start(bf16[560,128]{1,0:T(8,128)(2,1)S(1)} %pad_maximum_fusion.1), channel_id=1, source_target_pairs={{0,4},{2,6},{4,0},{6,2},{8,12},{10,14},{12,8},{14,10},{16,20},{18,... | collective-permute-start | bytes 430088 | tf_op jit(solution)/shard_map/ppermute | solution.py:447
  26.0 3.0 %collective-permute-done.7 = bf16[560,128]{1,0:T(8,128)(2,1)S(1)} collective-permute-done((bf16[560,128]{1,0:T(8,128)(2,1)S(1)}, bf16[560,128]{1,0:T(8,128)(2,1)S(1)}, u32[]{:S(2)}, u32[]{:S(2)}) %collective-permute-start.7) | collective-permute-done | bytes 143392 | tf_op jit(solution)/shard_map/ppermute | solution.py:447
  29.0 2.7 %collective-permute-done.9 = bf16[560,128]{1,0:T(8,128)(2,1)S(1)} collective-permute-done((bf16[560,128]{1,0:T(8,128)(2,1)S(1)}, bf16[560,128]{1,0:T(8,128)(2,1)S(1)}, u32[]{:S(2)}, u32[]{:S(2)}) %collective-permute-start.9) | collective-permute-done | bytes 143392 | tf_op jit(solution)/shard_map/ppermute | solution.py:447
  31.6 1.6 %collective-permute-done.8 = bf16[560,128]{1,0:T(8,128)(2,1)S(1)} collective-permute-done((bf16[560,128]{1,0:T(8,128)(2,1)S(1)}, bf16[560,128]{1,0:T(8,128)(2,1)S(1)}, u32[]{:S(2)}, u32[]{:S(2)}) %collective-permute-start.8) | collective-permute-done | bytes 143392 | tf_op jit(solution)/shard_map/ppermute | solution.py:447
  33.3 2.7 %collective-permute-start.10 = (bf16[560,128]{1,0:T(8,128)(2,1)S(1)}, bf16[560,128]{1,0:T(8,128)(2,1)S(1)}, u32[]{:S(2)}, u32[]{:S(2)}) collective-permute-start(bf16[560,128]{1,0:T(8,128)(2,1)S(1)} %add_convert_fusion.1), channel_id=1, source_target_pairs={{0,16},{2,18},{4,20},{6,22},{8,24},{10,26},{12,28},{14,30},{16,0},... | collective-permute-start | bytes 430088 | tf_op jit(solution)/shard_map/ppermute | solution.py:447
  36.0 1.2 %outputs.1 = (bf16[128,128]{1,0:T(8,128)(2,1)}, bf16[128,256]{1,0:T(8,128)(2,1)}) custom-call(bf16[256,256]{1,0:T(8,128)(2,1)S(1)} %get-tuple-element.68.near_mid, bf16[256,256]{1,0:T(8,128)(2,1)S(1)} %get-tuple-element.63.own_mid, bf16[256,256]{1,0:T(8,128)(2,1)S(1)} %get-tuple-element.52.mate_mid, bf16[512,256]{1,0:T(8,128)(2,1)S(1)} %get-tuple-element.69.grad, ...), custom_call_target="tpu_custom_call" | custom-call | flops 1000000000 | bytes 4000000 | tf_op jit(solution)/shard_map/outputs/pallas_call | solution.py:459
  37.2 4.9 %collective-permute-done.10 = bf16[560,128]{1,0:T(8,128)(2,1)S(1)} collective-permute-done((bf16[560,128]{1,0:T(8,128)(2,1)S(1)}, bf16[560,128]{1,0:T(8,128)(2,1)S(1)}, u32[]{:S(2)}, u32[]{:S(2)}) %collective-permute-start.10) | collective-permute-done | bytes 143392 | tf_op jit(solution)/shard_map/ppermute | solution.py:447
  42.1 2.4 %collective-permute-start.16 = (bf16[560,128]{1,0:T(8,128)(2,1)S(1)}, bf16[560,128]{1,0:T(8,128)(2,1)S(1)}, u32[]{:S(2)}, u32[]{:S(2)}) collective-permute-start(bf16[560,128]{1,0:T(8,128)(2,1)S(1)} %add_convert_fusion.refs_0_), channel_id=1, source_target_pairs={{0,5},{1,4},{2,7},{3,6},{4,1},{5,0},{6,3},{7,2},{8,13},{9,12},{10,... | collective-permute-start | bytes 430088 | tf_op jit(solution)/shard_map/ppermute | solution.py:587
  45.7 3.4 %collective-permute-done.16.refs_3_ = bf16[560,128]{1,0:T(8,128)(2,1)S(1)} collective-permute-done((bf16[560,128]{1,0:T(8,128)(2,1)S(1)}, bf16[560,128]{1,0:T(8,128)(2,1)S(1)}, u32[]{:S(2)}, u32[]{:S(2)}) %collective-permute-start.16) | collective-permute-done | bytes 143392 | tf_op jit(solution)/shard_map/ppermute | solution.py:587
  49.1 1.7 %collective-permute-done.14.refs_2_ = bf16[560,128]{1,0:T(8,128)(2,1)S(1)} collective-permute-done((bf16[560,128]{1,0:T(8,128)(2,1)S(1)}, bf16[560,128]{1,0:T(8,128)(2,1)S(1)}, u32[]{:S(2)}, u32[]{:S(2)}) %collective-permute-start.14) | collective-permute-done | bytes 143392 | tf_op jit(solution)/shard_map/ppermute | solution.py:450
  51.2 1.1 %unpack_sums.2 = (f32[256,512]{1,0:T(8,128)}, f32[3,3,256,128]{3,2,1,0:T(8,128)}, f32[3,3,128,128]{3,2,1,0:T(8,128)}) custom-call(bf16[560,128]{1,0:T(8,128)(2,1)S(1)} %add_convert_fusion.refs_0_, bf16[560,128]{1,0:T(8,128)(2,1)S(1)} %collective-permute-done.12.refs_1_, bf16[560,128]{1,0:T(8,128)(2,1)S(1)} %collective-permute-done.14.refs_2_, ...), custom_call_target="tpu_custom_call" | custom-call | flops 1000000000 | bytes 4194304 | tf_op jit(solution)/shard_map/unpack_sums/pallas_call | solution.py:414
  52.4 1.1 %unpack_sums.3 = (f32[256,512]{1,0:T(8,128)}, f32[3,3,256,128]{3,2,1,0:T(8,128)}, f32[3,3,128,128]{3,2,1,0:T(8,128)}) custom-call(bf16[560,128]{1,0:T(8,128)(2,1)S(1)} %collective-permute-done.11.refs_0_, bf16[560,128]{1,0:T(8,128)(2,1)S(1)} %collective-permute-done.13.refs_1_, ...), custom_call_target="tpu_custom_call", output_to_operand_aliasing={{0}: (4, {}), {1}: (5, {}), {2}: (6, {})} | custom-call | flops 1000000000 | bytes 4194304 | tf_op jit(solution)/shard_map/unpack_sums/pallas_call | solution.py:414
  (41 shorter events, 4.7 us)
Async XLA Ops:
  0.6 5.6 %collective-permute-start.1 = (bf16[128,256]{1,0:T(8,128)(2,1)}, bf16[128,256]{1,0:T(8,128)(2,1)S(1)}, u32[]{:S(2)}, u32[]{:S(2)}) collective-permute-start(bf16[128,256]{1,0:T(8,128)(2,1)} %bitcast.8), channel_id=1, source_target_pairs={{0,1},{1,0},{2,3},{3,2},{4,5},{5,4},{6,7},{7,6},{8,9},{9,8},{10,11... | collective-permute-start | bytes 196616 | tf_op jit(solution)/shard_map/ppermute | solution.py:450
  3.6 4.1 %collective-permute-start = (bf16[128,128]{1,0:T(8,128)(2,1)}, bf16[128,128]{1,0:T(8,128)(2,1)S(1)}, u32[]{:S(2)}, u32[]{:S(2)}) collective-permute-start(bf16[128,128]{1,0:T(8,128)(2,1)} %bitcast.10), channel_id=1, source_target_pairs={{0,1},{1,0},{2,3},{3,2},{4,5},{5,4},{6,7},{7,6},{8,9},{9,8},{10,11... | collective-permute-start | bytes 98312 | tf_op jit(solution)/shard_map/ppermute | solution.py:450
  3.7 0.9 %copy-start.2 = (bf16[256,512]{1,0:T(8,128)(2,1)S(1)}, bf16[256,512]{1,0:T(8,128)(2,1)}, u32[]{:S(2)}) copy-start(bf16[256,512]{1,0:T(8,128)(2,1)} %refs_0_.2) | copy-start | bytes 786436
  4.7 0.8 %copy-start.3 = (bf16[1,128,256]{2,1,0:T(8,128)(2,1)S(1)}, bf16[1,128,256]{2,1,0:T(8,128)(2,1)}, u32[]{:S(2)}) copy-start(bf16[1,128,256]{2,1,0:T(8,128)(2,1)} %param.5) | copy-start | bytes 196612
  6.2 1.5 %copy-start = (bf16[3,3,256,128]{3,2,1,0:T(8,128)(2,1)S(1)}, bf16[3,3,256,128]{3,2,1,0:T(8,128)(2,1)}, u32[]{:S(2)}) copy-start(bf16[3,3,256,128]{3,2,1,0:T(8,128)(2,1)} %refs_0_.3) | copy-start | bytes 1769476
  6.2 1.5 %copy-start.4 = (bf16[1,128,128]{2,1,0:T(8,128)(2,1)S(1)}, bf16[1,128,128]{2,1,0:T(8,128)(2,1)}, u32[]{:S(2)}) copy-start(bf16[1,128,128]{2,1,0:T(8,128)(2,1)} %param.9) | copy-start | bytes 98308
  7.8 2.5 %copy-start.1 = (bf16[3,3,128,128]{3,2,1,0:T(8,128)(2,1)S(1)}, bf16[3,3,128,128]{3,2,1,0:T(8,128)(2,1)}, u32[]{:S(2)}) copy-start(bf16[3,3,128,128]{3,2,1,0:T(8,128)(2,1)} %refs_1_.1) | copy-start | bytes 884740
  8.0 6.4 %collective-permute-start.2 = (bf16[256,384]{1,0:T(8,128)(2,1)S(1)}, bf16[256,384]{1,0:T(8,128)(2,1)S(1)}, u32[]{:S(2)}, u32[]{:S(2)}) collective-permute-start(bf16[256,384]{1,0:T(8,128)(2,1)S(1)} %get-tuple-element.46.own), channel_id=1, source_target_pairs={{4,0},{8,4},{12,8},{16,12},{20,16},{24,20},{28,24},{2,6},{6,10},{1... | collective-permute-start | bytes 589832 | tf_op jit(solution)/shard_map/ppermute | solution.py:505
  8.1 7.7 %collective-permute-start.5 = (bf16[256,256]{1,0:T(8,128)(2,1)S(1)}, bf16[256,256]{1,0:T(8,128)(2,1)S(1)}, u32[]{:S(2)}, u32[]{:S(2)}) collective-permute-start(bf16[256,256]{1,0:T(8,128)(2,1)S(1)} %get-tuple-element.47), channel_id=1, source_target_pairs={{0,4},{4,8},{8,12},{12,16},{16,20},{20,24},{24,28},{6,2},{10,6},{1... | collective-permute-start | bytes 393224 | tf_op jit(solution)/shard_map/ppermute | solution.py:506
  10.3 5.8 %collective-permute-start.4 = (bf16[256,384]{1,0:T(8,128)(2,1)S(1)}, bf16[256,384]{1,0:T(8,128)(2,1)S(1)}, u32[]{:S(2)}, u32[]{:S(2)}) collective-permute-start(bf16[256,384]{1,0:T(8,128)(2,1)S(1)} %get-tuple-element.46.own), channel_id=1, source_target_pairs={{0,2},{2,0},{4,6},{6,4},{8,10},{10,8},{12,14},{14,12},{16,18},{18,... | collective-permute-start | bytes 589832 | tf_op jit(solution)/shard_map/ppermute | solution.py:447
  14.5 2.5 %collective-permute-start.3 = (bf16[256,384]{1,0:T(8,128)(2,1)S(1)}, bf16[256,384]{1,0:T(8,128)(2,1)S(1)}, u32[]{:S(2)}, u32[]{:S(2)}) collective-permute-start(bf16[256,384]{1,0:T(8,128)(2,1)S(1)} %collective-permute-done.2.mate1), channel_id=1, source_target_pairs={{0,2},{2,0},{4,6},{6,4},{8,10},{10,8},{12,14},{14,12},{16,18},{18,... | collective-permute-start | bytes 589832 | tf_op jit(solution)/shard_map/ppermute | solution.py:447
  19.3 1.3 %collective-permute-start.6 = (bf16[2,128,128]{2,1,0:T(8,128)(2,1)S(1)}, bf16[2,128,128]{2,1,0:T(8,128)(2,1)S(1)}, u32[]{:S(2)}, u32[]{:S(2)}) collective-permute-start(bf16[2,128,128]{2,1,0:T(8,128)(2,1)S(1)} %get-tuple-element.66), channel_id=1, source_target_pairs={{0,2},{2,0},{4,6},{6,4},{8,10},{10,8},{12,14},{14,12},{16,18},{18,... | collective-permute-start | bytes 196616 | tf_op jit(solution)/shard_map/ppermute | solution.py:447
  20.7 8.3 %collective-permute-start.7 = (bf16[560,128]{1,0:T(8,128)(2,1)S(1)}, bf16[560,128]{1,0:T(8,128)(2,1)S(1)}, u32[]{:S(2)}, u32[]{:S(2)}) collective-permute-start(bf16[560,128]{1,0:T(8,128)(2,1)S(1)} %pad_maximum_fusion), channel_id=1, source_target_pairs={{0,8},{2,10},{4,12},{6,14},{8,0},{10,2},{12,4},{14,6},{16,24},{18,... | collective-permute-start | bytes 430088 | tf_op jit(solution)/shard_map/ppermute | solution.py:447
  24.4 7.2 %collective-permute-start.9 = (bf16[560,128]{1,0:T(8,128)(2,1)S(1)}, bf16[560,128]{1,0:T(8,128)(2,1)S(1)}, u32[]{:S(2)}, u32[]{:S(2)}) collective-permute-start(bf16[560,128]{1,0:T(8,128)(2,1)S(1)} %pad_maximum_fusion.1), channel_id=1, source_target_pairs={{0,12},{2,14},{4,8},{6,10},{8,4},{10,6},{12,0},{14,2},{16,28},{18,... | collective-permute-start | bytes 430088 | tf_op jit(solution)/shard_map/ppermute | solution.py:447
  24.7 8.5 %collective-permute-start.8 = (bf16[560,128]{1,0:T(8,128)(2,1)S(1)}, bf16[560,128]{1,0:T(8,128)(2,1)S(1)}, u32[]{:S(2)}, u32[]{:S(2)}) collective-permute-start(bf16[560,128]{1,0:T(8,128)(2,1)S(1)} %pad_maximum_fusion.1), channel_id=1, source_target_pairs={{0,4},{2,6},{4,0},{6,2},{8,12},{10,14},{12,8},{14,10},{16,20},{18,... | collective-permute-start | bytes 430088 | tf_op jit(solution)/shard_map/ppermute | solution.py:447
  33.3 8.7 %collective-permute-start.10 = (bf16[560,128]{1,0:T(8,128)(2,1)S(1)}, bf16[560,128]{1,0:T(8,128)(2,1)S(1)}, u32[]{:S(2)}, u32[]{:S(2)}) collective-permute-start(bf16[560,128]{1,0:T(8,128)(2,1)S(1)} %add_convert_fusion.1), channel_id=1, source_target_pairs={{0,16},{2,18},{4,20},{6,22},{8,24},{10,26},{12,28},{14,30},{16,0},... | collective-permute-start | bytes 430088 | tf_op jit(solution)/shard_map/ppermute | solution.py:447
  42.1 6.9 %collective-permute-start.16 = (bf16[560,128]{1,0:T(8,128)(2,1)S(1)}, bf16[560,128]{1,0:T(8,128)(2,1)S(1)}, u32[]{:S(2)}, u32[]{:S(2)}) collective-permute-start(bf16[560,128]{1,0:T(8,128)(2,1)S(1)} %add_convert_fusion.refs_0_), channel_id=1, source_target_pairs={{0,5},{1,4},{2,7},{3,6},{4,1},{5,0},{6,3},{7,2},{8,13},{9,12},{10,... | collective-permute-start | bytes 430088 | tf_op jit(solution)/shard_map/ppermute | solution.py:587
  44.6 6.2 %collective-permute-start.14 = (bf16[560,128]{1,0:T(8,128)(2,1)S(1)}, bf16[560,128]{1,0:T(8,128)(2,1)S(1)}, u32[]{:S(2)}, u32[]{:S(2)}) collective-permute-start(bf16[560,128]{1,0:T(8,128)(2,1)S(1)} %add_convert_fusion.refs_0_), channel_id=1, source_target_pairs={{0,1},{1,0},{2,3},{3,2},{4,5},{5,4},{6,7},{7,6},{8,9},{9,8},{10,11... | collective-permute-start | bytes 430088 | tf_op jit(solution)/shard_map/ppermute | solution.py:450
  45.1 5.6 %collective-permute-start.12 = (bf16[560,128]{1,0:T(8,128)(2,1)S(1)}, bf16[560,128]{1,0:T(8,128)(2,1)S(1)}, u32[]{:S(2)}, u32[]{:S(2)}) collective-permute-start(bf16[560,128]{1,0:T(8,128)(2,1)S(1)} %add_convert_fusion.refs_0_), channel_id=1, source_target_pairs={{0,4},{2,6},{4,0},{6,2},{8,12},{10,14},{12,8},{14,10},{16,20},{18,... | collective-permute-start | bytes 430088 | tf_op jit(solution)/shard_map/ppermute | solution.py:447
  45.7 6.6 %collective-permute-start.11 = (bf16[560,128]{1,0:T(8,128)(2,1)S(1)}, bf16[560,128]{1,0:T(8,128)(2,1)S(1)}, u32[]{:S(2)}, u32[]{:S(2)}) collective-permute-start(bf16[560,128]{1,0:T(8,128)(2,1)S(1)} %add_convert_fusion.refs_0_), channel_id=1, source_target_pairs={{0,2},{2,0},{4,6},{6,4},{8,10},{10,8},{12,14},{14,12},{16,18},{18,... | collective-permute-start | bytes 430088 | tf_op jit(solution)/shard_map/ppermute | solution.py:447
  49.1 3.3 %collective-permute-start.17 = (bf16[560,128]{1,0:T(8,128)(2,1)S(1)}, bf16[560,128]{1,0:T(8,128)(2,1)S(1)}, u32[]{:S(2)}, u32[]{:S(2)}) collective-permute-start(bf16[560,128]{1,0:T(8,128)(2,1)S(1)} %collective-permute-done.16.refs_3_), channel_id=1, source_target_pairs={{0,2},{2,0},{4,6},{6,4},{8,10},{10,8},{12,14},{14,12},{16,18},{18,... | collective-permute-start | bytes 430088 | tf_op jit(solution)/shard_map/ppermute | solution.py:447
  50.7 1.6 %collective-permute-start.15 = (bf16[560,128]{1,0:T(8,128)(2,1)S(1)}, bf16[560,128]{1,0:T(8,128)(2,1)S(1)}, u32[]{:S(2)}, u32[]{:S(2)}) collective-permute-start(bf16[560,128]{1,0:T(8,128)(2,1)S(1)} %collective-permute-done.14.refs_2_), channel_id=1, source_target_pairs={{0,2},{2,0},{4,6},{6,4},{8,10},{10,8},{12,14},{14,12},{16,18},{18,... | collective-permute-start | bytes 430088 | tf_op jit(solution)/shard_map/ppermute | solution.py:447
  50.7 1.6 %collective-permute-start.13 = (bf16[560,128]{1,0:T(8,128)(2,1)S(1)}, bf16[560,128]{1,0:T(8,128)(2,1)S(1)}, u32[]{:S(2)}, u32[]{:S(2)}) collective-permute-start(bf16[560,128]{1,0:T(8,128)(2,1)S(1)} %collective-permute-done.12.refs_1_), channel_id=1, source_target_pairs={{0,2},{2,0},{4,6},{6,4},{8,10},{10,8},{12,14},{14,12},{16,18},{18,... | collective-permute-start | bytes 430088 | tf_op jit(solution)/shard_map/ppermute | solution.py:447

commit v9 on v8

--- a/solution.py
+++ b/solution.py
@@ -169,18 +169,16 @@
     )
 
 
-def rows_kernel(count, *refs):
-    attended, first_kernel, row, term = refs[count:]
-    lay_out(refs[:count], row, slice(VAL, None))
-    lay_out(refs[:count], term, slice(CONV, None))
-    row[:, :VAL] = attended[...]
-    term[:, :CONV] = side(mm(attended[...], Place().beside(first_kernel, 0)), CONV, 1).astype(BF)
-
-
-def far_back_kernel(far, second_t, out):
-    back = side(mm(far[:, CONV:], second_t[2]), CONV, -1)
-    out[:, :CONV] = far[:, :CONV].astype(F32)
-    out[:, CONV:] = back
+def rows_kernel(attended, first_kernel, far_cot, cotangent, mate1_cot, term, bundle):
+    term[...] = side(mm(attended[...], Place().beside(first_kernel, 0)), CONV, 1).astype(BF)
+    for row, half in enumerate((far_cot, cotangent, mate1_cot)):
+        bundle[row] = half[...]
+
+
+def assemble_kernel(count, *refs):
+    far, pair = refs[count:]
+    for row, target in enumerate((far, pair.at[0], pair.at[1])):
+        lay_out([piece.at[row] for piece in refs[:count]], target, slice(None))
 
 
 def turn_kernel(first_kernel, second_kernel, first_t, second_t):
@@ -205,7 +203,7 @@
         at = block_at(index)
         queries = local[at, :QK]
         queries_t[:, at] = mm_t(identity(QK), queries).astype(BF)
-        attended_t[:, at] = mm_t(identity(VAL), own[at, :VAL]).astype(BF)
+        attended_t[:, at] = mm_t(identity(VAL), own[at, :]).astype(BF)
         scores = mm_t(jnp.concatenate([head_of(keys, h, HEAD_QK) for h in range(HEADS)], axis=0), queries)
         for head in range(HEADS):
             rows = slice(head * across, (head + 1) * across)
@@ -219,11 +217,27 @@
 
 
 def conv_term(place, row, kernel, tap):
-    return side(mm(row[:, :VAL], place.beside(kernel, tap)), CONV, 1)
+    return side(mm(row[...], place.beside(kernel, tap)), CONV, 1)
 
 
 def back_term(row, second_t, tap):
-    return side(mm(row[:, VAL:], second_t[tap]), CONV, -1)
+    return side(mm(row[...], second_t[tap]), CONV, -1)
+
+
+def cotangent_terms_kernel(far_cot, pair_cot, second_t, near_back, own_back, mate_back):
+    place = Place()
+    own = pair_cot[0]
+    near_back[...] = back_term(far_cot, second_t, 2) + back_term(own, second_t, 0)
+    own_back[...] = back_term(own, second_t, 1)
+    mate1 = masked(place.mate_inside, pair_cot[1])
+    mate_back[...] = back_term(own, second_t, 2) + back_term(mate1, second_t, 0)
+
+
+def attended_terms_kernel(own, mate, first_kernel, near_pre, own_pre, mate_pre):
+    place = Place()
+    near_pre[...] = conv_term(place, own, first_kernel, 2)
+    own_pre[...] = conv_term(place, own, first_kernel, 1) + conv_term(place, mate, first_kernel, 2)
+    mate_pre[...] = conv_term(place, own, first_kernel, 0) + conv_term(place, mate, first_kernel, 1)
 
 
 def store_middle(pre, back, out):
@@ -232,31 +246,28 @@
     out[:, CONV:] = (back * (sigma * (1.0 + pre * (1.0 - sigma)))).astype(BF)
 
 
-def inner_kernel(own, mate, mate1, first_kernel, second_t, mate_mid, near_part, own_part):
-    place = Place()
-    mate1 = masked(place.mate_inside, mate1[...])
-    near_part[:, :CONV] = conv_term(place, own, first_kernel, 2)
-    near_part[:, CONV:] = back_term(own, second_t, 0)
-    own_part[:, :CONV] = conv_term(place, own, first_kernel, 1) + conv_term(place, mate, first_kernel, 2)
-    own_part[:, CONV:] = back_term(own, second_t, 1) + back_term(mate, second_t, 0)
-    rows = (own, mate, mate1)
-    pre = sum(conv_term(place, row, first_kernel, a) for a, row in enumerate(rows))
-    back = sum(back_term(row, second_t, 2 - a) for a, row in enumerate(rows))
-    store_middle(pre, back, mate_mid)
-
-
-def middle(place, far, near, near_part, own_part, first_kernel, second_t, near_mid, own_mid):
-    pre = near_part[:, :CONV] + far[:, :CONV] + conv_term(place, near, first_kernel, 1)
-    back = near_part[:, CONV:] + far[:, CONV:] + back_term(near, second_t, 1)
-    store_middle(masked(place.near_inside, pre), masked(place.near_inside, back), near_mid)
-    pre = own_part[:, :CONV] + conv_term(place, near, first_kernel, 0)
-    back = own_part[:, CONV:] + back_term(near, second_t, 2)
-    store_middle(pre, back, own_mid)
-
-
-def conv_grads_kernel(near, own, mate, mate1, own_mid, mate_mid, keep, send):
+def near_terms_kernel(far_term, near_pre, near_terms):
+    near_terms[...] = near_pre[...] + far_term[...].astype(F32)
+
+
+def mate_middle_kernel(
+    mate1, mate_cot, mate_pre, mate_back, own_back, first_kernel, second_t, mate_mid, own_terms
+):
+    place = Place()
+    own_terms[...] = own_back[...] + back_term(mate_cot[0], second_t, 0)
+    pre = mate_pre[...] + conv_term(place, masked(place.mate_inside, mate1[...]), first_kernel, 2)
+    store_middle(pre, mate_back[...] + back_term(mate_cot[0], second_t, 1), mate_mid)
+
+
+def conv_grads_kernel(near, own, mate, mate1, pair_cot, mate_cot, own_mid, mate_mid, keep, send):
     place = Place()
     slots = (masked(place.near_inside, near[...]), own[...], mate[...], masked(place.mate_inside, mate1[...]))
+    cots = (
+        masked(place.near_inside, mate_cot[1]),
+        pair_cot[0],
+        mate_cot[0],
+        masked(place.mate_inside, pair_cot[1]),
+    )
     mids = {1: own_mid, 2: mate_mid}
 
     def store(total, start, step, a):
@@ -266,25 +277,27 @@
             send[at, :] = total[step:, b * CONV : (b + 1) * CONV]
 
     pick = place.chosen(VAL, place.core)
-    attended_t = [mm_t(pick, slot[:, :VAL]).astype(BF) for slot in slots]
+    attended_t = [mm_t(pick, slot).astype(BF) for slot in slots]
     slope = {slot: spread(mid[:, CONV:].astype(F32)) for slot, mid in mids.items()}
     for a in range(3):
         total = sum(mm(attended_t[slot + a - 1], slope[slot]) for slot in mids).astype(BF)
         store(total, 0, VAL // PARTS, a)
     pick = place.chosen(CONV, place.core)
     hidden_t = {slot: mm_t(pick, mid[:, :CONV]).astype(BF) for slot, mid in mids.items()}
-    cotangent = [spread(slot[:, VAL:].astype(F32)) for slot in slots]
+    cotangent = [spread(cot.astype(F32)) for cot in cots]
     for a in range(3):
         total = sum(mm(hidden_t[slot], cotangent[slot + 1 - a]) for slot in mids).astype(BF)
         store(total, FIRST_ROWS, CONV // PARTS, a)
 
 
 def backward_kernel(
-    far,
     near,
+    mate_cot,
     mate_mid,
-    near_part,
-    own_part,
+    near_pre,
+    near_back,
+    own_pre,
+    own_back,
     values,
     soft,
     keys_t,
@@ -306,7 +319,12 @@
     across = near.shape[0]
     near = masked(place.near_inside, near[...])
     mids = (near_mid, own_mid, mate_mid)
-    middle(place, far, near, near_part, own_part, first_kernel, second_t, near_mid, own_mid)
+    pre = near_pre[...] + conv_term(place, near, first_kernel, 1)
+    near_cot = masked(place.near_inside, mate_cot[1])
+    back = near_back[...] + back_term(near_cot, second_t, 1)
+    store_middle(masked(place.near_inside, pre), masked(place.near_inside, back), near_mid)
+    pre = own_pre[...] + conv_term(place, near, first_kernel, 0)
+    store_middle(pre, own_back[...] + back_term(near_cot, second_t, 2), own_mid)
     slopes_beside = jnp.concatenate([mids[2 - a][:, CONV:] for a in range(3)], axis=1)
     upstream_ref[...] = side(mm(slopes_beside, first_t[...]), VAL, -1).astype(BF)
     blocks = across // BLOCK
@@ -468,46 +486,61 @@
         )(*operands)
 
     features, cotangent = (features[0], cotangent[0])
+    last = rows_size - 1
+    out = [(i, i + 2) for i in range(0, last - 1, 2)] + [(i, i - 2) for i in range(3, rows_size, 2)]
+    out += [(last - 1, last), (1, 0)]
+    back = [(j, i) for i, j in out]
     if cols_size == 2:
         swapped = cols_flip(features)
-        cotangent = (cotangent, cols_flip(cotangent))
+        out_cot = lax.ppermute(cotangent, "rows", out)
+        back_cot = lax.ppermute(cotangent, "rows", back)
         projection, features = fetch((projection, features))
         features = (features, swapped)
     else:
-        features, cotangent = (
-            (lax.all_gather(array, "cols", axis=0, tiled=True),) for array in (features, cotangent)
-        )
-    attended, local, lse = call(
+        out_cot = lax.ppermute(cotangent, "rows", out)
+        back_cot = lax.ppermute(cotangent, "rows", back)
+        features = (lax.all_gather(features, "cols", axis=0, tiled=True),)
+    own, local, lse = call(
         functools.partial(forward_kernel, len(features)),
         (shape(across, VAL), shape(across, PACKED + channels), shape(HEADS, across, dtype=F32)),
         (*features, projection),
         (pltpu.VMEM((VAL, across), BF),),
         name="attention_forward",
     )
-    own, term = call(
-        functools.partial(rows_kernel, len(cotangent)),
-        (shape(across, VAL + CONV), shape(across, 2 * CONV)),
-        (*cotangent, attended, first_kernel),
+    term, bundle = call(
+        rows_kernel,
+        (shape(across, CONV), shape(3, part_width, CONV)),
+        (own, first_kernel, out_cot, cotangent, back_cot),
         name="rows",
     )
-    first_kernel, second_kernel = fetch((first_kernel, second_kernel), (lse,), 10**5)
-    last = rows_size - 1
-    out = [(i, i + 2) for i in range(0, last - 1, 2)] + [(i, i - 2) for i in range(3, rows_size, 2)]
-    out += [(last - 1, last), (1, 0)]
-    back = [(j, i) for i, j in out]
+    first_kernel, second_kernel = fetch((first_kernel, second_kernel), (lse,), 10**4)
     first_t, second_t = call(
         turn_kernel,
         (shape(3 * CONV, 3 * VAL), shape(3, CONV, 3 * CONV)),
         (first_kernel, second_kernel),
         name="turn",
-        flops=10**7,
+        flops=10**6,
     )
     mate1 = lax.ppermute(own, "rows", back)
+    if cols_size == 2:
+        bundles = (bundle, cols_flip(bundle))
+    else:
+        bundles = (lax.all_gather(bundle, "cols", axis=1, tiled=True),)
     far = lax.ppermute(term, "rows", out)
-    (far,) = call(
-        far_back_kernel, (shape(across, 2 * CONV, dtype=F32),), (far, second_t), name="far_back", flops=4 * 10**9
-    )
     mate = rows_flip(own, 1)
+    terms = (shape(across, CONV, dtype=F32),) * 3
+    near_pre, own_pre, mate_pre = call(
+        attended_terms_kernel, terms, (own, mate, first_kernel), name="attended_terms", flops=10**6
+    )
+    bundles, near_pre = lax.optimization_barrier((bundles, near_pre))
+    far_cot, pair_cot = call(
+        functools.partial(assemble_kernel, len(bundles)),
+        (shape(across, CONV), shape(2, across, CONV)),
+        bundles,
+        name="assemble",
+        flops=10**6,
+    )
+    mate_cot = rows_flip(pair_cot, 1)
     near = rows_flip(mate1, 1)
     soft, keys_t, queries_t, attended_t, features_t, values = call(
         prepare_kernel,
@@ -521,13 +554,17 @@
         ),
         (own, local, lse),
         name="prepare",
-        flops=10**7,
-    )
-    mate_mid, near_part, own_part = call(
-        inner_kernel,
-        (shape(across, 2 * CONV), shape(across, 2 * CONV, dtype=F32), shape(across, 2 * CONV, dtype=F32)),
-        (own, mate, mate1, first_kernel, second_t),
-        name="inner",
+        flops=10**6,
+    )
+    near_back, own_back, mate_back = call(
+        cotangent_terms_kernel, terms, (far_cot, pair_cot, second_t), name="cotangent_terms", flops=10**6
+    )
+    (near_pre,) = call(near_terms_kernel, terms[:1], (far, near_pre), name="near_terms", flops=4 * 10**9)
+    mate_mid, own_back = call(
+        mate_middle_kernel,
+        (shape(across, 2 * CONV), terms[0]),
+        (mate1, mate_cot, mate_pre, mate_back, own_back, first_kernel, second_t),
+        name="mate_middle",
     )
     near_mid, own_mid, grad, proj_own, proj_mate = call(
         backward_kernel,
@@ -539,11 +576,13 @@
             shape(2, PROJ_ROWS, CONV),
         ),
         (
-            far,
             near,
+            mate_cot,
             mate_mid,
-            near_part,
-            own_part,
+            near_pre,
+            near_back,
+            own_pre,
+            own_back,
             values,
             soft,
             keys_t,
@@ -560,7 +599,7 @@
     keep, send = call(
         conv_grads_kernel,
         (shape(FIRST_ROWS + SECOND_ROWS, CONV),) * 2,
-        (near, own, mate, mate1, own_mid, mate_mid),
+        (near, own, mate, mate1, pair_cot, mate_cot, own_mid, mate_mid),
         name="conv_grads",
     )
     output_map, input_grad = call(

time: 53.6 us -> 53.4 us (level)
  waiting for transfers between devices: 22.8 us -> 19.4 us
  starting transfers between devices: 17.4 us -> 20.3 us
    ppermute x1, waiting for transfers between devices: 2.98 us -> 0.01 us  [body(): mate1 = lax.ppermute(own, 'rows', back)]
    ppermute x0 -> x2, starting transfers between devices: none -> 2.03 us  [the longest x1 2.02 us: body(): out_cot = lax.ppermute(cotangent, 'rows', out)]
    ppermute x3, waiting for transfers between devices: 2.44 us -> 1.12 us  [cols_flip(): return lax.ppermute(values, 'cols', [(i, i ^ 1) for i in range(cols_size)])]
    ppermute x12 -> x13, waiting for transfers between devices: 12.6 us -> 13.9 us  [rows_flip(): lax.ppermute(values, 'rows', [(i, i ^ bit) for i in range(rows_size)])]
    ppermute x1, starting transfers between devices: 2.43 us -> 1.62 us  [body(): lax.ppermute(total, ('rows', 'cols'), [(i * cols_size + j, (i ^ 2) * cols...]
    ppermute x3, starting transfers between devices: 3.65 us -> 4.36 us  [cols_flip(): return lax.ppermute(values, 'cols', [(i, i ^ 1) for i in range(cols_size)])]
    ppermute x1, waiting for transfers between devices: 1.34 us -> 0.68 us  [body(): far = lax.ppermute(term, 'rows', out)]
    ppermute x12 -> x13, starting transfers between devices: 9.12 us -> 9.75 us  [rows_flip(): lax.ppermute(values, 'rows', [(i, i ^ bit) for i in range(rows_size)])]
  transfers between devices with their start and end apart: 18 -> 21, of which waited for: 11 -> 11; matrix products, arithmetic and copies ran while one was open for 0% -> 0% of each run, Pallas kernels for 13% -> 14%
where the time goes in v9:
time: 53.4 us; the launch traced here: 53.2 us
  starting transfers between devices  20.3 us (38%)
  waiting for transfers between devices  19.4 us (36%)
  Pallas kernels  10.7 us (20%)
  local copies, waits for them, and re-layouts  1.81 us (3%)
  between operations  0.88 us (2%)
    ppermute x13, waiting for transfers between devices, rows_flip(): lax.ppermute(values, 'rows', [(i, i ^ bit) for i in range(rows_size)])  13.9 us
    ppermute x13, starting transfers between devices, rows_flip(): lax.ppermute(values, 'rows', [(i, i ^ bit) for i in range(rows_size)])  9.75 us
    pallas_call x12, Pallas kernels, call(): pl.pallas_call(kernel, out_shape=out_shape, in_specs=[VMEM] * len(operand...  8.2 us
    ppermute x3, starting transfers between devices, cols_flip(): return lax.ppermute(values, 'cols', [(i, i ^ 1) for i in range(cols_size)])  4.36 us
    ppermute x1, waiting for transfers between devices, body(): lax.ppermute(total, ('rows', 'cols'), [(i * cols_size + j, (i ^ 2) * cols...  3.65 us
    pallas_call x2, Pallas kernels, unpack(): pl.pallas_call(functools.partial(unpack_kernel, factor, core_flip), out_s...  2.16 us
    ppermute x1, starting transfers between devices, body(): far = lax.ppermute(term, 'rows', out)  2.04 us
    ppermute x1, starting transfers between devices, body(): out_cot = lax.ppermute(cotangent, 'rows', out)  2.02 us
  transfers between devices with their start and end apart: 21, of which 11 were waited for; matrix products, arithmetic and copies ran while one was open for 0% of the time, Pallas kernels for 14%

profile of v9, /device:TPU:0, one launch (start us, length us, event | category | flops | bytes accessed | tf_op | source)
XLA Modules:
  0.0 53.2 jit_solution(16747360817096406898)
XLA Ops:
  0.6 3.0 %collective-permute-start = (bf16[128,256]{1,0:T(8,128)(2,1)}, bf16[128,256]{1,0:T(8,128)(2,1)S(1)}, u32[]{:S(2)}, u32[]{:S(2)}) collective-permute-start(bf16[128,256]{1,0:T(8,128)(2,1)} %bitcast.8), channel_id=1, source_target_pairs={{0,1},{1,0},{2,3},{3,2},{4,5},{5,4},{6,7},{7,6},{8,9},{9,8},{10,11... | collective-permute-start | bytes 196616 | tf_op jit(solution)/shard_map/ppermute | solution.py:468
  3.6 2.0 %collective-permute-start.4 = (bf16[128,128]{1,0:T(8,128)(2,1)}, bf16[128,128]{1,0:T(8,128)(2,1)S(1)}, u32[]{:S(2)}, u32[]{:S(2)}) collective-permute-start(bf16[128,128]{1,0:T(8,128)(2,1)} %bitcast.11), channel_id=1, source_target_pairs={{0,4},{4,8},{8,12},{12,16},{16,20},{20,24},{24,28},{6,2},{10,6},{1... | collective-permute-start | bytes 98312 | tf_op jit(solution)/shard_map/ppermute | solution.py:495
  5.7 0.9 %copy-done.2 = bf16[256,512]{1,0:T(8,128)(2,1)S(1)} copy-done((bf16[256,512]{1,0:T(8,128)(2,1)S(1)}, bf16[256,512]{1,0:T(8,128)(2,1)}, u32[]{:S(2)}) %copy-start.2) | copy-done | bytes 262168
  6.6 0.8 %copy-done.3 = bf16[1,128,256]{2,1,0:T(8,128)(2,1)S(1)} copy-done((bf16[1,128,256]{2,1,0:T(8,128)(2,1)S(1)}, bf16[1,128,256]{2,1,0:T(8,128)(2,1)}, u32[]{:S(2)}) %copy-start.3) | copy-done | bytes 65560
  7.6 1.3 %attention_forward.1 = (bf16[256,256]{1,0:T(8,128)(2,1)S(1)}, bf16[256,768]{1,0:T(8,128)(2,1)S(1)}, f32[8,256]{1,0:T(8,128)S(1)}) custom-call(bf16[128,256]{1,0:T(8,128)(2,1)S(1)} %get-tuple-element.53.refs_0_, bf16[128,256]{1,0:T(8,128)(2,1)S(1)} %collective-permute-done.refs_1_, bf16[256,512]{1,0:T(8,128)(2,1)S(1)} %get-tuple-element.54.refs_2_.projection), custom_call_target="tpu_custom_call" | custom-call | flops 1000000000 | bytes 4000000 | tf_op jit(solution)/shard_map/attention_forward/pallas_call | solution.py:477
  10.4 2.0 %collective-permute-start.8 = (bf16[256,128]{1,0:T(8,128)(2,1)S(1)}, bf16[256,128]{1,0:T(8,128)(2,1)S(1)}, u32[]{:S(2)}, u32[]{:S(2)}) collective-permute-start(bf16[256,128]{1,0:T(8,128)(2,1)S(1)} %get-tuple-element.70), channel_id=1, source_target_pairs={{0,4},{4,8},{8,12},{12,16},{16,20},{20,24},{24,28},{6,2},{10,6},{1... | collective-permute-start | bytes 196616 | tf_op jit(solution)/shard_map/ppermute | solution.py:529
  14.5 1.1 %collective-permute-start.7 = (bf16[2,256,128]{2,1,0:T(8,128)(2,1)S(1)}, bf16[2,256,128]{2,1,0:T(8,128)(2,1)S(1)}, u32[]{:S(2)}, u32[]{:S(2)}) collective-permute-start(bf16[2,256,128]{2,1,0:T(8,128)(2,1)S(1)} %get-tuple-element.62.pair_cot), channel_id=1, source_target_pairs={{0,2},{2,0},{4,6},{6,4},{8,10},{10,8},{12,14},{14,12},{16,18},{18,... | collective-permute-start | bytes 393224 | tf_op jit(solution)/shard_map/ppermute | solution.py:465
  17.2 2.3 %block_backward.1 = (bf16[256,256]{1,0:T(8,128)(2,1)S(1)}, bf16[256,256]{1,0:T(8,128)(2,1)S(1)}, bf16[512,256]{1,0:T(8,128)(2,1)S(1)}, bf16[2,128,128]{2,1,0:T(8,128)(2,1)S(1)}, bf16[2,128,128]{2,1,0:T(8,128)(2,1)S(1)}) custom-call(bf16[256,256]{1,0:T(8,128)(2,1)S(1)} %collective-permute-done.2.near, ...), custom_call_target="tpu_custom_call" | custom-call | flops 1000000000 | bytes 4000000 | tf_op jit(solution)/shard_map/block_backward/pallas_call | solution.py:477
  19.7 0.8 %conv_grads.1 = (bf16[432,128]{1,0:T(8,128)(2,1)S(1)}, bf16[432,128]{1,0:T(8,128)(2,1)S(1)}) custom-call(bf16[256,256]{1,0:T(8,128)(2,1)S(1)} %collective-permute-done.2.near, bf16[256,256]{1,0:T(8,128)(2,1)S(1)} %get-tuple-element.55.attended.own, bf16[256,256]{1,0:T(8,128)(2,1)S(1)} %collective-permute-done.3.mate, ...), custom_call_target="tpu_custom_call" | custom-call | flops 1000000000 | bytes 4000000 | tf_op jit(solution)/shard_map/conv_grads/pallas_call | solution.py:477
  20.9 3.0 %collective-permute-start.10 = (bf16[560,128]{1,0:T(8,128)(2,1)S(1)}, bf16[560,128]{1,0:T(8,128)(2,1)S(1)}, u32[]{:S(2)}, u32[]{:S(2)}) collective-permute-start(bf16[560,128]{1,0:T(8,128)(2,1)S(1)} %pad_maximum_fusion), channel_id=1, source_target_pairs={{0,8},{2,10},{4,12},{6,14},{8,0},{10,2},{12,4},{14,6},{16,24},{18,... | collective-permute-start | bytes 430088 | tf_op jit(solution)/shard_map/ppermute | solution.py:465
  23.9 1.0 %collective-permute-start.12 = (bf16[560,128]{1,0:T(8,128)(2,1)S(1)}, bf16[560,128]{1,0:T(8,128)(2,1)S(1)}, u32[]{:S(2)}, u32[]{:S(2)}) collective-permute-start(bf16[560,128]{1,0:T(8,128)(2,1)S(1)} %pad_maximum_fusion.1), channel_id=1, source_target_pairs={{0,12},{2,14},{4,8},{6,10},{8,4},{10,6},{12,0},{14,2},{16,28},{18,... | collective-permute-start | bytes 430088 | tf_op jit(solution)/shard_map/ppermute | solution.py:465
  25.4 3.0 %collective-permute-done.10 = bf16[560,128]{1,0:T(8,128)(2,1)S(1)} collective-permute-done((bf16[560,128]{1,0:T(8,128)(2,1)S(1)}, bf16[560,128]{1,0:T(8,128)(2,1)S(1)}, u32[]{:S(2)}, u32[]{:S(2)}) %collective-permute-start.10) | collective-permute-done | bytes 143392 | tf_op jit(solution)/shard_map/ppermute | solution.py:465
  28.4 3.4 %collective-permute-done.12 = bf16[560,128]{1,0:T(8,128)(2,1)S(1)} collective-permute-done((bf16[560,128]{1,0:T(8,128)(2,1)S(1)}, bf16[560,128]{1,0:T(8,128)(2,1)S(1)}, u32[]{:S(2)}, u32[]{:S(2)}) %collective-permute-start.12) | collective-permute-done | bytes 143392 | tf_op jit(solution)/shard_map/ppermute | solution.py:465
  31.8 1.4 %collective-permute-done.11 = bf16[560,128]{1,0:T(8,128)(2,1)S(1)} collective-permute-done((bf16[560,128]{1,0:T(8,128)(2,1)S(1)}, bf16[560,128]{1,0:T(8,128)(2,1)S(1)}, u32[]{:S(2)}, u32[]{:S(2)}) %collective-permute-start.11) | collective-permute-done | bytes 143392 | tf_op jit(solution)/shard_map/ppermute | solution.py:465
  33.3 2.7 %collective-permute-start.13 = (bf16[560,128]{1,0:T(8,128)(2,1)S(1)}, bf16[560,128]{1,0:T(8,128)(2,1)S(1)}, u32[]{:S(2)}, u32[]{:S(2)}) collective-permute-start(bf16[560,128]{1,0:T(8,128)(2,1)S(1)} %add_convert_fusion.1), channel_id=1, source_target_pairs={{0,16},{2,18},{4,20},{6,22},{8,24},{10,26},{12,28},{14,30},{16,0},... | collective-permute-start | bytes 430088 | tf_op jit(solution)/shard_map/ppermute | solution.py:465
  36.0 1.2 %outputs.1 = (bf16[128,128]{1,0:T(8,128)(2,1)}, bf16[128,256]{1,0:T(8,128)(2,1)}) custom-call(bf16[256,256]{1,0:T(8,128)(2,1)S(1)} %get-tuple-element.88.near_mid, bf16[256,256]{1,0:T(8,128)(2,1)S(1)} %get-tuple-element.83.own_mid, bf16[256,256]{1,0:T(8,128)(2,1)S(1)} %get-tuple-element.69.mate_mid, bf16[512,256]{1,0:T(8,128)(2,1)S(1)} %get-tuple-element.89.grad, ...), custom_call_target="tpu_custom_call" | custom-call | flops 1000000000 | bytes 4000000 | tf_op jit(solution)/shard_map/outputs/pallas_call | solution.py:477
  37.2 4.9 %collective-permute-done.13 = bf16[560,128]{1,0:T(8,128)(2,1)S(1)} collective-permute-done((bf16[560,128]{1,0:T(8,128)(2,1)S(1)}, bf16[560,128]{1,0:T(8,128)(2,1)S(1)}, u32[]{:S(2)}, u32[]{:S(2)}) %collective-permute-start.13) | collective-permute-done | bytes 143392 | tf_op jit(solution)/shard_map/ppermute | solution.py:465
  42.1 1.6 %collective-permute-start.19 = (bf16[560,128]{1,0:T(8,128)(2,1)S(1)}, bf16[560,128]{1,0:T(8,128)(2,1)S(1)}, u32[]{:S(2)}, u32[]{:S(2)}) collective-permute-start(bf16[560,128]{1,0:T(8,128)(2,1)S(1)} %add_convert_fusion.refs_0_), channel_id=1, source_target_pairs={{0,5},{1,4},{2,7},{3,6},{4,1},{5,0},{6,3},{7,2},{8,13},{9,12},{10,... | collective-permute-start | bytes 430088 | tf_op jit(solution)/shard_map/ppermute | solution.py:626
  43.7 0.8 %collective-permute-start.17 = (bf16[560,128]{1,0:T(8,128)(2,1)S(1)}, bf16[560,128]{1,0:T(8,128)(2,1)S(1)}, u32[]{:S(2)}, u32[]{:S(2)}) collective-permute-start(bf16[560,128]{1,0:T(8,128)(2,1)S(1)} %add_convert_fusion.refs_0_), channel_id=1, source_target_pairs={{0,1},{1,0},{2,3},{3,2},{4,5},{5,4},{6,7},{7,6},{8,9},{9,8},{10,11... | collective-permute-start | bytes 430088 | tf_op jit(solution)/shard_map/ppermute | solution.py:468
  44.5 1.1 %collective-permute-start.15 = (bf16[560,128]{1,0:T(8,128)(2,1)S(1)}, bf16[560,128]{1,0:T(8,128)(2,1)S(1)}, u32[]{:S(2)}, u32[]{:S(2)}) collective-permute-start(bf16[560,128]{1,0:T(8,128)(2,1)S(1)} %add_convert_fusion.refs_0_), channel_id=1, source_target_pairs={{0,4},{2,6},{4,0},{6,2},{8,12},{10,14},{12,8},{14,10},{16,20},{18,... | collective-permute-start | bytes 430088 | tf_op jit(solution)/shard_map/ppermute | solution.py:465
  45.7 3.6 %collective-permute-done.19.refs_3_ = bf16[560,128]{1,0:T(8,128)(2,1)S(1)} collective-permute-done((bf16[560,128]{1,0:T(8,128)(2,1)S(1)}, bf16[560,128]{1,0:T(8,128)(2,1)S(1)}, u32[]{:S(2)}, u32[]{:S(2)}) %collective-permute-start.19) | collective-permute-done | bytes 143392 | tf_op jit(solution)/shard_map/ppermute | solution.py:626
  49.3 0.8 %collective-permute-done.17.refs_2_ = bf16[560,128]{1,0:T(8,128)(2,1)S(1)} collective-permute-done((bf16[560,128]{1,0:T(8,128)(2,1)S(1)}, bf16[560,128]{1,0:T(8,128)(2,1)S(1)}, u32[]{:S(2)}, u32[]{:S(2)}) %collective-permute-start.17) | collective-permute-done | bytes 143392 | tf_op jit(solution)/shard_map/ppermute | solution.py:468
  50.7 1.1 %unpack_sums.2 = (f32[256,512]{1,0:T(8,128)}, f32[3,3,256,128]{3,2,1,0:T(8,128)}, f32[3,3,128,128]{3,2,1,0:T(8,128)}) custom-call(bf16[560,128]{1,0:T(8,128)(2,1)S(1)} %add_convert_fusion.refs_0_, bf16[560,128]{1,0:T(8,128)(2,1)S(1)} %collective-permute-done.15.refs_1_, bf16[560,128]{1,0:T(8,128)(2,1)S(1)} %collective-permute-done.17.refs_2_, ...), custom_call_target="tpu_custom_call" | custom-call | flops 1000000000 | bytes 4194304 | tf_op jit(solution)/shard_map/unpack_sums/pallas_call | solution.py:432
  52.1 1.1 %unpack_sums.3 = (f32[256,512]{1,0:T(8,128)}, f32[3,3,256,128]{3,2,1,0:T(8,128)}, f32[3,3,128,128]{3,2,1,0:T(8,128)}) custom-call(bf16[560,128]{1,0:T(8,128)(2,1)S(1)} %collective-permute-done.14.refs_0_, bf16[560,128]{1,0:T(8,128)(2,1)S(1)} %collective-permute-done.16.refs_1_, ...), custom_call_target="tpu_custom_call", output_to_operand_aliasing={{0}: (4, {}), {1}: (5, {}), {2}: (6, {})} | custom-call | flops 1000000000 | bytes 4194304 | tf_op jit(solution)/shard_map/unpack_sums/pallas_call | solution.py:432
  (50 shorter events, 7.2 us)
Async XLA Ops:
  0.6 7.0 %collective-permute-start = (bf16[128,256]{1,0:T(8,128)(2,1)}, bf16[128,256]{1,0:T(8,128)(2,1)S(1)}, u32[]{:S(2)}, u32[]{:S(2)}) collective-permute-start(bf16[128,256]{1,0:T(8,128)(2,1)} %bitcast.8), channel_id=1, source_target_pairs={{0,1},{1,0},{2,3},{3,2},{4,5},{5,4},{6,7},{7,6},{8,9},{9,8},{10,11... | collective-permute-start | bytes 196616 | tf_op jit(solution)/shard_map/ppermute | solution.py:468
  3.6 5.9 %collective-permute-start.5 = (bf16[128,128]{1,0:T(8,128)(2,1)}, bf16[128,128]{1,0:T(8,128)(2,1)S(1)}, u32[]{:S(2)}, u32[]{:S(2)}) collective-permute-start(bf16[128,128]{1,0:T(8,128)(2,1)} %bitcast.10), channel_id=1, source_target_pairs={{4,0},{8,4},{12,8},{16,12},{20,16},{24,20},{28,24},{2,6},{6,10},{1... | collective-permute-start | bytes 98312 | tf_op jit(solution)/shard_map/ppermute | solution.py:496
  3.6 5.9 %collective-permute-start.4 = (bf16[128,128]{1,0:T(8,128)(2,1)}, bf16[128,128]{1,0:T(8,128)(2,1)S(1)}, u32[]{:S(2)}, u32[]{:S(2)}) collective-permute-start(bf16[128,128]{1,0:T(8,128)(2,1)} %bitcast.11), channel_id=1, source_target_pairs={{0,4},{4,8},{8,12},{12,16},{16,20},{20,24},{24,28},{6,2},{10,6},{1... | collective-permute-start | bytes 98312 | tf_op jit(solution)/shard_map/ppermute | solution.py:495
  7.6 2.0 %copy-start = (bf16[3,3,256,128]{3,2,1,0:T(8,128)(2,1)S(1)}, bf16[3,3,256,128]{3,2,1,0:T(8,128)(2,1)}, u32[]{:S(2)}) copy-start(bf16[3,3,256,128]{3,2,1,0:T(8,128)(2,1)} %refs_0_.3) | copy-start | bytes 1769476
  7.6 2.0 %copy-start.4 = (bf16[1,128,128]{2,1,0:T(8,128)(2,1)S(1)}, bf16[1,128,128]{2,1,0:T(8,128)(2,1)}, u32[]{:S(2)}) copy-start(bf16[1,128,128]{2,1,0:T(8,128)(2,1)} %param.9) | copy-start | bytes 98308
  9.0 3.5 %copy-start.1 = (bf16[3,3,128,128]{3,2,1,0:T(8,128)(2,1)S(1)}, bf16[3,3,128,128]{3,2,1,0:T(8,128)(2,1)}, u32[]{:S(2)}) copy-start(bf16[3,3,128,128]{3,2,1,0:T(8,128)(2,1)} %refs_1_.1) | copy-start | bytes 884740
  9.0 4.7 %collective-permute-start.3 = (bf16[256,256]{1,0:T(8,128)(2,1)S(1)}, bf16[256,256]{1,0:T(8,128)(2,1)S(1)}, u32[]{:S(2)}, u32[]{:S(2)}) collective-permute-start(bf16[256,256]{1,0:T(8,128)(2,1)S(1)} %get-tuple-element.55.attended.own), channel_id=1, source_target_pairs={{0,2},{2,0},{4,6},{6,4},{8,10},{10,8},{12,14},{14,12},{16,18},{18,... | collective-permute-start | bytes 393224 | tf_op jit(solution)/shard_map/ppermute | solution.py:465
  9.0 6.5 %collective-permute-start.1 = (bf16[256,256]{1,0:T(8,128)(2,1)S(1)}, bf16[256,256]{1,0:T(8,128)(2,1)S(1)}, u32[]{:S(2)}, u32[]{:S(2)}) collective-permute-start(bf16[256,256]{1,0:T(8,128)(2,1)S(1)} %get-tuple-element.55.attended.own), channel_id=1, source_target_pairs={{4,0},{8,4},{12,8},{16,12},{20,16},{24,20},{28,24},{2,6},{6,10},{1... | collective-permute-start | bytes 393224 | tf_op jit(solution)/shard_map/ppermute | solution.py:524
  9.8 4.7 %collective-permute-start.6 = (bf16[3,128,128]{2,1,0:T(8,128)(2,1)S(1)}, bf16[3,128,128]{2,1,0:T(8,128)(2,1)S(1)}, u32[]{:S(2)}, u32[]{:S(2)}) collective-permute-start(bf16[3,128,128]{2,1,0:T(8,128)(2,1)S(1)} %get-tuple-element.60.refs_0_), channel_id=1, source_target_pairs={{0,1},{1,0},{2,3},{3,2},{4,5},{5,4},{6,7},{7,6},{8,9},{9,8},{10,11... | collective-permute-start | bytes 294920 | tf_op jit(solution)/shard_map/ppermute | solution.py:468
  10.4 6.0 %collective-permute-start.8 = (bf16[256,128]{1,0:T(8,128)(2,1)S(1)}, bf16[256,128]{1,0:T(8,128)(2,1)S(1)}, u32[]{:S(2)}, u32[]{:S(2)}) collective-permute-start(bf16[256,128]{1,0:T(8,128)(2,1)S(1)} %get-tuple-element.70), channel_id=1, source_target_pairs={{0,4},{4,8},{8,12},{12,16},{16,20},{20,24},{24,28},{6,2},{10,6},{1... | collective-permute-start | bytes 196616 | tf_op jit(solution)/shard_map/ppermute | solution.py:529
  14.5 2.3 %collective-permute-start.7 = (bf16[2,256,128]{2,1,0:T(8,128)(2,1)S(1)}, bf16[2,256,128]{2,1,0:T(8,128)(2,1)S(1)}, u32[]{:S(2)}, u32[]{:S(2)}) collective-permute-start(bf16[2,256,128]{2,1,0:T(8,128)(2,1)S(1)} %get-tuple-element.62.pair_cot), channel_id=1, source_target_pairs={{0,2},{2,0},{4,6},{6,4},{8,10},{10,8},{12,14},{14,12},{16,18},{18,... | collective-permute-start | bytes 393224 | tf_op jit(solution)/shard_map/ppermute | solution.py:465
  15.6 1.6 %collective-permute-start.2 = (bf16[256,256]{1,0:T(8,128)(2,1)S(1)}, bf16[256,256]{1,0:T(8,128)(2,1)S(1)}, u32[]{:S(2)}, u32[]{:S(2)}) collective-permute-start(bf16[256,256]{1,0:T(8,128)(2,1)S(1)} %collective-permute-done.1.mate1), channel_id=1, source_target_pairs={{0,2},{2,0},{4,6},{6,4},{8,10},{10,8},{12,14},{14,12},{16,18},{18,... | collective-permute-start | bytes 393224 | tf_op jit(solution)/shard_map/ppermute | solution.py:465
  19.5 1.3 %collective-permute-start.9 = (bf16[2,128,128]{2,1,0:T(8,128)(2,1)S(1)}, bf16[2,128,128]{2,1,0:T(8,128)(2,1)S(1)}, u32[]{:S(2)}, u32[]{:S(2)}) collective-permute-start(bf16[2,128,128]{2,1,0:T(8,128)(2,1)S(1)} %get-tuple-element.86), channel_id=1, source_target_pairs={{0,2},{2,0},{4,6},{6,4},{8,10},{10,8},{12,14},{14,12},{16,18},{18,... | collective-permute-start | bytes 196616 | tf_op jit(solution)/shard_map/ppermute | solution.py:465
  20.9 7.5 %collective-permute-start.10 = (bf16[560,128]{1,0:T(8,128)(2,1)S(1)}, bf16[560,128]{1,0:T(8,128)(2,1)S(1)}, u32[]{:S(2)}, u32[]{:S(2)}) collective-permute-start(bf16[560,128]{1,0:T(8,128)(2,1)S(1)} %pad_maximum_fusion), channel_id=1, source_target_pairs={{0,8},{2,10},{4,12},{6,14},{8,0},{10,2},{12,4},{14,6},{16,24},{18,... | collective-permute-start | bytes 430088 | tf_op jit(solution)/shard_map/ppermute | solution.py:465
  23.9 7.9 %collective-permute-start.12 = (bf16[560,128]{1,0:T(8,128)(2,1)S(1)}, bf16[560,128]{1,0:T(8,128)(2,1)S(1)}, u32[]{:S(2)}, u32[]{:S(2)}) collective-permute-start(bf16[560,128]{1,0:T(8,128)(2,1)S(1)} %pad_maximum_fusion.1), channel_id=1, source_target_pairs={{0,12},{2,14},{4,8},{6,10},{8,4},{10,6},{12,0},{14,2},{16,28},{18,... | collective-permute-start | bytes 430088 | tf_op jit(solution)/shard_map/ppermute | solution.py:465
  24.9 8.3 %collective-permute-start.11 = (bf16[560,128]{1,0:T(8,128)(2,1)S(1)}, bf16[560,128]{1,0:T(8,128)(2,1)S(1)}, u32[]{:S(2)}, u32[]{:S(2)}) collective-permute-start(bf16[560,128]{1,0:T(8,128)(2,1)S(1)} %pad_maximum_fusion.1), channel_id=1, source_target_pairs={{0,4},{2,6},{4,0},{6,2},{8,12},{10,14},{12,8},{14,10},{16,20},{18,... | collective-permute-start | bytes 430088 | tf_op jit(solution)/shard_map/ppermute | solution.py:465
  33.3 8.7 %collective-permute-start.13 = (bf16[560,128]{1,0:T(8,128)(2,1)S(1)}, bf16[560,128]{1,0:T(8,128)(2,1)S(1)}, u32[]{:S(2)}, u32[]{:S(2)}) collective-permute-start(bf16[560,128]{1,0:T(8,128)(2,1)S(1)} %add_convert_fusion.1), channel_id=1, source_target_pairs={{0,16},{2,18},{4,20},{6,22},{8,24},{10,26},{12,28},{14,30},{16,0},... | collective-permute-start | bytes 430088 | tf_op jit(solution)/shard_map/ppermute | solution.py:465
  42.1 7.2 %collective-permute-start.19 = (bf16[560,128]{1,0:T(8,128)(2,1)S(1)}, bf16[560,128]{1,0:T(8,128)(2,1)S(1)}, u32[]{:S(2)}, u32[]{:S(2)}) collective-permute-start(bf16[560,128]{1,0:T(8,128)(2,1)S(1)} %add_convert_fusion.refs_0_), channel_id=1, source_target_pairs={{0,5},{1,4},{2,7},{3,6},{4,1},{5,0},{6,3},{7,2},{8,13},{9,12},{10,... | collective-permute-start | bytes 430088 | tf_op jit(solution)/shard_map/ppermute | solution.py:626
  43.7 6.4 %collective-permute-start.17 = (bf16[560,128]{1,0:T(8,128)(2,1)S(1)}, bf16[560,128]{1,0:T(8,128)(2,1)S(1)}, u32[]{:S(2)}, u32[]{:S(2)}) collective-permute-start(bf16[560,128]{1,0:T(8,128)(2,1)S(1)} %add_convert_fusion.refs_0_), channel_id=1, source_target_pairs={{0,1},{1,0},{2,3},{3,2},{4,5},{5,4},{6,7},{7,6},{8,9},{9,8},{10,11... | collective-permute-start | bytes 430088 | tf_op jit(solution)/shard_map/ppermute | solution.py:468
  44.5 6.2 %collective-permute-start.15 = (bf16[560,128]{1,0:T(8,128)(2,1)S(1)}, bf16[560,128]{1,0:T(8,128)(2,1)S(1)}, u32[]{:S(2)}, u32[]{:S(2)}) collective-permute-start(bf16[560,128]{1,0:T(8,128)(2,1)S(1)} %add_convert_fusion.refs_0_), channel_id=1, source_target_pairs={{0,4},{2,6},{4,0},{6,2},{8,12},{10,14},{12,8},{14,10},{16,20},{18,... | collective-permute-start | bytes 430088 | tf_op jit(solution)/shard_map/ppermute | solution.py:465
  45.7 6.2 %collective-permute-start.14 = (bf16[560,128]{1,0:T(8,128)(2,1)S(1)}, bf16[560,128]{1,0:T(8,128)(2,1)S(1)}, u32[]{:S(2)}, u32[]{:S(2)}) collective-permute-start(bf16[560,128]{1,0:T(8,128)(2,1)S(1)} %add_convert_fusion.refs_0_), channel_id=1, source_target_pairs={{0,2},{2,0},{4,6},{6,4},{8,10},{10,8},{12,14},{14,12},{16,18},{18,... | collective-permute-start | bytes 430088 | tf_op jit(solution)/shard_map/ppermute | solution.py:465
  49.3 2.5 %collective-permute-start.20 = (bf16[560,128]{1,0:T(8,128)(2,1)S(1)}, bf16[560,128]{1,0:T(8,128)(2,1)S(1)}, u32[]{:S(2)}, u32[]{:S(2)}) collective-permute-start(bf16[560,128]{1,0:T(8,128)(2,1)S(1)} %collective-permute-done.19.refs_3_), channel_id=1, source_target_pairs={{0,2},{2,0},{4,6},{6,4},{8,10},{10,8},{12,14},{14,12},{16,18},{18,... | collective-permute-start | bytes 430088 | tf_op jit(solution)/shard_map/ppermute | solution.py:465
  50.1 1.7 %collective-permute-start.18 = (bf16[560,128]{1,0:T(8,128)(2,1)S(1)}, bf16[560,128]{1,0:T(8,128)(2,1)S(1)}, u32[]{:S(2)}, u32[]{:S(2)}) collective-permute-start(bf16[560,128]{1,0:T(8,128)(2,1)S(1)} %collective-permute-done.17.refs_2_), channel_id=1, source_target_pairs={{0,2},{2,0},{4,6},{6,4},{8,10},{10,8},{12,14},{14,12},{16,18},{18,... | collective-permute-start | bytes 430088 | tf_op jit(solution)/shard_map/ppermute | solution.py:465
  50.7 1.4 %collective-permute-start.16 = (bf16[560,128]{1,0:T(8,128)(2,1)S(1)}, bf16[560,128]{1,0:T(8,128)(2,1)S(1)}, u32[]{:S(2)}, u32[]{:S(2)}) collective-permute-start(bf16[560,128]{1,0:T(8,128)(2,1)S(1)} %collective-permute-done.15.refs_1_), channel_id=1, source_target_pairs={{0,2},{2,0},{4,6},{6,4},{8,10},{10,8},{12,14},{14,12},{16,18},{18,... | collective-permute-start | bytes 430088 | tf_op jit(solution)/shard_map/ppermute | solution.py:465
  (2 other events, 1.8 us)

commit v10 on v9

--- a/solution.py
+++ b/solution.py
@@ -103,7 +103,7 @@
 
 
 def forward_kernel(count, *refs):
-    projection, attended, local, lse, values_t = refs[count:]
+    projection, attended, local, stats, values_t = refs[count:]
     across = attended.shape[0]
     lay_out(refs[:count], local, slice(PACKED, None))
     packed = mm(local[:, PACKED:], projection[...]).astype(BF)
@@ -123,7 +123,8 @@
             totals = jnp.sum(exponent, axis=0, keepdims=True)
             weighted = mm(values_t[head * HEAD_VAL : (head + 1) * HEAD_VAL, :], exponent.astype(BF))
             rows.append((weighted * (1.0 / totals)).astype(BF))
-            lse[head : head + 1, at] = maxima * EXP2_SCALING + jnp.log2(totals)
+            stats[head : head + 1, at] = maxima
+            stats[HEADS + head : HEADS + head + 1, at] = jnp.log2(totals)
         attended[at, :] = mm_t(identity(BLOCK), jnp.concatenate(rows, axis=0)).astype(BF)
 
     for_blocks(across // BLOCK, block)
@@ -189,7 +190,7 @@
         second_t[a] = mm_t(eye, place.stacked(second_kernel, a)).astype(BF)
 
 
-def prepare_kernel(own, local, lse, soft, keys_t, queries_t, attended_t, features_t, values):
+def prepare_kernel(own, local, stats, soft, keys_t, queries_t, attended_t, features_t, values):
     place = Place()
     across = own.shape[0]
     keys = local[:, QK : 2 * QK]
@@ -207,7 +208,8 @@
         scores = mm_t(jnp.concatenate([head_of(keys, h, HEAD_QK) for h in range(HEADS)], axis=0), queries)
         for head in range(HEADS):
             rows = slice(head * across, (head + 1) * across)
-            soft[rows, at] = jnp.exp2(scores[rows, :] * EXP2_SCALING - lse[head : head + 1, at]).astype(BF)
+            below = (scores[rows, :] - stats[head : head + 1, at]) * EXP2_SCALING
+            soft[rows, at] = jnp.exp2(below - stats[HEADS + head : HEADS + head + 1, at]).astype(BF)
 
     for_blocks(across // BLOCK, block)
 
@@ -500,9 +502,9 @@
         out_cot = lax.ppermute(cotangent, "rows", out)
         back_cot = lax.ppermute(cotangent, "rows", back)
         features = (lax.all_gather(features, "cols", axis=0, tiled=True),)
-    own, local, lse = call(
+    own, local, stats = call(
         functools.partial(forward_kernel, len(features)),
-        (shape(across, VAL), shape(across, PACKED + channels), shape(HEADS, across, dtype=F32)),
+        (shape(across, VAL), shape(across, PACKED + channels), shape(2 * HEADS, across, dtype=F32)),
         (*features, projection),
         (pltpu.VMEM((VAL, across), BF),),
         name="attention_forward",
@@ -513,7 +515,7 @@
         (own, first_kernel, out_cot, cotangent, back_cot),
         name="rows",
     )
-    first_kernel, second_kernel = fetch((first_kernel, second_kernel), (lse,), 10**4)
+    first_kernel, second_kernel = fetch((first_kernel, second_kernel), (stats,), 10**4)
     first_t, second_t = call(
         turn_kernel,
         (shape(3 * CONV, 3 * VAL), shape(3, CONV, 3 * CONV)),
@@ -552,7 +554,7 @@
             shape(VAL // 2, across),
             shape(HEADS * across, VAL),
         ),
-        (own, local, lse),
+        (own, local, stats),
         name="prepare",
         flops=10**6,
     )

time: 53.4 us -> 53.4 us (level)
  no operation moved by 1% of the time
where the time goes in v10:
time: 53.4 us; the launch traced here: 53.2 us
  starting transfers between devices  20.3 us (38%)
  waiting for transfers between devices  19.3 us (36%)
  Pallas kernels  10.7 us (20%)
  local copies, waits for them, and re-layouts  1.81 us (3%)
  between operations  0.88 us (2%)
    ppermute x13, waiting for transfers between devices, rows_flip(): lax.ppermute(values, 'rows', [(i, i ^ bit) for i in range(rows_size)])  13.9 us
    ppermute x13, starting transfers between devices, rows_flip(): lax.ppermute(values, 'rows', [(i, i ^ bit) for i in range(rows_size)])  9.75 us
    pallas_call x12, Pallas kernels, call(): pl.pallas_call(kernel, out_shape=out_shape, in_specs=[VMEM] * len(operand...  8.24 us
    ppermute x3, starting transfers between devices, cols_flip(): return lax.ppermute(values, 'cols', [(i, i ^ 1) for i in range(cols_size)])  4.38 us
    ppermute x1, waiting for transfers between devices, body(): lax.ppermute(total, ('rows', 'cols'), [(i * cols_size + j, (i ^ 2) * cols...  3.65 us
    pallas_call x2, Pallas kernels, unpack(): pl.pallas_call(functools.partial(unpack_kernel, factor, core_flip), out_s...  2.16 us
    ppermute x1, starting transfers between devices, body(): far = lax.ppermute(term, 'rows', out)  2.04 us
    ppermute x1, starting transfers between devices, body(): out_cot = lax.ppermute(cotangent, 'rows', out)  2.02 us
  transfers between devices with their start and end apart: 21, of which 11 were waited for; matrix products, arithmetic and copies ran while one was open for 0% of the time, Pallas kernels for 14%

profile of v10, /device:TPU:0, one launch (start us, length us, event | category | flops | bytes accessed | tf_op | source)
XLA Modules:
  0.0 53.2 jit_solution(7043520686090183023)
XLA Ops:
  0.6 3.0 %collective-permute-start = (bf16[128,256]{1,0:T(8,128)(2,1)}, bf16[128,256]{1,0:T(8,128)(2,1)S(1)}, u32[]{:S(2)}, u32[]{:S(2)}) collective-permute-start(bf16[128,256]{1,0:T(8,128)(2,1)} %bitcast.8), channel_id=1, source_target_pairs={{0,1},{1,0},{2,3},{3,2},{4,5},{5,4},{6,7},{7,6},{8,9},{9,8},{10,11... | collective-permute-start | bytes 196616 | tf_op jit(solution)/shard_map/ppermute | solution.py:470
  3.6 2.0 %collective-permute-start.4 = (bf16[128,128]{1,0:T(8,128)(2,1)}, bf16[128,128]{1,0:T(8,128)(2,1)S(1)}, u32[]{:S(2)}, u32[]{:S(2)}) collective-permute-start(bf16[128,128]{1,0:T(8,128)(2,1)} %bitcast.11), channel_id=1, source_target_pairs={{0,4},{4,8},{8,12},{12,16},{16,20},{20,24},{24,28},{6,2},{10,6},{1... | collective-permute-start | bytes 98312 | tf_op jit(solution)/shard_map/ppermute | solution.py:497
  5.7 0.9 %copy-done.2 = bf16[256,512]{1,0:T(8,128)(2,1)S(1)} copy-done((bf16[256,512]{1,0:T(8,128)(2,1)S(1)}, bf16[256,512]{1,0:T(8,128)(2,1)}, u32[]{:S(2)}) %copy-start.2) | copy-done | bytes 262168
  6.6 0.8 %copy-done.3 = bf16[1,128,256]{2,1,0:T(8,128)(2,1)S(1)} copy-done((bf16[1,128,256]{2,1,0:T(8,128)(2,1)S(1)}, bf16[1,128,256]{2,1,0:T(8,128)(2,1)}, u32[]{:S(2)}) %copy-start.3) | copy-done | bytes 65560
  7.6 1.3 %attention_forward.1 = (bf16[256,256]{1,0:T(8,128)(2,1)S(1)}, bf16[256,768]{1,0:T(8,128)(2,1)S(1)}, f32[16,256]{1,0:T(8,128)S(1)}) custom-call(bf16[128,256]{1,0:T(8,128)(2,1)S(1)} %get-tuple-element.53.refs_0_, bf16[128,256]{1,0:T(8,128)(2,1)S(1)} %collective-permute-done.refs_1_, bf16[256,512]{1,0:T(8,128)(2,1)S(1)} %get-tuple-element.54.refs_2_.projection), custom_call_target="tpu_custom_call" | custom-call | flops 1000000000 | bytes 4000000 | tf_op jit(solution)/shard_map/attention_forward/pallas_call | solution.py:479
  10.4 2.0 %collective-permute-start.8 = (bf16[256,128]{1,0:T(8,128)(2,1)S(1)}, bf16[256,128]{1,0:T(8,128)(2,1)S(1)}, u32[]{:S(2)}, u32[]{:S(2)}) collective-permute-start(bf16[256,128]{1,0:T(8,128)(2,1)S(1)} %get-tuple-element.70), channel_id=1, source_target_pairs={{0,4},{4,8},{8,12},{12,16},{16,20},{20,24},{24,28},{6,2},{10,6},{1... | collective-permute-start | bytes 196616 | tf_op jit(solution)/shard_map/ppermute | solution.py:531
  14.5 1.1 %collective-permute-start.7 = (bf16[2,256,128]{2,1,0:T(8,128)(2,1)S(1)}, bf16[2,256,128]{2,1,0:T(8,128)(2,1)S(1)}, u32[]{:S(2)}, u32[]{:S(2)}) collective-permute-start(bf16[2,256,128]{2,1,0:T(8,128)(2,1)S(1)} %get-tuple-element.62.pair_cot), channel_id=1, source_target_pairs={{0,2},{2,0},{4,6},{6,4},{8,10},{10,8},{12,14},{14,12},{16,18},{18,... | collective-permute-start | bytes 393224 | tf_op jit(solution)/shard_map/ppermute | solution.py:467
  17.2 2.3 %block_backward.1 = (bf16[256,256]{1,0:T(8,128)(2,1)S(1)}, bf16[256,256]{1,0:T(8,128)(2,1)S(1)}, bf16[512,256]{1,0:T(8,128)(2,1)S(1)}, bf16[2,128,128]{2,1,0:T(8,128)(2,1)S(1)}, bf16[2,128,128]{2,1,0:T(8,128)(2,1)S(1)}) custom-call(bf16[256,256]{1,0:T(8,128)(2,1)S(1)} %collective-permute-done.2.near, ...), custom_call_target="tpu_custom_call" | custom-call | flops 1000000000 | bytes 4000000 | tf_op jit(solution)/shard_map/block_backward/pallas_call | solution.py:479
  19.7 0.8 %conv_grads.1 = (bf16[432,128]{1,0:T(8,128)(2,1)S(1)}, bf16[432,128]{1,0:T(8,128)(2,1)S(1)}) custom-call(bf16[256,256]{1,0:T(8,128)(2,1)S(1)} %collective-permute-done.2.near, bf16[256,256]{1,0:T(8,128)(2,1)S(1)} %get-tuple-element.55.attended.own, bf16[256,256]{1,0:T(8,128)(2,1)S(1)} %collective-permute-done.3.mate, ...), custom_call_target="tpu_custom_call" | custom-call | flops 1000000000 | bytes 4000000 | tf_op jit(solution)/shard_map/conv_grads/pallas_call | solution.py:479
  20.9 3.0 %collective-permute-start.10 = (bf16[560,128]{1,0:T(8,128)(2,1)S(1)}, bf16[560,128]{1,0:T(8,128)(2,1)S(1)}, u32[]{:S(2)}, u32[]{:S(2)}) collective-permute-start(bf16[560,128]{1,0:T(8,128)(2,1)S(1)} %pad_maximum_fusion), channel_id=1, source_target_pairs={{0,8},{2,10},{4,12},{6,14},{8,0},{10,2},{12,4},{14,6},{16,24},{18,... | collective-permute-start | bytes 430088 | tf_op jit(solution)/shard_map/ppermute | solution.py:467
  23.9 1.0 %collective-permute-start.12 = (bf16[560,128]{1,0:T(8,128)(2,1)S(1)}, bf16[560,128]{1,0:T(8,128)(2,1)S(1)}, u32[]{:S(2)}, u32[]{:S(2)}) collective-permute-start(bf16[560,128]{1,0:T(8,128)(2,1)S(1)} %pad_maximum_fusion.1), channel_id=1, source_target_pairs={{0,12},{2,14},{4,8},{6,10},{8,4},{10,6},{12,0},{14,2},{16,28},{18,... | collective-permute-start | bytes 430088 | tf_op jit(solution)/shard_map/ppermute | solution.py:467
  25.4 3.0 %collective-permute-done.10 = bf16[560,128]{1,0:T(8,128)(2,1)S(1)} collective-permute-done((bf16[560,128]{1,0:T(8,128)(2,1)S(1)}, bf16[560,128]{1,0:T(8,128)(2,1)S(1)}, u32[]{:S(2)}, u32[]{:S(2)}) %collective-permute-start.10) | collective-permute-done | bytes 143392 | tf_op jit(solution)/shard_map/ppermute | solution.py:467
  28.4 3.4 %collective-permute-done.12 = bf16[560,128]{1,0:T(8,128)(2,1)S(1)} collective-permute-done((bf16[560,128]{1,0:T(8,128)(2,1)S(1)}, bf16[560,128]{1,0:T(8,128)(2,1)S(1)}, u32[]{:S(2)}, u32[]{:S(2)}) %collective-permute-start.12) | collective-permute-done | bytes 143392 | tf_op jit(solution)/shard_map/ppermute | solution.py:467
  31.8 1.4 %collective-permute-done.11 = bf16[560,128]{1,0:T(8,128)(2,1)S(1)} collective-permute-done((bf16[560,128]{1,0:T(8,128)(2,1)S(1)}, bf16[560,128]{1,0:T(8,128)(2,1)S(1)}, u32[]{:S(2)}, u32[]{:S(2)}) %collective-permute-start.11) | collective-permute-done | bytes 143392 | tf_op jit(solution)/shard_map/ppermute | solution.py:467
  33.3 2.7 %collective-permute-start.13 = (bf16[560,128]{1,0:T(8,128)(2,1)S(1)}, bf16[560,128]{1,0:T(8,128)(2,1)S(1)}, u32[]{:S(2)}, u32[]{:S(2)}) collective-permute-start(bf16[560,128]{1,0:T(8,128)(2,1)S(1)} %add_convert_fusion.1), channel_id=1, source_target_pairs={{0,16},{2,18},{4,20},{6,22},{8,24},{10,26},{12,28},{14,30},{16,0},... | collective-permute-start | bytes 430088 | tf_op jit(solution)/shard_map/ppermute | solution.py:467
  36.0 1.2 %outputs.1 = (bf16[128,128]{1,0:T(8,128)(2,1)}, bf16[128,256]{1,0:T(8,128)(2,1)}) custom-call(bf16[256,256]{1,0:T(8,128)(2,1)S(1)} %get-tuple-element.88.near_mid, bf16[256,256]{1,0:T(8,128)(2,1)S(1)} %get-tuple-element.83.own_mid, bf16[256,256]{1,0:T(8,128)(2,1)S(1)} %get-tuple-element.69.mate_mid, bf16[512,256]{1,0:T(8,128)(2,1)S(1)} %get-tuple-element.89.grad, ...), custom_call_target="tpu_custom_call" | custom-call | flops 1000000000 | bytes 4000000 | tf_op jit(solution)/shard_map/outputs/pallas_call | solution.py:479
  37.2 4.9 %collective-permute-done.13 = bf16[560,128]{1,0:T(8,128)(2,1)S(1)} collective-permute-done((bf16[560,128]{1,0:T(8,128)(2,1)S(1)}, bf16[560,128]{1,0:T(8,128)(2,1)S(1)}, u32[]{:S(2)}, u32[]{:S(2)}) %collective-permute-start.13) | collective-permute-done | bytes 143392 | tf_op jit(solution)/shard_map/ppermute | solution.py:467
  42.1 1.6 %collective-permute-start.19 = (bf16[560,128]{1,0:T(8,128)(2,1)S(1)}, bf16[560,128]{1,0:T(8,128)(2,1)S(1)}, u32[]{:S(2)}, u32[]{:S(2)}) collective-permute-start(bf16[560,128]{1,0:T(8,128)(2,1)S(1)} %add_convert_fusion.refs_0_), channel_id=1, source_target_pairs={{0,5},{1,4},{2,7},{3,6},{4,1},{5,0},{6,3},{7,2},{8,13},{9,12},{10,... | collective-permute-start | bytes 430088 | tf_op jit(solution)/shard_map/ppermute | solution.py:628
  43.7 0.8 %collective-permute-start.17 = (bf16[560,128]{1,0:T(8,128)(2,1)S(1)}, bf16[560,128]{1,0:T(8,128)(2,1)S(1)}, u32[]{:S(2)}, u32[]{:S(2)}) collective-permute-start(bf16[560,128]{1,0:T(8,128)(2,1)S(1)} %add_convert_fusion.refs_0_), channel_id=1, source_target_pairs={{0,1},{1,0},{2,3},{3,2},{4,5},{5,4},{6,7},{7,6},{8,9},{9,8},{10,11... | collective-permute-start | bytes 430088 | tf_op jit(solution)/shard_map/ppermute | solution.py:470
  44.5 1.1 %collective-permute-start.15 = (bf16[560,128]{1,0:T(8,128)(2,1)S(1)}, bf16[560,128]{1,0:T(8,128)(2,1)S(1)}, u32[]{:S(2)}, u32[]{:S(2)}) collective-permute-start(bf16[560,128]{1,0:T(8,128)(2,1)S(1)} %add_convert_fusion.refs_0_), channel_id=1, source_target_pairs={{0,4},{2,6},{4,0},{6,2},{8,12},{10,14},{12,8},{14,10},{16,20},{18,... | collective-permute-start | bytes 430088 | tf_op jit(solution)/shard_map/ppermute | solution.py:467
  45.7 3.6 %collective-permute-done.19.refs_3_ = bf16[560,128]{1,0:T(8,128)(2,1)S(1)} collective-permute-done((bf16[560,128]{1,0:T(8,128)(2,1)S(1)}, bf16[560,128]{1,0:T(8,128)(2,1)S(1)}, u32[]{:S(2)}, u32[]{:S(2)}) %collective-permute-start.19) | collective-permute-done | bytes 143392 | tf_op jit(solution)/shard_map/ppermute | solution.py:628
  49.3 0.8 %collective-permute-done.17.refs_2_ = bf16[560,128]{1,0:T(8,128)(2,1)S(1)} collective-permute-done((bf16[560,128]{1,0:T(8,128)(2,1)S(1)}, bf16[560,128]{1,0:T(8,128)(2,1)S(1)}, u32[]{:S(2)}, u32[]{:S(2)}) %collective-permute-start.17) | collective-permute-done | bytes 143392 | tf_op jit(solution)/shard_map/ppermute | solution.py:470
  50.7 1.1 %unpack_sums.2 = (f32[256,512]{1,0:T(8,128)}, f32[3,3,256,128]{3,2,1,0:T(8,128)}, f32[3,3,128,128]{3,2,1,0:T(8,128)}) custom-call(bf16[560,128]{1,0:T(8,128)(2,1)S(1)} %add_convert_fusion.refs_0_, bf16[560,128]{1,0:T(8,128)(2,1)S(1)} %collective-permute-done.15.refs_1_, bf16[560,128]{1,0:T(8,128)(2,1)S(1)} %collective-permute-done.17.refs_2_, ...), custom_call_target="tpu_custom_call" | custom-call | flops 1000000000 | bytes 4194304 | tf_op jit(solution)/shard_map/unpack_sums/pallas_call | solution.py:434
  52.1 1.1 %unpack_sums.3 = (f32[256,512]{1,0:T(8,128)}, f32[3,3,256,128]{3,2,1,0:T(8,128)}, f32[3,3,128,128]{3,2,1,0:T(8,128)}) custom-call(bf16[560,128]{1,0:T(8,128)(2,1)S(1)} %collective-permute-done.14.refs_0_, bf16[560,128]{1,0:T(8,128)(2,1)S(1)} %collective-permute-done.16.refs_1_, ...), custom_call_target="tpu_custom_call", output_to_operand_aliasing={{0}: (4, {}), {1}: (5, {}), {2}: (6, {})} | custom-call | flops 1000000000 | bytes 4194304 | tf_op jit(solution)/shard_map/unpack_sums/pallas_call | solution.py:434
  (50 shorter events, 7.2 us)
Async XLA Ops:
  0.6 7.0 %collective-permute-start = (bf16[128,256]{1,0:T(8,128)(2,1)}, bf16[128,256]{1,0:T(8,128)(2,1)S(1)}, u32[]{:S(2)}, u32[]{:S(2)}) collective-permute-start(bf16[128,256]{1,0:T(8,128)(2,1)} %bitcast.8), channel_id=1, source_target_pairs={{0,1},{1,0},{2,3},{3,2},{4,5},{5,4},{6,7},{7,6},{8,9},{9,8},{10,11... | collective-permute-start | bytes 196616 | tf_op jit(solution)/shard_map/ppermute | solution.py:470
  3.6 5.9 %collective-permute-start.5 = (bf16[128,128]{1,0:T(8,128)(2,1)}, bf16[128,128]{1,0:T(8,128)(2,1)S(1)}, u32[]{:S(2)}, u32[]{:S(2)}) collective-permute-start(bf16[128,128]{1,0:T(8,128)(2,1)} %bitcast.10), channel_id=1, source_target_pairs={{4,0},{8,4},{12,8},{16,12},{20,16},{24,20},{28,24},{2,6},{6,10},{1... | collective-permute-start | bytes 98312 | tf_op jit(solution)/shard_map/ppermute | solution.py:498
  3.6 5.9 %collective-permute-start.4 = (bf16[128,128]{1,0:T(8,128)(2,1)}, bf16[128,128]{1,0:T(8,128)(2,1)S(1)}, u32[]{:S(2)}, u32[]{:S(2)}) collective-permute-start(bf16[128,128]{1,0:T(8,128)(2,1)} %bitcast.11), channel_id=1, source_target_pairs={{0,4},{4,8},{8,12},{12,16},{16,20},{20,24},{24,28},{6,2},{10,6},{1... | collective-permute-start | bytes 98312 | tf_op jit(solution)/shard_map/ppermute | solution.py:497
  7.6 2.0 %copy-start = (bf16[3,3,256,128]{3,2,1,0:T(8,128)(2,1)S(1)}, bf16[3,3,256,128]{3,2,1,0:T(8,128)(2,1)}, u32[]{:S(2)}) copy-start(bf16[3,3,256,128]{3,2,1,0:T(8,128)(2,1)} %refs_0_.3) | copy-start | bytes 1769476
  7.6 2.0 %copy-start.4 = (bf16[1,128,128]{2,1,0:T(8,128)(2,1)S(1)}, bf16[1,128,128]{2,1,0:T(8,128)(2,1)}, u32[]{:S(2)}) copy-start(bf16[1,128,128]{2,1,0:T(8,128)(2,1)} %param.9) | copy-start | bytes 98308
  9.0 3.5 %copy-start.1 = (bf16[3,3,128,128]{3,2,1,0:T(8,128)(2,1)S(1)}, bf16[3,3,128,128]{3,2,1,0:T(8,128)(2,1)}, u32[]{:S(2)}) copy-start(bf16[3,3,128,128]{3,2,1,0:T(8,128)(2,1)} %refs_1_.1) | copy-start | bytes 884740
  9.0 4.7 %collective-permute-start.3 = (bf16[256,256]{1,0:T(8,128)(2,1)S(1)}, bf16[256,256]{1,0:T(8,128)(2,1)S(1)}, u32[]{:S(2)}, u32[]{:S(2)}) collective-permute-start(bf16[256,256]{1,0:T(8,128)(2,1)S(1)} %get-tuple-element.55.attended.own), channel_id=1, source_target_pairs={{0,2},{2,0},{4,6},{6,4},{8,10},{10,8},{12,14},{14,12},{16,18},{18,... | collective-permute-start | bytes 393224 | tf_op jit(solution)/shard_map/ppermute | solution.py:467
  9.0 6.5 %collective-permute-start.1 = (bf16[256,256]{1,0:T(8,128)(2,1)S(1)}, bf16[256,256]{1,0:T(8,128)(2,1)S(1)}, u32[]{:S(2)}, u32[]{:S(2)}) collective-permute-start(bf16[256,256]{1,0:T(8,128)(2,1)S(1)} %get-tuple-element.55.attended.own), channel_id=1, source_target_pairs={{4,0},{8,4},{12,8},{16,12},{20,16},{24,20},{28,24},{2,6},{6,10},{1... | collective-permute-start | bytes 393224 | tf_op jit(solution)/shard_map/ppermute | solution.py:526
  9.8 4.7 %collective-permute-start.6 = (bf16[3,128,128]{2,1,0:T(8,128)(2,1)S(1)}, bf16[3,128,128]{2,1,0:T(8,128)(2,1)S(1)}, u32[]{:S(2)}, u32[]{:S(2)}) collective-permute-start(bf16[3,128,128]{2,1,0:T(8,128)(2,1)S(1)} %get-tuple-element.60.refs_0_), channel_id=1, source_target_pairs={{0,1},{1,0},{2,3},{3,2},{4,5},{5,4},{6,7},{7,6},{8,9},{9,8},{10,11... | collective-permute-start | bytes 294920 | tf_op jit(solution)/shard_map/ppermute | solution.py:470
  10.4 6.0 %collective-permute-start.8 = (bf16[256,128]{1,0:T(8,128)(2,1)S(1)}, bf16[256,128]{1,0:T(8,128)(2,1)S(1)}, u32[]{:S(2)}, u32[]{:S(2)}) collective-permute-start(bf16[256,128]{1,0:T(8,128)(2,1)S(1)} %get-tuple-element.70), channel_id=1, source_target_pairs={{0,4},{4,8},{8,12},{12,16},{16,20},{20,24},{24,28},{6,2},{10,6},{1... | collective-permute-start | bytes 196616 | tf_op jit(solution)/shard_map/ppermute | solution.py:531
  14.5 2.3 %collective-permute-start.7 = (bf16[2,256,128]{2,1,0:T(8,128)(2,1)S(1)}, bf16[2,256,128]{2,1,0:T(8,128)(2,1)S(1)}, u32[]{:S(2)}, u32[]{:S(2)}) collective-permute-start(bf16[2,256,128]{2,1,0:T(8,128)(2,1)S(1)} %get-tuple-element.62.pair_cot), channel_id=1, source_target_pairs={{0,2},{2,0},{4,6},{6,4},{8,10},{10,8},{12,14},{14,12},{16,18},{18,... | collective-permute-start | bytes 393224 | tf_op jit(solution)/shard_map/ppermute | solution.py:467
  15.6 1.6 %collective-permute-start.2 = (bf16[256,256]{1,0:T(8,128)(2,1)S(1)}, bf16[256,256]{1,0:T(8,128)(2,1)S(1)}, u32[]{:S(2)}, u32[]{:S(2)}) collective-permute-start(bf16[256,256]{1,0:T(8,128)(2,1)S(1)} %collective-permute-done.1.mate1), channel_id=1, source_target_pairs={{0,2},{2,0},{4,6},{6,4},{8,10},{10,8},{12,14},{14,12},{16,18},{18,... | collective-permute-start | bytes 393224 | tf_op jit(solution)/shard_map/ppermute | solution.py:467
  19.5 1.3 %collective-permute-start.9 = (bf16[2,128,128]{2,1,0:T(8,128)(2,1)S(1)}, bf16[2,128,128]{2,1,0:T(8,128)(2,1)S(1)}, u32[]{:S(2)}, u32[]{:S(2)}) collective-permute-start(bf16[2,128,128]{2,1,0:T(8,128)(2,1)S(1)} %get-tuple-element.86), channel_id=1, source_target_pairs={{0,2},{2,0},{4,6},{6,4},{8,10},{10,8},{12,14},{14,12},{16,18},{18,... | collective-permute-start | bytes 196616 | tf_op jit(solution)/shard_map/ppermute | solution.py:467
  20.9 7.6 %collective-permute-start.10 = (bf16[560,128]{1,0:T(8,128)(2,1)S(1)}, bf16[560,128]{1,0:T(8,128)(2,1)S(1)}, u32[]{:S(2)}, u32[]{:S(2)}) collective-permute-start(bf16[560,128]{1,0:T(8,128)(2,1)S(1)} %pad_maximum_fusion), channel_id=1, source_target_pairs={{0,8},{2,10},{4,12},{6,14},{8,0},{10,2},{12,4},{14,6},{16,24},{18,... | collective-permute-start | bytes 430088 | tf_op jit(solution)/shard_map/ppermute | solution.py:467
  23.9 7.9 %collective-permute-start.12 = (bf16[560,128]{1,0:T(8,128)(2,1)S(1)}, bf16[560,128]{1,0:T(8,128)(2,1)S(1)}, u32[]{:S(2)}, u32[]{:S(2)}) collective-permute-start(bf16[560,128]{1,0:T(8,128)(2,1)S(1)} %pad_maximum_fusion.1), channel_id=1, source_target_pairs={{0,12},{2,14},{4,8},{6,10},{8,4},{10,6},{12,0},{14,2},{16,28},{18,... | collective-permute-start | bytes 430088 | tf_op jit(solution)/shard_map/ppermute | solution.py:467
  24.9 8.3 %collective-permute-start.11 = (bf16[560,128]{1,0:T(8,128)(2,1)S(1)}, bf16[560,128]{1,0:T(8,128)(2,1)S(1)}, u32[]{:S(2)}, u32[]{:S(2)}) collective-permute-start(bf16[560,128]{1,0:T(8,128)(2,1)S(1)} %pad_maximum_fusion.1), channel_id=1, source_target_pairs={{0,4},{2,6},{4,0},{6,2},{8,12},{10,14},{12,8},{14,10},{16,20},{18,... | collective-permute-start | bytes 430088 | tf_op jit(solution)/shard_map/ppermute | solution.py:467
  33.3 8.7 %collective-permute-start.13 = (bf16[560,128]{1,0:T(8,128)(2,1)S(1)}, bf16[560,128]{1,0:T(8,128)(2,1)S(1)}, u32[]{:S(2)}, u32[]{:S(2)}) collective-permute-start(bf16[560,128]{1,0:T(8,128)(2,1)S(1)} %add_convert_fusion.1), channel_id=1, source_target_pairs={{0,16},{2,18},{4,20},{6,22},{8,24},{10,26},{12,28},{14,30},{16,0},... | collective-permute-start | bytes 430088 | tf_op jit(solution)/shard_map/ppermute | solution.py:467
  42.1 7.2 %collective-permute-start.19 = (bf16[560,128]{1,0:T(8,128)(2,1)S(1)}, bf16[560,128]{1,0:T(8,128)(2,1)S(1)}, u32[]{:S(2)}, u32[]{:S(2)}) collective-permute-start(bf16[560,128]{1,0:T(8,128)(2,1)S(1)} %add_convert_fusion.refs_0_), channel_id=1, source_target_pairs={{0,5},{1,4},{2,7},{3,6},{4,1},{5,0},{6,3},{7,2},{8,13},{9,12},{10,... | collective-permute-start | bytes 430088 | tf_op jit(solution)/shard_map/ppermute | solution.py:628
  43.7 6.4 %collective-permute-start.17 = (bf16[560,128]{1,0:T(8,128)(2,1)S(1)}, bf16[560,128]{1,0:T(8,128)(2,1)S(1)}, u32[]{:S(2)}, u32[]{:S(2)}) collective-permute-start(bf16[560,128]{1,0:T(8,128)(2,1)S(1)} %add_convert_fusion.refs_0_), channel_id=1, source_target_pairs={{0,1},{1,0},{2,3},{3,2},{4,5},{5,4},{6,7},{7,6},{8,9},{9,8},{10,11... | collective-permute-start | bytes 430088 | tf_op jit(solution)/shard_map/ppermute | solution.py:470
  44.5 6.2 %collective-permute-start.15 = (bf16[560,128]{1,0:T(8,128)(2,1)S(1)}, bf16[560,128]{1,0:T(8,128)(2,1)S(1)}, u32[]{:S(2)}, u32[]{:S(2)}) collective-permute-start(bf16[560,128]{1,0:T(8,128)(2,1)S(1)} %add_convert_fusion.refs_0_), channel_id=1, source_target_pairs={{0,4},{2,6},{4,0},{6,2},{8,12},{10,14},{12,8},{14,10},{16,20},{18,... | collective-permute-start | bytes 430088 | tf_op jit(solution)/shard_map/ppermute | solution.py:467
  45.7 6.2 %collective-permute-start.14 = (bf16[560,128]{1,0:T(8,128)(2,1)S(1)}, bf16[560,128]{1,0:T(8,128)(2,1)S(1)}, u32[]{:S(2)}, u32[]{:S(2)}) collective-permute-start(bf16[560,128]{1,0:T(8,128)(2,1)S(1)} %add_convert_fusion.refs_0_), channel_id=1, source_target_pairs={{0,2},{2,0},{4,6},{6,4},{8,10},{10,8},{12,14},{14,12},{16,18},{18,... | collective-permute-start | bytes 430088 | tf_op jit(solution)/shard_map/ppermute | solution.py:467
  49.3 2.5 %collective-permute-start.20 = (bf16[560,128]{1,0:T(8,128)(2,1)S(1)}, bf16[560,128]{1,0:T(8,128)(2,1)S(1)}, u32[]{:S(2)}, u32[]{:S(2)}) collective-permute-start(bf16[560,128]{1,0:T(8,128)(2,1)S(1)} %collective-permute-done.19.refs_3_), channel_id=1, source_target_pairs={{0,2},{2,0},{4,6},{6,4},{8,10},{10,8},{12,14},{14,12},{16,18},{18,... | collective-permute-start | bytes 430088 | tf_op jit(solution)/shard_map/ppermute | solution.py:467
  50.1 1.7 %collective-permute-start.18 = (bf16[560,128]{1,0:T(8,128)(2,1)S(1)}, bf16[560,128]{1,0:T(8,128)(2,1)S(1)}, u32[]{:S(2)}, u32[]{:S(2)}) collective-permute-start(bf16[560,128]{1,0:T(8,128)(2,1)S(1)} %collective-permute-done.17.refs_2_), channel_id=1, source_target_pairs={{0,2},{2,0},{4,6},{6,4},{8,10},{10,8},{12,14},{14,12},{16,18},{18,... | collective-permute-start | bytes 430088 | tf_op jit(solution)/shard_map/ppermute | solution.py:467
  50.7 1.4 %collective-permute-start.16 = (bf16[560,128]{1,0:T(8,128)(2,1)S(1)}, bf16[560,128]{1,0:T(8,128)(2,1)S(1)}, u32[]{:S(2)}, u32[]{:S(2)}) collective-permute-start(bf16[560,128]{1,0:T(8,128)(2,1)S(1)} %collective-permute-done.15.refs_1_), channel_id=1, source_target_pairs={{0,2},{2,0},{4,6},{6,4},{8,10},{10,8},{12,14},{14,12},{16,18},{18,... | collective-permute-start | bytes 430088 | tf_op jit(solution)/shard_map/ppermute | solution.py:467
  (2 other events, 1.8 us)

commit v11 on v10

--- a/solution.py
+++ b/solution.py
@@ -496,7 +496,7 @@
         swapped = cols_flip(features)
         out_cot = lax.ppermute(cotangent, "rows", out)
         back_cot = lax.ppermute(cotangent, "rows", back)
-        projection, features = fetch((projection, features))
+        (projection,) = fetch((projection,))
         features = (features, swapped)
     else:
         out_cot = lax.ppermute(cotangent, "rows", out)

time: 53.4 us -> 53.3 us (level)
    ppermute x3, starting transfers between devices: 4.38 us -> 5.25 us  [cols_flip(): return lax.ppermute(values, 'cols', [(i, i ^ 1) for i in range(cols_size)])]
  transfers between devices with their start and end apart: 21 -> 21, of which waited for: 11 -> 10; matrix products, arithmetic and copies ran while one was open for 0% -> 0% of each run, Pallas kernels for 14% -> 14%
where the time goes in v11:
time: 53.3 us; the launch traced here: 53.2 us
  starting transfers between devices  20.6 us (39%)
  waiting for transfers between devices  19.1 us (36%)
  Pallas kernels  10.6 us (20%)
  local copies, waits for them, and re-layouts  1.87 us (4%)
  between operations  0.89 us (2%)
    ppermute x13, waiting for transfers between devices, rows_flip(): lax.ppermute(values, 'rows', [(i, i ^ bit) for i in range(rows_size)])  13.9 us
    ppermute x13, starting transfers between devices, rows_flip(): lax.ppermute(values, 'rows', [(i, i ^ bit) for i in range(rows_size)])  9.58 us
    pallas_call x12, Pallas kernels, call(): pl.pallas_call(kernel, out_shape=out_shape, in_specs=[VMEM] * len(operand...  8.24 us
    ppermute x3, starting transfers between devices, cols_flip(): return lax.ppermute(values, 'cols', [(i, i ^ 1) for i in range(cols_size)])  5.25 us
    ppermute x1, waiting for transfers between devices, body(): lax.ppermute(total, ('rows', 'cols'), [(i * cols_size + j, (i ^ 2) * cols...  3.65 us
    pallas_call x2, Pallas kernels, unpack(): pl.pallas_call(functools.partial(unpack_kernel, factor, core_flip), out_s...  2.16 us
    ppermute x1, starting transfers between devices, body(): out_cot = lax.ppermute(cotangent, 'rows', out)  2.02 us
    unnamed x10, local copies, waits for them, and re-layouts  1.86 us
  transfers between devices with their start and end apart: 21, of which 10 were waited for; matrix products, arithmetic and copies ran while one was open for 0% of the time, Pallas kernels for 14%

profile of v11, /device:TPU:0, one launch (start us, length us, event | category | flops | bytes accessed | tf_op | source)
XLA Modules:
  0.0 53.2 jit_solution(5924796466585741848)
XLA Ops:
  0.6 3.0 %collective-permute-start = (bf16[128,256]{1,0:T(8,128)(2,1)}, bf16[128,256]{1,0:T(8,128)(2,1)S(1)}, u32[]{:S(2)}, u32[]{:S(2)}) collective-permute-start(bf16[128,256]{1,0:T(8,128)(2,1)} %bitcast.8), channel_id=1, source_target_pairs={{0,1},{1,0},{2,3},{3,2},{4,5},{5,4},{6,7},{7,6},{8,9},{9,8},{10,11... | collective-permute-start | bytes 196616 | tf_op jit(solution)/shard_map/ppermute | solution.py:470
  3.6 2.0 %collective-permute-start.4 = (bf16[128,128]{1,0:T(8,128)(2,1)}, bf16[128,128]{1,0:T(8,128)(2,1)S(1)}, u32[]{:S(2)}, u32[]{:S(2)}) collective-permute-start(bf16[128,128]{1,0:T(8,128)(2,1)} %bitcast.11), channel_id=1, source_target_pairs={{0,4},{4,8},{8,12},{12,16},{16,20},{20,24},{24,28},{6,2},{10,6},{1... | collective-permute-start | bytes 98312 | tf_op jit(solution)/shard_map/ppermute | solution.py:497
  5.7 0.9 %copy-done.2 = bf16[256,512]{1,0:T(8,128)(2,1)S(1)} copy-done((bf16[256,512]{1,0:T(8,128)(2,1)S(1)}, bf16[256,512]{1,0:T(8,128)(2,1)}, u32[]{:S(2)}) %copy-start.2) | copy-done | bytes 262168
  6.7 0.9 %copy-done.3 = bf16[1,128,256]{2,1,0:T(8,128)(2,1)S(1)} copy-done((bf16[1,128,256]{2,1,0:T(8,128)(2,1)S(1)}, bf16[1,128,256]{2,1,0:T(8,128)(2,1)}, u32[]{:S(2)}) %copy-start.3) | copy-done | bytes 65560
  7.6 1.3 %attention_forward.1 = (bf16[256,256]{1,0:T(8,128)(2,1)S(1)}, bf16[256,768]{1,0:T(8,128)(2,1)S(1)}, f32[16,256]{1,0:T(8,128)S(1)}) custom-call(bf16[128,256]{1,0:T(8,128)(2,1)S(1)} %bitcast.9, bf16[128,256]{1,0:T(8,128)(2,1)S(1)} %collective-permute-done.refs_1_, bf16[256,512]{1,0:T(8,128)(2,1)S(1)} %fetch.2.refs_2_.projection), custom_call_target="tpu_custom_call" | custom-call | flops 1000000000 | bytes 4000000 | tf_op jit(solution)/shard_map/attention_forward/pallas_call | solution.py:479
  9.8 1.4 %collective-permute-start.6 = (bf16[3,128,128]{2,1,0:T(8,128)(2,1)S(1)}, bf16[3,128,128]{2,1,0:T(8,128)(2,1)S(1)}, u32[]{:S(2)}, u32[]{:S(2)}) collective-permute-start(bf16[3,128,128]{2,1,0:T(8,128)(2,1)S(1)} %get-tuple-element.56.refs_0_), channel_id=1, source_target_pairs={{0,1},{1,0},{2,3},{3,2},{4,5},{5,4},{6,7},{7,6},{8,9},{9,8},{10,11... | collective-permute-start | bytes 294920 | tf_op jit(solution)/shard_map/ppermute | solution.py:470
  11.2 1.6 %collective-permute-start.8 = (bf16[256,128]{1,0:T(8,128)(2,1)S(1)}, bf16[256,128]{1,0:T(8,128)(2,1)S(1)}, u32[]{:S(2)}, u32[]{:S(2)}) collective-permute-start(bf16[256,128]{1,0:T(8,128)(2,1)S(1)} %get-tuple-element.66), channel_id=1, source_target_pairs={{0,4},{4,8},{8,12},{12,16},{16,20},{20,24},{24,28},{6,2},{10,6},{1... | collective-permute-start | bytes 196616 | tf_op jit(solution)/shard_map/ppermute | solution.py:531
  14.7 0.9 %collective-permute-start.7 = (bf16[2,256,128]{2,1,0:T(8,128)(2,1)S(1)}, bf16[2,256,128]{2,1,0:T(8,128)(2,1)S(1)}, u32[]{:S(2)}, u32[]{:S(2)}) collective-permute-start(bf16[2,256,128]{2,1,0:T(8,128)(2,1)S(1)} %get-tuple-element.58.pair_cot), channel_id=1, source_target_pairs={{0,2},{2,0},{4,6},{6,4},{8,10},{10,8},{12,14},{14,12},{16,18},{18,... | collective-permute-start | bytes 393224 | tf_op jit(solution)/shard_map/ppermute | solution.py:467
  17.1 2.3 %block_backward.1 = (bf16[256,256]{1,0:T(8,128)(2,1)S(1)}, bf16[256,256]{1,0:T(8,128)(2,1)S(1)}, bf16[512,256]{1,0:T(8,128)(2,1)S(1)}, bf16[2,128,128]{2,1,0:T(8,128)(2,1)S(1)}, bf16[2,128,128]{2,1,0:T(8,128)(2,1)S(1)}) custom-call(bf16[256,256]{1,0:T(8,128)(2,1)S(1)} %collective-permute-done.2.near, ...), custom_call_target="tpu_custom_call" | custom-call | flops 1000000000 | bytes 4000000 | tf_op jit(solution)/shard_map/block_backward/pallas_call | solution.py:479
  20.8 3.0 %collective-permute-start.10 = (bf16[560,128]{1,0:T(8,128)(2,1)S(1)}, bf16[560,128]{1,0:T(8,128)(2,1)S(1)}, u32[]{:S(2)}, u32[]{:S(2)}) collective-permute-start(bf16[560,128]{1,0:T(8,128)(2,1)S(1)} %pad_maximum_fusion), channel_id=1, source_target_pairs={{0,8},{2,10},{4,12},{6,14},{8,0},{10,2},{12,4},{14,6},{16,24},{18,... | collective-permute-start | bytes 430088 | tf_op jit(solution)/shard_map/ppermute | solution.py:467
  23.9 1.0 %collective-permute-start.12 = (bf16[560,128]{1,0:T(8,128)(2,1)S(1)}, bf16[560,128]{1,0:T(8,128)(2,1)S(1)}, u32[]{:S(2)}, u32[]{:S(2)}) collective-permute-start(bf16[560,128]{1,0:T(8,128)(2,1)S(1)} %pad_maximum_fusion.1), channel_id=1, source_target_pairs={{0,12},{2,14},{4,8},{6,10},{8,4},{10,6},{12,0},{14,2},{16,28},{18,... | collective-permute-start | bytes 430088 | tf_op jit(solution)/shard_map/ppermute | solution.py:467
  25.4 3.0 %collective-permute-done.10 = bf16[560,128]{1,0:T(8,128)(2,1)S(1)} collective-permute-done((bf16[560,128]{1,0:T(8,128)(2,1)S(1)}, bf16[560,128]{1,0:T(8,128)(2,1)S(1)}, u32[]{:S(2)}, u32[]{:S(2)}) %collective-permute-start.10) | collective-permute-done | bytes 143392 | tf_op jit(solution)/shard_map/ppermute | solution.py:467
  28.4 3.4 %collective-permute-done.12 = bf16[560,128]{1,0:T(8,128)(2,1)S(1)} collective-permute-done((bf16[560,128]{1,0:T(8,128)(2,1)S(1)}, bf16[560,128]{1,0:T(8,128)(2,1)S(1)}, u32[]{:S(2)}, u32[]{:S(2)}) %collective-permute-start.12) | collective-permute-done | bytes 143392 | tf_op jit(solution)/shard_map/ppermute | solution.py:467
  31.8 1.4 %collective-permute-done.11 = bf16[560,128]{1,0:T(8,128)(2,1)S(1)} collective-permute-done((bf16[560,128]{1,0:T(8,128)(2,1)S(1)}, bf16[560,128]{1,0:T(8,128)(2,1)S(1)}, u32[]{:S(2)}, u32[]{:S(2)}) %collective-permute-start.11) | collective-permute-done | bytes 143392 | tf_op jit(solution)/shard_map/ppermute | solution.py:467
  33.3 2.6 %collective-permute-start.13 = (bf16[560,128]{1,0:T(8,128)(2,1)S(1)}, bf16[560,128]{1,0:T(8,128)(2,1)S(1)}, u32[]{:S(2)}, u32[]{:S(2)}) collective-permute-start(bf16[560,128]{1,0:T(8,128)(2,1)S(1)} %add_convert_fusion.1), channel_id=1, source_target_pairs={{0,16},{2,18},{4,20},{6,22},{8,24},{10,26},{12,28},{14,30},{16,0},... | collective-permute-start | bytes 430088 | tf_op jit(solution)/shard_map/ppermute | solution.py:467
  36.0 1.2 %outputs.1 = (bf16[128,128]{1,0:T(8,128)(2,1)}, bf16[128,256]{1,0:T(8,128)(2,1)}) custom-call(bf16[256,256]{1,0:T(8,128)(2,1)S(1)} %get-tuple-element.84.near_mid, bf16[256,256]{1,0:T(8,128)(2,1)S(1)} %get-tuple-element.79.own_mid, bf16[256,256]{1,0:T(8,128)(2,1)S(1)} %get-tuple-element.65.mate_mid, bf16[512,256]{1,0:T(8,128)(2,1)S(1)} %get-tuple-element.85.grad, ...), custom_call_target="tpu_custom_call" | custom-call | flops 1000000000 | bytes 4000000 | tf_op jit(solution)/shard_map/outputs/pallas_call | solution.py:479
  37.1 4.9 %collective-permute-done.13 = bf16[560,128]{1,0:T(8,128)(2,1)S(1)} collective-permute-done((bf16[560,128]{1,0:T(8,128)(2,1)S(1)}, bf16[560,128]{1,0:T(8,128)(2,1)S(1)}, u32[]{:S(2)}, u32[]{:S(2)}) %collective-permute-start.13) | collective-permute-done | bytes 143392 | tf_op jit(solution)/shard_map/ppermute | solution.py:467
  42.1 1.6 %collective-permute-start.19 = (bf16[560,128]{1,0:T(8,128)(2,1)S(1)}, bf16[560,128]{1,0:T(8,128)(2,1)S(1)}, u32[]{:S(2)}, u32[]{:S(2)}) collective-permute-start(bf16[560,128]{1,0:T(8,128)(2,1)S(1)} %add_convert_fusion.refs_0_), channel_id=1, source_target_pairs={{0,5},{1,4},{2,7},{3,6},{4,1},{5,0},{6,3},{7,2},{8,13},{9,12},{10,... | collective-permute-start | bytes 430088 | tf_op jit(solution)/shard_map/ppermute | solution.py:628
  43.7 0.8 %collective-permute-start.17 = (bf16[560,128]{1,0:T(8,128)(2,1)S(1)}, bf16[560,128]{1,0:T(8,128)(2,1)S(1)}, u32[]{:S(2)}, u32[]{:S(2)}) collective-permute-start(bf16[560,128]{1,0:T(8,128)(2,1)S(1)} %add_convert_fusion.refs_0_), channel_id=1, source_target_pairs={{0,1},{1,0},{2,3},{3,2},{4,5},{5,4},{6,7},{7,6},{8,9},{9,8},{10,11... | collective-permute-start | bytes 430088 | tf_op jit(solution)/shard_map/ppermute | solution.py:470
  44.5 1.1 %collective-permute-start.15 = (bf16[560,128]{1,0:T(8,128)(2,1)S(1)}, bf16[560,128]{1,0:T(8,128)(2,1)S(1)}, u32[]{:S(2)}, u32[]{:S(2)}) collective-permute-start(bf16[560,128]{1,0:T(8,128)(2,1)S(1)} %add_convert_fusion.refs_0_), channel_id=1, source_target_pairs={{0,4},{2,6},{4,0},{6,2},{8,12},{10,14},{12,8},{14,10},{16,20},{18,... | collective-permute-start | bytes 430088 | tf_op jit(solution)/shard_map/ppermute | solution.py:467
  45.6 3.7 %collective-permute-done.19.refs_3_ = bf16[560,128]{1,0:T(8,128)(2,1)S(1)} collective-permute-done((bf16[560,128]{1,0:T(8,128)(2,1)S(1)}, bf16[560,128]{1,0:T(8,128)(2,1)S(1)}, u32[]{:S(2)}, u32[]{:S(2)}) %collective-permute-start.19) | collective-permute-done | bytes 143392 | tf_op jit(solution)/shard_map/ppermute | solution.py:628
  49.3 0.8 %collective-permute-done.17.refs_2_ = bf16[560,128]{1,0:T(8,128)(2,1)S(1)} collective-permute-done((bf16[560,128]{1,0:T(8,128)(2,1)S(1)}, bf16[560,128]{1,0:T(8,128)(2,1)S(1)}, u32[]{:S(2)}, u32[]{:S(2)}) %collective-permute-start.17) | collective-permute-done | bytes 143392 | tf_op jit(solution)/shard_map/ppermute | solution.py:470
  50.7 1.1 %unpack_sums.2 = (f32[256,512]{1,0:T(8,128)}, f32[3,3,256,128]{3,2,1,0:T(8,128)}, f32[3,3,128,128]{3,2,1,0:T(8,128)}) custom-call(bf16[560,128]{1,0:T(8,128)(2,1)S(1)} %add_convert_fusion.refs_0_, bf16[560,128]{1,0:T(8,128)(2,1)S(1)} %collective-permute-done.15.refs_1_, bf16[560,128]{1,0:T(8,128)(2,1)S(1)} %collective-permute-done.17.refs_2_, ...), custom_call_target="tpu_custom_call" | custom-call | flops 1000000000 | bytes 4194304 | tf_op jit(solution)/shard_map/unpack_sums/pallas_call | solution.py:434
  52.1 1.1 %unpack_sums.3 = (f32[256,512]{1,0:T(8,128)}, f32[3,3,256,128]{3,2,1,0:T(8,128)}, f32[3,3,128,128]{3,2,1,0:T(8,128)}) custom-call(bf16[560,128]{1,0:T(8,128)(2,1)S(1)} %collective-permute-done.14.refs_0_, bf16[560,128]{1,0:T(8,128)(2,1)S(1)} %collective-permute-done.16.refs_1_, ...), custom_call_target="tpu_custom_call", output_to_operand_aliasing={{0}: (4, {}), {1}: (5, {}), {2}: (6, {})} | custom-call | flops 1000000000 | bytes 4194304 | tf_op jit(solution)/shard_map/unpack_sums/pallas_call | solution.py:434
  (50 shorter events, 7.1 us)
Async XLA Ops:
  0.6 6.0 %collective-permute-start = (bf16[128,256]{1,0:T(8,128)(2,1)}, bf16[128,256]{1,0:T(8,128)(2,1)S(1)}, u32[]{:S(2)}, u32[]{:S(2)}) collective-permute-start(bf16[128,256]{1,0:T(8,128)(2,1)} %bitcast.8), channel_id=1, source_target_pairs={{0,1},{1,0},{2,3},{3,2},{4,5},{5,4},{6,7},{7,6},{8,9},{9,8},{10,11... | collective-permute-start | bytes 196616 | tf_op jit(solution)/shard_map/ppermute | solution.py:470
  3.6 5.9 %collective-permute-start.5 = (bf16[128,128]{1,0:T(8,128)(2,1)}, bf16[128,128]{1,0:T(8,128)(2,1)S(1)}, u32[]{:S(2)}, u32[]{:S(2)}) collective-permute-start(bf16[128,128]{1,0:T(8,128)(2,1)} %bitcast.10), channel_id=1, source_target_pairs={{4,0},{8,4},{12,8},{16,12},{20,16},{24,20},{28,24},{2,6},{6,10},{1... | collective-permute-start | bytes 98312 | tf_op jit(solution)/shard_map/ppermute | solution.py:498
  3.6 5.9 %collective-permute-start.4 = (bf16[128,128]{1,0:T(8,128)(2,1)}, bf16[128,128]{1,0:T(8,128)(2,1)S(1)}, u32[]{:S(2)}, u32[]{:S(2)}) collective-permute-start(bf16[128,128]{1,0:T(8,128)(2,1)} %bitcast.11), channel_id=1, source_target_pairs={{0,4},{4,8},{8,12},{12,16},{16,20},{20,24},{24,28},{6,2},{10,6},{1... | collective-permute-start | bytes 98312 | tf_op jit(solution)/shard_map/ppermute | solution.py:497
  6.6 2.9 %copy-start = (bf16[3,3,256,128]{3,2,1,0:T(8,128)(2,1)S(1)}, bf16[3,3,256,128]{3,2,1,0:T(8,128)(2,1)}, u32[]{:S(2)}) copy-start(bf16[3,3,256,128]{3,2,1,0:T(8,128)(2,1)} %refs_0_.3) | copy-start | bytes 1769476
  7.6 1.9 %copy-start.4 = (bf16[1,128,128]{2,1,0:T(8,128)(2,1)S(1)}, bf16[1,128,128]{2,1,0:T(8,128)(2,1)}, u32[]{:S(2)}) copy-start(bf16[1,128,128]{2,1,0:T(8,128)(2,1)} %param.9) | copy-start | bytes 98308
  8.9 3.9 %copy-start.1 = (bf16[3,3,128,128]{3,2,1,0:T(8,128)(2,1)S(1)}, bf16[3,3,128,128]{3,2,1,0:T(8,128)(2,1)}, u32[]{:S(2)}) copy-start(bf16[3,3,128,128]{3,2,1,0:T(8,128)(2,1)} %refs_1_.1) | copy-start | bytes 884740
  8.9 5.2 %collective-permute-start.3 = (bf16[256,256]{1,0:T(8,128)(2,1)S(1)}, bf16[256,256]{1,0:T(8,128)(2,1)S(1)}, u32[]{:S(2)}, u32[]{:S(2)}) collective-permute-start(bf16[256,256]{1,0:T(8,128)(2,1)S(1)} %get-tuple-element.51.attended.own), channel_id=1, source_target_pairs={{0,2},{2,0},{4,6},{6,4},{8,10},{10,8},{12,14},{14,12},{16,18},{18,... | collective-permute-start | bytes 393224 | tf_op jit(solution)/shard_map/ppermute | solution.py:467
  9.0 6.5 %collective-permute-start.1 = (bf16[256,256]{1,0:T(8,128)(2,1)S(1)}, bf16[256,256]{1,0:T(8,128)(2,1)S(1)}, u32[]{:S(2)}, u32[]{:S(2)}) collective-permute-start(bf16[256,256]{1,0:T(8,128)(2,1)S(1)} %get-tuple-element.51.attended.own), channel_id=1, source_target_pairs={{4,0},{8,4},{12,8},{16,12},{20,16},{24,20},{28,24},{2,6},{6,10},{1... | collective-permute-start | bytes 393224 | tf_op jit(solution)/shard_map/ppermute | solution.py:526
  9.8 4.8 %collective-permute-start.6 = (bf16[3,128,128]{2,1,0:T(8,128)(2,1)S(1)}, bf16[3,128,128]{2,1,0:T(8,128)(2,1)S(1)}, u32[]{:S(2)}, u32[]{:S(2)}) collective-permute-start(bf16[3,128,128]{2,1,0:T(8,128)(2,1)S(1)} %get-tuple-element.56.refs_0_), channel_id=1, source_target_pairs={{0,1},{1,0},{2,3},{3,2},{4,5},{5,4},{6,7},{7,6},{8,9},{9,8},{10,11... | collective-permute-start | bytes 294920 | tf_op jit(solution)/shard_map/ppermute | solution.py:470
  11.2 5.1 %collective-permute-start.8 = (bf16[256,128]{1,0:T(8,128)(2,1)S(1)}, bf16[256,128]{1,0:T(8,128)(2,1)S(1)}, u32[]{:S(2)}, u32[]{:S(2)}) collective-permute-start(bf16[256,128]{1,0:T(8,128)(2,1)S(1)} %get-tuple-element.66), channel_id=1, source_target_pairs={{0,4},{4,8},{8,12},{12,16},{16,20},{20,24},{24,28},{6,2},{10,6},{1... | collective-permute-start | bytes 196616 | tf_op jit(solution)/shard_map/ppermute | solution.py:531
  14.7 2.1 %collective-permute-start.7 = (bf16[2,256,128]{2,1,0:T(8,128)(2,1)S(1)}, bf16[2,256,128]{2,1,0:T(8,128)(2,1)S(1)}, u32[]{:S(2)}, u32[]{:S(2)}) collective-permute-start(bf16[2,256,128]{2,1,0:T(8,128)(2,1)S(1)} %get-tuple-element.58.pair_cot), channel_id=1, source_target_pairs={{0,2},{2,0},{4,6},{6,4},{8,10},{10,8},{12,14},{14,12},{16,18},{18,... | collective-permute-start | bytes 393224 | tf_op jit(solution)/shard_map/ppermute | solution.py:467
  15.5 1.6 %collective-permute-start.2 = (bf16[256,256]{1,0:T(8,128)(2,1)S(1)}, bf16[256,256]{1,0:T(8,128)(2,1)S(1)}, u32[]{:S(2)}, u32[]{:S(2)}) collective-permute-start(bf16[256,256]{1,0:T(8,128)(2,1)S(1)} %collective-permute-done.1.mate1), channel_id=1, source_target_pairs={{0,2},{2,0},{4,6},{6,4},{8,10},{10,8},{12,14},{14,12},{16,18},{18,... | collective-permute-start | bytes 393224 | tf_op jit(solution)/shard_map/ppermute | solution.py:467
  19.5 1.3 %collective-permute-start.9 = (bf16[2,128,128]{2,1,0:T(8,128)(2,1)S(1)}, bf16[2,128,128]{2,1,0:T(8,128)(2,1)S(1)}, u32[]{:S(2)}, u32[]{:S(2)}) collective-permute-start(bf16[2,128,128]{2,1,0:T(8,128)(2,1)S(1)} %get-tuple-element.82), channel_id=1, source_target_pairs={{0,2},{2,0},{4,6},{6,4},{8,10},{10,8},{12,14},{14,12},{16,18},{18,... | collective-permute-start | bytes 196616 | tf_op jit(solution)/shard_map/ppermute | solution.py:467
  20.8 7.6 %collective-permute-start.10 = (bf16[560,128]{1,0:T(8,128)(2,1)S(1)}, bf16[560,128]{1,0:T(8,128)(2,1)S(1)}, u32[]{:S(2)}, u32[]{:S(2)}) collective-permute-start(bf16[560,128]{1,0:T(8,128)(2,1)S(1)} %pad_maximum_fusion), channel_id=1, source_target_pairs={{0,8},{2,10},{4,12},{6,14},{8,0},{10,2},{12,4},{14,6},{16,24},{18,... | collective-permute-start | bytes 430088 | tf_op jit(solution)/shard_map/ppermute | solution.py:467
  23.9 7.9 %collective-permute-start.12 = (bf16[560,128]{1,0:T(8,128)(2,1)S(1)}, bf16[560,128]{1,0:T(8,128)(2,1)S(1)}, u32[]{:S(2)}, u32[]{:S(2)}) collective-permute-start(bf16[560,128]{1,0:T(8,128)(2,1)S(1)} %pad_maximum_fusion.1), channel_id=1, source_target_pairs={{0,12},{2,14},{4,8},{6,10},{8,4},{10,6},{12,0},{14,2},{16,28},{18,... | collective-permute-start | bytes 430088 | tf_op jit(solution)/shard_map/ppermute | solution.py:467
  24.9 8.3 %collective-permute-start.11 = (bf16[560,128]{1,0:T(8,128)(2,1)S(1)}, bf16[560,128]{1,0:T(8,128)(2,1)S(1)}, u32[]{:S(2)}, u32[]{:S(2)}) collective-permute-start(bf16[560,128]{1,0:T(8,128)(2,1)S(1)} %pad_maximum_fusion.1), channel_id=1, source_target_pairs={{0,4},{2,6},{4,0},{6,2},{8,12},{10,14},{12,8},{14,10},{16,20},{18,... | collective-permute-start | bytes 430088 | tf_op jit(solution)/shard_map/ppermute | solution.py:467
  33.3 8.7 %collective-permute-start.13 = (bf16[560,128]{1,0:T(8,128)(2,1)S(1)}, bf16[560,128]{1,0:T(8,128)(2,1)S(1)}, u32[]{:S(2)}, u32[]{:S(2)}) collective-permute-start(bf16[560,128]{1,0:T(8,128)(2,1)S(1)} %add_convert_fusion.1), channel_id=1, source_target_pairs={{0,16},{2,18},{4,20},{6,22},{8,24},{10,26},{12,28},{14,30},{16,0},... | collective-permute-start | bytes 430088 | tf_op jit(solution)/shard_map/ppermute | solution.py:467
  42.1 7.2 %collective-permute-start.19 = (bf16[560,128]{1,0:T(8,128)(2,1)S(1)}, bf16[560,128]{1,0:T(8,128)(2,1)S(1)}, u32[]{:S(2)}, u32[]{:S(2)}) collective-permute-start(bf16[560,128]{1,0:T(8,128)(2,1)S(1)} %add_convert_fusion.refs_0_), channel_id=1, source_target_pairs={{0,5},{1,4},{2,7},{3,6},{4,1},{5,0},{6,3},{7,2},{8,13},{9,12},{10,... | collective-permute-start | bytes 430088 | tf_op jit(solution)/shard_map/ppermute | solution.py:628
  43.7 6.4 %collective-permute-start.17 = (bf16[560,128]{1,0:T(8,128)(2,1)S(1)}, bf16[560,128]{1,0:T(8,128)(2,1)S(1)}, u32[]{:S(2)}, u32[]{:S(2)}) collective-permute-start(bf16[560,128]{1,0:T(8,128)(2,1)S(1)} %add_convert_fusion.refs_0_), channel_id=1, source_target_pairs={{0,1},{1,0},{2,3},{3,2},{4,5},{5,4},{6,7},{7,6},{8,9},{9,8},{10,11... | collective-permute-start | bytes 430088 | tf_op jit(solution)/shard_map/ppermute | solution.py:470
  44.5 6.2 %collective-permute-start.15 = (bf16[560,128]{1,0:T(8,128)(2,1)S(1)}, bf16[560,128]{1,0:T(8,128)(2,1)S(1)}, u32[]{:S(2)}, u32[]{:S(2)}) collective-permute-start(bf16[560,128]{1,0:T(8,128)(2,1)S(1)} %add_convert_fusion.refs_0_), channel_id=1, source_target_pairs={{0,4},{2,6},{4,0},{6,2},{8,12},{10,14},{12,8},{14,10},{16,20},{18,... | collective-permute-start | bytes 430088 | tf_op jit(solution)/shard_map/ppermute | solution.py:467
  45.6 6.2 %collective-permute-start.14 = (bf16[560,128]{1,0:T(8,128)(2,1)S(1)}, bf16[560,128]{1,0:T(8,128)(2,1)S(1)}, u32[]{:S(2)}, u32[]{:S(2)}) collective-permute-start(bf16[560,128]{1,0:T(8,128)(2,1)S(1)} %add_convert_fusion.refs_0_), channel_id=1, source_target_pairs={{0,2},{2,0},{4,6},{6,4},{8,10},{10,8},{12,14},{14,12},{16,18},{18,... | collective-permute-start | bytes 430088 | tf_op jit(solution)/shard_map/ppermute | solution.py:467
  49.3 2.5 %collective-permute-start.20 = (bf16[560,128]{1,0:T(8,128)(2,1)S(1)}, bf16[560,128]{1,0:T(8,128)(2,1)S(1)}, u32[]{:S(2)}, u32[]{:S(2)}) collective-permute-start(bf16[560,128]{1,0:T(8,128)(2,1)S(1)} %collective-permute-done.19.refs_3_), channel_id=1, source_target_pairs={{0,2},{2,0},{4,6},{6,4},{8,10},{10,8},{12,14},{14,12},{16,18},{18,... | collective-permute-start | bytes 430088 | tf_op jit(solution)/shard_map/ppermute | solution.py:467
  50.1 1.7 %collective-permute-start.18 = (bf16[560,128]{1,0:T(8,128)(2,1)S(1)}, bf16[560,128]{1,0:T(8,128)(2,1)S(1)}, u32[]{:S(2)}, u32[]{:S(2)}) collective-permute-start(bf16[560,128]{1,0:T(8,128)(2,1)S(1)} %collective-permute-done.17.refs_2_), channel_id=1, source_target_pairs={{0,2},{2,0},{4,6},{6,4},{8,10},{10,8},{12,14},{14,12},{16,18},{18,... | collective-permute-start | bytes 430088 | tf_op jit(solution)/shard_map/ppermute | solution.py:467
  50.7 1.4 %collective-permute-start.16 = (bf16[560,128]{1,0:T(8,128)(2,1)S(1)}, bf16[560,128]{1,0:T(8,128)(2,1)S(1)}, u32[]{:S(2)}, u32[]{:S(2)}) collective-permute-start(bf16[560,128]{1,0:T(8,128)(2,1)S(1)} %collective-permute-done.15.refs_1_), channel_id=1, source_target_pairs={{0,2},{2,0},{4,6},{6,4},{8,10},{10,8},{12,14},{14,12},{16,18},{18,... | collective-permute-start | bytes 430088 | tf_op jit(solution)/shard_map/ppermute | solution.py:467
  (2 other events, 1.9 us)

commit v12 on v11

--- a/solution.py
+++ b/solution.py
@@ -418,13 +418,12 @@
             )
     send(3, projection_block, outs[0].at[half_of(VAL // 2), :])
     step = CONV // PARTS
-    for which, piece in enumerate(pieces):
-        for tap in range(9):
-            begin = FIRST_ROWS + tap * step
-            second_block[tap // 3, tap % 3, rows_of(which, step), :] = (
-                piece[begin : begin + step, :].astype(F32) * factor
-            )
-    send(4, second_block, outs[2].at[:, :, half_of(CONV // 2), :])
+    for a in range(3):
+        for which, piece in enumerate(pieces):
+            for b in range(3):
+                begin = FIRST_ROWS + (3 * a + b) * step
+                second_block[a, b, rows_of(which, step), :] = piece[begin : begin + step, :].astype(F32) * factor
+        send(4 + a, second_block.at[a], outs[2].at[a, :, half_of(CONV // 2), :])
     for copy in copies:
         copy.wait()
 
@@ -437,7 +436,7 @@
         in_specs=[VMEM] * 4 + [HBM] * len(into),
         out_specs=[HBM] * 3,
         scratch_shapes=[pltpu.VMEM(size[:-2] + (size[-2] // 2, size[-1]), F32) for size in dims]
-        + [pltpu.SemaphoreType.DMA((5,))],
+        + [pltpu.SemaphoreType.DMA((7,))],
         input_output_aliases={4 + i: i for i in range(len(into))},
         cost_estimate=pl.CostEstimate(flops=10**9, bytes_accessed=4 * 1024 * 1024, transcendentals=0),
         name="unpack_sums",

time: 53.3 us -> 53.3 us (level)
  no operation moved by 1% of the time
where the time goes in v12:
time: 53.3 us; the launch traced here: 53.2 us
  starting transfers between devices  20.6 us (39%)
  waiting for transfers between devices  19 us (36%)
  Pallas kernels  10.6 us (20%)
  local copies, waits for them, and re-layouts  1.87 us (4%)
  between operations  0.89 us (2%)
    ppermute x13, waiting for transfers between devices, rows_flip(): lax.ppermute(values, 'rows', [(i, i ^ bit) for i in range(rows_size)])  13.9 us
    ppermute x13, starting transfers between devices, rows_flip(): lax.ppermute(values, 'rows', [(i, i ^ bit) for i in range(rows_size)])  9.58 us
    pallas_call x12, Pallas kernels, call(): pl.pallas_call(kernel, out_shape=out_shape, in_specs=[VMEM] * len(operand...  8.24 us
    ppermute x3, starting transfers between devices, cols_flip(): return lax.ppermute(values, 'cols', [(i, i ^ 1) for i in range(cols_size)])  5.25 us
    ppermute x1, waiting for transfers between devices, body(): lax.ppermute(total, ('rows', 'cols'), [(i * cols_size + j, (i ^ 2) * cols...  3.65 us
    pallas_call x2, Pallas kernels, unpack(): pl.pallas_call(functools.partial(unpack_kernel, factor, core_flip), out_s...  2.17 us
    ppermute x1, starting transfers between devices, body(): out_cot = lax.ppermute(cotangent, 'rows', out)  2.02 us
    unnamed x10, local copies, waits for them, and re-layouts  1.86 us
  transfers between devices with their start and end apart: 21, of which 10 were waited for; matrix products, arithmetic and copies ran while one was open for 0% of the time, Pallas kernels for 14%

profile of v12, /device:TPU:0, one launch (start us, length us, event | category | flops | bytes accessed | tf_op | source)
XLA Modules:
  0.0 53.2 jit_solution(2983130192254452365)
XLA Ops:
  0.6 3.0 %collective-permute-start = (bf16[128,256]{1,0:T(8,128)(2,1)}, bf16[128,256]{1,0:T(8,128)(2,1)S(1)}, u32[]{:S(2)}, u32[]{:S(2)}) collective-permute-start(bf16[128,256]{1,0:T(8,128)(2,1)} %bitcast.8), channel_id=1, source_target_pairs={{0,1},{1,0},{2,3},{3,2},{4,5},{5,4},{6,7},{7,6},{8,9},{9,8},{10,11... | collective-permute-start | bytes 196616 | tf_op jit(solution)/shard_map/ppermute | solution.py:469
  3.6 2.0 %collective-permute-start.4 = (bf16[128,128]{1,0:T(8,128)(2,1)}, bf16[128,128]{1,0:T(8,128)(2,1)S(1)}, u32[]{:S(2)}, u32[]{:S(2)}) collective-permute-start(bf16[128,128]{1,0:T(8,128)(2,1)} %bitcast.11), channel_id=1, source_target_pairs={{0,4},{4,8},{8,12},{12,16},{16,20},{20,24},{24,28},{6,2},{10,6},{1... | collective-permute-start | bytes 98312 | tf_op jit(solution)/shard_map/ppermute | solution.py:496
  5.7 0.9 %copy-done.2 = bf16[256,512]{1,0:T(8,128)(2,1)S(1)} copy-done((bf16[256,512]{1,0:T(8,128)(2,1)S(1)}, bf16[256,512]{1,0:T(8,128)(2,1)}, u32[]{:S(2)}) %copy-start.2) | copy-done | bytes 262168
  6.7 0.9 %copy-done.3 = bf16[1,128,256]{2,1,0:T(8,128)(2,1)S(1)} copy-done((bf16[1,128,256]{2,1,0:T(8,128)(2,1)S(1)}, bf16[1,128,256]{2,1,0:T(8,128)(2,1)}, u32[]{:S(2)}) %copy-start.3) | copy-done | bytes 65560
  7.6 1.3 %attention_forward.1 = (bf16[256,256]{1,0:T(8,128)(2,1)S(1)}, bf16[256,768]{1,0:T(8,128)(2,1)S(1)}, f32[16,256]{1,0:T(8,128)S(1)}) custom-call(bf16[128,256]{1,0:T(8,128)(2,1)S(1)} %bitcast.9, bf16[128,256]{1,0:T(8,128)(2,1)S(1)} %collective-permute-done.refs_1_, bf16[256,512]{1,0:T(8,128)(2,1)S(1)} %fetch.2.refs_2_.projection), custom_call_target="tpu_custom_call" | custom-call | flops 1000000000 | bytes 4000000 | tf_op jit(solution)/shard_map/attention_forward/pallas_call | solution.py:478
  9.8 1.4 %collective-permute-start.6 = (bf16[3,128,128]{2,1,0:T(8,128)(2,1)S(1)}, bf16[3,128,128]{2,1,0:T(8,128)(2,1)S(1)}, u32[]{:S(2)}, u32[]{:S(2)}) collective-permute-start(bf16[3,128,128]{2,1,0:T(8,128)(2,1)S(1)} %get-tuple-element.56.refs_0_), channel_id=1, source_target_pairs={{0,1},{1,0},{2,3},{3,2},{4,5},{5,4},{6,7},{7,6},{8,9},{9,8},{10,11... | collective-permute-start | bytes 294920 | tf_op jit(solution)/shard_map/ppermute | solution.py:469
  11.2 1.6 %collective-permute-start.8 = (bf16[256,128]{1,0:T(8,128)(2,1)S(1)}, bf16[256,128]{1,0:T(8,128)(2,1)S(1)}, u32[]{:S(2)}, u32[]{:S(2)}) collective-permute-start(bf16[256,128]{1,0:T(8,128)(2,1)S(1)} %get-tuple-element.66), channel_id=1, source_target_pairs={{0,4},{4,8},{8,12},{12,16},{16,20},{20,24},{24,28},{6,2},{10,6},{1... | collective-permute-start | bytes 196616 | tf_op jit(solution)/shard_map/ppermute | solution.py:530
  14.7 0.9 %collective-permute-start.7 = (bf16[2,256,128]{2,1,0:T(8,128)(2,1)S(1)}, bf16[2,256,128]{2,1,0:T(8,128)(2,1)S(1)}, u32[]{:S(2)}, u32[]{:S(2)}) collective-permute-start(bf16[2,256,128]{2,1,0:T(8,128)(2,1)S(1)} %get-tuple-element.58.pair_cot), channel_id=1, source_target_pairs={{0,2},{2,0},{4,6},{6,4},{8,10},{10,8},{12,14},{14,12},{16,18},{18,... | collective-permute-start | bytes 393224 | tf_op jit(solution)/shard_map/ppermute | solution.py:466
  17.1 2.3 %block_backward.1 = (bf16[256,256]{1,0:T(8,128)(2,1)S(1)}, bf16[256,256]{1,0:T(8,128)(2,1)S(1)}, bf16[512,256]{1,0:T(8,128)(2,1)S(1)}, bf16[2,128,128]{2,1,0:T(8,128)(2,1)S(1)}, bf16[2,128,128]{2,1,0:T(8,128)(2,1)S(1)}) custom-call(bf16[256,256]{1,0:T(8,128)(2,1)S(1)} %collective-permute-done.2.near, ...), custom_call_target="tpu_custom_call" | custom-call | flops 1000000000 | bytes 4000000 | tf_op jit(solution)/shard_map/block_backward/pallas_call | solution.py:478
  20.8 3.0 %collective-permute-start.10 = (bf16[560,128]{1,0:T(8,128)(2,1)S(1)}, bf16[560,128]{1,0:T(8,128)(2,1)S(1)}, u32[]{:S(2)}, u32[]{:S(2)}) collective-permute-start(bf16[560,128]{1,0:T(8,128)(2,1)S(1)} %pad_maximum_fusion), channel_id=1, source_target_pairs={{0,8},{2,10},{4,12},{6,14},{8,0},{10,2},{12,4},{14,6},{16,24},{18,... | collective-permute-start | bytes 430088 | tf_op jit(solution)/shard_map/ppermute | solution.py:466
  23.9 1.0 %collective-permute-start.12 = (bf16[560,128]{1,0:T(8,128)(2,1)S(1)}, bf16[560,128]{1,0:T(8,128)(2,1)S(1)}, u32[]{:S(2)}, u32[]{:S(2)}) collective-permute-start(bf16[560,128]{1,0:T(8,128)(2,1)S(1)} %pad_maximum_fusion.1), channel_id=1, source_target_pairs={{0,12},{2,14},{4,8},{6,10},{8,4},{10,6},{12,0},{14,2},{16,28},{18,... | collective-permute-start | bytes 430088 | tf_op jit(solution)/shard_map/ppermute | solution.py:466
  25.4 3.0 %collective-permute-done.10 = bf16[560,128]{1,0:T(8,128)(2,1)S(1)} collective-permute-done((bf16[560,128]{1,0:T(8,128)(2,1)S(1)}, bf16[560,128]{1,0:T(8,128)(2,1)S(1)}, u32[]{:S(2)}, u32[]{:S(2)}) %collective-permute-start.10) | collective-permute-done | bytes 143392 | tf_op jit(solution)/shard_map/ppermute | solution.py:466
  28.4 3.4 %collective-permute-done.12 = bf16[560,128]{1,0:T(8,128)(2,1)S(1)} collective-permute-done((bf16[560,128]{1,0:T(8,128)(2,1)S(1)}, bf16[560,128]{1,0:T(8,128)(2,1)S(1)}, u32[]{:S(2)}, u32[]{:S(2)}) %collective-permute-start.12) | collective-permute-done | bytes 143392 | tf_op jit(solution)/shard_map/ppermute | solution.py:466
  31.8 1.4 %collective-permute-done.11 = bf16[560,128]{1,0:T(8,128)(2,1)S(1)} collective-permute-done((bf16[560,128]{1,0:T(8,128)(2,1)S(1)}, bf16[560,128]{1,0:T(8,128)(2,1)S(1)}, u32[]{:S(2)}, u32[]{:S(2)}) %collective-permute-start.11) | collective-permute-done | bytes 143392 | tf_op jit(solution)/shard_map/ppermute | solution.py:466
  33.3 2.6 %collective-permute-start.13 = (bf16[560,128]{1,0:T(8,128)(2,1)S(1)}, bf16[560,128]{1,0:T(8,128)(2,1)S(1)}, u32[]{:S(2)}, u32[]{:S(2)}) collective-permute-start(bf16[560,128]{1,0:T(8,128)(2,1)S(1)} %add_convert_fusion.1), channel_id=1, source_target_pairs={{0,16},{2,18},{4,20},{6,22},{8,24},{10,26},{12,28},{14,30},{16,0},... | collective-permute-start | bytes 430088 | tf_op jit(solution)/shard_map/ppermute | solution.py:466
  36.0 1.2 %outputs.1 = (bf16[128,128]{1,0:T(8,128)(2,1)}, bf16[128,256]{1,0:T(8,128)(2,1)}) custom-call(bf16[256,256]{1,0:T(8,128)(2,1)S(1)} %get-tuple-element.84.near_mid, bf16[256,256]{1,0:T(8,128)(2,1)S(1)} %get-tuple-element.79.own_mid, bf16[256,256]{1,0:T(8,128)(2,1)S(1)} %get-tuple-element.65.mate_mid, bf16[512,256]{1,0:T(8,128)(2,1)S(1)} %get-tuple-element.85.grad, ...), custom_call_target="tpu_custom_call" | custom-call | flops 1000000000 | bytes 4000000 | tf_op jit(solution)/shard_map/outputs/pallas_call | solution.py:478
  37.1 4.9 %collective-permute-done.13 = bf16[560,128]{1,0:T(8,128)(2,1)S(1)} collective-permute-done((bf16[560,128]{1,0:T(8,128)(2,1)S(1)}, bf16[560,128]{1,0:T(8,128)(2,1)S(1)}, u32[]{:S(2)}, u32[]{:S(2)}) %collective-permute-start.13) | collective-permute-done | bytes 143392 | tf_op jit(solution)/shard_map/ppermute | solution.py:466
  42.1 1.6 %collective-permute-start.19 = (bf16[560,128]{1,0:T(8,128)(2,1)S(1)}, bf16[560,128]{1,0:T(8,128)(2,1)S(1)}, u32[]{:S(2)}, u32[]{:S(2)}) collective-permute-start(bf16[560,128]{1,0:T(8,128)(2,1)S(1)} %add_convert_fusion.refs_0_), channel_id=1, source_target_pairs={{0,5},{1,4},{2,7},{3,6},{4,1},{5,0},{6,3},{7,2},{8,13},{9,12},{10,... | collective-permute-start | bytes 430088 | tf_op jit(solution)/shard_map/ppermute | solution.py:627
  43.7 0.8 %collective-permute-start.17 = (bf16[560,128]{1,0:T(8,128)(2,1)S(1)}, bf16[560,128]{1,0:T(8,128)(2,1)S(1)}, u32[]{:S(2)}, u32[]{:S(2)}) collective-permute-start(bf16[560,128]{1,0:T(8,128)(2,1)S(1)} %add_convert_fusion.refs_0_), channel_id=1, source_target_pairs={{0,1},{1,0},{2,3},{3,2},{4,5},{5,4},{6,7},{7,6},{8,9},{9,8},{10,11... | collective-permute-start | bytes 430088 | tf_op jit(solution)/shard_map/ppermute | solution.py:469
  44.5 1.1 %collective-permute-start.15 = (bf16[560,128]{1,0:T(8,128)(2,1)S(1)}, bf16[560,128]{1,0:T(8,128)(2,1)S(1)}, u32[]{:S(2)}, u32[]{:S(2)}) collective-permute-start(bf16[560,128]{1,0:T(8,128)(2,1)S(1)} %add_convert_fusion.refs_0_), channel_id=1, source_target_pairs={{0,4},{2,6},{4,0},{6,2},{8,12},{10,14},{12,8},{14,10},{16,20},{18,... | collective-permute-start | bytes 430088 | tf_op jit(solution)/shard_map/ppermute | solution.py:466
  45.6 3.7 %collective-permute-done.19.refs_3_ = bf16[560,128]{1,0:T(8,128)(2,1)S(1)} collective-permute-done((bf16[560,128]{1,0:T(8,128)(2,1)S(1)}, bf16[560,128]{1,0:T(8,128)(2,1)S(1)}, u32[]{:S(2)}, u32[]{:S(2)}) %collective-permute-start.19) | collective-permute-done | bytes 143392 | tf_op jit(solution)/shard_map/ppermute | solution.py:627
  49.3 0.8 %collective-permute-done.17.refs_2_ = bf16[560,128]{1,0:T(8,128)(2,1)S(1)} collective-permute-done((bf16[560,128]{1,0:T(8,128)(2,1)S(1)}, bf16[560,128]{1,0:T(8,128)(2,1)S(1)}, u32[]{:S(2)}, u32[]{:S(2)}) %collective-permute-start.17) | collective-permute-done | bytes 143392 | tf_op jit(solution)/shard_map/ppermute | solution.py:469
  50.7 1.1 %unpack_sums.2 = (f32[256,512]{1,0:T(8,128)}, f32[3,3,256,128]{3,2,1,0:T(8,128)}, f32[3,3,128,128]{3,2,1,0:T(8,128)}) custom-call(bf16[560,128]{1,0:T(8,128)(2,1)S(1)} %add_convert_fusion.refs_0_, bf16[560,128]{1,0:T(8,128)(2,1)S(1)} %collective-permute-done.15.refs_1_, bf16[560,128]{1,0:T(8,128)(2,1)S(1)} %collective-permute-done.17.refs_2_, ...), custom_call_target="tpu_custom_call" | custom-call | flops 1000000000 | bytes 4194304 | tf_op jit(solution)/shard_map/unpack_sums/pallas_call | solution.py:433
  52.1 1.1 %unpack_sums.3 = (f32[256,512]{1,0:T(8,128)}, f32[3,3,256,128]{3,2,1,0:T(8,128)}, f32[3,3,128,128]{3,2,1,0:T(8,128)}) custom-call(bf16[560,128]{1,0:T(8,128)(2,1)S(1)} %collective-permute-done.14.refs_0_, bf16[560,128]{1,0:T(8,128)(2,1)S(1)} %collective-permute-done.16.refs_1_, ...), custom_call_target="tpu_custom_call", output_to_operand_aliasing={{0}: (4, {}), {1}: (5, {}), {2}: (6, {})} | custom-call | flops 1000000000 | bytes 4194304 | tf_op jit(solution)/shard_map/unpack_sums/pallas_call | solution.py:433
  (50 shorter events, 7.1 us)
Async XLA Ops:
  0.6 6.0 %collective-permute-start = (bf16[128,256]{1,0:T(8,128)(2,1)}, bf16[128,256]{1,0:T(8,128)(2,1)S(1)}, u32[]{:S(2)}, u32[]{:S(2)}) collective-permute-start(bf16[128,256]{1,0:T(8,128)(2,1)} %bitcast.8), channel_id=1, source_target_pairs={{0,1},{1,0},{2,3},{3,2},{4,5},{5,4},{6,7},{7,6},{8,9},{9,8},{10,11... | collective-permute-start | bytes 196616 | tf_op jit(solution)/shard_map/ppermute | solution.py:469
  3.6 5.9 %collective-permute-start.5 = (bf16[128,128]{1,0:T(8,128)(2,1)}, bf16[128,128]{1,0:T(8,128)(2,1)S(1)}, u32[]{:S(2)}, u32[]{:S(2)}) collective-permute-start(bf16[128,128]{1,0:T(8,128)(2,1)} %bitcast.10), channel_id=1, source_target_pairs={{4,0},{8,4},{12,8},{16,12},{20,16},{24,20},{28,24},{2,6},{6,10},{1... | collective-permute-start | bytes 98312 | tf_op jit(solution)/shard_map/ppermute | solution.py:497
  3.6 5.9 %collective-permute-start.4 = (bf16[128,128]{1,0:T(8,128)(2,1)}, bf16[128,128]{1,0:T(8,128)(2,1)S(1)}, u32[]{:S(2)}, u32[]{:S(2)}) collective-permute-start(bf16[128,128]{1,0:T(8,128)(2,1)} %bitcast.11), channel_id=1, source_target_pairs={{0,4},{4,8},{8,12},{12,16},{16,20},{20,24},{24,28},{6,2},{10,6},{1... | collective-permute-start | bytes 98312 | tf_op jit(solution)/shard_map/ppermute | solution.py:496
  6.6 2.9 %copy-start = (bf16[3,3,256,128]{3,2,1,0:T(8,128)(2,1)S(1)}, bf16[3,3,256,128]{3,2,1,0:T(8,128)(2,1)}, u32[]{:S(2)}) copy-start(bf16[3,3,256,128]{3,2,1,0:T(8,128)(2,1)} %refs_0_.3) | copy-start | bytes 1769476
  7.6 1.9 %copy-start.4 = (bf16[1,128,128]{2,1,0:T(8,128)(2,1)S(1)}, bf16[1,128,128]{2,1,0:T(8,128)(2,1)}, u32[]{:S(2)}) copy-start(bf16[1,128,128]{2,1,0:T(8,128)(2,1)} %param.9) | copy-start | bytes 98308
  8.9 3.9 %copy-start.1 = (bf16[3,3,128,128]{3,2,1,0:T(8,128)(2,1)S(1)}, bf16[3,3,128,128]{3,2,1,0:T(8,128)(2,1)}, u32[]{:S(2)}) copy-start(bf16[3,3,128,128]{3,2,1,0:T(8,128)(2,1)} %refs_1_.1) | copy-start | bytes 884740
  8.9 5.2 %collective-permute-start.3 = (bf16[256,256]{1,0:T(8,128)(2,1)S(1)}, bf16[256,256]{1,0:T(8,128)(2,1)S(1)}, u32[]{:S(2)}, u32[]{:S(2)}) collective-permute-start(bf16[256,256]{1,0:T(8,128)(2,1)S(1)} %get-tuple-element.51.attended.own), channel_id=1, source_target_pairs={{0,2},{2,0},{4,6},{6,4},{8,10},{10,8},{12,14},{14,12},{16,18},{18,... | collective-permute-start | bytes 393224 | tf_op jit(solution)/shard_map/ppermute | solution.py:466
  9.0 6.5 %collective-permute-start.1 = (bf16[256,256]{1,0:T(8,128)(2,1)S(1)}, bf16[256,256]{1,0:T(8,128)(2,1)S(1)}, u32[]{:S(2)}, u32[]{:S(2)}) collective-permute-start(bf16[256,256]{1,0:T(8,128)(2,1)S(1)} %get-tuple-element.51.attended.own), channel_id=1, source_target_pairs={{4,0},{8,4},{12,8},{16,12},{20,16},{24,20},{28,24},{2,6},{6,10},{1... | collective-permute-start | bytes 393224 | tf_op jit(solution)/shard_map/ppermute | solution.py:525
  9.8 4.8 %collective-permute-start.6 = (bf16[3,128,128]{2,1,0:T(8,128)(2,1)S(1)}, bf16[3,128,128]{2,1,0:T(8,128)(2,1)S(1)}, u32[]{:S(2)}, u32[]{:S(2)}) collective-permute-start(bf16[3,128,128]{2,1,0:T(8,128)(2,1)S(1)} %get-tuple-element.56.refs_0_), channel_id=1, source_target_pairs={{0,1},{1,0},{2,3},{3,2},{4,5},{5,4},{6,7},{7,6},{8,9},{9,8},{10,11... | collective-permute-start | bytes 294920 | tf_op jit(solution)/shard_map/ppermute | solution.py:469
  11.2 5.1 %collective-permute-start.8 = (bf16[256,128]{1,0:T(8,128)(2,1)S(1)}, bf16[256,128]{1,0:T(8,128)(2,1)S(1)}, u32[]{:S(2)}, u32[]{:S(2)}) collective-permute-start(bf16[256,128]{1,0:T(8,128)(2,1)S(1)} %get-tuple-element.66), channel_id=1, source_target_pairs={{0,4},{4,8},{8,12},{12,16},{16,20},{20,24},{24,28},{6,2},{10,6},{1... | collective-permute-start | bytes 196616 | tf_op jit(solution)/shard_map/ppermute | solution.py:530
  14.7 2.1 %collective-permute-start.7 = (bf16[2,256,128]{2,1,0:T(8,128)(2,1)S(1)}, bf16[2,256,128]{2,1,0:T(8,128)(2,1)S(1)}, u32[]{:S(2)}, u32[]{:S(2)}) collective-permute-start(bf16[2,256,128]{2,1,0:T(8,128)(2,1)S(1)} %get-tuple-element.58.pair_cot), channel_id=1, source_target_pairs={{0,2},{2,0},{4,6},{6,4},{8,10},{10,8},{12,14},{14,12},{16,18},{18,... | collective-permute-start | bytes 393224 | tf_op jit(solution)/shard_map/ppermute | solution.py:466
  15.5 1.6 %collective-permute-start.2 = (bf16[256,256]{1,0:T(8,128)(2,1)S(1)}, bf16[256,256]{1,0:T(8,128)(2,1)S(1)}, u32[]{:S(2)}, u32[]{:S(2)}) collective-permute-start(bf16[256,256]{1,0:T(8,128)(2,1)S(1)} %collective-permute-done.1.mate1), channel_id=1, source_target_pairs={{0,2},{2,0},{4,6},{6,4},{8,10},{10,8},{12,14},{14,12},{16,18},{18,... | collective-permute-start | bytes 393224 | tf_op jit(solution)/shard_map/ppermute | solution.py:466
  19.5 1.3 %collective-permute-start.9 = (bf16[2,128,128]{2,1,0:T(8,128)(2,1)S(1)}, bf16[2,128,128]{2,1,0:T(8,128)(2,1)S(1)}, u32[]{:S(2)}, u32[]{:S(2)}) collective-permute-start(bf16[2,128,128]{2,1,0:T(8,128)(2,1)S(1)} %get-tuple-element.82), channel_id=1, source_target_pairs={{0,2},{2,0},{4,6},{6,4},{8,10},{10,8},{12,14},{14,12},{16,18},{18,... | collective-permute-start | bytes 196616 | tf_op jit(solution)/shard_map/ppermute | solution.py:466
  20.8 7.6 %collective-permute-start.10 = (bf16[560,128]{1,0:T(8,128)(2,1)S(1)}, bf16[560,128]{1,0:T(8,128)(2,1)S(1)}, u32[]{:S(2)}, u32[]{:S(2)}) collective-permute-start(bf16[560,128]{1,0:T(8,128)(2,1)S(1)} %pad_maximum_fusion), channel_id=1, source_target_pairs={{0,8},{2,10},{4,12},{6,14},{8,0},{10,2},{12,4},{14,6},{16,24},{18,... | collective-permute-start | bytes 430088 | tf_op jit(solution)/shard_map/ppermute | solution.py:466
  23.9 7.9 %collective-permute-start.12 = (bf16[560,128]{1,0:T(8,128)(2,1)S(1)}, bf16[560,128]{1,0:T(8,128)(2,1)S(1)}, u32[]{:S(2)}, u32[]{:S(2)}) collective-permute-start(bf16[560,128]{1,0:T(8,128)(2,1)S(1)} %pad_maximum_fusion.1), channel_id=1, source_target_pairs={{0,12},{2,14},{4,8},{6,10},{8,4},{10,6},{12,0},{14,2},{16,28},{18,... | collective-permute-start | bytes 430088 | tf_op jit(solution)/shard_map/ppermute | solution.py:466
  24.9 8.3 %collective-permute-start.11 = (bf16[560,128]{1,0:T(8,128)(2,1)S(1)}, bf16[560,128]{1,0:T(8,128)(2,1)S(1)}, u32[]{:S(2)}, u32[]{:S(2)}) collective-permute-start(bf16[560,128]{1,0:T(8,128)(2,1)S(1)} %pad_maximum_fusion.1), channel_id=1, source_target_pairs={{0,4},{2,6},{4,0},{6,2},{8,12},{10,14},{12,8},{14,10},{16,20},{18,... | collective-permute-start | bytes 430088 | tf_op jit(solution)/shard_map/ppermute | solution.py:466
  33.3 8.7 %collective-permute-start.13 = (bf16[560,128]{1,0:T(8,128)(2,1)S(1)}, bf16[560,128]{1,0:T(8,128)(2,1)S(1)}, u32[]{:S(2)}, u32[]{:S(2)}) collective-permute-start(bf16[560,128]{1,0:T(8,128)(2,1)S(1)} %add_convert_fusion.1), channel_id=1, source_target_pairs={{0,16},{2,18},{4,20},{6,22},{8,24},{10,26},{12,28},{14,30},{16,0},... | collective-permute-start | bytes 430088 | tf_op jit(solution)/shard_map/ppermute | solution.py:466
  42.1 7.2 %collective-permute-start.19 = (bf16[560,128]{1,0:T(8,128)(2,1)S(1)}, bf16[560,128]{1,0:T(8,128)(2,1)S(1)}, u32[]{:S(2)}, u32[]{:S(2)}) collective-permute-start(bf16[560,128]{1,0:T(8,128)(2,1)S(1)} %add_convert_fusion.refs_0_), channel_id=1, source_target_pairs={{0,5},{1,4},{2,7},{3,6},{4,1},{5,0},{6,3},{7,2},{8,13},{9,12},{10,... | collective-permute-start | bytes 430088 | tf_op jit(solution)/shard_map/ppermute | solution.py:627
  43.7 6.4 %collective-permute-start.17 = (bf16[560,128]{1,0:T(8,128)(2,1)S(1)}, bf16[560,128]{1,0:T(8,128)(2,1)S(1)}, u32[]{:S(2)}, u32[]{:S(2)}) collective-permute-start(bf16[560,128]{1,0:T(8,128)(2,1)S(1)} %add_convert_fusion.refs_0_), channel_id=1, source_target_pairs={{0,1},{1,0},{2,3},{3,2},{4,5},{5,4},{6,7},{7,6},{8,9},{9,8},{10,11... | collective-permute-start | bytes 430088 | tf_op jit(solution)/shard_map/ppermute | solution.py:469
  44.5 6.2 %collective-permute-start.15 = (bf16[560,128]{1,0:T(8,128)(2,1)S(1)}, bf16[560,128]{1,0:T(8,128)(2,1)S(1)}, u32[]{:S(2)}, u32[]{:S(2)}) collective-permute-start(bf16[560,128]{1,0:T(8,128)(2,1)S(1)} %add_convert_fusion.refs_0_), channel_id=1, source_target_pairs={{0,4},{2,6},{4,0},{6,2},{8,12},{10,14},{12,8},{14,10},{16,20},{18,... | collective-permute-start | bytes 430088 | tf_op jit(solution)/shard_map/ppermute | solution.py:466
  45.6 6.2 %collective-permute-start.14 = (bf16[560,128]{1,0:T(8,128)(2,1)S(1)}, bf16[560,128]{1,0:T(8,128)(2,1)S(1)}, u32[]{:S(2)}, u32[]{:S(2)}) collective-permute-start(bf16[560,128]{1,0:T(8,128)(2,1)S(1)} %add_convert_fusion.refs_0_), channel_id=1, source_target_pairs={{0,2},{2,0},{4,6},{6,4},{8,10},{10,8},{12,14},{14,12},{16,18},{18,... | collective-permute-start | bytes 430088 | tf_op jit(solution)/shard_map/ppermute | solution.py:466
  49.3 2.5 %collective-permute-start.20 = (bf16[560,128]{1,0:T(8,128)(2,1)S(1)}, bf16[560,128]{1,0:T(8,128)(2,1)S(1)}, u32[]{:S(2)}, u32[]{:S(2)}) collective-permute-start(bf16[560,128]{1,0:T(8,128)(2,1)S(1)} %collective-permute-done.19.refs_3_), channel_id=1, source_target_pairs={{0,2},{2,0},{4,6},{6,4},{8,10},{10,8},{12,14},{14,12},{16,18},{18,... | collective-permute-start | bytes 430088 | tf_op jit(solution)/shard_map/ppermute | solution.py:466
  50.1 1.7 %collective-permute-start.18 = (bf16[560,128]{1,0:T(8,128)(2,1)S(1)}, bf16[560,128]{1,0:T(8,128)(2,1)S(1)}, u32[]{:S(2)}, u32[]{:S(2)}) collective-permute-start(bf16[560,128]{1,0:T(8,128)(2,1)S(1)} %collective-permute-done.17.refs_2_), channel_id=1, source_target_pairs={{0,2},{2,0},{4,6},{6,4},{8,10},{10,8},{12,14},{14,12},{16,18},{18,... | collective-permute-start | bytes 430088 | tf_op jit(solution)/shard_map/ppermute | solution.py:466
  50.7 1.4 %collective-permute-start.16 = (bf16[560,128]{1,0:T(8,128)(2,1)S(1)}, bf16[560,128]{1,0:T(8,128)(2,1)S(1)}, u32[]{:S(2)}, u32[]{:S(2)}) collective-permute-start(bf16[560,128]{1,0:T(8,128)(2,1)S(1)} %collective-permute-done.15.refs_1_), channel_id=1, source_target_pairs={{0,2},{2,0},{4,6},{6,4},{8,10},{10,8},{12,14},{14,12},{16,18},{18,... | collective-permute-start | bytes 430088 | tf_op jit(solution)/shard_map/ppermute | solution.py:466
  (2 other events, 1.9 us)
